TPU v7x, 32 devices: a whole 2x2x4 slice. The times are simulated.
32 devices in a mesh: path: 4 (over x, core), shard: 8 (over z, y).
Axes of the slice: x: 2, y: 2, z: 4, core: 2. Of those that a mesh axis runs over, the one named last changes fastest.
Arguments:
- tokens: bfloat16 [384, 2048], P(('path', 'shard')), may hold values from -6 to 6
- routes: int32 [384, 1], P(('path', 'shard')), may hold values from 0 to 3; in each aligned block of 12 rows (0 to 11, 12 to 23, ...) at most 4 rows name the same one
- cotangent: bfloat16 [384, 2048], P(('path', 'shard')), may hold values from -6 to 6
- gains: bfloat16 [4, 2, 2048], P('path'), may hold values from 0.099609375 to 1.8984375
- w_in: bfloat16 [4, 2, 2048, 8192], P('path', None, None, 'shard'), may hold values from -0.125 to 0.125
- w_out: bfloat16 [4, 2, 8192, 2048], P('path', None, 'shard'), may hold values from -0.0625 to 0.0625
- partners: int32 [2, 4], replicated, may hold values from 0 to 3, as said below
Outputs:
- delta_in: bfloat16 [4, 2, 2048, 8192], P('path', None, None, 'shard')
- delta_out: bfloat16 [4, 2, 8192, 2048], P('path', None, 'shard')
Inputs may be any that keep to these rules, and one draw needn't show every extreme that they name: `routes`: in each device's block of 12 rows at most 4 rows name one path, and some path gets exactly 4 rows of some block. Each row pairs the paths: partners[l, partners[l, p]] = p and partners[l, p] != p.
All inputs are finite; a program needn't handle non-finite values.
Results may differ from a plain program's by a relative error of at most 0.03.
Values may be sent and summed in bfloat16 or wider, within the bound.
No kernel may reach another device: no remote copies, remote signals or barrier semaphores. Data moves between devices by JAX's collectives and lax.ppermute only.
A program may use at most 128 MiB of HBM per device.

v0:
```python
import jax
import jax.numpy as jnp
from jax import lax
from jax.sharding import PartitionSpec as P

SLOTS = 16


def norm_value(v, gain):
    return v * lax.rsqrt(jnp.mean(v * v, axis=-1, keepdims=True) + 1e-05) * gain.astype(jnp.float32)


def norm_pull(h, gain, grad):

    def value(v):
        return norm_value(v, gain)

    return jax.vjp(value, h.astype(jnp.float32))[1](grad)[0]


def gelu_pull(pre, grad):
    return jax.vjp(jax.nn.gelu, pre)[1](grad)[0]


def pair_mean(piece, table):
    paths = table.shape[0]
    pick = (table[:, None] == jnp.arange(paths, dtype=jnp.int32)[None, :]).astype(jnp.float32)
    values = piece.astype(jnp.float32)
    other = jnp.einsum("pq,qrc->prc", pick, values, precision=lax.Precision.HIGHEST)
    return ((values + other) * 0.5).astype(jnp.bfloat16)


def body(tokens, routes, cotangent, gains, w_in, w_out, partners):
    paths = lax.axis_size("path")
    slots = SLOTS
    cap = slots // paths
    width = tokens.shape[1]
    route = routes[:, 0]
    order = jnp.arange(route.shape[0], dtype=jnp.int32)
    same = (route[:, None] == route[None, :]) & (order[None, :] < order[:, None])
    rank = jnp.sum(same.astype(jnp.int32), axis=1)
    target = route * cap + rank
    select = (jnp.arange(slots, dtype=jnp.int32)[:, None] == target[None, :]).astype(jnp.bfloat16)
    packed_x = (
        jnp.dot(select, tokens, preferred_element_type=jnp.float32)
        .astype(jnp.bfloat16)
        .reshape(paths, cap, width)
    )
    packed_dy = (
        jnp.dot(select, cotangent, preferred_element_type=jnp.float32)
        .astype(jnp.bfloat16)
        .reshape(paths, cap, width)
    )
    got_x, got_dy = (
        lax.all_to_all(packed_x, "path", split_axis=0, concat_axis=0, tiled=True),
        lax.all_to_all(packed_dy, "path", split_axis=0, concat_axis=0, tiled=True),
    )
    own_x = got_x.reshape(slots, width)
    own_dy = got_dy.reshape(slots, width)
    full_x, full_dy = (
        lax.all_gather(own_x, "shard", axis=0, tiled=True),
        lax.all_gather(own_dy, "shard", axis=0, tiled=True),
    )
    gain_low = gains[0, 0]
    gain_high = gains[0, 1]
    wi_low = w_in[0, 0]
    wi_high = w_in[0, 1]
    wo_low = w_out[0, 0]
    wo_high = w_out[0, 1]
    hidden = wi_low.shape[1]
    scale = 1.0 / jnp.sqrt(jnp.float32(full_x.shape[0]))
    n1 = norm_value(full_x.astype(jnp.float32), gain_low).astype(jnp.bfloat16)
    a1 = jnp.dot(n1, wi_low, preferred_element_type=jnp.float32)
    u1 = jax.nn.gelu(a1).astype(jnp.bfloat16)
    part_low = jnp.dot(u1, wo_low, preferred_element_type=jnp.float32)
    mixed_own = lax.psum_scatter(
        part_low.astype(jnp.bfloat16), "shard", scatter_dimension=0, tiled=True
    ).astype(jnp.float32)
    h_own = (own_x.astype(jnp.float32) + mixed_own).astype(jnp.bfloat16)
    full_h = lax.all_gather(h_own, "shard", axis=0, tiled=True)
    n2 = norm_value(full_h.astype(jnp.float32), gain_high).astype(jnp.bfloat16)
    a2 = jnp.dot(n2, wi_high, preferred_element_type=jnp.float32)
    u2 = jax.nn.gelu(a2).astype(jnp.bfloat16)
    g_out2 = jnp.dot(u2.T, full_dy, preferred_element_type=jnp.float32)
    du2 = jnp.dot(full_dy, wo_high.T, preferred_element_type=jnp.float32)
    da2 = gelu_pull(a2, du2).astype(jnp.bfloat16)
    g_in2 = jnp.dot(n2.T, da2, preferred_element_type=jnp.float32)
    part_back = jnp.dot(da2, wi_high.T, preferred_element_type=jnp.float32)
    e_in2 = (-g_in2 * scale).astype(jnp.bfloat16).reshape(paths, width // paths, hidden)
    e_out2 = (-g_out2 * scale).astype(jnp.bfloat16).reshape(paths, width // paths, hidden)
    back_own = lax.psum_scatter(
        part_back.astype(jnp.bfloat16), "shard", scatter_dimension=0, tiled=True
    ).astype(jnp.float32)
    dh_own = (own_dy.astype(jnp.float32) + norm_pull(h_own, gain_high, back_own)).astype(
        jnp.bfloat16
    )
    full_dh = lax.all_gather(dh_own, "shard", axis=0, tiled=True)
    g_out1 = jnp.dot(u1.T, full_dh, preferred_element_type=jnp.float32)
    du1 = jnp.dot(full_dh, wo_low.T, preferred_element_type=jnp.float32)
    da1 = gelu_pull(a1, du1).astype(jnp.bfloat16)
    g_in1 = jnp.dot(n1.T, da1, preferred_element_type=jnp.float32)
    e_in1 = (-g_in1 * scale).astype(jnp.bfloat16).reshape(paths, width // paths, hidden)
    e_out1 = (-g_out1 * scale).astype(jnp.bfloat16).reshape(paths, width // paths, hidden)
    avg_in1 = lax.all_to_all(
        pair_mean(
            lax.all_to_all(e_in1, "path", split_axis=0, concat_axis=0, tiled=True), partners[0]
        ),
        "path",
        split_axis=0,
        concat_axis=0,
        tiled=True,
    )
    avg_out1 = lax.all_to_all(
        pair_mean(
            lax.all_to_all(e_out1, "path", split_axis=0, concat_axis=0, tiled=True), partners[0]
        ),
        "path",
        split_axis=0,
        concat_axis=0,
        tiled=True,
    )
    avg_in2 = lax.all_to_all(
        pair_mean(
            lax.all_to_all(e_in2, "path", split_axis=0, concat_axis=0, tiled=True), partners[1]
        ),
        "path",
        split_axis=0,
        concat_axis=0,
        tiled=True,
    )
    avg_out2 = lax.all_to_all(
        pair_mean(
            lax.all_to_all(e_out2, "path", split_axis=0, concat_axis=0, tiled=True), partners[1]
        ),
        "path",
        split_axis=0,
        concat_axis=0,
        tiled=True,
    )
    delta_in = jnp.stack([avg_in1.reshape(width, hidden), avg_in2.reshape(width, hidden)])[None]
    delta_out = jnp.stack([avg_out1.reshape(hidden, width), avg_out2.reshape(hidden, width)])[None]
    return (delta_in, delta_out)


def solution(mesh):
    in_specs = (
        P(("path", "shard"), None),
        P(("path", "shard"), None),
        P(("path", "shard"), None),
        P("path", None, None),
        P("path", None, None, "shard"),
        P("path", None, "shard", None),
        P(),
    )
    out_specs = (P("path", None, None, "shard"), P("path", None, "shard", None))
    return jax.shard_map(body, mesh=mesh, in_specs=in_specs, out_specs=out_specs, check_vma=False)
```

profile of v0, /device:TPU:0, one launch (start us, length us, event | category | flops | bytes accessed | tf_op | source)
XLA Modules:
  0.0 668.5 jit_solution(9276861405470540086)
XLA Ops:
  9.6 4.2 all-to-all-start
  14.6 3.3 all-to-all-done
  17.9 32.4 %all_gather.12 = bf16[128,2048]{1,0:T(8,128)(2,1)S(1)} all-gather(bf16[16,2048]{1,0:T(8,128)(2,1)S(1)} %reshape.86), channel_id=1, replica_groups=mesh['path'=4,'shard'=8] {'shard'}, dimensions={0}, use_global_device_ids=true | all-gather | bytes 589824 | tf_op jit(solution)/shard_map/all_gather | solution.py:61
  50.5 2.9 fusion.16
  53.4 3.8 fusion.34
  57.4 6.5 all_to_all.50
  63.9 31.7 %all_gather.13 = bf16[128,2048]{1,0:T(8,128)(2,1)S(1)} all-gather(bf16[16,2048]{1,0:T(8,128)(2,1)S(1)} %reshape.88), channel_id=1, replica_groups=mesh['path'=4,'shard'=8] {'shard'}, dimensions={0}, use_global_device_ids=true | all-gather | bytes 589824 | tf_op jit(solution)/shard_map/all_gather | solution.py:62
  95.7 23.9 %reduce-scatter.3.cloned.1.call-done = bf16[16,2048]{1,0:T(8,128)(2,1)} async-done(((bf16[128,2048]{1,0:T(8,128)(2,1)}), bf16[16,2048]{1,0:T(8,128)(2,1)}) %reduce-scatter.3.cloned.1.call-update) | async-done | bytes 65552 | tf_op jit(solution)/shard_map/reduce_scatter | solution.py:76
  120.4 31.4 %all_gather.14 = bf16[128,2048]{1,0:T(8,128)(2,1)S(1)} all-gather(bf16[16,2048]{1,0:T(8,128)(2,1)S(1)} %add_convert_fusion), channel_id=1, replica_groups=mesh['path'=4,'shard'=8] {'shard'}, dimensions={0}, use_global_device_ids=true | all-gather | bytes 589824 | tf_op jit(solution)/shard_map/all_gather | solution.py:80
  152.0 2.9 fusion.10
  155.0 3.3 multiply_convert_fusion
  158.3 7.1 %reshape.92 = bf16[4,512,1024]{2,1,0:T(8,128)(2,1)} reshape(bf16[1024,2048]{1,0:T(8,128)(2,1)} %multiply_convert_fusion) | data formatting | bytes 8388608 | tf_op jit(solution)/shard_map/reshape | solution.py:90
  165.4 4.8 all-to-all-start.8
  170.3 3.9 fusion.59
  174.1 3.4 multiply_convert_fusion.2
  177.5 41.0 %all-to-all-done.8 = bf16[4,512,1024]{2,1,0:T(8,128)(2,1)} async-done(((bf16[4,512,1024]{2,1,0:T(8,128)(2,1)}), bf16[4,512,1024]{2,1,0:T(8,128)(2,1)}, u32[]{:S(2)}, u32[]{:S(2)}) %all-to-all-start.8) | async-done | bytes 4194336 | tf_op jit(solution)/shard_map/all_to_all | solution.py:133
  218.5 4.8 all-to-all-start.4
  223.4 4.5 fusion.37
  227.9 62.0 %reduce-scatter.5.cloned.1.call-done = bf16[16,2048]{1,0:T(8,128)(2,1)} async-done(((bf16[128,2048]{1,0:T(8,128)(2,1)}), bf16[16,2048]{1,0:T(8,128)(2,1)}) %reduce-scatter.5.cloned.1.call-update) | async-done | bytes 65552 | tf_op jit(solution)/shard_map/reduce_scatter | solution.py:91
  289.9 1.0 fusion.83
  291.8 31.5 %all_gather.15 = bf16[128,2048]{1,0:T(8,128)(2,1)S(1)} all-gather(bf16[16,2048]{1,0:T(8,128)(2,1)S(1)} %fusion.86), channel_id=1, replica_groups=mesh['path'=4,'shard'=8] {'shard'}, dimensions={0}, use_global_device_ids=true | all-gather | bytes 589824 | tf_op jit(solution)/shard_map/all_gather | solution.py:97
  323.3 3.3 multiply_convert_fusion.1
  326.6 7.1 %reshape.91 = bf16[4,512,1024]{2,1,0:T(8,128)(2,1)} reshape(bf16[1024,2048]{1,0:T(8,128)(2,1)} %multiply_convert_fusion.1) | data formatting | bytes 8388608 | tf_op jit(solution)/shard_map/reshape | solution.py:103
  333.7 5.4 all-to-all-start.6
  339.1 6.9 %multiply_convert_fusion.3 = bf16[2048,1024]{1,0:T(8,128)(2,1)} fusion(f32[128,1024]{1,0:T(8,128)S(1)} %fusion.16, bf16[128,2048]{1,0:T(8,128)(2,1)S(1)} %all_gather.15, bf16[1,2,1024,2048]{3,2,1,0:T(8,128)(2,1)} %param.12, bf16[128,2048]{1,0:T(8,128)(2,1)S(1)} %all_gather.12, f32[2048]{0:T(1024)S(1)} %bitcast.65, f32[128]{0:T(128)S(1)} %add_rsqrt_fusion.1), kind=kOutput, calls=%fused_computation.17 | convolution fusion | flops 1083703296 | bytes 9970176 | tf_op jit(solution)/shard_map/dot_general | solution.py:101
  346.1 41.3 %all-to-all-done.6 = bf16[4,512,1024]{2,1,0:T(8,128)(2,1)} async-done(((bf16[4,512,1024]{2,1,0:T(8,128)(2,1)}), bf16[4,512,1024]{2,1,0:T(8,128)(2,1)}, u32[]{:S(2)}, u32[]{:S(2)}) %all-to-all-start.6) | async-done | bytes 4194336 | tf_op jit(solution)/shard_map/all_to_all | solution.py:115
  387.3 4.9 all-to-all-start.2
  392.3 5.6 fusion.20
  397.9 10.0 %fusion.1 = bf16[4,512,1024]{2,1,0:T(8,128)(2,1)} fusion(f32[4,512,1024]{2,0,1:T(4,128)S(1)} %fusion.20, bf16[4,512,1024]{2,1,0:T(8,128)(2,1)} %all-to-all-done.8), kind=kLoop, calls=%fused_computation.4 | loop fusion | flops 8388608 | bytes 16777216 | tf_op jit(solution)/shard_map/convert_element_type | solution.py:30
  407.8 32.7 %all-to-all-done.2 = bf16[4,512,1024]{2,1,0:T(8,128)(2,1)} async-done(((bf16[4,512,1024]{2,1,0:T(8,128)(2,1)}), bf16[4,512,1024]{2,1,0:T(8,128)(2,1)}, u32[]{:S(2)}, u32[]{:S(2)}) %all-to-all-start.2) | async-done | bytes 4194336 | tf_op jit(solution)/shard_map/all_to_all | solution.py:106
  440.5 5.0 all-to-all-start.9
  445.5 5.6 fusion.24
  451.1 10.0 %fusion.5 = bf16[4,512,1024]{2,1,0:T(8,128)(2,1)} fusion(f32[4,512,1024]{2,0,1:T(4,128)S(1)} %fusion.24, bf16[4,512,1024]{2,1,0:T(8,128)(2,1)} %all-to-all-done.4), kind=kLoop, calls=%fused_computation.10 | loop fusion | flops 8388608 | bytes 16777216 | tf_op jit(solution)/shard_map/convert_element_type | solution.py:30
  461.1 32.7 %all-to-all-done.9 = bf16[4,512,1024]{2,1,0:T(8,128)(2,1)} async-done(((bf16[4,512,1024]{2,1,0:T(8,128)(2,1)}), bf16[4,512,1024]{2,1,0:T(8,128)(2,1)}, u32[]{:S(2)}, u32[]{:S(2)}) %all-to-all-start.9) | async-done | bytes 4194336 | tf_op jit(solution)/shard_map/all_to_all | solution.py:131
  493.7 5.1 all-to-all-start.5
  498.8 5.6 fusion.22
  504.4 9.9 %fusion.3 = bf16[4,512,1024]{2,1,0:T(8,128)(2,1)} fusion(f32[4,512,1024]{2,0,1:T(4,128)S(1)} %fusion.22, bf16[4,512,1024]{2,1,0:T(8,128)(2,1)} %all-to-all-done.6), kind=kLoop, calls=%fused_computation.7 | loop fusion | flops 8388608 | bytes 16777216 | tf_op jit(solution)/shard_map/convert_element_type | solution.py:30
  514.3 32.8 %all-to-all-done.5 = bf16[4,512,1024]{2,1,0:T(8,128)(2,1)} async-done(((bf16[4,512,1024]{2,1,0:T(8,128)(2,1)}), bf16[4,512,1024]{2,1,0:T(8,128)(2,1)}, u32[]{:S(2)}, u32[]{:S(2)}) %all-to-all-start.5) | async-done | bytes 4194336 | tf_op jit(solution)/shard_map/all_to_all | solution.py:122
  547.0 5.2 all-to-all-start.7
  552.2 5.6 fusion.26
  557.8 10.0 %fusion.7 = bf16[4,512,1024]{2,1,0:T(8,128)(2,1)} fusion(f32[4,512,1024]{2,0,1:T(4,128)S(1)} %fusion.26, bf16[4,512,1024]{2,1,0:T(8,128)(2,1)} %all-to-all-done.2), kind=kLoop, calls=%fused_computation.13 | loop fusion | flops 8388608 | bytes 16777216 | tf_op jit(solution)/shard_map/convert_element_type | solution.py:30
  567.7 32.7 %all-to-all-done.7 = bf16[4,512,1024]{2,1,0:T(8,128)(2,1)} async-done(((bf16[4,512,1024]{2,1,0:T(8,128)(2,1)}), bf16[4,512,1024]{2,1,0:T(8,128)(2,1)}, u32[]{:S(2)}, u32[]{:S(2)}) %all-to-all-start.7) | async-done | bytes 4194336 | tf_op jit(solution)/shard_map/all_to_all | solution.py:113
  600.4 4.9 all-to-all-start.3
  605.4 7.1 %stack_reshape.15 = bf16[1,1024,2048]{2,1,0:T(8,128)(2,1)} reshape(bf16[4,512,1024]{2,1,0:T(8,128)(2,1)} %all-to-all-done.9) | data formatting | bytes 8388608 | tf_op jit(solution)/shard_map/stack;reshape | solution.py:141
  612.5 7.2 %stack_reshape.14 = bf16[1,1024,2048]{2,1,0:T(8,128)(2,1)} reshape(bf16[4,512,1024]{2,1,0:T(8,128)(2,1)} %all-to-all-done.7) | data formatting | bytes 8388608 | tf_op jit(solution)/shard_map/stack;reshape | solution.py:141
  619.6 7.6 %maximum_bitcast_fusion.1 = bf16[1,2,1024,2048]{3,2,1,0:T(8,128)(2,1)} fusion(bf16[1,1024,2048]{2,1,0:T(8,128)(2,1)} %stack_reshape.15, bf16[1,1024,2048]{2,1,0:T(8,128)(2,1)} %stack_reshape.14), kind=kLoop, calls=%fused_computation.1 | loop fusion | flops 4194304 | bytes 16777216 | tf_op jit(solution)/shard_map/broadcast_in_dim | solution.py:141
  627.3 26.3 %all-to-all-done.3 = bf16[4,512,1024]{2,1,0:T(8,128)(2,1)} async-done(((bf16[4,512,1024]{2,1,0:T(8,128)(2,1)}), bf16[4,512,1024]{2,1,0:T(8,128)(2,1)}, u32[]{:S(2)}, u32[]{:S(2)}) %all-to-all-start.3) | async-done | bytes 4194336 | tf_op jit(solution)/shard_map/all_to_all | solution.py:104
  653.6 7.7 %maximum_bitcast_fusion = bf16[1,2,2048,1024]{3,2,1,0:T(8,128)(2,1)} fusion(bf16[1,2048,1024]{2,1,0:T(8,128)(2,1)} %bitcast.14, bf16[1,2048,1024]{2,1,0:T(8,128)(2,1)} %bitcast.10), kind=kLoop, calls=%fused_computation | loop fusion | flops 4194304 | bytes 16777216 | tf_op jit(solution)/shard_map/broadcast_in_dim | solution.py:140
  (30 shorter events, 5.7 us)
Async XLA Ops:
  7.2 1.6 copy-start
  7.2 50.1 %copy-start.2 = (bf16[12,2048]{1,0:T(8,128)(2,1)S(1)}, bf16[12,2048]{1,0:T(8,128)(2,1)}, u32[]{:S(2)}) copy-start(bf16[12,2048]{1,0:T(8,128)(2,1)} %param.9) | copy-start | bytes 147460
  9.6 8.3 %all-to-all-start = ((bf16[4,4,2048]{2,1,0:T(4,128)(2,1)}), bf16[4,4,2048]{2,1,0:T(4,128)(2,1)S(1)}, u32[]{:S(2)}, u32[]{:S(2)}) async-start(bf16[4,4,2048]{2,1,0:T(4,128)(2,1)} %reshape.85), calls=%async_computation | async-start | bytes 131072 | tf_op jit(solution)/shard_map/all_to_all | solution.py:55
  13.8 105.8 %reduce-scatter.3.cloned.1.call-start = ((), (), s32[]{:S(2)}) async-start(), calls=%async_computation.12 | async-start | bytes 589824 | tf_op jit(solution)/shard_map/reduce_scatter | solution.py:76
  165.4 53.1 %all-to-all-start.8 = ((bf16[4,512,1024]{2,1,0:T(8,128)(2,1)}), bf16[4,512,1024]{2,1,0:T(8,128)(2,1)}, u32[]{:S(2)}, u32[]{:S(2)}) async-start(bf16[4,512,1024]{2,1,0:T(8,128)(2,1)} %reshape.92), calls=%async_computation.10 | async-start | bytes 8388608 | tf_op jit(solution)/shard_map/all_to_all | solution.py:133
  218.5 115.2 %all-to-all-start.4 = ((bf16[4,512,1024]{2,1,0:T(8,128)(2,1)}), bf16[4,512,1024]{2,1,0:T(8,128)(2,1)}, u32[]{:S(2)}, u32[]{:S(2)}) async-start(bf16[4,512,1024]{2,1,0:T(8,128)(2,1)} %bitcast.58), calls=%async_computation.6 | async-start | bytes 8388608 | tf_op jit(solution)/shard_map/all_to_all | solution.py:124
  223.3 66.6 %reduce-scatter.5.cloned.1.call-start = ((), (), s32[]{:S(2)}) async-start(), calls=%async_computation.13 | async-start | bytes 589824 | tf_op jit(solution)/shard_map/reduce_scatter | solution.py:91
  333.7 53.6 %all-to-all-start.6 = ((bf16[4,512,1024]{2,1,0:T(8,128)(2,1)}), bf16[4,512,1024]{2,1,0:T(8,128)(2,1)}, u32[]{:S(2)}, u32[]{:S(2)}) async-start(bf16[4,512,1024]{2,1,0:T(8,128)(2,1)} %reshape.91), calls=%async_computation.8 | async-start | bytes 8388608 | tf_op jit(solution)/shard_map/all_to_all | solution.py:115
  339.1 53.2 %copy-start.3 = (s32[2,4]{1,0:T(2,128)S(1)}, s32[2,4]{1,0:T(2,128)}, u32[]{:S(2)}) copy-start(s32[2,4]{1,0:T(2,128)} %param.13) | copy-start | bytes 100
  387.3 53.2 %all-to-all-start.2 = ((bf16[4,512,1024]{2,1,0:T(8,128)(2,1)}), bf16[4,512,1024]{2,1,0:T(8,128)(2,1)}, u32[]{:S(2)}, u32[]{:S(2)}) async-start(bf16[4,512,1024]{2,1,0:T(8,128)(2,1)} %bitcast.59), calls=%async_computation.4 | async-start | bytes 8388608 | tf_op jit(solution)/shard_map/all_to_all | solution.py:106
  440.5 53.2 %all-to-all-start.9 = ((bf16[4,512,1024]{2,1,0:T(8,128)(2,1)}), bf16[4,512,1024]{2,1,0:T(8,128)(2,1)}, u32[]{:S(2)}, u32[]{:S(2)}) async-start(bf16[4,512,1024]{2,1,0:T(8,128)(2,1)} %fusion.1), calls=%async_computation.11 | async-start | bytes 8388608 | tf_op jit(solution)/shard_map/all_to_all | solution.py:131
  493.7 53.3 %all-to-all-start.5 = ((bf16[4,512,1024]{2,1,0:T(8,128)(2,1)}), bf16[4,512,1024]{2,1,0:T(8,128)(2,1)}, u32[]{:S(2)}, u32[]{:S(2)}) async-start(bf16[4,512,1024]{2,1,0:T(8,128)(2,1)} %fusion.5), calls=%async_computation.7 | async-start | bytes 8388608 | tf_op jit(solution)/shard_map/all_to_all | solution.py:122
  547.0 53.4 %all-to-all-start.7 = ((bf16[4,512,1024]{2,1,0:T(8,128)(2,1)}), bf16[4,512,1024]{2,1,0:T(8,128)(2,1)}, u32[]{:S(2)}, u32[]{:S(2)}) async-start(bf16[4,512,1024]{2,1,0:T(8,128)(2,1)} %fusion.3), calls=%async_computation.9 | async-start | bytes 8388608 | tf_op jit(solution)/shard_map/all_to_all | solution.py:113
  600.4 53.2 %all-to-all-start.3 = ((bf16[4,512,1024]{2,1,0:T(8,128)(2,1)}), bf16[4,512,1024]{2,1,0:T(8,128)(2,1)}, u32[]{:S(2)}, u32[]{:S(2)}) async-start(bf16[4,512,1024]{2,1,0:T(8,128)(2,1)} %fusion.7), calls=%async_computation.5 | async-start | bytes 8388608 | tf_op jit(solution)/shard_map/all_to_all | solution.py:104
  653.6 7.7 %copy-start.1 = (bf16[12,2048]{1,0:T(8,128)(2,1)S(1)}, bf16[12,2048]{1,0:T(8,128)(2,1)}, u32[]{:S(2)}) copy-start(bf16[12,2048]{1,0:T(8,128)(2,1)} %param.7) | copy-start | bytes 147460
Sparse Core Ops, SparseCore 0:
  57.4 62.1 reduce-scatter.2
  228.5 61.3 reduce-scatter.4
where the time goes:
time: 678 us; the launch traced here: 669 us
  waiting for transfers between devices  329 us (49%)
  blocking collectives  133 us (20%)
  other arithmetic  60.6 us (9%)
  matrix products  57.6 us (8%)
  starting transfers between devices  44.4 us (7%)
  local copies, waits for them, and re-layouts  29.2 us (4%)
  between operations  14.7 us (2%)
    reduce_scatter x1, waiting for transfers between devices, body(): lax.psum_scatter(part_back.astype(jnp.bfloat16), 'shard', scatter_dimensi...  62 us
    all_to_all x1, waiting for transfers between devices, body(): lax.all_to_all(e_out1, 'path', split_axis=0, concat_axis=0, tiled=True)  41.3 us
    all_to_all x1, waiting for transfers between devices, body(): lax.all_to_all(e_out2, 'path', split_axis=0, concat_axis=0, tiled=True)  41 us
    convert_element_type x4, other arithmetic, pair_mean(): return ((values + other) * 0.5).astype(jnp.bfloat16)  39.8 us
    all_to_all x1, waiting for transfers between devices, body(): lax.all_to_all(pair_mean(lax.all_to_all(e_in2, 'path', split_axis=0, conc...  32.8 us
    all_to_all x1, waiting for transfers between devices, body(): lax.all_to_all(pair_mean(lax.all_to_all(e_out2, 'path', split_axis=0, con...  32.7 us
    all_to_all x1, waiting for transfers between devices, body(): lax.all_to_all(pair_mean(lax.all_to_all(e_out1, 'path', split_axis=0, con...  32.7 us
    all_to_all x1, waiting for transfers between devices, body(): lax.all_to_all(e_in1, 'path', split_axis=0, concat_axis=0, tiled=True)  32.7 us
  transfers between devices with their start and end apart: 11, of which 10 were waited for; matrix products, arithmetic and copies ran while one was open for 17% of the time, Pallas kernels for 0%

commit v1 on v0

v1 whole, which is shorter than its diff:
```python
import functools

import jax
import jax.numpy as jnp
from jax import lax
from jax.experimental import pallas as pl
from jax.experimental.pallas import tpu as pltpu
from jax.sharding import PartitionSpec as P

SLOTS = 16


def norm_value(v, gain):
    return v * lax.rsqrt(jnp.mean(v * v, axis=-1, keepdims=True) + 1e-05) * gain.astype(jnp.float32)


def norm_pull(h, gain, grad):

    def value(v):
        return norm_value(v, gain)

    return jax.vjp(value, h.astype(jnp.float32))[1](grad)[0]


def gelu_pull(pre, grad):
    return jax.vjp(jax.nn.gelu, pre)[1](grad)[0]


def gather_shard(own):
    shards = lax.axis_size("shard")
    spread = jnp.broadcast_to(own[None], (shards, *own.shape))
    got = lax.all_to_all(spread, "shard", split_axis=0, concat_axis=0, tiled=True)
    return got.reshape(shards * own.shape[0], own.shape[1])


def reduce_shard(part):
    shards = lax.axis_size("shard")
    blocks = part.reshape(shards, part.shape[0] // shards, part.shape[1])
    got = lax.all_to_all(blocks, "shard", split_axis=0, concat_axis=0, tiled=True)
    return jnp.sum(got.astype(jnp.float32), axis=0)


def from_mate(value, mate):
    paths = lax.axis_size("path")
    if paths == 4:
        near = lax.ppermute(value, "path", [(i, i ^ 1) for i in range(4)])
        sent = jnp.where(mate == 3, near, value)
        far = lax.ppermute(sent, "path", [(i, i ^ 2) for i in range(4)])
        return near, far
    me = lax.axis_index("path")
    behind = (me - (me ^ mate)) % paths
    mine = value
    for shift in range(1, paths):
        got = lax.ppermute(value, "path", [(i, (i + shift) % paths) for i in range(paths)])
        mine = jnp.where(behind == shift, got, mine)
    return mine, mine


def pair_grad_kernel(factor, mate_ref, a_ref, an_ref, af_ref, b_ref, bn_ref, bf_ref, *rest):
    out_ref = rest[-1]
    near = mate_ref[0] == 1
    contract = (((0,), (0,)), ((), ()))
    own = lax.dot_general(a_ref[...], b_ref[...], contract, preferred_element_type=jnp.float32)
    a_mate = jnp.where(near, an_ref[...], af_ref[...])
    b_mate = jnp.where(near, bn_ref[...], bf_ref[...])
    other = lax.dot_general(a_mate, b_mate, contract, preferred_element_type=jnp.float32)
    out_ref[0, 0] = ((own + other) * factor).astype(jnp.bfloat16)


def pair_grad(mate, a, a_mate, b, b_mate, level, before):
    rows, left = a.shape
    right = b.shape[1]
    factor = -0.5 / rows**0.5
    block = min(256, left)
    a_spec = pl.BlockSpec((rows, block), lambda i: (0, i))
    b_spec = pl.BlockSpec((rows, right), lambda i: (0, 0))
    operands = [mate.reshape(1), a, *a_mate, b, *b_mate]
    in_specs = [pl.BlockSpec(memory_space=pltpu.SMEM), a_spec, a_spec, a_spec, b_spec, b_spec, b_spec]
    aliases = {}
    if before is not None:
        aliases = {len(operands): 0}
        operands.append(before)
        in_specs.append(pl.BlockSpec(memory_space=pl.ANY))
    return pl.pallas_call(
        functools.partial(pair_grad_kernel, factor),
        grid=(left // block,),
        in_specs=in_specs,
        out_specs=pl.BlockSpec((1, 1, block, right), lambda i: (0, level, i, 0)),
        out_shape=jax.ShapeDtypeStruct((1, 2, left, right), jnp.bfloat16),
        input_output_aliases=aliases,
        compiler_params=pltpu.CompilerParams(vmem_limit_bytes=32 * 1024 * 1024),
        cost_estimate=pl.CostEstimate(
            flops=4 * rows * left * right, bytes_accessed=2 * left * right + 6 * rows * (left + right), transcendentals=0
        ),
    )(*operands)


def body(tokens, routes, cotangent, gains, w_in, w_out, partners):
    paths = lax.axis_size("path")
    shards = lax.axis_size("shard")
    slots = SLOTS
    cap = slots // paths
    width = tokens.shape[1]
    me = lax.axis_index("path")
    mate_low = partners[0, me] ^ me
    mate_high = partners[1, me] ^ me
    route = routes[:, 0]
    order = jnp.arange(route.shape[0], dtype=jnp.int32)
    same = (route[:, None] == route[None, :]) & (order[None, :] < order[:, None])
    rank = jnp.sum(same.astype(jnp.int32), axis=1)
    target = route * cap + rank
    select = (jnp.arange(slots, dtype=jnp.int32)[:, None] == target[None, :]).astype(jnp.bfloat16)
    packed_x = jnp.dot(select, tokens, preferred_element_type=jnp.float32).astype(jnp.bfloat16)
    packed_dy = jnp.dot(select, cotangent, preferred_element_type=jnp.float32).astype(jnp.bfloat16)

    spread = jnp.broadcast_to(packed_x.reshape(paths, 1, cap, width), (paths, shards, cap, width))
    got = lax.all_to_all(
        spread.reshape(paths * shards, cap, width), ("path", "shard"), split_axis=0, concat_axis=0, tiled=True
    ).reshape(paths, shards, cap, width)
    full_x = got.transpose(1, 0, 2, 3).reshape(shards * slots, width)
    own_x = lax.dynamic_slice_in_dim(full_x, lax.axis_index("shard") * slots, slots, 0)

    got_dy = lax.all_to_all(packed_dy.reshape(paths, cap, width), "path", split_axis=0, concat_axis=0, tiled=True)
    own_dy = got_dy.reshape(slots, width)
    full_dy = gather_shard(own_dy)

    gain_low = gains[0, 0]
    gain_high = gains[0, 1]
    wi_low = w_in[0, 0]
    wi_high = w_in[0, 1]
    wo_low = w_out[0, 0]
    wo_high = w_out[0, 1]
    n1 = norm_value(full_x.astype(jnp.float32), gain_low).astype(jnp.bfloat16)
    a1 = jnp.dot(n1, wi_low, preferred_element_type=jnp.float32)
    u1 = jax.nn.gelu(a1).astype(jnp.bfloat16)
    part_low = jnp.dot(u1, wo_low, preferred_element_type=jnp.float32).astype(jnp.bfloat16)
    n1_mate = from_mate(n1, mate_low)
    u1_mate = from_mate(u1, mate_low)
    mixed_own = reduce_shard(part_low)
    h_own = (own_x.astype(jnp.float32) + mixed_own).astype(jnp.bfloat16)
    full_h = gather_shard(h_own)

    du2 = jnp.dot(full_dy, wo_high.T, preferred_element_type=jnp.float32)
    dy_mate = from_mate(full_dy, mate_high)
    n2 = norm_value(full_h.astype(jnp.float32), gain_high).astype(jnp.bfloat16)
    a2 = jnp.dot(n2, wi_high, preferred_element_type=jnp.float32)
    u2 = jax.nn.gelu(a2).astype(jnp.bfloat16)
    da2 = gelu_pull(a2, du2).astype(jnp.bfloat16)
    part_back = jnp.dot(da2, wi_high.T, preferred_element_type=jnp.float32).astype(jnp.bfloat16)
    u2_mate = from_mate(u2, mate_high)
    n2_mate = from_mate(n2, mate_high)
    da2_mate = from_mate(da2, mate_high)
    back_own = reduce_shard(part_back)
    dh_own = (own_dy.astype(jnp.float32) + norm_pull(h_own, gain_high, back_own)).astype(jnp.bfloat16)
    full_dh = gather_shard(dh_own)

    delta_in = pair_grad(mate_high, n2, n2_mate, da2, da2_mate, 1, None)
    delta_out = pair_grad(mate_high, u2, u2_mate, full_dy, dy_mate, 1, None)

    du1 = jnp.dot(full_dh, wo_low.T, preferred_element_type=jnp.float32)
    da1 = gelu_pull(a1, du1).astype(jnp.bfloat16)
    dh_mate = from_mate(full_dh, mate_low)
    da1_mate = from_mate(da1, mate_low)
    delta_out = pair_grad(mate_low, u1, u1_mate, full_dh, dh_mate, 0, delta_out)
    delta_in = pair_grad(mate_low, n1, n1_mate, da1, da1_mate, 0, delta_in)
    return (delta_in, delta_out)


def solution(mesh):
    in_specs = (
        P(("path", "shard"), None),
        P(("path", "shard"), None),
        P(("path", "shard"), None),
        P("path", None, None),
        P("path", None, None, "shard"),
        P("path", None, "shard", None),
        P(),
    )
    out_specs = (P("path", None, None, "shard"), P("path", None, "shard", None))
    return jax.shard_map(body, mesh=mesh, in_specs=in_specs, out_specs=out_specs, check_vma=False)
```

time: 678 us -> 209 us (0.31); the launches traced: 669 us -> 207 us
  waiting for transfers between devices: 329 us -> 92.3 us
  blocking collectives: 133 us -> 0 us
  other arithmetic: 60.6 us -> 12.8 us
  matrix products: 57.6 us -> 24.6 us
  Pallas kernels: 0 us -> 25.3 us
  local copies, waits for them, and re-layouts: 29.2 us -> 9.94 us
  between operations: 14.7 us -> 2.27 us
    all_to_all x9 -> x7, waiting for transfers between devices: 243 us -> 71.2 us  [the longest x3 33.2 us: gather_shard(): lax.all_to_all(spread, 'shard', split_axis=0, concat_axis=0, tiled=True)]
    all_gather x4 -> x0, blocking collectives: 127 us -> none  [the longest x1 32.4 us: body(): lax.all_gather(own_x, 'shard', axis=0, tiled=True)]
    reduce_scatter x2 -> x0, waiting for transfers between devices: 85.8 us -> none  [the longest x1 62 us: body(): lax.psum_scatter(part_back.astype(jnp.bfloat16), 'shard', scatter_dimensi...]
    convert_element_type x4, other arithmetic: 39.8 us -> 1.93 us  [the longest x2 1.42 us: body(): n2 = norm_value(full_h.astype(jnp.float32), gain_high).astype(jnp.bfloat16)]
    dot_general x10 -> x3, matrix products: 47.5 us -> 11 us  [the longest x1 4.06 us: body(): du1 = jnp.dot(full_dh, wo_low.T, preferred_element_type=jnp.float32)]
    pallas_call x0 -> x4, Pallas kernels: none -> 25.3 us  [pair_grad(): pl.pallas_call(functools.partial(pair_grad_kernel, factor), grid=(left //...]
    ppermute x0 -> x16, waiting for transfers between devices: none -> 21.1 us  [the longest x8 20.2 us: from_mate(): far = lax.ppermute(sent, 'path', [(i, i ^ 2) for i in range(4)])]
    all_to_all x9 -> x7, starting transfers between devices: 44.4 us -> 28.6 us  [the longest x3 10.9 us: gather_shard(): lax.all_to_all(spread, 'shard', split_axis=0, concat_axis=0, tiled=True)]
  transfers between devices with their start and end apart: 11 -> 23, of which waited for: 10 -> 11; matrix products, arithmetic and copies ran while one was open for 17% -> 20% of each run, Pallas kernels for 0% -> 10%
where the time goes in v1:
time: 209 us; the launch traced here: 207 us
  waiting for transfers between devices  92.3 us (44%)
  starting transfers between devices  39.8 us (19%)
  Pallas kernels  25.3 us (12%)
  matrix products  24.6 us (12%)
  other arithmetic  12.8 us (6%)
  local copies, waits for them, and re-layouts  9.94 us (5%)
  between operations  2.27 us (1%)
    all_to_all x3, waiting for transfers between devices, gather_shard(): lax.all_to_all(spread, 'shard', split_axis=0, concat_axis=0, tiled=True)  33.2 us
    pallas_call x4, Pallas kernels, pair_grad(): pl.pallas_call(functools.partial(pair_grad_kernel, factor), grid=(left //...  25.3 us
    all_to_all x2, waiting for transfers between devices, reduce_shard(): lax.all_to_all(blocks, 'shard', split_axis=0, concat_axis=0, tiled=True)  24 us
    ppermute x8, waiting for transfers between devices, from_mate(): far = lax.ppermute(sent, 'path', [(i, i ^ 2) for i in range(4)])  20.2 us
    all_to_all x1, waiting for transfers between devices, body(): lax.all_to_all(spread.reshape(paths * shards, cap, width), ('path', 'shar...  13.9 us
    all_to_all x3, starting transfers between devices, gather_shard(): lax.all_to_all(spread, 'shard', split_axis=0, concat_axis=0, tiled=True)  10.9 us
    ppermute x8, starting transfers between devices, from_mate(): far = lax.ppermute(sent, 'path', [(i, i ^ 2) for i in range(4)])  9.42 us
    all_to_all x1, starting transfers between devices, body(): lax.all_to_all(spread.reshape(paths * shards, cap, width), ('path', 'shar...  7.3 us
  transfers between devices with their start and end apart: 23, of which 11 were waited for; matrix products, arithmetic and copies ran while one was open for 20% of the time, Pallas kernels for 10%

profile of v1, /device:TPU:0, one launch (start us, length us, event | category | flops | bytes accessed | tf_op | source)
XLA Modules:
  0.0 207.0 jit_solution(12876637805855052698)
XLA Ops:
  0.6 0.9 convert_reduce_fusion.2
  2.4 1.0 broadcast_in_dim.13
  3.4 7.3 %all-to-all-start = ((bf16[32,4,2048]{2,1,0:T(4,128)(2,1)}), bf16[32,4,2048]{2,1,0:T(4,128)(2,1)S(1)}, u32[]{:S(2)}, u32[]{:S(2)}) async-start(bf16[32,4,2048]{2,1,0:T(4,128)(2,1)} %bitcast.3), calls=%async_computation | async-start | bytes 1048576 | tf_op jit(solution)/shard_map/all_to_all | solution.py:117
  10.7 1.0 convolution_convert_fusion
  12.4 0.8 slice_convert_fusion
  13.2 13.9 %all-to-all-done = bf16[32,4,2048]{2,1,0:T(4,128)(2,1)S(1)} async-done(((bf16[32,4,2048]{2,1,0:T(4,128)(2,1)}), bf16[32,4,2048]{2,1,0:T(4,128)(2,1)S(1)}, u32[]{:S(2)}, u32[]{:S(2)}) %all-to-all-start) | async-done | bytes 524320 | tf_op jit(solution)/shard_map/all_to_all | solution.py:117
  27.1 3.3 %all-to-all-start.1 = ((bf16[4,4,2048]{2,1,0:T(4,128)(2,1)}), bf16[4,4,2048]{2,1,0:T(4,128)(2,1)S(1)}, u32[]{:S(2)}, u32[]{:S(2)}) async-start(bf16[4,4,2048]{2,1,0:T(4,128)(2,1)} %reshape.146), calls=%async_computation.1 | async-start | bytes 131072 | tf_op jit(solution)/shard_map/all_to_all | solution.py:123
  31.9 3.8 %multiply_convert_fusion.3 = (bf16[128,1024]{1,0:T(8,128)(2,1)S(1)}, f32[128,1024]{1,0:T(8,128)}) fusion(bf16[128,2048]{1,0:T(8,128)(2,1)S(1)} %convert_element_type.112, bf16[1,2,2048,1024]{3,2,1,0:T(8,128)(2,1)} %param.11), kind=kOutput, calls=%fused_computation.55 | convolution fusion | flops 538050560 | bytes 5505024 | tf_op jit(solution)/shard_map/dot_general | solution.py:134
  35.7 3.7 %fusion.18 = bf16[128,2048]{1,0:T(8,128)(2,1)} fusion(bf16[128,1024]{1,0:T(8,128)(2,1)S(1)} %get-tuple-element.10.a_ref, bf16[1,2,1024,2048]{3,2,1,0:T(8,128)(2,1)} %param.12), kind=kOutput, calls=%fused_computation.18 | convolution fusion | flops 537133056 | bytes 4980736 | tf_op jit(solution)/shard_map/dot_general | solution.py:136
  39.4 3.5 %all-to-all-start.3 = ((bf16[8,16,2048]{2,1,0:T(8,128)(2,1)}), bf16[8,16,2048]{2,1,0:T(8,128)(2,1)S(1)}, u32[]{:S(2)}, u32[]{:S(2)}) async-start(bf16[8,16,2048]{2,1,0:T(8,128)(2,1)} %bitcast.12), calls=%async_computation.3 | async-start | bytes 1048576 | tf_op jit(solution)/shard_map/all_to_all | solution.py:39
  42.9 15.3 %all-to-all-done.3 = bf16[8,16,2048]{2,1,0:T(8,128)(2,1)S(1)} async-done(((bf16[8,16,2048]{2,1,0:T(8,128)(2,1)}), bf16[8,16,2048]{2,1,0:T(8,128)(2,1)S(1)}, u32[]{:S(2)}, u32[]{:S(2)}) %all-to-all-start.3) | async-done | bytes 524320 | tf_op jit(solution)/shard_map/all_to_all | solution.py:39
  58.3 0.8 broadcast_in_dim.14
  59.1 3.6 %all-to-all-start.2 = ((bf16[8,16,2048]{2,1,0:T(8,128)(2,1)}), bf16[8,16,2048]{2,1,0:T(8,128)(2,1)S(1)}, u32[]{:S(2)}, u32[]{:S(2)}) async-start(bf16[8,16,2048]{2,1,0:T(8,128)(2,1)} %broadcast_in_dim.14), calls=%async_computation.2 | async-start | bytes 1048576 | tf_op jit(solution)/shard_map/all_to_all | solution.py:32
  63.7 13.8 %all-to-all-done.2 = bf16[8,16,2048]{2,1,0:T(8,128)(2,1)S(1)} async-done(((bf16[8,16,2048]{2,1,0:T(8,128)(2,1)}), bf16[8,16,2048]{2,1,0:T(8,128)(2,1)S(1)}, u32[]{:S(2)}, u32[]{:S(2)}) %all-to-all-start.2) | async-done | bytes 524320 | tf_op jit(solution)/shard_map/all_to_all | solution.py:32
  77.4 0.8 broadcast_in_dim.15
  78.3 3.6 %all-to-all-start.4 = ((bf16[8,16,2048]{2,1,0:T(8,128)(2,1)}), bf16[8,16,2048]{2,1,0:T(8,128)(2,1)S(1)}, u32[]{:S(2)}, u32[]{:S(2)}) async-start(bf16[8,16,2048]{2,1,0:T(8,128)(2,1)} %broadcast_in_dim.15), calls=%async_computation.4 | async-start | bytes 1048576 | tf_op jit(solution)/shard_map/all_to_all | solution.py:32
  81.9 1.4 constant_dynamic-slice_fusion
  84.7 0.8 copy.24
  87.0 9.6 %all-to-all-done.4 = bf16[8,16,2048]{2,1,0:T(8,128)(2,1)S(1)} async-done(((bf16[8,16,2048]{2,1,0:T(8,128)(2,1)}), bf16[8,16,2048]{2,1,0:T(8,128)(2,1)S(1)}, u32[]{:S(2)}, u32[]{:S(2)}) %all-to-all-start.4) | async-done | bytes 524320 | tf_op jit(solution)/shard_map/all_to_all | solution.py:32
  97.6 3.9 %multiply_convert_fusion.2 = (bf16[128,1024]{1,0:T(8,128)(2,1)}, f32[128,1024]{1,0:T(8,128)S(1)}) fusion(bf16[128,2048]{1,0:T(8,128)(2,1)S(1)} %bitcast.77, bf16[1,2,2048,1024]{3,2,1,0:T(8,128)(2,1)} %param.11), kind=kOutput, calls=%fused_computation.54 | convolution fusion | flops 538050560 | bytes 5505024 | tf_op jit(solution)/shard_map/dot_general | solution.py:146
  101.5 4.8 %fusion.42.b_ref = bf16[128,1024]{1,0:T(8,128)(2,1)} fusion(f32[128,1024]{1,0:T(8,128)S(1)} %get-tuple-element.13, bf16[128,2048]{1,0:T(8,128)(2,1)S(1)} %bitcast.73, bf16[1,2,1024,2048]{3,2,1,0:T(8,128)(2,1)} %param.12), kind=kOutput, calls=%fused_computation.52 | convolution fusion | flops 539492352 | bytes 5505024 | tf_op jit(solution)/shard_map/dot_general | solution.py:143
  106.3 3.3 %fusion.21 = bf16[128,2048]{1,0:T(8,128)(2,1)} fusion(bf16[128,1024]{1,0:T(8,128)(2,1)} %fusion.42.b_ref, bf16[1,2,2048,1024]{3,2,1,0:T(8,128)(2,1)S(1)} %bitcast.87), kind=kOutput, calls=%fused_computation.19 | convolution fusion | flops 537133056 | bytes 4980736 | tf_op jit(solution)/shard_map/dot_general | solution.py:149
  109.5 3.6 %all-to-all-start.5 = ((bf16[8,16,2048]{2,1,0:T(8,128)(2,1)}), bf16[8,16,2048]{2,1,0:T(8,128)(2,1)S(1)}, u32[]{:S(2)}, u32[]{:S(2)}) async-start(bf16[8,16,2048]{2,1,0:T(8,128)(2,1)} %bitcast.76), calls=%async_computation.5 | async-start | bytes 1048576 | tf_op jit(solution)/shard_map/all_to_all | solution.py:39
  113.2 0.9 broadcast_select_fusion
  114.1 1.6 collective-permute-start.15
  115.7 1.8 broadcast_select_fusion.3
  119.1 8.7 %all-to-all-done.5 = bf16[8,16,2048]{2,1,0:T(8,128)(2,1)S(1)} async-done(((bf16[8,16,2048]{2,1,0:T(8,128)(2,1)}), bf16[8,16,2048]{2,1,0:T(8,128)(2,1)S(1)}, u32[]{:S(2)}, u32[]{:S(2)}) %all-to-all-start.5) | async-done | bytes 524320 | tf_op jit(solution)/shard_map/all_to_all | solution.py:39
  128.1 0.9 fusion.50
  129.0 0.8 broadcast_in_dim.17
  129.9 3.7 %all-to-all-start.6 = ((bf16[8,16,2048]{2,1,0:T(8,128)(2,1)}), bf16[8,16,2048]{2,1,0:T(8,128)(2,1)S(1)}, u32[]{:S(2)}, u32[]{:S(2)}) async-start(bf16[8,16,2048]{2,1,0:T(8,128)(2,1)} %broadcast_in_dim.17), calls=%async_computation.6 | async-start | bytes 1048576 | tf_op jit(solution)/shard_map/all_to_all | solution.py:32
  133.5 1.2 fusion.28.a_ref
  134.9 1.7 broadcast_select_fusion.4
  136.6 1.7 broadcast_select_fusion.5
  138.3 9.9 %all-to-all-done.6 = bf16[8,16,2048]{2,1,0:T(8,128)(2,1)S(1)} async-done(((bf16[8,16,2048]{2,1,0:T(8,128)(2,1)}), bf16[8,16,2048]{2,1,0:T(8,128)(2,1)S(1)}, u32[]{:S(2)}, u32[]{:S(2)}) %all-to-all-start.6) | async-done | bytes 524320 | tf_op jit(solution)/shard_map/all_to_all | solution.py:32
  148.2 4.1 %fusion.35.b_ref = bf16[128,1024]{1,0:T(8,128)(2,1)S(1)} fusion(f32[128,1024]{1,0:T(8,128)} %get-tuple-element.11, bf16[128,2048]{1,0:T(8,128)(2,1)S(1)} %bitcast.70, bf16[1,2,1024,2048]{3,2,1,0:T(8,128)(2,1)} %param.12), kind=kOutput, calls=%fused_computation.45 | convolution fusion | flops 539492352 | bytes 5505024 | tf_op jit(solution)/shard_map/dot_general | solution.py:160
  153.0 0.9 collective-permute-done.2.bn_ref
  153.9 1.6 collective-permute-start.13
  156.1 1.6 collective-permute-start.5
  158.3 4.8 %collective-permute-done.13.af_ref = bf16[128,1024]{1,0:T(8,128)(2,1)S(1)} collective-permute-done((bf16[128,1024]{1,0:T(8,128)(2,1)S(1)}, bf16[128,1024]{1,0:T(8,128)(2,1)S(1)}, u32[]{:S(2)}, u32[]{:S(2)}) %collective-permute-start.13) | collective-permute-done | bytes 262176 | tf_op jit(solution)/shard_map/ppermute | solution.py:48
  163.0 1.6 collective-permute-start.11
  164.7 4.0 %collective-permute-done.7.bf_ref = bf16[128,1024]{1,0:T(8,128)(2,1)S(1)} collective-permute-done((bf16[128,1024]{1,0:T(8,128)(2,1)S(1)}, bf16[128,1024]{1,0:T(8,128)(2,1)S(1)}, u32[]{:S(2)}, u32[]{:S(2)}) %collective-permute-start.7) | collective-permute-done | bytes 262176 | tf_op jit(solution)/shard_map/ppermute | solution.py:48
  168.7 1.6 collective-permute-start.9
  170.3 5.6 %shard_map.88.rest_0_ = bf16[1,2,1024,2048]{3,2,1,0:T(8,128)(2,1)} custom-call(s32[1]{0:T(128)} %bitcast.19.mate_ref, bf16[128,1024]{1,0:T(8,128)(2,1)} %get-tuple-element.12.a_ref, bf16[128,1024]{1,0:T(8,128)(2,1)} %collective-permute-done.12.an_ref, bf16[128,1024]{1,0:T(8,128)(2,1)S(1)} %collective-permute-done.13.af_ref, bf16[128,2048]{1,0:T(8,128)(2,1)S(1)} %bitcast.74, ...), custom_call_target="tpu_custom_call" | custom-call | flops 1073741824 | bytes 6553600 | tf_op jit(solution)/shard_map/pallas_call | solution.py:84
  175.8 4.1 %collective-permute-done.5.af_ref = bf16[128,2048]{1,0:T(8,128)(2,1)S(1)} collective-permute-done((bf16[128,2048]{1,0:T(8,128)(2,1)S(1)}, bf16[128,2048]{1,0:T(8,128)(2,1)S(1)}, u32[]{:S(2)}, u32[]{:S(2)}) %collective-permute-start.5) | collective-permute-done | bytes 524320 | tf_op jit(solution)/shard_map/ppermute | solution.py:48
  179.9 7.4 %shard_map.86.rest_0_ = bf16[1,2,2048,1024]{3,2,1,0:T(8,128)(2,1)} custom-call(s32[1]{0:T(128)} %bitcast.19.mate_ref, bf16[128,2048]{1,0:T(8,128)(2,1)S(1)} %fusion.28.a_ref, bf16[128,2048]{1,0:T(8,128)(2,1)} %collective-permute-done.4.an_ref, bf16[128,2048]{1,0:T(8,128)(2,1)S(1)} %collective-permute-done.5.af_ref, bf16[128,1024]{1,0:T(8,128)(2,1)} %fusion.42.b_ref, ...), custom_call_target="tpu_custom_call" | custom-call | flops 1073741824 | bytes 6553600 | tf_op jit(solution)/shard_map/pallas_call | solution.py:84
  187.3 7.2 %shard_map.87 = bf16[1,2,2048,1024]{3,2,1,0:T(8,128)(2,1)} custom-call(s32[1]{0:T(128)} %bitcast.1.mate_ref, bf16[128,2048]{1,0:T(8,128)(2,1)S(1)} %multiply_convert_fusion.1.a_ref, bf16[128,2048]{1,0:T(8,128)(2,1)S(1)} %collective-permute-done.an_ref, bf16[128,2048]{1,0:T(8,128)(2,1)} %collective-permute-done.1.af_ref, ...), custom_call_target="tpu_custom_call", output_to_operand_aliasing={{}: (7, {})} | custom-call | flops 1073741824 | bytes 6553600 | tf_op jit(solution)/shard_map/pallas_call | solution.py:84
  194.5 7.4 %collective-permute-done.9.af_ref = bf16[128,1024]{1,0:T(8,128)(2,1)S(1)} collective-permute-done((bf16[128,1024]{1,0:T(8,128)(2,1)S(1)}, bf16[128,1024]{1,0:T(8,128)(2,1)S(1)}, u32[]{:S(2)}, u32[]{:S(2)}) %collective-permute-start.9) | collective-permute-done | bytes 262176 | tf_op jit(solution)/shard_map/ppermute | solution.py:48
  201.8 5.2 %shard_map.89 = bf16[1,2,1024,2048]{3,2,1,0:T(8,128)(2,1)} custom-call(s32[1]{0:T(128)} %bitcast.1.mate_ref, bf16[128,1024]{1,0:T(8,128)(2,1)S(1)} %get-tuple-element.10.a_ref, bf16[128,1024]{1,0:T(8,128)(2,1)} %collective-permute-done.8.an_ref, bf16[128,1024]{1,0:T(8,128)(2,1)S(1)} %collective-permute-done.9.af_ref, ...), custom_call_target="tpu_custom_call", output_to_operand_aliasing={{}: (7, {})} | custom-call | flops 1073741824 | bytes 6553600 | tf_op jit(solution)/shard_map/pallas_call | solution.py:84
  (74 shorter events, 10.4 us)
Async XLA Ops:
  0.6 1.6 copy-start
  3.4 23.7 %all-to-all-start = ((bf16[32,4,2048]{2,1,0:T(4,128)(2,1)}), bf16[32,4,2048]{2,1,0:T(4,128)(2,1)S(1)}, u32[]{:S(2)}, u32[]{:S(2)}) async-start(bf16[32,4,2048]{2,1,0:T(4,128)(2,1)} %bitcast.3), calls=%async_computation | async-start | bytes 1048576 | tf_op jit(solution)/shard_map/all_to_all | solution.py:117
  27.1 12.3 %all-to-all-start.1 = ((bf16[4,4,2048]{2,1,0:T(4,128)(2,1)}), bf16[4,4,2048]{2,1,0:T(4,128)(2,1)S(1)}, u32[]{:S(2)}, u32[]{:S(2)}) async-start(bf16[4,4,2048]{2,1,0:T(4,128)(2,1)} %reshape.146), calls=%async_computation.1 | async-start | bytes 131072 | tf_op jit(solution)/shard_map/all_to_all | solution.py:123
  31.0 0.8 copy-start.6
  39.4 18.9 %all-to-all-start.3 = ((bf16[8,16,2048]{2,1,0:T(8,128)(2,1)}), bf16[8,16,2048]{2,1,0:T(8,128)(2,1)S(1)}, u32[]{:S(2)}, u32[]{:S(2)}) async-start(bf16[8,16,2048]{2,1,0:T(8,128)(2,1)} %bitcast.12), calls=%async_computation.3 | async-start | bytes 1048576 | tf_op jit(solution)/shard_map/all_to_all | solution.py:39
  42.9 16.2 %copy-start.3 = (bf16[16,2048]{1,0:T(8,128)(2,1)}, bf16[16,2048]{1,0:T(8,128)(2,1)S(1)}, u32[]{:S(2)}) copy-start(bf16[16,2048]{1,0:T(8,128)(2,1)S(1)} %reshape.147) | copy-start | bytes 196612
  59.1 18.3 %all-to-all-start.2 = ((bf16[8,16,2048]{2,1,0:T(8,128)(2,1)}), bf16[8,16,2048]{2,1,0:T(8,128)(2,1)S(1)}, u32[]{:S(2)}, u32[]{:S(2)}) async-start(bf16[8,16,2048]{2,1,0:T(8,128)(2,1)} %broadcast_in_dim.14), calls=%async_computation.2 | async-start | bytes 1048576 | tf_op jit(solution)/shard_map/all_to_all | solution.py:32
  78.3 18.3 %all-to-all-start.4 = ((bf16[8,16,2048]{2,1,0:T(8,128)(2,1)}), bf16[8,16,2048]{2,1,0:T(8,128)(2,1)S(1)}, u32[]{:S(2)}, u32[]{:S(2)}) async-start(bf16[8,16,2048]{2,1,0:T(8,128)(2,1)} %broadcast_in_dim.15), calls=%async_computation.4 | async-start | bytes 1048576 | tf_op jit(solution)/shard_map/all_to_all | solution.py:32
  84.7 28.5 %collective-permute-start.14 = (bf16[128,2048]{1,0:T(8,128)(2,1)S(1)}, bf16[128,2048]{1,0:T(8,128)(2,1)S(1)}, u32[]{:S(2)}, u32[]{:S(2)}) collective-permute-start(bf16[128,2048]{1,0:T(8,128)(2,1)S(1)} %bitcast.72), channel_id=1, source_target_pairs={{0,8},{8,0},{16,24},{24,16},{1,9},{9,1},{17,25},{25,17},{2,10},{10... | collective-permute-start | bytes 1572872 | tf_op jit(solution)/shard_map/ppermute | solution.py:46
  85.5 70.0 %collective-permute-start.8 = (bf16[128,1024]{1,0:T(8,128)(2,1)S(1)}, bf16[128,1024]{1,0:T(8,128)(2,1)}, u32[]{:S(2)}, u32[]{:S(2)}) collective-permute-start(bf16[128,1024]{1,0:T(8,128)(2,1)S(1)} %get-tuple-element.10.a_ref), channel_id=1, source_target_pairs={{0,8},{8,0},{16,24},{24,16},{1,9},{9,1},{17,25},{25,17},{2,10},{10... | collective-permute-start | bytes 786440 | tf_op jit(solution)/shard_map/ppermute | solution.py:46
  86.1 0.6 copy-start.8
  86.9 28.7 %collective-permute-start = (bf16[128,2048]{1,0:T(8,128)(2,1)S(1)}, bf16[128,2048]{1,0:T(8,128)(2,1)S(1)}, u32[]{:S(2)}, u32[]{:S(2)}) collective-permute-start(bf16[128,2048]{1,0:T(8,128)(2,1)S(1)} %multiply_convert_fusion.1.a_ref), channel_id=1, source_target_pairs={{0,8},{8,0},{16,24},{24,16},{1,9},{9,1},{17,25},{25,17},{2,10},{10... | collective-permute-start | bytes 1572872 | tf_op jit(solution)/shard_map/ppermute | solution.py:46
  96.6 9.7 %copy-start.1 = (bf16[8,16,2048]{2,1,0:T(8,128)(2,1)}, bf16[8,16,2048]{2,1,0:T(8,128)(2,1)S(1)}, u32[]{:S(2)}) copy-start(bf16[8,16,2048]{2,1,0:T(8,128)(2,1)S(1)} %all-to-all-done.4) | copy-start | bytes 1572868
  96.8 0.6 copy-start.7
  97.4 8.9 %slice-start = ((s8[8388608]{0:T(1024)(128)(4,1)}), s8[4194304]{0:T(1024)(128)(4,1)S(1)}, s32[]{:S(2)}) async-start(s8[8388608]{0:T(1024)(128)(4,1)} %bitcast.86), calls=%async_computation.7 | async-start | bytes 8388608
  101.5 4.8 %slice-start.1 = ((s8[8388608]{0:T(1024)(128)(4,1)}), s8[4194304]{0:T(1024)(128)(4,1)S(1)}, s32[]{:S(2)}) async-start(s8[8388608]{0:T(1024)(128)(4,1)} %bitcast.86), calls=%async_computation.8 | async-start | bytes 8388608
  109.5 18.3 %all-to-all-start.5 = ((bf16[8,16,2048]{2,1,0:T(8,128)(2,1)}), bf16[8,16,2048]{2,1,0:T(8,128)(2,1)S(1)}, u32[]{:S(2)}, u32[]{:S(2)}) async-start(bf16[8,16,2048]{2,1,0:T(8,128)(2,1)} %bitcast.76), calls=%async_computation.5 | async-start | bytes 1048576 | tf_op jit(solution)/shard_map/all_to_all | solution.py:39
  114.1 43.7 %collective-permute-start.15 = (bf16[128,2048]{1,0:T(8,128)(2,1)}, bf16[128,2048]{1,0:T(8,128)(2,1)}, u32[]{:S(2)}, u32[]{:S(2)}) collective-permute-start(bf16[128,2048]{1,0:T(8,128)(2,1)} %broadcast_select_fusion), channel_id=1, source_target_pairs={{0,16},{8,24},{16,0},{24,8},{1,17},{9,25},{17,1},{25,9},{2,18},{10... | collective-permute-start | bytes 1572872 | tf_op jit(solution)/shard_map/ppermute | solution.py:48
  117.4 69.9 %collective-permute-start.1 = (bf16[128,2048]{1,0:T(8,128)(2,1)}, bf16[128,2048]{1,0:T(8,128)(2,1)}, u32[]{:S(2)}, u32[]{:S(2)}) collective-permute-start(bf16[128,2048]{1,0:T(8,128)(2,1)} %broadcast_select_fusion.3), channel_id=1, source_target_pairs={{0,16},{8,24},{16,0},{24,8},{1,17},{9,25},{17,1},{25,9},{2,18},{10... | collective-permute-start | bytes 1572872 | tf_op jit(solution)/shard_map/ppermute | solution.py:48
  118.6 18.0 %collective-permute-start.6 = (bf16[128,1024]{1,0:T(8,128)(2,1)}, bf16[128,1024]{1,0:T(8,128)(2,1)}, u32[]{:S(2)}, u32[]{:S(2)}) collective-permute-start(bf16[128,1024]{1,0:T(8,128)(2,1)} %fusion.42.b_ref), channel_id=1, source_target_pairs={{0,8},{8,0},{16,24},{24,16},{1,9},{9,1},{17,25},{25,17},{2,10},{10... | collective-permute-start | bytes 786440 | tf_op jit(solution)/shard_map/ppermute | solution.py:46
  118.6 16.2 %collective-permute-start.12 = (bf16[128,1024]{1,0:T(8,128)(2,1)}, bf16[128,1024]{1,0:T(8,128)(2,1)}, u32[]{:S(2)}, u32[]{:S(2)}) collective-permute-start(bf16[128,1024]{1,0:T(8,128)(2,1)} %get-tuple-element.12.a_ref), channel_id=1, source_target_pairs={{0,8},{8,0},{16,24},{24,16},{1,9},{9,1},{17,25},{25,17},{2,10},{10... | collective-permute-start | bytes 786440 | tf_op jit(solution)/shard_map/ppermute | solution.py:46
  129.9 18.3 %all-to-all-start.6 = ((bf16[8,16,2048]{2,1,0:T(8,128)(2,1)}), bf16[8,16,2048]{2,1,0:T(8,128)(2,1)S(1)}, u32[]{:S(2)}, u32[]{:S(2)}) async-start(bf16[8,16,2048]{2,1,0:T(8,128)(2,1)} %broadcast_in_dim.17), calls=%async_computation.6 | async-start | bytes 1048576 | tf_op jit(solution)/shard_map/all_to_all | solution.py:32
  134.8 17.5 %collective-permute-start.4 = (bf16[128,2048]{1,0:T(8,128)(2,1)S(1)}, bf16[128,2048]{1,0:T(8,128)(2,1)}, u32[]{:S(2)}, u32[]{:S(2)}) collective-permute-start(bf16[128,2048]{1,0:T(8,128)(2,1)S(1)} %fusion.28.a_ref), channel_id=1, source_target_pairs={{0,8},{8,0},{16,24},{24,16},{1,9},{9,1},{17,25},{25,17},{2,10},{10... | collective-permute-start | bytes 1572872 | tf_op jit(solution)/shard_map/ppermute | solution.py:46
  148.2 4.6 %copy-start.2 = (bf16[8,16,2048]{2,1,0:T(8,128)(2,1)S(1)}, bf16[8,16,2048]{2,1,0:T(8,128)(2,1)}, u32[]{:S(2)}) copy-start(bf16[8,16,2048]{2,1,0:T(8,128)(2,1)} %copy-done.1) | copy-start | bytes 1572868
  148.2 5.7 %copy-start.5 = (bf16[128,1024]{1,0:T(8,128)(2,1)S(1)}, bf16[128,1024]{1,0:T(8,128)(2,1)}, u32[]{:S(2)}) copy-start(bf16[128,1024]{1,0:T(8,128)(2,1)} %broadcast_select_fusion.4) | copy-start | bytes 786436
  148.2 7.4 %copy-start.4 = (bf16[128,1024]{1,0:T(8,128)(2,1)S(1)}, bf16[128,1024]{1,0:T(8,128)(2,1)}, u32[]{:S(2)}) copy-start(bf16[128,1024]{1,0:T(8,128)(2,1)} %broadcast_select_fusion.5) | copy-start | bytes 786436
  148.2 7.9 %collective-permute-start.10 = (bf16[128,2048]{1,0:T(8,128)(2,1)S(1)}, bf16[128,2048]{1,0:T(8,128)(2,1)S(1)}, u32[]{:S(2)}, u32[]{:S(2)}) collective-permute-start(bf16[128,2048]{1,0:T(8,128)(2,1)S(1)} %bitcast.69), channel_id=1, source_target_pairs={{0,8},{8,0},{16,24},{24,16},{1,9},{9,1},{17,25},{25,17},{2,10},{10... | collective-permute-start | bytes 1572872 | tf_op jit(solution)/shard_map/ppermute | solution.py:46
  152.3 1.6 collective-permute-start.2
  153.9 9.1 %collective-permute-start.13 = (bf16[128,1024]{1,0:T(8,128)(2,1)S(1)}, bf16[128,1024]{1,0:T(8,128)(2,1)S(1)}, u32[]{:S(2)}, u32[]{:S(2)}) collective-permute-start(bf16[128,1024]{1,0:T(8,128)(2,1)S(1)} %copy-done.5), channel_id=1, source_target_pairs={{0,16},{8,24},{16,0},{24,8},{1,17},{9,25},{17,1},{25,9},{2,18},{10... | collective-permute-start | bytes 786440 | tf_op jit(solution)/shard_map/ppermute | solution.py:48
  155.6 13.1 %collective-permute-start.7 = (bf16[128,1024]{1,0:T(8,128)(2,1)S(1)}, bf16[128,1024]{1,0:T(8,128)(2,1)S(1)}, u32[]{:S(2)}, u32[]{:S(2)}) collective-permute-start(bf16[128,1024]{1,0:T(8,128)(2,1)S(1)} %copy-done.4), channel_id=1, source_target_pairs={{0,16},{8,24},{16,0},{24,8},{1,17},{9,25},{17,1},{25,9},{2,18},{10... | collective-permute-start | bytes 786440 | tf_op jit(solution)/shard_map/ppermute | solution.py:48
  156.1 23.8 %collective-permute-start.5 = (bf16[128,2048]{1,0:T(8,128)(2,1)S(1)}, bf16[128,2048]{1,0:T(8,128)(2,1)S(1)}, u32[]{:S(2)}, u32[]{:S(2)}) collective-permute-start(bf16[128,2048]{1,0:T(8,128)(2,1)S(1)} %broadcast_select_fusion.1), channel_id=1, source_target_pairs={{0,16},{8,24},{16,0},{24,8},{1,17},{9,25},{17,1},{25,9},{2,18},{10... | collective-permute-start | bytes 1572872 | tf_op jit(solution)/shard_map/ppermute | solution.py:48
  157.8 29.5 %collective-permute-start.3 = (bf16[128,1024]{1,0:T(8,128)(2,1)S(1)}, bf16[128,1024]{1,0:T(8,128)(2,1)S(1)}, u32[]{:S(2)}, u32[]{:S(2)}) collective-permute-start(bf16[128,1024]{1,0:T(8,128)(2,1)S(1)} %broadcast_select_fusion.7), channel_id=1, source_target_pairs={{0,16},{8,24},{16,0},{24,8},{1,17},{9,25},{17,1},{25,9},{2,18},{10... | collective-permute-start | bytes 786440 | tf_op jit(solution)/shard_map/ppermute | solution.py:48
  163.0 38.8 %collective-permute-start.11 = (bf16[128,2048]{1,0:T(8,128)(2,1)S(1)}, bf16[128,2048]{1,0:T(8,128)(2,1)S(1)}, u32[]{:S(2)}, u32[]{:S(2)}) collective-permute-start(bf16[128,2048]{1,0:T(8,128)(2,1)S(1)} %broadcast_select_fusion.2), channel_id=1, source_target_pairs={{0,16},{8,24},{16,0},{24,8},{1,17},{9,25},{17,1},{25,9},{2,18},{10... | collective-permute-start | bytes 1572872 | tf_op jit(solution)/shard_map/ppermute | solution.py:48
  168.7 33.2 %collective-permute-start.9 = (bf16[128,1024]{1,0:T(8,128)(2,1)S(1)}, bf16[128,1024]{1,0:T(8,128)(2,1)S(1)}, u32[]{:S(2)}, u32[]{:S(2)}) collective-permute-start(bf16[128,1024]{1,0:T(8,128)(2,1)S(1)} %broadcast_select_fusion.6), channel_id=1, source_target_pairs={{0,16},{8,24},{16,0},{24,8},{1,17},{9,25},{17,1},{25,9},{2,18},{10... | collective-permute-start | bytes 786440 | tf_op jit(solution)/shard_map/ppermute | solution.py:48

commit v2 on v1

v2 whole, which is shorter than its diff:
```python
import functools

import jax
import jax.numpy as jnp
from jax import lax
from jax.experimental import pallas as pl
from jax.experimental.pallas import tpu as pltpu
from jax.sharding import PartitionSpec as P

SLOTS = 16
BLOCK = 256
ROOT = 0.7978845608028654
CUBE = 0.044715
NT = (((1,), (1,)), ((), ()))
TN = (((0,), (0,)), ((), ()))
PARAMS = pltpu.CompilerParams(vmem_limit_bytes=16 * 1024 * 1024)
SMALL = pltpu.CompilerParams(vmem_limit_bytes=56 * 1024 * 1024)
IN_VMEM = pl.BlockSpec(memory_space=pltpu.VMEM)
IN_SMEM = pl.BlockSpec(memory_space=pltpu.SMEM)
ANYWHERE = pl.BlockSpec(memory_space=pl.ANY)
FREE = pl.CostEstimate(flops=0, bytes_accessed=0, transcendentals=0)


def bf16(*shape):
    return jax.ShapeDtypeStruct(shape, jnp.bfloat16)


def f32(*shape):
    return jax.ShapeDtypeStruct(shape, jnp.float32)


def cuts(size, step=BLOCK):
    step = min(step, size)
    return [pl.ds(start, step) for start in range(0, size, step)]


def tie(*values):
    return lax.optimization_barrier(values)


def call(kernel, name, where, arrays, outs):
    operands = [] if where is None else [where]
    return pl.pallas_call(
        kernel,
        in_specs=[IN_SMEM] * len(operands) + [IN_VMEM] * len(arrays),
        out_specs=[IN_VMEM] * len(outs),
        out_shape=outs,
        compiler_params=PARAMS,
        cost_estimate=FREE,
        name=name,
    )(*operands, *arrays)


def norm_value(v, gain):
    return v * lax.rsqrt(jnp.mean(v * v, axis=-1, keepdims=True) + 1e-05) * gain.astype(jnp.float32)


def gelu_both(a):
    t = jnp.tanh(ROOT * (a + CUBE * (a * a * a)))
    half = 0.5 * (1.0 + t)
    slope = half + 0.5 * a * (1.0 - t * t) * (ROOT * (1.0 + (3.0 * CUBE) * (a * a)))
    return a * half, slope


def slots_of_rows(routes_ref, cap, flip):
    count = routes_ref.shape[0]
    down = lax.broadcasted_iota(jnp.int32, (count, count), 0)
    along = lax.broadcasted_iota(jnp.int32, (count, count), 1)
    route_down = jnp.zeros((count, count), jnp.int32)
    route_along = jnp.zeros((count, count), jnp.int32)
    for r in range(count):
        route = routes_ref[r]
        route_down = jnp.where(down == r, route, route_down)
        route_along = jnp.where(along == r, route, route_along)
    earlier = jnp.where((route_down == route_along) & (down < along), 1, 0)
    rank = jnp.sum(earlier, axis=0, keepdims=True)
    return (route_along[0:1, :] ^ flip) * cap + rank


def pack_kernel(copies, flip_ref, routes_ref, rows_ref, *out_refs):
    count = routes_ref.shape[0]
    cap = out_refs[0].shape[-2]
    slots = slots_of_rows(routes_ref, cap, flip_ref[0])
    for group in range(SLOTS // cap):
        want = group * cap + lax.broadcasted_iota(jnp.int32, (cap, count), 0)
        pick = (want == slots).astype(jnp.float32).astype(jnp.bfloat16)
        value = jnp.dot(pick, rows_ref[...], preferred_element_type=jnp.float32).astype(jnp.bfloat16)
        if copies == 0:
            out_refs[group][...] = value
        for copy in range(copies):
            out_refs[0][group * copies + copy] = value


def pack(flip, routes, rows, paths, copies):
    cap, width = SLOTS // paths, rows.shape[1]
    outs = [bf16(paths * copies, cap, width)] if copies else [bf16(cap, width)] * paths
    got = pl.pallas_call(
        functools.partial(pack_kernel, copies),
        in_specs=[IN_SMEM, IN_SMEM, IN_VMEM],
        out_specs=[IN_VMEM] * len(outs),
        out_shape=outs,
        compiler_params=SMALL,
        cost_estimate=FREE,
        name="pack",
    )(flip.reshape(1), routes, rows)
    return got[0] if copies else got


def settle_kernel(where_ref, got_ref, x_ref, own_ref, spread_ref):
    count, rows, _ = got_ref.shape
    total = x_ref[pl.ds(pl.multiple_of(where_ref[2] * rows, rows), rows), :].astype(jnp.float32)
    for i in range(count):
        total += got_ref[i].astype(jnp.float32)
    total = total.astype(jnp.bfloat16)
    own_ref[...] = total
    for i in range(count):
        spread_ref[i] = total


def settle(where, got, x):
    count, rows, width = got.shape
    return call(settle_kernel, "settle", where, [got, x], [bf16(rows, width), bf16(count, rows, width)])


def settle_back_kernel(where_ref, got_ref, dy_ref, h_ref, gain_ref, own_ref, spread_ref):
    count, rows, _ = got_ref.shape
    grad = got_ref[0].astype(jnp.float32)
    for i in range(1, count):
        grad += got_ref[i].astype(jnp.float32)
    grad = grad * gain_ref[1:2, :].astype(jnp.float32)
    h = h_ref[...].astype(jnp.float32)
    scale = lax.rsqrt(jnp.mean(h * h, axis=-1, keepdims=True) + 1e-05)
    unit = h * scale
    pull = scale * (grad - unit * jnp.mean(grad * unit, axis=-1, keepdims=True))
    dy = dy_ref[pl.ds(pl.multiple_of(where_ref[2] * rows, rows), rows), :].astype(jnp.float32)
    total = (dy + pull).astype(jnp.bfloat16)
    own_ref[...] = total
    for i in range(count):
        spread_ref[i] = total


def settle_back(where, got, dy, h_own, gains):
    count, rows, width = got.shape
    outs = [bf16(rows, width), bf16(count, rows, width)]
    return call(settle_back_kernel, "settle_back", where, [got, dy, h_own, gains], outs)


def low_kernel(x_ref, gain_ref, wi_ref, wo_ref, n_ref, u_ref, slope_ref, part_ref):
    n_ref[...] = norm_value(x_ref[...].astype(jnp.float32), gain_ref[0:1, :]).astype(jnp.bfloat16)
    for cut in cuts(wi_ref.shape[1]):
        a = jnp.dot(n_ref[...], wi_ref[:, cut], preferred_element_type=jnp.float32)
        u, slope = gelu_both(a)
        u_ref[:, cut] = u.astype(jnp.bfloat16)
        slope_ref[:, cut] = slope
    for cut in cuts(wo_ref.shape[1]):
        part = jnp.dot(u_ref[...], wo_ref[:, cut], preferred_element_type=jnp.float32)
        part_ref[:, cut] = part.astype(jnp.bfloat16)


def low_forward(x, gains, wi, wo):
    rows, width = x.shape
    hidden = wi.shape[-1]
    outs = [bf16(rows, width), bf16(rows, hidden), f32(rows, hidden), bf16(rows, width)]
    return call(low_kernel, "low_forward", None, [x, gains, wi, wo], outs)


def high_kernel(h_ref, gain_ref, wi_ref, du_ref, n_ref, pair_ref, part_ref):
    hidden = wi_ref.shape[1]
    n_ref[...] = norm_value(h_ref[...].astype(jnp.float32), gain_ref[1:2, :]).astype(jnp.bfloat16)
    for cut in cuts(hidden):
        a = jnp.dot(n_ref[...], wi_ref[:, cut], preferred_element_type=jnp.float32)
        u, slope = gelu_both(a)
        pair_ref[:, cut] = u.astype(jnp.bfloat16)
        pair_ref[:, pl.ds(hidden + cut.start, cut.size)] = (slope * du_ref[:, cut]).astype(jnp.bfloat16)
    for cut in cuts(wi_ref.shape[0]):
        part = lax.dot_general(pair_ref[:, hidden:], wi_ref[cut, :], NT, preferred_element_type=jnp.float32)
        part_ref[:, cut] = part.astype(jnp.bfloat16)


def high_both(h, gains, wi, du):
    rows, width = h.shape
    outs = [bf16(rows, width), bf16(rows, 2 * wi.shape[-1]), bf16(rows, width)]
    return call(high_kernel, "high_both", None, [h, gains, wi, du], outs)


def places(order, rows, path, shard):
    to = lax.broadcasted_iota(jnp.int32, (rows, rows), 0)
    source = lax.broadcasted_iota(jnp.int32, (rows, rows), 1)
    if order == "dispatch":
        far = ((to >> 2) & 7) ^ shard
        block = ((far & 1) << 2) | (far & 2) | (far >> 2)
        wanted = block * 16 + ((to >> 5) ^ path) * 4 + (to & 3)
    else:
        far = (to >> 4) ^ shard
        block = ((far & 1) << 2) | (far & 2) | (far >> 2)
        wanted = block * 16 + (to & 15)
    return (source == wanted).astype(jnp.float32).astype(jnp.bfloat16)


def high_grad_kernel(ordered, where_ref, raw_ref, wo_ref, dy_ref, du_ref):
    if ordered:
        dy_ref[...] = raw_ref[...]
    else:
        pick = places("dispatch", raw_ref.shape[0], where_ref[3], where_ref[2])
        dy_ref[...] = jnp.dot(pick, raw_ref[...], preferred_element_type=jnp.float32).astype(jnp.bfloat16)
    for cut in cuts(wo_ref.shape[0]):
        du_ref[:, cut] = lax.dot_general(dy_ref[...], wo_ref[cut, :], NT, preferred_element_type=jnp.float32)


def high_grad(where, raw, wo, ordered):
    rows, width = raw.shape
    kernel = functools.partial(high_grad_kernel, ordered)
    return call(kernel, "high_grad", where, [raw, wo], [bf16(rows, width), f32(rows, wo.shape[-2])])


def low_grad_kernel(dh_ref, wo_ref, slope_ref, da_ref):
    for cut in cuts(wo_ref.shape[0]):
        du = lax.dot_general(dh_ref[...], wo_ref[cut, :], NT, preferred_element_type=jnp.float32)
        da_ref[:, cut] = (du * slope_ref[:, cut]).astype(jnp.bfloat16)


def low_grad(dh, wo, slope):
    return call(low_grad_kernel, "low_grad", None, [dh, wo, slope], [bf16(dh.shape[0], wo.shape[-2])])[0]


def pair_kernel(level, factor, order, a_cut, b_cut, where_ref, a_ref, an_ref, af_ref, b_ref, bn_ref, bf_ref, *rest):
    out_ref, right, both, slots, raw, sems = rest[-6:]
    rows = a_ref.shape[0]
    mine, theirs = pl.ds(0, rows), pl.ds(rows, rows)
    own = [
        pltpu.make_async_copy(a_ref.at[:, a_cut], both.at[mine, :], sems.at[2]),
        pltpu.make_async_copy(b_ref.at[:, b_cut], right.at[mine, :], sems.at[3]),
    ]
    if order:
        half = rows // 2
        own.append(pltpu.make_async_copy(bn_ref, raw.at[pl.ds(0, half), :], sems.at[6]))
        own.append(pltpu.make_async_copy(bf_ref, raw.at[pl.ds(half, half), :], sems.at[7]))
    for copy in own:
        copy.start()

    def take(a_mate, b_mate):
        copies = [pltpu.make_async_copy(a_mate.at[:, a_cut], both.at[theirs, :], sems.at[4])]
        if not order:
            copies.append(pltpu.make_async_copy(b_mate.at[:, b_cut], right.at[theirs, :], sems.at[5]))
        for copy in copies:
            copy.start()
        for copy in copies:
            copy.wait()

    @pl.when(where_ref[level] == 1)
    def _():
        take(an_ref, bn_ref)

    @pl.when(where_ref[level] != 1)
    def _():
        take(af_ref, bf_ref)

    for copy in own:
        copy.wait()
    if order:
        pick = places(order, rows, where_ref[3] ^ where_ref[level], where_ref[2])
        right[rows:, :] = jnp.dot(pick, raw[...], preferred_element_type=jnp.float32).astype(jnp.bfloat16)
    copies = []
    for i, cut in enumerate(cuts(both.shape[1], 2 * BLOCK)):
        slot = i % 2
        if i >= 2:
            copies[i - 2].wait()
        value = lax.dot_general(both[:, cut], right[...], TN, preferred_element_type=jnp.float32)
        slots[slot] = (value * factor).astype(jnp.bfloat16)
        copies.append(pltpu.make_async_copy(slots.at[slot], out_ref.at[0, level, cut, :], sems.at[slot]))
        copies[-1].start()
    for copy in copies[-2:]:
        copy.wait()


def pair_grad(where, a, a_mate, a_cut, b, b_mate, b_cut, level, before, order=""):
    rows, left, right = a.shape[0], a_cut.size, b_cut.size
    factor = -0.5 / rows**0.5
    arrays = [a, *a_mate, b, *b_mate]
    aliases = {}
    if before is not None:
        arrays.append(before)
        aliases = {len(arrays): 0}
    return pl.pallas_call(
        functools.partial(pair_kernel, level, factor, order, a_cut, b_cut),
        in_specs=[IN_SMEM] + [ANYWHERE] * len(arrays),
        out_specs=ANYWHERE,
        out_shape=bf16(1, 2, left, right),
        scratch_shapes=[
            pltpu.VMEM((2 * rows, right), jnp.bfloat16),
            pltpu.VMEM((2 * rows, left), jnp.bfloat16),
            pltpu.VMEM((2, min(2 * BLOCK, left), right), jnp.bfloat16),
            pltpu.VMEM((rows, right), jnp.bfloat16),
            pltpu.SemaphoreType.DMA((8,)),
        ],
        input_output_aliases=aliases,
        compiler_params=pltpu.CompilerParams(vmem_limit_bytes=56 * 1024 * 1024),
        cost_estimate=FREE,
        name="pair_grad",
    )(where, *arrays)


def dispatch(spread):
    got = lax.all_to_all(spread, ("path", "shard"), split_axis=0, concat_axis=0, tiled=True)
    return got.reshape(got.shape[0] * got.shape[1], got.shape[2])


def gather_shard(spread):
    got = lax.all_to_all(spread, "shard", split_axis=0, concat_axis=0, tiled=True)
    return got.reshape(got.shape[0] * got.shape[1], got.shape[2])


def scatter_shard(part):
    shards = lax.axis_size("shard")
    blocks = part.reshape(shards, part.shape[0] // shards, part.shape[1])
    return lax.all_to_all(blocks, "shard", split_axis=0, concat_axis=0, tiled=True)


def swap(value, axis, bit):
    return lax.ppermute(value, axis, [(i, i ^ bit) for i in range(lax.axis_size(axis))])


def join(*values):
    return lax.optimization_barrier(jnp.concatenate(values, axis=0))


def from_mate(values, *mates):
    paths = lax.axis_size("path")
    mates = mates if len(mates) == len(values) else mates * len(values)
    if paths == 4:
        nears = [swap(v, "path", 1) for v in values]
        sent = [jnp.where(mate == 3, near, v) for near, v, mate in zip(nears, values, mates)]
        return [[near, swap(v, "path", 2)] for near, v in zip(nears, sent)]
    me = lax.axis_index("path")
    pairs = []
    for value, mate in zip(values, mates):
        behind = (me - (me ^ mate)) % paths
        mine = value
        for shift in range(1, paths):
            got = lax.ppermute(value, "path", [(i, (i + shift) % paths) for i in range(paths)])
            value, mine = tie(value, jnp.where(behind == shift, got, mine))
        pairs.append([mine, mine])
    return pairs


def level_of(w, level, after):
    index, _ = tie(jnp.int32(level), after)
    return lax.dynamic_index_in_dim(w[0], index, 0, keepdims=False)


def body(tokens, routes, cotangent, gains, w_in, w_out, partners):
    paths = lax.axis_size("path")
    shards = lax.axis_size("shard")
    cubes = paths == 4 and shards == 8
    me = lax.axis_index("path")
    shard = lax.axis_index("shard")
    mate_low = partners[0, me] ^ me
    mate_high = partners[1, me] ^ me
    where = jnp.stack([mate_low, mate_high, shard, me])
    none = jnp.int32(0)
    gain = gains[0]
    routes = routes.reshape(-1)

    width, hidden = w_in.shape[2:]
    wide, first, second = pl.ds(0, width), pl.ds(0, hidden), pl.ds(hidden, hidden)

    spread = pack(none, routes, tokens, paths, shards)
    x = dispatch(spread)
    wi_low = level_of(w_in, 0, spread)
    if cubes:
        by_path = pack(me, routes, cotangent, paths, 0)
        rows_1 = join(by_path[0], *[swap(by_path[k], "path", k) for k in (1, 2, 3)])
        hop_1 = swap(rows_1, "shard", 4)
        wo_low = level_of(w_out, 0, rows_1)
        x, hop_1, where, mate_low, mate_high = tie(x, hop_1, where, mate_low, mate_high)
    else:
        wo_low = level_of(w_out, 0, spread)
    n1, u1, slope1, part_low = low_forward(x, gain, wi_low, wo_low)

    (n1_mate,) = from_mate([n1], mate_low)
    wi_high, wo_high = level_of(w_in, 1, n1_mate[0]), level_of(w_out, 1, n1_mate[0])
    got = scatter_shard(part_low)
    if cubes:
        rows_2 = join(rows_1, hop_1)
        hop_2 = swap(rows_2, "shard", 2)
        got, n1_mate[1], hop_2 = tie(got, n1_mate[1], hop_2)
    h_own, h_spread = settle(where, got, x)

    h = gather_shard(h_spread)
    if cubes:
        rows_4 = join(rows_2, hop_2)
        hop_3 = swap(rows_4, "shard", 1)
        (u1_mate, half_mate) = from_mate([u1, rows_4], mate_low, mate_high)
        dy, du2 = high_grad(where, join(rows_4, hop_3), wo_high, False)
        h, u1_mate[1], half_mate[1], du2 = tie(h, u1_mate[1], half_mate[1], du2)
    else:
        (u1_mate,) = from_mate([u1], mate_low)
        dy, du2 = high_grad(where, dispatch(pack(none, routes, cotangent, paths, shards)), wo_high, True)
    n2, f2, part_back = high_both(h, gain, wi_high, du2)

    (f2_mate,) = from_mate([f2], mate_high)
    wo_again = level_of(w_out, 0, f2_mate[0])
    got = scatter_shard(part_back)
    if cubes:
        half = jnp.where(mate_high == 1, *half_mate)
        hop_4 = swap(half, "shard", 1)
        got, f2_mate[1], hop_4 = tie(got, f2_mate[1], hop_4)
    dh_own, dh_spread = settle_back(where, got, dy, h_own, gain)

    dh = gather_shard(dh_spread)
    (n2_mate,) = from_mate([n2], mate_high)
    if cubes:
        delta_out = pair_grad(where, f2, f2_mate, first, dy, [half, hop_4], wide, 1, None, "dispatch")
        (dh_pair,) = from_mate([dh_own], mate_low)
        dh, n2_mate[1], delta_out = tie(dh, n2_mate[1], delta_out)
    da1 = low_grad(dh, wo_again, slope1)

    (da1_mate,) = from_mate([da1], mate_low)
    delta_in = pair_grad(where, n2, n2_mate, wide, f2, f2_mate, second, 1, None)
    if cubes:
        dh_piece, _ = tie(jnp.where(mate_low == 1, *dh_pair), da1)
        dh_half = join(dh_piece, *[swap(dh_piece, "shard", bit) for bit in (4, 2, 6)])
        dh_mate = [dh_half, swap(dh_half, "shard", 1)]
    else:
        (dh_mate,) = from_mate([dh], mate_low)
        (dy_mate,) = from_mate([dy], mate_high)
        delta_out = pair_grad(where, f2, f2_mate, first, dy, dy_mate, wide, 1, None)
    delta_in = pair_grad(where, n1, n1_mate, wide, da1, da1_mate, first, 0, delta_in)
    delta_out = pair_grad(where, u1, u1_mate, first, dh, dh_mate, wide, 0, delta_out, "gather" if cubes else "")
    return (delta_in, delta_out)


def solution(mesh):
    in_specs = (
        P(("path", "shard"), None),
        P(("path", "shard"), None),
        P(("path", "shard"), None),
        P("path", None, None),
        P("path", None, None, "shard"),
        P("path", None, "shard", None),
        P(),
    )
    out_specs = (P("path", None, None, "shard"), P("path", None, "shard", None))
    return jax.shard_map(body, mesh=mesh, in_specs=in_specs, out_specs=out_specs, check_vma=False)
```

time: 209 us -> 169 us (0.81)
  waiting for transfers between devices: 92.3 us -> 35.2 us
  matrix products: 24.6 us -> 0 us
  local copies, waits for them, and re-layouts: 9.94 us -> 33.3 us
  starting transfers between devices: 39.8 us -> 51.9 us
  Pallas kernels: 25.3 us -> 37.2 us
  other arithmetic: 12.8 us -> 6.8 us
    all_to_all x4 -> x3, waiting for transfers between devices: 38 us -> 2.89 us  [the longest x2 2.89 us: scatter_shard(): lax.all_to_all(blocks, 'shard', split_axis=0, concat_axis=0, tiled=True)]
    dot_general x8 -> x0, matrix products: 24.6 us -> none  [the longest x1 4.75 us: body(): du2 = jnp.dot(full_dy, wo_high.T, preferred_element_type=jnp.float32)]
    all_to_all x3 -> x2, waiting for transfers between devices: 33.2 us -> 10.9 us  [gather_shard(): lax.all_to_all(spread, 'shard', split_axis=0, concat_axis=0, tiled=True)]
    squeeze x0 -> x5, local copies, waits for them, and re-layouts: none -> 21.4 us  [level_of(): return lax.dynamic_index_in_dim(w[0], index, 0, keepdims=False)]
    ppermute x16 -> x25, starting transfers between devices: 11.1 us -> 25.6 us  [swap(): lax.ppermute(value, axis, [(i, i ^ bit) for i in range(lax.axis_size(axis...]
    pallas_call x4 -> x12, Pallas kernels: 25.3 us -> 37.2 us  [the longest x4 20.8 us: pair_grad(): pl.pallas_call(functools.partial(pair_kernel, level, factor, order, a_cut...]
    unnamed x22 -> x48, local copies, waits for them, and re-layouts: 1.23 us -> 10.4 us
    convert_element_type x7 -> x0, other arithmetic: 3.69 us -> none  [the longest x2 1.42 us: body(): n2 = norm_value(full_h.astype(jnp.float32), gain_high).astype(jnp.bfloat16)]
  transfers between devices with their start and end apart: 23 -> 30, of which waited for: 11 -> 11; matrix products, arithmetic and copies ran while one was open for 20% -> 18% of each run, Pallas kernels for 10% -> 13%
where the time goes in v2:
time: 169 us; the launch traced here: 167 us
  starting transfers between devices  51.9 us (31%)
  Pallas kernels  37.2 us (22%)
  waiting for transfers between devices  35.2 us (21%)
  local copies, waits for them, and re-layouts  33.3 us (20%)
  other arithmetic  6.8 us (4%)
  between operations  2.49 us (1%)
    ppermute x25, starting transfers between devices, swap(): lax.ppermute(value, axis, [(i, i ^ bit) for i in range(lax.axis_size(axis...  25.6 us
    ppermute x25, waiting for transfers between devices, swap(): lax.ppermute(value, axis, [(i, i ^ bit) for i in range(lax.axis_size(axis...  21.4 us
    squeeze x5, local copies, waits for them, and re-layouts, level_of(): return lax.dynamic_index_in_dim(w[0], index, 0, keepdims=False)  21.4 us
    pallas_call x4, Pallas kernels, pair_grad(): pl.pallas_call(functools.partial(pair_kernel, level, factor, order, a_cut...  20.8 us
    pallas_call x6, Pallas kernels, call(): pl.pallas_call(kernel, in_specs=[IN_SMEM] * len(operands) + [IN_VMEM] * l...  12.8 us
    all_to_all x2, waiting for transfers between devices, gather_shard(): lax.all_to_all(spread, 'shard', split_axis=0, concat_axis=0, tiled=True)  10.9 us
    all_to_all x2, starting transfers between devices, gather_shard(): lax.all_to_all(spread, 'shard', split_axis=0, concat_axis=0, tiled=True)  10.5 us
    unnamed x48, local copies, waits for them, and re-layouts  10.4 us
  transfers between devices with their start and end apart: 30, of which 11 were waited for; matrix products, arithmetic and copies ran while one was open for 18% of the time, Pallas kernels for 13%

profile of v2, /device:TPU:0, one launch (start us, length us, event | category | flops | bytes accessed | tf_op | source)
XLA Modules:
  0.0 166.8 jit_solution(1378111987180010199)
XLA Ops:
  0.6 1.9 %pack.2 = bf16[32,4,2048]{2,1,0:T(4,128)(2,1)} custom-call(s32[1]{0:T(128)} %constant.30.clone.1.flip_ref, s32[12]{0:T(128)} %bitcast.28, bf16[12,2048]{1,0:T(8,128)(2,1)} %rows_ref.2), custom_call_target="tpu_custom_call" | custom-call | tf_op jit(solution)/shard_map/pack/pallas_call | solution.py:97
  2.5 7.3 %all-to-all-start = ((bf16[32,4,2048]{2,1,0:T(4,128)(2,1)}), bf16[32,4,2048]{2,1,0:T(4,128)(2,1)S(1)}, u32[]{:S(2)}, u32[]{:S(2)}) async-start(bf16[32,4,2048]{2,1,0:T(4,128)(2,1)} %pack.2), calls=%async_computation | async-start | bytes 1048576 | tf_op jit(solution)/shard_map/all_to_all | solution.py:304
  9.8 1.7 %pack.3 = (bf16[4,2048]{1,0:T(4,128)(2,1)}, bf16[4,2048]{1,0:T(4,128)(2,1)}, bf16[4,2048]{1,0:T(4,128)(2,1)}, bf16[4,2048]{1,0:T(4,128)(2,1)}) custom-call(s32[1]{0:T(128)} %bitcast.1.flip_ref, s32[12]{0:T(128)} %bitcast.29, bf16[12,2048]{1,0:T(8,128)(2,1)} %rows_ref.3), custom_call_target="tpu_custom_call" | custom-call | tf_op jit(solution)/shard_map/pack/pallas_call | solution.py:97
  11.8 1.7 %collective-permute-start.1 = (bf16[4,2048]{1,0:T(4,128)(2,1)}, bf16[4,2048]{1,0:T(4,128)(2,1)S(1)}, u32[]{:S(2)}, u32[]{:S(2)}) collective-permute-start(bf16[4,2048]{1,0:T(4,128)(2,1)} %get-tuple-element.44), channel_id=1, source_target_pairs={{0,16},{8,24},{16,0},{24,8},{1,17},{9,25},{17,1},{25,9},{2,18},{10... | collective-permute-start | bytes 49160 | tf_op jit(solution)/shard_map/ppermute | solution.py:320
  13.4 1.4 constant_dynamic-slice_fusion
  16.1 4.6 %dynamic-slice_bitcast_fusion.4.wi_ref = bf16[2048,1024]{1,0:T(8,128)(2,1)} fusion(bf16[1,2,2048,1024]{3,2,1,0:T(8,128)(2,1)} %param.11, s32[]{:T(128)S(6)} %select_n.78), kind=kLoop, calls=%fused_computation.4 | loop fusion | bytes 8388612 | tf_op jit(solution)/shard_map/jit(dynamic_index_in_dim)/squeeze | solution.py:348
  20.9 2.7 %collective-permute-start.3 = (bf16[16,2048]{1,0:T(8,128)(2,1)S(1)}, bf16[16,2048]{1,0:T(8,128)(2,1)S(1)}, u32[]{:S(2)}, u32[]{:S(2)}) collective-permute-start(bf16[16,2048]{1,0:T(8,128)(2,1)S(1)} %pad_maximum_fusion.4), channel_id=1, source_target_pairs={{0,4},{1,5},{2,6},{3,7},{4,0},{5,1},{6,2},{7,3},{8,12},{9,13},{10,... | collective-permute-start | bytes 196616 | tf_op jit(solution)/shard_map/ppermute | solution.py:320
  23.6 4.8 %dynamic-slice_bitcast_fusion.3.wo_ref = bf16[1024,2048]{1,0:T(8,128)(2,1)} fusion(bf16[1,2,1024,2048]{3,2,1,0:T(8,128)(2,1)} %param.12, s32[]{:T(128)S(6)} %select_n.79), kind=kLoop, calls=%fused_computation.3 | loop fusion | bytes 8388612 | tf_op jit(solution)/shard_map/jit(dynamic_index_in_dim)/squeeze | solution.py:348
  28.6 2.2 %copy-done.1 = bf16[2048,1024]{1,0:T(8,128)(2,1)S(1)} copy-done((bf16[2048,1024]{1,0:T(8,128)(2,1)S(1)}, bf16[2048,1024]{1,0:T(8,128)(2,1)}, u32[]{:S(2)}) %copy-start.1) | copy-done | bytes 4194328
  30.7 2.2 %copy-done.2 = bf16[1024,2048]{1,0:T(8,128)(2,1)S(1)} copy-done((bf16[1024,2048]{1,0:T(8,128)(2,1)S(1)}, bf16[1024,2048]{1,0:T(8,128)(2,1)}, u32[]{:S(2)}) %copy-start.2) | copy-done | bytes 4194328
  32.9 2.6 %low_forward.1 = (bf16[128,2048]{1,0:T(8,128)(2,1)S(1)}, bf16[128,1024]{1,0:T(8,128)(2,1)S(1)}, f32[128,1024]{1,0:T(8,128)S(1)}, bf16[128,2048]{1,0:T(8,128)(2,1)}) custom-call(bf16[128,2048]{1,0:T(8,128)(2,1)S(1)} %reshape.36.x_ref, bf16[2,2048]{1,0:T(2,128)(2,1)S(1)} %bitcast.25, bf16[2048,1024]{1,0:T(8,128)(2,1)S(1)} %copy-done.1, ...), custom_call_target="tpu_custom_call" | custom-call | tf_op jit(solution)/shard_map/low_forward/pallas_call | solution.py:43
  35.7 4.8 %all-to-all-start.1 = ((bf16[8,16,2048]{2,1,0:T(8,128)(2,1)}), bf16[8,16,2048]{2,1,0:T(8,128)(2,1)S(1)}, u32[]{:S(2)}, u32[]{:S(2)}) async-start(bf16[8,16,2048]{2,1,0:T(8,128)(2,1)} %bitcast.10), calls=%async_computation.1 | async-start | bytes 1048576 | tf_op jit(solution)/shard_map/all_to_all | solution.py:316
  41.5 1.5 collective-permute-start.5
  43.0 2.1 %collective-permute-start.6 = (bf16[32,2048]{1,0:T(8,128)(2,1)S(1)}, bf16[32,2048]{1,0:T(8,128)(2,1)S(1)}, u32[]{:S(2)}, u32[]{:S(2)}) collective-permute-start(bf16[32,2048]{1,0:T(8,128)(2,1)S(1)} %pad_maximum_fusion.3), channel_id=1, source_target_pairs={{0,2},{1,3},{2,0},{3,1},{4,6},{5,7},{6,4},{7,5},{8,10},{9,11},{10,... | collective-permute-start | bytes 393224 | tf_op jit(solution)/shard_map/ppermute | solution.py:320
  46.4 6.4 %collective-permute-done.6 = bf16[32,2048]{1,0:T(8,128)(2,1)S(1)} collective-permute-done((bf16[32,2048]{1,0:T(8,128)(2,1)S(1)}, bf16[32,2048]{1,0:T(8,128)(2,1)S(1)}, u32[]{:S(2)}, u32[]{:S(2)}) %collective-permute-start.6) | collective-permute-done | bytes 131104 | tf_op jit(solution)/shard_map/ppermute | solution.py:320
  52.8 2.8 %all-to-all-done.1.got_ref = bf16[8,16,2048]{2,1,0:T(8,128)(2,1)S(1)} async-done(((bf16[8,16,2048]{2,1,0:T(8,128)(2,1)}), bf16[8,16,2048]{2,1,0:T(8,128)(2,1)S(1)}, u32[]{:S(2)}, u32[]{:S(2)}) %all-to-all-start.1) | async-done | bytes 524320 | tf_op jit(solution)/shard_map/all_to_all | solution.py:316
  56.6 1.0 pad_maximum_fusion.1
  57.6 4.6 %dynamic-slice_bitcast_fusion.1.wi_ref = bf16[2048,1024]{1,0:T(8,128)(2,1)} fusion(bf16[1,2,2048,1024]{3,2,1,0:T(8,128)(2,1)} %param.11, s32[]{:T(128)S(6)} %select_n.86), kind=kLoop, calls=%fused_computation.1 | loop fusion | bytes 8388612 | tf_op jit(solution)/shard_map/jit(dynamic_index_in_dim)/squeeze | solution.py:348
  62.3 2.0 %collective-permute-start.11 = (bf16[64,2048]{1,0:T(8,128)(2,1)S(1)}, bf16[64,2048]{1,0:T(8,128)(2,1)}, u32[]{:S(2)}, u32[]{:S(2)}) collective-permute-start(bf16[64,2048]{1,0:T(8,128)(2,1)S(1)} %pad_maximum_fusion.1), channel_id=1, source_target_pairs={{0,1},{1,0},{2,3},{3,2},{4,5},{5,4},{6,7},{7,6},{8,9},{9,8},{10,11... | collective-permute-start | bytes 786440 | tf_op jit(solution)/shard_map/ppermute | solution.py:320
  64.3 1.4 settle.1
  65.7 4.5 %all-to-all-start.2 = ((bf16[8,16,2048]{2,1,0:T(8,128)(2,1)}), bf16[8,16,2048]{2,1,0:T(8,128)(2,1)S(1)}, u32[]{:S(2)}, u32[]{:S(2)}) async-start(bf16[8,16,2048]{2,1,0:T(8,128)(2,1)} %get-tuple-element.56), calls=%async_computation.2 | async-start | bytes 1048576 | tf_op jit(solution)/shard_map/all_to_all | solution.py:309
  70.4 1.5 collective-permute-start.10
  71.9 2.5 %dynamic-slice_bitcast_fusion.2.wo_ref = bf16[1024,2048]{1,0:T(8,128)(2,1)S(1)} fusion(bf16[1,2,1024,2048]{3,2,1,0:T(8,128)(2,1)} %param.12, s32[]{:T(128)S(6)} %select_n.86), kind=kLoop, calls=%fused_computation.2 | loop fusion | bytes 8388612 | tf_op jit(solution)/shard_map/jit(dynamic_index_in_dim)/squeeze | solution.py:348
  74.4 1.0 pad_maximum_fusion.raw_ref
  75.4 2.2 %high_grad.1 = (bf16[128,2048]{1,0:T(8,128)(2,1)S(1)}, f32[128,1024]{1,0:T(8,128)S(1)}) custom-call(s32[4]{0:T(128)S(1)} %pad_add_fusion.where_ref, bf16[128,2048]{1,0:T(8,128)(2,1)S(1)} %pad_maximum_fusion.raw_ref, bf16[1024,2048]{1,0:T(8,128)(2,1)S(1)} %dynamic-slice_bitcast_fusion.2.wo_ref), custom_call_target="tpu_custom_call" | custom-call | tf_op jit(solution)/shard_map/high_grad/pallas_call | solution.py:43
  78.7 6.5 %all-to-all-done.2 = bf16[8,16,2048]{2,1,0:T(8,128)(2,1)S(1)} async-done(((bf16[8,16,2048]{2,1,0:T(8,128)(2,1)}), bf16[8,16,2048]{2,1,0:T(8,128)(2,1)S(1)}, u32[]{:S(2)}, u32[]{:S(2)}) %all-to-all-start.2) | async-done | bytes 524320 | tf_op jit(solution)/shard_map/all_to_all | solution.py:309
  85.2 2.2 %copy-done = bf16[2048,1024]{1,0:T(8,128)(2,1)S(1)} copy-done((bf16[2048,1024]{1,0:T(8,128)(2,1)S(1)}, bf16[2048,1024]{1,0:T(8,128)(2,1)}, u32[]{:S(2)}) %copy-start) | copy-done | bytes 4194328
  87.3 3.4 %high_both.1 = (bf16[128,2048]{1,0:T(8,128)(2,1)S(1)}, bf16[128,2048]{1,0:T(8,128)(2,1)S(1)}, bf16[128,2048]{1,0:T(8,128)(2,1)}) custom-call(bf16[128,2048]{1,0:T(8,128)(2,1)S(1)} %bitcast.24, bf16[2,2048]{1,0:T(2,128)(2,1)S(1)} %bitcast.26, bf16[2048,1024]{1,0:T(8,128)(2,1)S(1)} %copy-done, f32[128,1024]{1,0:T(8,128)S(1)} %get-tuple-element.63.du_ref), custom_call_target="tpu_custom_call" | custom-call | tf_op jit(solution)/shard_map/high_both/pallas_call | solution.py:43
  90.7 3.6 %all-to-all-start.3 = ((bf16[8,16,2048]{2,1,0:T(8,128)(2,1)}), bf16[8,16,2048]{2,1,0:T(8,128)(2,1)S(1)}, u32[]{:S(2)}, u32[]{:S(2)}) async-start(bf16[8,16,2048]{2,1,0:T(8,128)(2,1)} %bitcast.14), calls=%async_computation.3 | async-start | bytes 1048576 | tf_op jit(solution)/shard_map/all_to_all | solution.py:316
  95.7 1.5 collective-permute-start.13
  97.2 1.0 broadcast_select_fusion.3.bn_ref
  98.2 1.7 %collective-permute-start.14 = (bf16[64,2048]{1,0:T(8,128)(2,1)S(1)}, bf16[64,2048]{1,0:T(8,128)(2,1)}, u32[]{:S(2)}, u32[]{:S(2)}) collective-permute-start(bf16[64,2048]{1,0:T(8,128)(2,1)S(1)} %broadcast_select_fusion.3.bn_ref), channel_id=1, source_target_pairs={{0,1},{1,0},{2,3},{3,2},{4,5},{5,4},{6,7},{7,6},{8,9},{9,8},{10,11... | collective-permute-start | bytes 786440 | tf_op jit(solution)/shard_map/ppermute | solution.py:320
  99.9 9.6 %collective-permute-done.14.bf_ref = bf16[64,2048]{1,0:T(8,128)(2,1)} collective-permute-done((bf16[64,2048]{1,0:T(8,128)(2,1)S(1)}, bf16[64,2048]{1,0:T(8,128)(2,1)}, u32[]{:S(2)}, u32[]{:S(2)}) %collective-permute-start.14) | collective-permute-done | bytes 262176 | tf_op jit(solution)/shard_map/ppermute | solution.py:320
  110.0 1.6 settle_back.1
  112.5 1.5 collective-permute-start.16
  113.9 6.0 %all-to-all-start.4 = ((bf16[8,16,2048]{2,1,0:T(8,128)(2,1)}), bf16[8,16,2048]{2,1,0:T(8,128)(2,1)S(1)}, u32[]{:S(2)}, u32[]{:S(2)}) async-start(bf16[8,16,2048]{2,1,0:T(8,128)(2,1)} %get-tuple-element.70), calls=%async_computation.4 | async-start | bytes 1048576 | tf_op jit(solution)/shard_map/all_to_all | solution.py:309
  120.6 4.8 %dynamic-slice_bitcast_fusion.wo_ref = bf16[1024,2048]{1,0:T(8,128)(2,1)} fusion(bf16[1,2,1024,2048]{3,2,1,0:T(8,128)(2,1)} %param.12, s32[]{:T(128)S(6)} %select_n.92), kind=kLoop, calls=%fused_computation | loop fusion | bytes 8388612 | tf_op jit(solution)/shard_map/jit(dynamic_index_in_dim)/squeeze | solution.py:348
  125.4 5.0 %pair_grad.4.rest_0_ = bf16[1,2,1024,2048]{3,2,1,0:T(8,128)(2,1)} custom-call(s32[4]{0:T(128)} %copy-done.12, bf16[128,2048]{1,0:T(8,128)(2,1)} %copy-done.4, bf16[128,2048]{1,0:T(8,128)(2,1)} %copy-done.13, bf16[128,2048]{1,0:T(8,128)(2,1)} %collective-permute-done.13.af_ref.bf_ref, bf16[128,2048]{1,0:T(8,128)(2,1)} %copy-done.9, ...), custom_call_target="tpu_custom_call" | custom-call | tf_op jit(solution)/shard_map/pair_grad/pallas_call | solution.py:284
  130.4 4.4 %all-to-all-done.4 = bf16[8,16,2048]{2,1,0:T(8,128)(2,1)S(1)} async-done(((bf16[8,16,2048]{2,1,0:T(8,128)(2,1)}), bf16[8,16,2048]{2,1,0:T(8,128)(2,1)S(1)}, u32[]{:S(2)}, u32[]{:S(2)}) %all-to-all-start.4) | async-done | bytes 524320 | tf_op jit(solution)/shard_map/all_to_all | solution.py:309
  134.8 2.4 %copy-done.3 = bf16[1024,2048]{1,0:T(8,128)(2,1)S(1)} copy-done((bf16[1024,2048]{1,0:T(8,128)(2,1)S(1)}, bf16[1024,2048]{1,0:T(8,128)(2,1)}, u32[]{:S(2)}) %copy-start.3) | copy-done | bytes 4194328
  137.2 1.6 low_grad.1.b_ref
  138.8 1.2 collective-permute-start.23
  140.0 3.2 %collective-permute-start.21 = (bf16[16,2048]{1,0:T(8,128)(2,1)S(1)}, bf16[16,2048]{1,0:T(8,128)(2,1)S(1)}, u32[]{:S(2)}, u32[]{:S(2)}) collective-permute-start(bf16[16,2048]{1,0:T(8,128)(2,1)S(1)} %broadcast_select_fusion.8), channel_id=1, source_target_pairs={{0,4},{1,5},{2,6},{3,7},{4,0},{5,1},{6,2},{7,3},{8,12},{9,13},{10,... | collective-permute-start | bytes 196616 | tf_op jit(solution)/shard_map/ppermute | solution.py:320
  143.2 2.4 %collective-permute-done.23 = bf16[16,2048]{1,0:T(8,128)(2,1)S(1)} collective-permute-done((bf16[16,2048]{1,0:T(8,128)(2,1)S(1)}, bf16[16,2048]{1,0:T(8,128)(2,1)S(1)}, u32[]{:S(2)}, u32[]{:S(2)}) %collective-permute-start.23) | collective-permute-done | bytes 65568 | tf_op jit(solution)/shard_map/ppermute | solution.py:320
  146.3 2.3 %collective-permute-start.24 = (bf16[64,2048]{1,0:T(8,128)(2,1)S(1)}, bf16[64,2048]{1,0:T(8,128)(2,1)S(1)}, u32[]{:S(2)}, u32[]{:S(2)}) collective-permute-start(bf16[64,2048]{1,0:T(8,128)(2,1)S(1)} %pad_maximum_fusion.2.bn_ref), channel_id=1, source_target_pairs={{0,1},{1,0},{2,3},{3,2},{4,5},{5,4},{6,7},{7,6},{8,9},{9,8},{10,11... | collective-permute-start | bytes 786440 | tf_op jit(solution)/shard_map/ppermute | solution.py:320
  149.3 5.4 %pair_grad.5.rest_0_ = bf16[1,2,2048,1024]{3,2,1,0:T(8,128)(2,1)} custom-call(s32[4]{0:T(128)} %copy-done.12, bf16[128,2048]{1,0:T(8,128)(2,1)} %copy-done.8, bf16[128,2048]{1,0:T(8,128)(2,1)} %collective-permute-done.15.an_ref, bf16[128,2048]{1,0:T(8,128)(2,1)} %collective-permute-done.16.af_ref, bf16[128,2048]{1,0:T(8,128)(2,1)} %copy-done.4, ...), custom_call_target="tpu_custom_call" | custom-call | tf_op jit(solution)/shard_map/pair_grad/pallas_call | solution.py:284
  155.5 5.0 %pair_grad.7 = bf16[1,2,1024,2048]{3,2,1,0:T(8,128)(2,1)} custom-call(s32[4]{0:T(128)} %copy-done.12, bf16[128,1024]{1,0:T(8,128)(2,1)} %copy-done.10, bf16[128,1024]{1,0:T(8,128)(2,1)} %copy-done.16, bf16[128,1024]{1,0:T(8,128)(2,1)} %collective-permute-done.8.af_ref, bf16[128,2048]{1,0:T(8,128)(2,1)} %bitcast.23, ...), custom_call_target="tpu_custom_call", output_to_operand_aliasing={{}: (7, {})} | custom-call | tf_op jit(solution)/shard_map/pair_grad/pallas_call | solution.py:284
  161.2 5.4 %pair_grad.6 = bf16[1,2,2048,1024]{3,2,1,0:T(8,128)(2,1)} custom-call(s32[4]{0:T(128)} %copy-done.12, bf16[128,2048]{1,0:T(8,128)(2,1)} %copy-done.7, bf16[128,2048]{1,0:T(8,128)(2,1)} %copy-done.14, bf16[128,2048]{1,0:T(8,128)(2,1)} %collective-permute-done.5.af_ref, bf16[128,1024]{1,0:T(8,128)(2,1)} %copy-done.6, ...), custom_call_target="tpu_custom_call", output_to_operand_aliasing={{}: (7, {})} | custom-call | tf_op jit(solution)/shard_map/pair_grad/pallas_call | solution.py:284
  (94 shorter events, 11.3 us)
Async XLA Ops:
  2.5 25.9 %all-to-all-start = ((bf16[32,4,2048]{2,1,0:T(4,128)(2,1)}), bf16[32,4,2048]{2,1,0:T(4,128)(2,1)S(1)}, u32[]{:S(2)}, u32[]{:S(2)}) async-start(bf16[32,4,2048]{2,1,0:T(4,128)(2,1)} %pack.2), calls=%async_computation | async-start | bytes 1048576 | tf_op jit(solution)/shard_map/all_to_all | solution.py:304
  11.5 9.4 %copy-start.23 = (bf16[4,2048]{1,0:T(4,128)(2,1)S(1)}, bf16[4,2048]{1,0:T(4,128)(2,1)}, u32[]{:S(2)}) copy-start(bf16[4,2048]{1,0:T(4,128)(2,1)} %get-tuple-element.42) | copy-start | bytes 49156
  11.5 9.4 %collective-permute-start = (bf16[4,2048]{1,0:T(4,128)(2,1)}, bf16[4,2048]{1,0:T(4,128)(2,1)S(1)}, u32[]{:S(2)}, u32[]{:S(2)}) collective-permute-start(bf16[4,2048]{1,0:T(4,128)(2,1)} %get-tuple-element.43), channel_id=1, source_target_pairs={{0,8},{8,0},{16,24},{24,16},{1,9},{9,1},{17,25},{25,17},{2,10},{10... | collective-permute-start | bytes 49160 | tf_op jit(solution)/shard_map/ppermute | solution.py:320
  11.8 9.1 %collective-permute-start.1 = (bf16[4,2048]{1,0:T(4,128)(2,1)}, bf16[4,2048]{1,0:T(4,128)(2,1)S(1)}, u32[]{:S(2)}, u32[]{:S(2)}) collective-permute-start(bf16[4,2048]{1,0:T(4,128)(2,1)} %get-tuple-element.44), channel_id=1, source_target_pairs={{0,16},{8,24},{16,0},{24,8},{1,17},{9,25},{17,1},{25,9},{2,18},{10... | collective-permute-start | bytes 49160 | tf_op jit(solution)/shard_map/ppermute | solution.py:320
  13.4 7.4 %collective-permute-start.2 = (bf16[4,2048]{1,0:T(4,128)(2,1)}, bf16[4,2048]{1,0:T(4,128)(2,1)S(1)}, u32[]{:S(2)}, u32[]{:S(2)}) collective-permute-start(bf16[4,2048]{1,0:T(4,128)(2,1)} %get-tuple-element.45), channel_id=1, source_target_pairs={{0,24},{8,16},{16,8},{24,0},{1,25},{9,17},{17,9},{25,1},{2,26},{10... | collective-permute-start | bytes 49160 | tf_op jit(solution)/shard_map/ppermute | solution.py:320
  16.1 12.4 %copy-start.11 = (bf16[1,2,2048]{2,1,0:T(2,128)(2,1)S(1)}, bf16[1,2,2048]{2,1,0:T(2,128)(2,1)}, u32[]{:S(2)}) copy-start(bf16[1,2,2048]{2,1,0:T(2,128)(2,1)} %param.10) | copy-start | bytes 24580
  20.9 89.1 %copy-start.12 = (s32[4]{0:T(128)}, s32[4]{0:T(128)S(1)}, u32[]{:S(2)}) copy-start(s32[4]{0:T(128)S(1)} %pad_add_fusion.where_ref) | copy-start | bytes 52
  20.9 7.6 %collective-permute-start.3 = (bf16[16,2048]{1,0:T(8,128)(2,1)S(1)}, bf16[16,2048]{1,0:T(8,128)(2,1)S(1)}, u32[]{:S(2)}, u32[]{:S(2)}) collective-permute-start(bf16[16,2048]{1,0:T(8,128)(2,1)S(1)} %pad_maximum_fusion.4), channel_id=1, source_target_pairs={{0,4},{1,5},{2,6},{3,7},{4,0},{5,1},{6,2},{7,3},{8,12},{9,13},{10,... | collective-permute-start | bytes 196616 | tf_op jit(solution)/shard_map/ppermute | solution.py:320
  35.6 38.8 %copy-start.7 = (bf16[128,2048]{1,0:T(8,128)(2,1)}, bf16[128,2048]{1,0:T(8,128)(2,1)S(1)}, u32[]{:S(2)}) copy-start(bf16[128,2048]{1,0:T(8,128)(2,1)S(1)} %get-tuple-element.50.a_ref) | copy-start | bytes 1572868
  35.6 38.8 %copy-start.10 = (bf16[128,1024]{1,0:T(8,128)(2,1)}, bf16[128,1024]{1,0:T(8,128)(2,1)S(1)}, u32[]{:S(2)}) copy-start(bf16[128,1024]{1,0:T(8,128)(2,1)S(1)} %get-tuple-element.57.a_ref) | copy-start | bytes 786436
  35.6 5.0 %collective-permute-start.4 = (bf16[128,2048]{1,0:T(8,128)(2,1)S(1)}, bf16[128,2048]{1,0:T(8,128)(2,1)S(1)}, u32[]{:S(2)}, u32[]{:S(2)}) collective-permute-start(bf16[128,2048]{1,0:T(8,128)(2,1)S(1)} %get-tuple-element.50.a_ref), channel_id=1, source_target_pairs={{0,8},{8,0},{16,24},{24,16},{1,9},{9,1},{17,25},{25,17},{2,10},{10... | collective-permute-start | bytes 1572872 | tf_op jit(solution)/shard_map/ppermute | solution.py:320
  35.7 19.9 %all-to-all-start.1 = ((bf16[8,16,2048]{2,1,0:T(8,128)(2,1)}), bf16[8,16,2048]{2,1,0:T(8,128)(2,1)S(1)}, u32[]{:S(2)}, u32[]{:S(2)}) async-start(bf16[8,16,2048]{2,1,0:T(8,128)(2,1)} %bitcast.10), calls=%async_computation.1 | async-start | bytes 1048576 | tf_op jit(solution)/shard_map/all_to_all | solution.py:316
  40.5 33.9 %copy-start.14 = (bf16[128,2048]{1,0:T(8,128)(2,1)}, bf16[128,2048]{1,0:T(8,128)(2,1)S(1)}, u32[]{:S(2)}) copy-start(bf16[128,2048]{1,0:T(8,128)(2,1)S(1)} %collective-permute-done.4.an_ref) | copy-start | bytes 1572868
  41.5 15.1 %collective-permute-start.5 = (bf16[128,2048]{1,0:T(8,128)(2,1)}, bf16[128,2048]{1,0:T(8,128)(2,1)}, u32[]{:S(2)}, u32[]{:S(2)}) collective-permute-start(bf16[128,2048]{1,0:T(8,128)(2,1)} %broadcast_select_fusion.2), channel_id=1, source_target_pairs={{0,16},{8,24},{16,0},{24,8},{1,17},{9,25},{17,1},{25,9},{2,18},{10... | collective-permute-start | bytes 1572872 | tf_op jit(solution)/shard_map/ppermute | solution.py:320
  42.9 2.1 %collective-permute-start.7 = (bf16[128,1024]{1,0:T(8,128)(2,1)S(1)}, bf16[128,1024]{1,0:T(8,128)(2,1)S(1)}, u32[]{:S(2)}, u32[]{:S(2)}) collective-permute-start(bf16[128,1024]{1,0:T(8,128)(2,1)S(1)} %get-tuple-element.57.a_ref), channel_id=1, source_target_pairs={{0,8},{8,0},{16,24},{24,16},{1,9},{9,1},{17,25},{25,17},{2,10},{10... | collective-permute-start | bytes 786440 | tf_op jit(solution)/shard_map/ppermute | solution.py:320
  43.0 12.7 %copy-start.19 = (bf16[32,2048]{1,0:T(8,128)(2,1)}, bf16[32,2048]{1,0:T(8,128)(2,1)S(1)}, u32[]{:S(2)}) copy-start(bf16[32,2048]{1,0:T(8,128)(2,1)S(1)} %pad_maximum_fusion.3) | copy-start | bytes 393220
  43.0 9.8 %collective-permute-start.6 = (bf16[32,2048]{1,0:T(8,128)(2,1)S(1)}, bf16[32,2048]{1,0:T(8,128)(2,1)S(1)}, u32[]{:S(2)}, u32[]{:S(2)}) collective-permute-start(bf16[32,2048]{1,0:T(8,128)(2,1)S(1)} %pad_maximum_fusion.3), channel_id=1, source_target_pairs={{0,2},{1,3},{2,0},{3,1},{4,6},{5,7},{6,4},{7,5},{8,10},{9,11},{10,... | collective-permute-start | bytes 393224 | tf_op jit(solution)/shard_map/ppermute | solution.py:320
  45.0 29.4 %copy-start.16 = (bf16[128,1024]{1,0:T(8,128)(2,1)}, bf16[128,1024]{1,0:T(8,128)(2,1)S(1)}, u32[]{:S(2)}) copy-start(bf16[128,1024]{1,0:T(8,128)(2,1)S(1)} %collective-permute-done.7.an_ref) | copy-start | bytes 786436
  45.8 31.8 %collective-permute-start.8 = (bf16[128,1024]{1,0:T(8,128)(2,1)}, bf16[128,1024]{1,0:T(8,128)(2,1)}, u32[]{:S(2)}, u32[]{:S(2)}) collective-permute-start(bf16[128,1024]{1,0:T(8,128)(2,1)} %broadcast_select_fusion.6), channel_id=1, source_target_pairs={{0,16},{8,24},{16,0},{24,8},{1,17},{9,25},{17,1},{25,9},{2,18},{10... | collective-permute-start | bytes 786440 | tf_op jit(solution)/shard_map/ppermute | solution.py:320
  52.8 2.8 %copy-start.22 = (bf16[32,2048]{1,0:T(8,128)(2,1)}, bf16[32,2048]{1,0:T(8,128)(2,1)S(1)}, u32[]{:S(2)}) copy-start(bf16[32,2048]{1,0:T(8,128)(2,1)S(1)} %collective-permute-done.6) | copy-start | bytes 393220
  57.6 12.7 %collective-permute-start.9 = (bf16[64,2048]{1,0:T(8,128)(2,1)S(1)}, bf16[64,2048]{1,0:T(8,128)(2,1)}, u32[]{:S(2)}, u32[]{:S(2)}) collective-permute-start(bf16[64,2048]{1,0:T(8,128)(2,1)S(1)} %pad_maximum_fusion.1), channel_id=1, source_target_pairs={{0,8},{8,0},{16,24},{24,16},{1,9},{9,1},{17,25},{25,17},{2,10},{10... | collective-permute-start | bytes 786440 | tf_op jit(solution)/shard_map/ppermute | solution.py:320
  62.3 12.2 %collective-permute-start.11 = (bf16[64,2048]{1,0:T(8,128)(2,1)S(1)}, bf16[64,2048]{1,0:T(8,128)(2,1)}, u32[]{:S(2)}, u32[]{:S(2)}) collective-permute-start(bf16[64,2048]{1,0:T(8,128)(2,1)S(1)} %pad_maximum_fusion.1), channel_id=1, source_target_pairs={{0,1},{1,0},{2,3},{3,2},{4,5},{5,4},{6,7},{7,6},{8,9},{9,8},{10,11... | collective-permute-start | bytes 786440 | tf_op jit(solution)/shard_map/ppermute | solution.py:320
  65.7 19.4 %all-to-all-start.2 = ((bf16[8,16,2048]{2,1,0:T(8,128)(2,1)}), bf16[8,16,2048]{2,1,0:T(8,128)(2,1)S(1)}, u32[]{:S(2)}, u32[]{:S(2)}) async-start(bf16[8,16,2048]{2,1,0:T(8,128)(2,1)} %get-tuple-element.56), calls=%async_computation.2 | async-start | bytes 1048576 | tf_op jit(solution)/shard_map/all_to_all | solution.py:309
  70.4 8.3 %collective-permute-start.10 = (bf16[64,2048]{1,0:T(8,128)(2,1)S(1)}, bf16[64,2048]{1,0:T(8,128)(2,1)}, u32[]{:S(2)}, u32[]{:S(2)}) collective-permute-start(bf16[64,2048]{1,0:T(8,128)(2,1)S(1)} %broadcast_select_fusion.4), channel_id=1, source_target_pairs={{0,16},{8,24},{16,0},{24,8},{1,17},{9,25},{17,1},{25,9},{2,18},{10... | collective-permute-start | bytes 786440 | tf_op jit(solution)/shard_map/ppermute | solution.py:320
  77.7 47.7 %copy-start.9 = (bf16[128,2048]{1,0:T(8,128)(2,1)}, bf16[128,2048]{1,0:T(8,128)(2,1)S(1)}, u32[]{:S(2)}) copy-start(bf16[128,2048]{1,0:T(8,128)(2,1)S(1)} %get-tuple-element.68.dy_ref.b_ref) | copy-start | bytes 1572868
  90.7 34.6 %copy-start.4 = (bf16[128,2048]{1,0:T(8,128)(2,1)}, bf16[128,2048]{1,0:T(8,128)(2,1)S(1)}, u32[]{:S(2)}) copy-start(bf16[128,2048]{1,0:T(8,128)(2,1)S(1)} %get-tuple-element.65.a_ref.b_ref) | copy-start | bytes 1572868
  90.7 39.6 %copy-start.8 = (bf16[128,2048]{1,0:T(8,128)(2,1)}, bf16[128,2048]{1,0:T(8,128)(2,1)S(1)}, u32[]{:S(2)}) copy-start(bf16[128,2048]{1,0:T(8,128)(2,1)S(1)} %get-tuple-element.71.a_ref) | copy-start | bytes 1572868
  90.7 4.1 %collective-permute-start.12 = (bf16[128,2048]{1,0:T(8,128)(2,1)S(1)}, bf16[128,2048]{1,0:T(8,128)(2,1)S(1)}, u32[]{:S(2)}, u32[]{:S(2)}) collective-permute-start(bf16[128,2048]{1,0:T(8,128)(2,1)S(1)} %get-tuple-element.65.a_ref.b_ref), channel_id=1, source_target_pairs={{0,8},{8,0},{16,24},{24,16},{1,9},{9,1},{17,25},{25,17},{2,10},{10... | collective-permute-start | bytes 1572872 | tf_op jit(solution)/shard_map/ppermute | solution.py:320
  90.7 18.9 %all-to-all-start.3 = ((bf16[8,16,2048]{2,1,0:T(8,128)(2,1)}), bf16[8,16,2048]{2,1,0:T(8,128)(2,1)S(1)}, u32[]{:S(2)}, u32[]{:S(2)}) async-start(bf16[8,16,2048]{2,1,0:T(8,128)(2,1)} %bitcast.14), calls=%async_computation.3 | async-start | bytes 1048576 | tf_op jit(solution)/shard_map/all_to_all | solution.py:316
  94.4 17.2 %collective-permute-start.15 = (bf16[128,2048]{1,0:T(8,128)(2,1)S(1)}, bf16[128,2048]{1,0:T(8,128)(2,1)}, u32[]{:S(2)}, u32[]{:S(2)}) collective-permute-start(bf16[128,2048]{1,0:T(8,128)(2,1)S(1)} %get-tuple-element.71.a_ref), channel_id=1, source_target_pairs={{0,8},{8,0},{16,24},{24,16},{1,9},{9,1},{17,25},{25,17},{2,10},{10... | collective-permute-start | bytes 1572872 | tf_op jit(solution)/shard_map/ppermute | solution.py:320
  94.8 30.6 %copy-start.13 = (bf16[128,2048]{1,0:T(8,128)(2,1)}, bf16[128,2048]{1,0:T(8,128)(2,1)S(1)}, u32[]{:S(2)}) copy-start(bf16[128,2048]{1,0:T(8,128)(2,1)S(1)} %collective-permute-done.12.an_ref.bn_ref) | copy-start | bytes 1572868
  95.7 14.2 %collective-permute-start.13 = (bf16[128,2048]{1,0:T(8,128)(2,1)}, bf16[128,2048]{1,0:T(8,128)(2,1)}, u32[]{:S(2)}, u32[]{:S(2)}) collective-permute-start(bf16[128,2048]{1,0:T(8,128)(2,1)} %broadcast_select_fusion.1), channel_id=1, source_target_pairs={{0,16},{8,24},{16,0},{24,8},{1,17},{9,25},{17,1},{25,9},{2,18},{10... | collective-permute-start | bytes 1572872 | tf_op jit(solution)/shard_map/ppermute | solution.py:320
  98.2 27.2 %copy-start.18 = (bf16[64,2048]{1,0:T(8,128)(2,1)}, bf16[64,2048]{1,0:T(8,128)(2,1)S(1)}, u32[]{:S(2)}) copy-start(bf16[64,2048]{1,0:T(8,128)(2,1)S(1)} %broadcast_select_fusion.3.bn_ref) | copy-start | bytes 786436
  98.2 11.3 %collective-permute-start.14 = (bf16[64,2048]{1,0:T(8,128)(2,1)S(1)}, bf16[64,2048]{1,0:T(8,128)(2,1)}, u32[]{:S(2)}, u32[]{:S(2)}) collective-permute-start(bf16[64,2048]{1,0:T(8,128)(2,1)S(1)} %broadcast_select_fusion.3.bn_ref), channel_id=1, source_target_pairs={{0,1},{1,0},{2,3},{3,2},{4,5},{5,4},{6,7},{7,6},{8,9},{9,8},{10,11... | collective-permute-start | bytes 786440 | tf_op jit(solution)/shard_map/ppermute | solution.py:320
  111.6 8.4 %collective-permute-start.19 = (bf16[16,2048]{1,0:T(8,128)(2,1)S(1)}, bf16[16,2048]{1,0:T(8,128)(2,1)S(1)}, u32[]{:S(2)}, u32[]{:S(2)}) collective-permute-start(bf16[16,2048]{1,0:T(8,128)(2,1)S(1)} %get-tuple-element.79), channel_id=1, source_target_pairs={{0,8},{8,0},{16,24},{24,16},{1,9},{9,1},{17,25},{25,17},{2,10},{10... | collective-permute-start | bytes 196616 | tf_op jit(solution)/shard_map/ppermute | solution.py:320
  112.5 17.9 %collective-permute-start.16 = (bf16[128,2048]{1,0:T(8,128)(2,1)}, bf16[128,2048]{1,0:T(8,128)(2,1)}, u32[]{:S(2)}, u32[]{:S(2)}) collective-permute-start(bf16[128,2048]{1,0:T(8,128)(2,1)} %broadcast_select_fusion), channel_id=1, source_target_pairs={{0,16},{8,24},{16,0},{24,8},{1,17},{9,25},{17,1},{25,9},{2,18},{10... | collective-permute-start | bytes 1572872 | tf_op jit(solution)/shard_map/ppermute | solution.py:320
  113.9 20.9 %all-to-all-start.4 = ((bf16[8,16,2048]{2,1,0:T(8,128)(2,1)}), bf16[8,16,2048]{2,1,0:T(8,128)(2,1)S(1)}, u32[]{:S(2)}, u32[]{:S(2)}) async-start(bf16[8,16,2048]{2,1,0:T(8,128)(2,1)} %get-tuple-element.70), calls=%async_computation.4 | async-start | bytes 1048576 | tf_op jit(solution)/shard_map/all_to_all | solution.py:309
  120.0 10.4 %collective-permute-start.20 = (bf16[16,2048]{1,0:T(8,128)(2,1)S(1)}, bf16[16,2048]{1,0:T(8,128)(2,1)S(1)}, u32[]{:S(2)}, u32[]{:S(2)}) collective-permute-start(bf16[16,2048]{1,0:T(8,128)(2,1)S(1)} %broadcast_select_fusion.7), channel_id=1, source_target_pairs={{0,16},{8,24},{16,0},{24,8},{1,17},{9,25},{17,1},{25,9},{2,18},{10... | collective-permute-start | bytes 196616 | tf_op jit(solution)/shard_map/ppermute | solution.py:320
  134.8 19.9 %copy-start.5 = (bf16[8,16,2048]{2,1,0:T(8,128)(2,1)}, bf16[8,16,2048]{2,1,0:T(8,128)(2,1)S(1)}, u32[]{:S(2)}) copy-start(bf16[8,16,2048]{2,1,0:T(8,128)(2,1)S(1)} %all-to-all-done.4) | copy-start | bytes 1572868
  138.8 21.7 %copy-start.6 = (bf16[128,1024]{1,0:T(8,128)(2,1)}, bf16[128,1024]{1,0:T(8,128)(2,1)S(1)}, u32[]{:S(2)}) copy-start(bf16[128,1024]{1,0:T(8,128)(2,1)S(1)} %low_grad.1.b_ref) | copy-start | bytes 786436
  138.8 6.9 %collective-permute-start.23 = (bf16[16,2048]{1,0:T(8,128)(2,1)S(1)}, bf16[16,2048]{1,0:T(8,128)(2,1)S(1)}, u32[]{:S(2)}, u32[]{:S(2)}) collective-permute-start(bf16[16,2048]{1,0:T(8,128)(2,1)S(1)} %broadcast_select_fusion.8), channel_id=1, source_target_pairs={{0,6},{1,7},{2,4},{3,5},{4,2},{5,3},{6,0},{7,1},{8,14},{9,15},{10,... | collective-permute-start | bytes 196616 | tf_op jit(solution)/shard_map/ppermute | solution.py:320
  140.0 5.6 %collective-permute-start.22 = (bf16[16,2048]{1,0:T(8,128)(2,1)S(1)}, bf16[16,2048]{1,0:T(8,128)(2,1)S(1)}, u32[]{:S(2)}, u32[]{:S(2)}) collective-permute-start(bf16[16,2048]{1,0:T(8,128)(2,1)S(1)} %broadcast_select_fusion.8), channel_id=1, source_target_pairs={{0,2},{1,3},{2,0},{3,1},{4,6},{5,7},{6,4},{7,5},{8,10},{9,11},{10,... | collective-permute-start | bytes 196616 | tf_op jit(solution)/shard_map/ppermute | solution.py:320
  140.0 6.3 %collective-permute-start.21 = (bf16[16,2048]{1,0:T(8,128)(2,1)S(1)}, bf16[16,2048]{1,0:T(8,128)(2,1)S(1)}, u32[]{:S(2)}, u32[]{:S(2)}) collective-permute-start(bf16[16,2048]{1,0:T(8,128)(2,1)S(1)} %broadcast_select_fusion.8), channel_id=1, source_target_pairs={{0,4},{1,5},{2,6},{3,7},{4,0},{5,1},{6,2},{7,3},{8,12},{9,13},{10,... | collective-permute-start | bytes 196616 | tf_op jit(solution)/shard_map/ppermute | solution.py:320
  143.2 5.4 %collective-permute-start.17 = (bf16[128,1024]{1,0:T(8,128)(2,1)S(1)}, bf16[128,1024]{1,0:T(8,128)(2,1)S(1)}, u32[]{:S(2)}, u32[]{:S(2)}) collective-permute-start(bf16[128,1024]{1,0:T(8,128)(2,1)S(1)} %low_grad.1.b_ref), channel_id=1, source_target_pairs={{0,8},{8,0},{16,24},{24,16},{1,9},{9,1},{17,25},{25,17},{2,10},{10... | collective-permute-start | bytes 786440 | tf_op jit(solution)/shard_map/ppermute | solution.py:320
  146.3 8.5 %copy-start.15 = (bf16[64,2048]{1,0:T(8,128)(2,1)}, bf16[64,2048]{1,0:T(8,128)(2,1)S(1)}, u32[]{:S(2)}) copy-start(bf16[64,2048]{1,0:T(8,128)(2,1)S(1)} %pad_maximum_fusion.2.bn_ref) | copy-start | bytes 786436
  146.3 8.4 %collective-permute-start.24 = (bf16[64,2048]{1,0:T(8,128)(2,1)S(1)}, bf16[64,2048]{1,0:T(8,128)(2,1)S(1)}, u32[]{:S(2)}, u32[]{:S(2)}) collective-permute-start(bf16[64,2048]{1,0:T(8,128)(2,1)S(1)} %pad_maximum_fusion.2.bn_ref), channel_id=1, source_target_pairs={{0,1},{1,0},{2,3},{3,2},{4,5},{5,4},{6,7},{7,6},{8,9},{9,8},{10,11... | collective-permute-start | bytes 786440 | tf_op jit(solution)/shard_map/ppermute | solution.py:320
  148.6 11.9 %copy-start.17 = (bf16[128,1024]{1,0:T(8,128)(2,1)}, bf16[128,1024]{1,0:T(8,128)(2,1)S(1)}, u32[]{:S(2)}) copy-start(bf16[128,1024]{1,0:T(8,128)(2,1)S(1)} %collective-permute-done.17.bn_ref) | copy-start | bytes 786436
  148.6 11.9 %collective-permute-start.18 = (bf16[128,1024]{1,0:T(8,128)(2,1)S(1)}, bf16[128,1024]{1,0:T(8,128)(2,1)S(1)}, u32[]{:S(2)}, u32[]{:S(2)}) collective-permute-start(bf16[128,1024]{1,0:T(8,128)(2,1)S(1)} %broadcast_select_fusion.5), channel_id=1, source_target_pairs={{0,16},{8,24},{16,0},{24,8},{1,17},{9,25},{17,1},{25,9},{2,18},{10... | collective-permute-start | bytes 786440 | tf_op jit(solution)/shard_map/ppermute | solution.py:320
  (6 other events, 10.4 us)

commit v3 on v2

--- a/solution.py
+++ b/solution.py
@@ -15,6 +15,7 @@
 TN = (((0,), (0,)), ((), ()))
 PARAMS = pltpu.CompilerParams(vmem_limit_bytes=16 * 1024 * 1024)
 SMALL = pltpu.CompilerParams(vmem_limit_bytes=56 * 1024 * 1024)
+STREAM = pltpu.CompilerParams(vmem_limit_bytes=50 * 1024 * 1024)
 IN_VMEM = pl.BlockSpec(memory_space=pltpu.VMEM)
 IN_SMEM = pl.BlockSpec(memory_space=pltpu.SMEM)
 ANYWHERE = pl.BlockSpec(memory_space=pl.ANY)
@@ -49,6 +50,31 @@
         cost_estimate=FREE,
         name=name,
     )(*operands, *arrays)
+
+
+def stream(kernel, name, where, arrays, weights, outs, buffers, copies):
+    operands = [] if where is None else [where]
+    return pl.pallas_call(
+        kernel,
+        in_specs=[IN_SMEM] * len(operands) + [IN_VMEM] * len(arrays) + [ANYWHERE] * len(weights),
+        out_specs=[IN_VMEM] * len(outs),
+        out_shape=outs,
+        scratch_shapes=[pltpu.VMEM(shape, jnp.bfloat16) for shape in buffers] + [pltpu.SemaphoreType.DMA((copies,))],
+        compiler_params=STREAM,
+        cost_estimate=FREE,
+        name=name,
+    )(*operands, *arrays, *weights)
+
+
+def bring(w_ref, level, buffer, sems, first, along):
+    pieces = []
+    for i, cut in enumerate(cuts(buffer.shape[along])):
+        source = w_ref.at[0, level, cut, :] if along == 0 else w_ref.at[0, level, :, cut]
+        target = buffer.at[cut, :] if along == 0 else buffer.at[:, cut]
+        copy = pltpu.make_async_copy(source, target, sems.at[first + i])
+        copy.start()
+        pieces.append((cut, copy))
+    return pieces
 
 
 def norm_value(v, gain):
@@ -145,42 +171,54 @@
     return call(settle_back_kernel, "settle_back", where, [got, dy, h_own, gains], outs)
 
 
-def low_kernel(x_ref, gain_ref, wi_ref, wo_ref, n_ref, u_ref, slope_ref, part_ref):
+def low_kernel(x_ref, gain_ref, wi_ref, wo_ref, n_ref, u_ref, slope_ref, part_ref, wi, wo, sems):
+    into = bring(wi_ref, 0, wi, sems, 0, 1)
     n_ref[...] = norm_value(x_ref[...].astype(jnp.float32), gain_ref[0:1, :]).astype(jnp.bfloat16)
-    for cut in cuts(wi_ref.shape[1]):
-        a = jnp.dot(n_ref[...], wi_ref[:, cut], preferred_element_type=jnp.float32)
+    for i, (cut, copy) in enumerate(into):
+        copy.wait()
+        if i == 0:
+            out_of = bring(wo_ref, 0, wo, sems, len(into), 1)
+        a = jnp.dot(n_ref[...], wi[:, cut], preferred_element_type=jnp.float32)
         u, slope = gelu_both(a)
         u_ref[:, cut] = u.astype(jnp.bfloat16)
         slope_ref[:, cut] = slope
-    for cut in cuts(wo_ref.shape[1]):
-        part = jnp.dot(u_ref[...], wo_ref[:, cut], preferred_element_type=jnp.float32)
+    for cut, copy in out_of:
+        copy.wait()
+        part = jnp.dot(u_ref[...], wo[:, cut], preferred_element_type=jnp.float32)
         part_ref[:, cut] = part.astype(jnp.bfloat16)
 
 
-def low_forward(x, gains, wi, wo):
+def low_forward(x, gains, w_in, w_out):
     rows, width = x.shape
-    hidden = wi.shape[-1]
+    hidden = w_in.shape[3]
     outs = [bf16(rows, width), bf16(rows, hidden), f32(rows, hidden), bf16(rows, width)]
-    return call(low_kernel, "low_forward", None, [x, gains, wi, wo], outs)
-
-
-def high_kernel(h_ref, gain_ref, wi_ref, du_ref, n_ref, pair_ref, part_ref):
-    hidden = wi_ref.shape[1]
+    copies = len(cuts(hidden)) + len(cuts(width))
+    buffers = [(width, hidden), (hidden, width)]
+    return stream(low_kernel, "low_forward", None, [x, gains], [w_in, w_out], outs, buffers, copies)
+
+
+def high_kernel(h_ref, gain_ref, du_ref, wi_ref, n_ref, pair_ref, part_ref, wi, sems):
+    into = bring(wi_ref, 1, wi, sems, 0, 1)
+    hidden = wi.shape[1]
     n_ref[...] = norm_value(h_ref[...].astype(jnp.float32), gain_ref[1:2, :]).astype(jnp.bfloat16)
-    for cut in cuts(hidden):
-        a = jnp.dot(n_ref[...], wi_ref[:, cut], preferred_element_type=jnp.float32)
+    for cut, copy in into:
+        copy.wait()
+        a = jnp.dot(n_ref[...], wi[:, cut], preferred_element_type=jnp.float32)
         u, slope = gelu_both(a)
         pair_ref[:, cut] = u.astype(jnp.bfloat16)
         pair_ref[:, pl.ds(hidden + cut.start, cut.size)] = (slope * du_ref[:, cut]).astype(jnp.bfloat16)
-    for cut in cuts(wi_ref.shape[0]):
-        part = lax.dot_general(pair_ref[:, hidden:], wi_ref[cut, :], NT, preferred_element_type=jnp.float32)
+    for cut in cuts(wi.shape[0]):
+        part = lax.dot_general(pair_ref[:, hidden:], wi[cut, :], NT, preferred_element_type=jnp.float32)
         part_ref[:, cut] = part.astype(jnp.bfloat16)
 
 
-def high_both(h, gains, wi, du):
+def high_both(h, gains, w_in, du):
     rows, width = h.shape
-    outs = [bf16(rows, width), bf16(rows, 2 * wi.shape[-1]), bf16(rows, width)]
-    return call(high_kernel, "high_both", None, [h, gains, wi, du], outs)
+    hidden = w_in.shape[3]
+    outs = [bf16(rows, width), bf16(rows, 2 * hidden), bf16(rows, width)]
+    return stream(
+        high_kernel, "high_both", None, [h, gains, du], [w_in], outs, [(width, hidden)], len(cuts(hidden))
+    )
 
 
 def places(order, rows, path, shard):
@@ -197,30 +235,38 @@
     return (source == wanted).astype(jnp.float32).astype(jnp.bfloat16)
 
 
-def high_grad_kernel(ordered, where_ref, raw_ref, wo_ref, dy_ref, du_ref):
+def high_grad_kernel(ordered, where_ref, raw_ref, wo_ref, dy_ref, du_ref, wo, sems):
+    pieces = bring(wo_ref, 1, wo, sems, 0, 0)
     if ordered:
         dy_ref[...] = raw_ref[...]
     else:
         pick = places("dispatch", raw_ref.shape[0], where_ref[3], where_ref[2])
         dy_ref[...] = jnp.dot(pick, raw_ref[...], preferred_element_type=jnp.float32).astype(jnp.bfloat16)
-    for cut in cuts(wo_ref.shape[0]):
-        du_ref[:, cut] = lax.dot_general(dy_ref[...], wo_ref[cut, :], NT, preferred_element_type=jnp.float32)
-
-
-def high_grad(where, raw, wo, ordered):
+    for cut, copy in pieces:
+        copy.wait()
+        du_ref[:, cut] = lax.dot_general(dy_ref[...], wo[cut, :], NT, preferred_element_type=jnp.float32)
+
+
+def high_grad(where, raw, w_out, ordered):
     rows, width = raw.shape
+    hidden = w_out.shape[2]
+    outs = [bf16(rows, width), f32(rows, hidden)]
     kernel = functools.partial(high_grad_kernel, ordered)
-    return call(kernel, "high_grad", where, [raw, wo], [bf16(rows, width), f32(rows, wo.shape[-2])])
-
-
-def low_grad_kernel(dh_ref, wo_ref, slope_ref, da_ref):
-    for cut in cuts(wo_ref.shape[0]):
-        du = lax.dot_general(dh_ref[...], wo_ref[cut, :], NT, preferred_element_type=jnp.float32)
+    return stream(kernel, "high_grad", where, [raw], [w_out], outs, [(hidden, width)], len(cuts(hidden)))
+
+
+def low_grad_kernel(dh_ref, slope_ref, wo_ref, da_ref, wo, sems):
+    for cut, copy in bring(wo_ref, 0, wo, sems, 0, 0):
+        copy.wait()
+        du = lax.dot_general(dh_ref[...], wo[cut, :], NT, preferred_element_type=jnp.float32)
         da_ref[:, cut] = (du * slope_ref[:, cut]).astype(jnp.bfloat16)
 
 
-def low_grad(dh, wo, slope):
-    return call(low_grad_kernel, "low_grad", None, [dh, wo, slope], [bf16(dh.shape[0], wo.shape[-2])])[0]
+def low_grad(dh, w_out, slope):
+    rows, width = dh.shape
+    hidden = w_out.shape[2]
+    outs = [bf16(rows, hidden)]
+    return stream(low_grad_kernel, "low_grad", None, [dh, slope], [w_out], outs, [(hidden, width)], len(cuts(hidden)))[0]
 
 
 def pair_kernel(level, factor, order, a_cut, b_cut, where_ref, a_ref, an_ref, af_ref, b_ref, bn_ref, bf_ref, *rest):
@@ -343,11 +389,6 @@
     return pairs
 
 
-def level_of(w, level, after):
-    index, _ = tie(jnp.int32(level), after)
-    return lax.dynamic_index_in_dim(w[0], index, 0, keepdims=False)
-
-
 def body(tokens, routes, cotangent, gains, w_in, w_out, partners):
     paths = lax.axis_size("path")
     shards = lax.axis_size("shard")
@@ -366,40 +407,34 @@
 
     spread = pack(none, routes, tokens, paths, shards)
     x = dispatch(spread)
-    wi_low = level_of(w_in, 0, spread)
     if cubes:
         by_path = pack(me, routes, cotangent, paths, 0)
         rows_1 = join(by_path[0], *[swap(by_path[k], "path", k) for k in (1, 2, 3)])
         hop_1 = swap(rows_1, "shard", 4)
-        wo_low = level_of(w_out, 0, rows_1)
         x, hop_1, where, mate_low, mate_high = tie(x, hop_1, where, mate_low, mate_high)
-    else:
-        wo_low = level_of(w_out, 0, spread)
-    n1, u1, slope1, part_low = low_forward(x, gain, wi_low, wo_low)
+    n1, u1, slope1, part_low = low_forward(x, gain, w_in, w_out)
 
     (n1_mate,) = from_mate([n1], mate_low)
-    wi_high, wo_high = level_of(w_in, 1, n1_mate[0]), level_of(w_out, 1, n1_mate[0])
     got = scatter_shard(part_low)
     if cubes:
         rows_2 = join(rows_1, hop_1)
-        hop_2 = swap(rows_2, "shard", 2)
-        got, n1_mate[1], hop_2 = tie(got, n1_mate[1], hop_2)
+        hops = [swap(rows_2, "shard", bit) for bit in (2, 1, 3)]
+        got, n1_mate[1], *hops = tie(got, n1_mate[1], *hops)
     h_own, h_spread = settle(where, got, x)
 
     h = gather_shard(h_spread)
-    if cubes:
-        rows_4 = join(rows_2, hop_2)
-        hop_3 = swap(rows_4, "shard", 1)
-        (u1_mate, half_mate) = from_mate([u1, rows_4], mate_low, mate_high)
-        dy, du2 = high_grad(where, join(rows_4, hop_3), wo_high, False)
+    (u1_mate,) = from_mate([u1], mate_low)
+    if cubes:
+        hops[0], _ = tie(hops[0], u1_mate[0])
+        rows_4 = join(rows_2, hops[0])
+        (half_mate,) = from_mate([rows_4], mate_high)
+        dy, du2 = high_grad(where, join(rows_4, *hops[1:]), w_out, False)
         h, u1_mate[1], half_mate[1], du2 = tie(h, u1_mate[1], half_mate[1], du2)
     else:
-        (u1_mate,) = from_mate([u1], mate_low)
-        dy, du2 = high_grad(where, dispatch(pack(none, routes, cotangent, paths, shards)), wo_high, True)
-    n2, f2, part_back = high_both(h, gain, wi_high, du2)
+        dy, du2 = high_grad(where, dispatch(pack(none, routes, cotangent, paths, shards)), w_out, True)
+    n2, f2, part_back = high_both(h, gain, w_in, du2)
 
     (f2_mate,) = from_mate([f2], mate_high)
-    wo_again = level_of(w_out, 0, f2_mate[0])
     got = scatter_shard(part_back)
     if cubes:
         half = jnp.where(mate_high == 1, *half_mate)
@@ -411,15 +446,19 @@
     (n2_mate,) = from_mate([n2], mate_high)
     if cubes:
         delta_out = pair_grad(where, f2, f2_mate, first, dy, [half, hop_4], wide, 1, None, "dispatch")
+        dh_own, _ = tie(dh_own, n2_mate[0])
         (dh_pair,) = from_mate([dh_own], mate_low)
-        dh, n2_mate[1], delta_out = tie(dh, n2_mate[1], delta_out)
-    da1 = low_grad(dh, wo_again, slope1)
-
+        dh_piece = jnp.where(mate_low == 1, *dh_pair)
+        pieces = [swap(dh_piece, "shard", bit) for bit in (4, 2, 6)]
+        dh, n2_mate[1], delta_out, dh_piece = tie(dh, n2_mate[1], delta_out, dh_piece)
+    da1 = low_grad(dh, w_out, slope1)
+
+    if cubes:
+        da1, *pieces = tie(da1, *pieces)
     (da1_mate,) = from_mate([da1], mate_low)
     delta_in = pair_grad(where, n2, n2_mate, wide, f2, f2_mate, second, 1, None)
     if cubes:
-        dh_piece, _ = tie(jnp.where(mate_low == 1, *dh_pair), da1)
-        dh_half = join(dh_piece, *[swap(dh_piece, "shard", bit) for bit in (4, 2, 6)])
+        dh_half = join(dh_piece, *pieces)
         dh_mate = [dh_half, swap(dh_half, "shard", 1)]
     else:
         (dh_mate,) = from_mate([dh], mate_low)

time: 169 us -> 156 us (0.923)
  local copies, waits for them, and re-layouts: 33.3 us -> 3.67 us
  Pallas kernels: 37.2 us -> 48 us
  waiting for transfers between devices: 35.2 us -> 42.2 us
    squeeze x5 -> x0, local copies, waits for them, and re-layouts: 21.4 us -> none  [level_of(): return lax.dynamic_index_in_dim(w[0], index, 0, keepdims=False)]
    pallas_call x0 -> x4, Pallas kernels: none -> 20.6 us  [stream(): pl.pallas_call(kernel, in_specs=[IN_SMEM] * len(operands) + [IN_VMEM] * l...]
    ppermute x25 -> x26, waiting for transfers between devices: 21.4 us -> 32.2 us  [swap(): lax.ppermute(value, axis, [(i, i ^ bit) for i in range(lax.axis_size(axis...]
    pallas_call x6 -> x2, Pallas kernels: 12.8 us -> 3 us  [call(): pl.pallas_call(kernel, in_specs=[IN_SMEM] * len(operands) + [IN_VMEM] * l...]
    unnamed x48 -> x38, local copies, waits for them, and re-layouts: 10.4 us -> 2.16 us
    all_to_all x2, waiting for transfers between devices: 10.9 us -> 2.71 us  [gather_shard(): lax.all_to_all(spread, 'shard', split_axis=0, concat_axis=0, tiled=True)]
    all_to_all x1, waiting for transfers between devices: 0.01 us -> 7.18 us  [dispatch(): lax.all_to_all(spread, ('path', 'shard'), split_axis=0, concat_axis=0, ti...]
    all_to_all x2, waiting for transfers between devices: 2.89 us -> 0.14 us  [scatter_shard(): lax.all_to_all(blocks, 'shard', split_axis=0, concat_axis=0, tiled=True)]
  transfers between devices with their start and end apart: 30 -> 31, of which waited for: 11 -> 15; matrix products, arithmetic and copies ran while one was open for 18% -> 6% of each run, Pallas kernels for 13% -> 19%
where the time goes in v3:
time: 156 us; the launch traced here: 155 us
  starting transfers between devices  51.3 us (33%)
  Pallas kernels  48 us (31%)
  waiting for transfers between devices  42.2 us (27%)
  other arithmetic  7.16 us (5%)
  local copies, waits for them, and re-layouts  3.67 us (2%)
  between operations  2.39 us (2%)
    ppermute x26, waiting for transfers between devices, swap(): lax.ppermute(value, axis, [(i, i ^ bit) for i in range(lax.axis_size(axis...  32.2 us
    ppermute x26, starting transfers between devices, swap(): lax.ppermute(value, axis, [(i, i ^ bit) for i in range(lax.axis_size(axis...  25.2 us
    pallas_call x4, Pallas kernels, pair_grad(): pl.pallas_call(functools.partial(pair_kernel, level, factor, order, a_cut...  20.8 us
    pallas_call x4, Pallas kernels, stream(): pl.pallas_call(kernel, in_specs=[IN_SMEM] * len(operands) + [IN_VMEM] * l...  20.6 us
    all_to_all x2, starting transfers between devices, gather_shard(): lax.all_to_all(spread, 'shard', split_axis=0, concat_axis=0, tiled=True)  10.4 us
    all_to_all x2, starting transfers between devices, scatter_shard(): lax.all_to_all(blocks, 'shard', split_axis=0, concat_axis=0, tiled=True)  8.47 us
    all_to_all x1, starting transfers between devices, dispatch(): lax.all_to_all(spread, ('path', 'shard'), split_axis=0, concat_axis=0, ti...  7.3 us
    all_to_all x1, waiting for transfers between devices, dispatch(): lax.all_to_all(spread, ('path', 'shard'), split_axis=0, concat_axis=0, ti...  7.18 us
  transfers between devices with their start and end apart: 31, of which 15 were waited for; matrix products, arithmetic and copies ran while one was open for 6% of the time, Pallas kernels for 19%

profile of v3, /device:TPU:0, one launch (start us, length us, event | category | flops | bytes accessed | tf_op | source)
XLA Modules:
  0.0 154.7 jit_solution(14287618454745669385)
XLA Ops:
  0.6 1.9 %pack.2 = bf16[32,4,2048]{2,1,0:T(4,128)(2,1)} custom-call(s32[1]{0:T(128)} %constant.7.clone.1.flip_ref, s32[12]{0:T(128)} %bitcast.18, bf16[12,2048]{1,0:T(8,128)(2,1)} %rows_ref.2), custom_call_target="tpu_custom_call" | custom-call | tf_op jit(solution)/shard_map/pack/pallas_call | solution.py:123
  2.5 7.3 %all-to-all-start = ((bf16[32,4,2048]{2,1,0:T(4,128)(2,1)}), bf16[32,4,2048]{2,1,0:T(4,128)(2,1)S(1)}, u32[]{:S(2)}, u32[]{:S(2)}) async-start(bf16[32,4,2048]{2,1,0:T(4,128)(2,1)} %pack.2), calls=%async_computation | async-start | bytes 1048576 | tf_op jit(solution)/shard_map/all_to_all | solution.py:350
  9.8 1.7 %pack.3 = (bf16[4,2048]{1,0:T(4,128)(2,1)}, bf16[4,2048]{1,0:T(4,128)(2,1)}, bf16[4,2048]{1,0:T(4,128)(2,1)}, bf16[4,2048]{1,0:T(4,128)(2,1)}) custom-call(s32[1]{0:T(128)} %bitcast.1.flip_ref, s32[12]{0:T(128)} %bitcast.19, bf16[12,2048]{1,0:T(8,128)(2,1)} %rows_ref.3), custom_call_target="tpu_custom_call" | custom-call | tf_op jit(solution)/shard_map/pack/pallas_call | solution.py:123
  11.7 1.7 %collective-permute-start.1 = (bf16[4,2048]{1,0:T(4,128)(2,1)}, bf16[4,2048]{1,0:T(4,128)(2,1)S(1)}, u32[]{:S(2)}, u32[]{:S(2)}) collective-permute-start(bf16[4,2048]{1,0:T(4,128)(2,1)} %get-tuple-element.48), channel_id=1, source_target_pairs={{0,16},{8,24},{16,0},{24,8},{1,17},{9,25},{17,1},{25,9},{2,18},{10... | collective-permute-start | bytes 49160 | tf_op jit(solution)/shard_map/ppermute | solution.py:366
  13.4 1.4 constant_dynamic-slice_fusion.1
  16.0 0.8 collective-permute-done.2
  16.8 0.8 pad_maximum_fusion.4
  17.6 2.7 %collective-permute-start.3 = (bf16[16,2048]{1,0:T(8,128)(2,1)S(1)}, bf16[16,2048]{1,0:T(8,128)(2,1)S(1)}, u32[]{:S(2)}, u32[]{:S(2)}) collective-permute-start(bf16[16,2048]{1,0:T(8,128)(2,1)S(1)} %pad_maximum_fusion.4), channel_id=1, source_target_pairs={{0,4},{1,5},{2,6},{3,7},{4,0},{5,1},{6,2},{7,3},{8,12},{9,13},{10,... | collective-permute-start | bytes 196616 | tf_op jit(solution)/shard_map/ppermute | solution.py:366
  20.4 7.2 %all-to-all-done = bf16[32,4,2048]{2,1,0:T(4,128)(2,1)S(1)} async-done(((bf16[32,4,2048]{2,1,0:T(4,128)(2,1)}), bf16[32,4,2048]{2,1,0:T(4,128)(2,1)S(1)}, u32[]{:S(2)}, u32[]{:S(2)}) %all-to-all-start) | async-done | bytes 524320 | tf_op jit(solution)/shard_map/all_to_all | solution.py:350
  28.4 6.4 %low_forward.1 = (bf16[128,2048]{1,0:T(8,128)(2,1)S(1)}, bf16[128,1024]{1,0:T(8,128)(2,1)S(1)}, f32[128,1024]{1,0:T(8,128)S(1)}, bf16[128,2048]{1,0:T(8,128)(2,1)}) custom-call(bf16[128,2048]{1,0:T(8,128)(2,1)S(1)} %reshape.26.x_ref, bf16[2,2048]{1,0:T(2,128)(2,1)S(1)} %bitcast.15, bf16[1,2,2048,1024]{3,2,1,0:T(8,128)(2,1)} %wi_ref.3, ...), custom_call_target="tpu_custom_call" | custom-call | tf_op jit(solution)/shard_map/low_forward/pallas_call | solution.py:57
  35.0 3.6 %all-to-all-start.1 = ((bf16[8,16,2048]{2,1,0:T(8,128)(2,1)}), bf16[8,16,2048]{2,1,0:T(8,128)(2,1)S(1)}, u32[]{:S(2)}, u32[]{:S(2)}) async-start(bf16[8,16,2048]{2,1,0:T(8,128)(2,1)} %bitcast.8), calls=%async_computation.1 | async-start | bytes 1048576 | tf_op jit(solution)/shard_map/all_to_all | solution.py:362
  38.6 0.9 broadcast_select_fusion.2
  39.6 1.5 collective-permute-start.5
  41.1 2.9 %collective-permute-start.8 = (bf16[32,2048]{1,0:T(8,128)(2,1)S(1)}, bf16[32,2048]{1,0:T(8,128)(2,1)}, u32[]{:S(2)}, u32[]{:S(2)}) collective-permute-start(bf16[32,2048]{1,0:T(8,128)(2,1)S(1)} %pad_maximum_fusion.3), channel_id=1, source_target_pairs={{0,3},{1,2},{2,1},{3,0},{4,7},{5,6},{6,5},{7,4},{8,11},{9,10},{10,... | collective-permute-start | bytes 393224 | tf_op jit(solution)/shard_map/ppermute | solution.py:366
  44.6 8.9 %collective-permute-done.8 = bf16[32,2048]{1,0:T(8,128)(2,1)} collective-permute-done((bf16[32,2048]{1,0:T(8,128)(2,1)S(1)}, bf16[32,2048]{1,0:T(8,128)(2,1)}, u32[]{:S(2)}, u32[]{:S(2)}) %collective-permute-start.8) | collective-permute-done | bytes 131104 | tf_op jit(solution)/shard_map/ppermute | solution.py:366
  54.0 2.2 %collective-permute-done.6 = bf16[32,2048]{1,0:T(8,128)(2,1)S(1)} collective-permute-done((bf16[32,2048]{1,0:T(8,128)(2,1)S(1)}, bf16[32,2048]{1,0:T(8,128)(2,1)S(1)}, u32[]{:S(2)}, u32[]{:S(2)}) %collective-permute-start.6) | collective-permute-done | bytes 131104 | tf_op jit(solution)/shard_map/ppermute | solution.py:366
  56.4 1.4 settle.1
  57.8 4.4 %all-to-all-start.2 = ((bf16[8,16,2048]{2,1,0:T(8,128)(2,1)}), bf16[8,16,2048]{2,1,0:T(8,128)(2,1)S(1)}, u32[]{:S(2)}, u32[]{:S(2)}) async-start(bf16[8,16,2048]{2,1,0:T(8,128)(2,1)} %get-tuple-element.58), calls=%async_computation.2 | async-start | bytes 1048576 | tf_op jit(solution)/shard_map/all_to_all | solution.py:355
  62.2 1.4 collective-permute-start.10
  63.6 0.8 collective-permute-start.12
  64.4 1.0 pad_maximum_fusion.raw_ref
  65.4 4.6 %high_grad.1 = (bf16[128,2048]{1,0:T(8,128)(2,1)S(1)}, f32[128,1024]{1,0:T(8,128)S(1)}) custom-call(s32[4]{0:T(128)S(1)} %pad_add_fusion.where_ref, bf16[128,2048]{1,0:T(8,128)(2,1)S(1)} %pad_maximum_fusion.raw_ref, bf16[1,2,1024,2048]{3,2,1,0:T(8,128)(2,1)} %wo_ref.5), custom_call_target="tpu_custom_call" | custom-call | tf_op jit(solution)/shard_map/high_grad/pallas_call | solution.py:57
  70.1 1.3 collective-permute-done.10.af_ref
  71.4 5.0 %collective-permute-done.12 = bf16[64,2048]{1,0:T(8,128)(2,1)} collective-permute-done((bf16[64,2048]{1,0:T(8,128)(2,1)S(1)}, bf16[64,2048]{1,0:T(8,128)(2,1)}, u32[]{:S(2)}, u32[]{:S(2)}) %collective-permute-start.12) | collective-permute-done | bytes 262176 | tf_op jit(solution)/shard_map/ppermute | solution.py:366
  76.4 0.9 all-to-all-done.2
  77.3 5.3 %high_both.1 = (bf16[128,2048]{1,0:T(8,128)(2,1)S(1)}, bf16[128,2048]{1,0:T(8,128)(2,1)S(1)}, bf16[128,2048]{1,0:T(8,128)(2,1)}) custom-call(bf16[128,2048]{1,0:T(8,128)(2,1)S(1)} %bitcast.14, bf16[2,2048]{1,0:T(2,128)(2,1)S(1)} %bitcast.16, f32[128,1024]{1,0:T(8,128)S(1)} %get-tuple-element.67.du_ref, bf16[1,2,2048,1024]{3,2,1,0:T(8,128)(2,1)} %wi_ref.3), custom_call_target="tpu_custom_call" | custom-call | tf_op jit(solution)/shard_map/high_both/pallas_call | solution.py:57
  82.8 4.8 %all-to-all-start.3 = ((bf16[8,16,2048]{2,1,0:T(8,128)(2,1)}), bf16[8,16,2048]{2,1,0:T(8,128)(2,1)S(1)}, u32[]{:S(2)}, u32[]{:S(2)}) async-start(bf16[8,16,2048]{2,1,0:T(8,128)(2,1)} %bitcast.10), calls=%async_computation.3 | async-start | bytes 1048576 | tf_op jit(solution)/shard_map/all_to_all | solution.py:362
  87.8 0.9 broadcast_select_fusion.1
  88.7 1.3 collective-permute-start.14
  90.0 1.0 broadcast_select_fusion.3.bn_ref
  91.0 1.9 %collective-permute-start.15 = (bf16[64,2048]{1,0:T(8,128)(2,1)S(1)}, bf16[64,2048]{1,0:T(8,128)(2,1)}, u32[]{:S(2)}, u32[]{:S(2)}) collective-permute-start(bf16[64,2048]{1,0:T(8,128)(2,1)S(1)} %broadcast_select_fusion.3.bn_ref), channel_id=1, source_target_pairs={{0,1},{1,0},{2,3},{3,2},{4,5},{5,4},{6,7},{7,6},{8,9},{9,8},{10,11... | collective-permute-start | bytes 786440 | tf_op jit(solution)/shard_map/ppermute | solution.py:366
  92.9 9.7 %collective-permute-done.15.bf_ref = bf16[64,2048]{1,0:T(8,128)(2,1)} collective-permute-done((bf16[64,2048]{1,0:T(8,128)(2,1)S(1)}, bf16[64,2048]{1,0:T(8,128)(2,1)}, u32[]{:S(2)}, u32[]{:S(2)}) %collective-permute-start.15) | collective-permute-done | bytes 262176 | tf_op jit(solution)/shard_map/ppermute | solution.py:366
  103.2 1.6 %settle_back.1 = (bf16[16,2048]{1,0:T(8,128)(2,1)S(1)}, bf16[8,16,2048]{2,1,0:T(8,128)(2,1)}) custom-call(s32[4]{0:T(128)S(1)} %pad_add_fusion.where_ref, bf16[8,16,2048]{2,1,0:T(8,128)(2,1)S(1)} %all-to-all-done.3.got_ref, bf16[128,2048]{1,0:T(8,128)(2,1)S(1)} %get-tuple-element.72.dy_ref.b_ref, bf16[16,2048]{1,0:T(8,128)(2,1)S(1)} %get-tuple-element.73.h_ref, ...), custom_call_target="tpu_custom_call" | custom-call | tf_op jit(solution)/shard_map/settle_back/pallas_call | solution.py:44
  104.8 6.0 %all-to-all-start.4 = ((bf16[8,16,2048]{2,1,0:T(8,128)(2,1)}), bf16[8,16,2048]{2,1,0:T(8,128)(2,1)S(1)}, u32[]{:S(2)}, u32[]{:S(2)}) async-start(bf16[8,16,2048]{2,1,0:T(8,128)(2,1)} %get-tuple-element.74), calls=%async_computation.4 | async-start | bytes 1048576 | tf_op jit(solution)/shard_map/all_to_all | solution.py:355
  111.4 1.3 collective-permute-start.19
  112.7 0.9 broadcast_select_fusion
  114.3 1.7 %collective-permute-done.19 = bf16[16,2048]{1,0:T(8,128)(2,1)} collective-permute-done((bf16[16,2048]{1,0:T(8,128)(2,1)}, bf16[16,2048]{1,0:T(8,128)(2,1)}, u32[]{:S(2)}, u32[]{:S(2)}) %collective-permute-start.19) | collective-permute-done | bytes 65568 | tf_op jit(solution)/shard_map/ppermute | solution.py:366
  116.0 0.9 broadcast_select_fusion.8
  116.9 3.9 %collective-permute-start.22 = (bf16[16,2048]{1,0:T(8,128)(2,1)S(1)}, bf16[16,2048]{1,0:T(8,128)(2,1)S(1)}, u32[]{:S(2)}, u32[]{:S(2)}) collective-permute-start(bf16[16,2048]{1,0:T(8,128)(2,1)S(1)} %broadcast_select_fusion.8), channel_id=1, source_target_pairs={{0,6},{1,7},{2,4},{3,5},{4,2},{5,3},{6,0},{7,1},{8,14},{9,15},{10,... | collective-permute-start | bytes 196616 | tf_op jit(solution)/shard_map/ppermute | solution.py:366
  121.4 5.0 %pair_grad.4.rest_0_ = bf16[1,2,1024,2048]{3,2,1,0:T(8,128)(2,1)} custom-call(s32[4]{0:T(128)} %copy-done.9, bf16[128,2048]{1,0:T(8,128)(2,1)} %copy-done, bf16[128,2048]{1,0:T(8,128)(2,1)} %copy-done.10, bf16[128,2048]{1,0:T(8,128)(2,1)} %collective-permute-done.14.af_ref.bf_ref, bf16[128,2048]{1,0:T(8,128)(2,1)} %copy-done.5, bf16[64,2048]{1,0:T(8,128)(2,1)} %copy-done.15, ...), custom_call_target="tpu_custom_call" | custom-call | tf_op jit(solution)/shard_map/pair_grad/pallas_call | solution.py:330
  126.4 1.3 collective-permute-done.17.af_ref
  127.7 1.8 %all-to-all-done.4 = bf16[8,16,2048]{2,1,0:T(8,128)(2,1)S(1)} async-done(((bf16[8,16,2048]{2,1,0:T(8,128)(2,1)}), bf16[8,16,2048]{2,1,0:T(8,128)(2,1)S(1)}, u32[]{:S(2)}, u32[]{:S(2)}) %all-to-all-start.4) | async-done | bytes 524320 | tf_op jit(solution)/shard_map/all_to_all | solution.py:355
  129.5 4.3 %low_grad.1.b_ref = bf16[128,1024]{1,0:T(8,128)(2,1)S(1)} custom-call(bf16[128,2048]{1,0:T(8,128)(2,1)S(1)} %bitcast.12, f32[128,1024]{1,0:T(8,128)S(1)} %get-tuple-element.81.slope_ref, bf16[1,2,1024,2048]{3,2,1,0:T(8,128)(2,1)} %wo_ref.5), custom_call_target="tpu_custom_call" | custom-call | tf_op jit(solution)/shard_map/low_grad/pallas_call | solution.py:57
  133.9 1.5 collective-permute-start.25
  135.5 1.4 collective-permute-start.24
  136.8 5.4 %pair_grad.5.rest_0_ = bf16[1,2,2048,1024]{3,2,1,0:T(8,128)(2,1)} custom-call(s32[4]{0:T(128)} %copy-done.9, bf16[128,2048]{1,0:T(8,128)(2,1)} %copy-done.4, bf16[128,2048]{1,0:T(8,128)(2,1)} %collective-permute-done.16.an_ref, bf16[128,2048]{1,0:T(8,128)(2,1)} %collective-permute-done.17.af_ref, bf16[128,2048]{1,0:T(8,128)(2,1)} %copy-done, ...), custom_call_target="tpu_custom_call" | custom-call | tf_op jit(solution)/shard_map/pair_grad/pallas_call | solution.py:330
  143.4 5.0 %pair_grad.7 = bf16[1,2,1024,2048]{3,2,1,0:T(8,128)(2,1)} custom-call(s32[4]{0:T(128)} %copy-done.9, bf16[128,1024]{1,0:T(8,128)(2,1)} %copy-done.6, bf16[128,1024]{1,0:T(8,128)(2,1)} %copy-done.13, bf16[128,1024]{1,0:T(8,128)(2,1)} %copy-done.16, bf16[128,2048]{1,0:T(8,128)(2,1)} %bitcast.13, ...), custom_call_target="tpu_custom_call", output_to_operand_aliasing={{}: (7, {})} | custom-call | tf_op jit(solution)/shard_map/pair_grad/pallas_call | solution.py:330
  149.1 5.4 %pair_grad.6 = bf16[1,2,2048,1024]{3,2,1,0:T(8,128)(2,1)} custom-call(s32[4]{0:T(128)} %copy-done.9, bf16[128,2048]{1,0:T(8,128)(2,1)} %copy-done.3, bf16[128,2048]{1,0:T(8,128)(2,1)} %copy-done.11, bf16[128,2048]{1,0:T(8,128)(2,1)} %collective-permute-done.5.af_ref, bf16[128,1024]{1,0:T(8,128)(2,1)} %copy-done.2, ...), custom_call_target="tpu_custom_call", output_to_operand_aliasing={{}: (7, {})} | custom-call | tf_op jit(solution)/shard_map/pair_grad/pallas_call | solution.py:330
  (81 shorter events, 7.6 us)
Async XLA Ops:
  2.5 25.1 %all-to-all-start = ((bf16[32,4,2048]{2,1,0:T(4,128)(2,1)}), bf16[32,4,2048]{2,1,0:T(4,128)(2,1)S(1)}, u32[]{:S(2)}, u32[]{:S(2)}) async-start(bf16[32,4,2048]{2,1,0:T(4,128)(2,1)} %pack.2), calls=%async_computation | async-start | bytes 1048576 | tf_op jit(solution)/shard_map/all_to_all | solution.py:350
  11.5 4.5 %collective-permute-start = (bf16[4,2048]{1,0:T(4,128)(2,1)}, bf16[4,2048]{1,0:T(4,128)(2,1)S(1)}, u32[]{:S(2)}, u32[]{:S(2)}) collective-permute-start(bf16[4,2048]{1,0:T(4,128)(2,1)} %get-tuple-element.47), channel_id=1, source_target_pairs={{0,8},{8,0},{16,24},{24,16},{1,9},{9,1},{17,25},{25,17},{2,10},{10... | collective-permute-start | bytes 49160 | tf_op jit(solution)/shard_map/ppermute | solution.py:366
  11.7 4.3 %collective-permute-start.1 = (bf16[4,2048]{1,0:T(4,128)(2,1)}, bf16[4,2048]{1,0:T(4,128)(2,1)S(1)}, u32[]{:S(2)}, u32[]{:S(2)}) collective-permute-start(bf16[4,2048]{1,0:T(4,128)(2,1)} %get-tuple-element.48), channel_id=1, source_target_pairs={{0,16},{8,24},{16,0},{24,8},{1,17},{9,25},{17,1},{25,9},{2,18},{10... | collective-permute-start | bytes 49160 | tf_op jit(solution)/shard_map/ppermute | solution.py:366
  13.4 3.4 %collective-permute-start.2 = (bf16[4,2048]{1,0:T(4,128)(2,1)}, bf16[4,2048]{1,0:T(4,128)(2,1)S(1)}, u32[]{:S(2)}, u32[]{:S(2)}) collective-permute-start(bf16[4,2048]{1,0:T(4,128)(2,1)} %get-tuple-element.49), channel_id=1, source_target_pairs={{0,24},{8,16},{16,8},{24,0},{1,25},{9,17},{17,9},{25,1},{2,26},{10... | collective-permute-start | bytes 49160 | tf_op jit(solution)/shard_map/ppermute | solution.py:366
  17.6 10.1 %collective-permute-start.3 = (bf16[16,2048]{1,0:T(8,128)(2,1)S(1)}, bf16[16,2048]{1,0:T(8,128)(2,1)S(1)}, u32[]{:S(2)}, u32[]{:S(2)}) collective-permute-start(bf16[16,2048]{1,0:T(8,128)(2,1)S(1)} %pad_maximum_fusion.4), channel_id=1, source_target_pairs={{0,4},{1,5},{2,6},{3,7},{4,0},{5,1},{6,2},{7,3},{8,12},{9,13},{10,... | collective-permute-start | bytes 196616 | tf_op jit(solution)/shard_map/ppermute | solution.py:366
  20.4 82.8 %copy-start.9 = (s32[4]{0:T(128)}, s32[4]{0:T(128)S(1)}, u32[]{:S(2)}) copy-start(s32[4]{0:T(128)S(1)} %pad_add_fusion.where_ref) | copy-start | bytes 52
  34.8 35.3 %copy-start.3 = (bf16[128,2048]{1,0:T(8,128)(2,1)}, bf16[128,2048]{1,0:T(8,128)(2,1)S(1)}, u32[]{:S(2)}) copy-start(bf16[128,2048]{1,0:T(8,128)(2,1)S(1)} %get-tuple-element.52.a_ref) | copy-start | bytes 1572868
  34.8 35.3 %copy-start.6 = (bf16[128,1024]{1,0:T(8,128)(2,1)}, bf16[128,1024]{1,0:T(8,128)(2,1)S(1)}, u32[]{:S(2)}) copy-start(bf16[128,1024]{1,0:T(8,128)(2,1)S(1)} %get-tuple-element.59.a_ref) | copy-start | bytes 786436
  34.8 3.8 %collective-permute-start.4 = (bf16[128,2048]{1,0:T(8,128)(2,1)S(1)}, bf16[128,2048]{1,0:T(8,128)(2,1)S(1)}, u32[]{:S(2)}, u32[]{:S(2)}) collective-permute-start(bf16[128,2048]{1,0:T(8,128)(2,1)S(1)} %get-tuple-element.52.a_ref), channel_id=1, source_target_pairs={{0,8},{8,0},{16,24},{24,16},{1,9},{9,1},{17,25},{25,17},{2,10},{10... | collective-permute-start | bytes 1572872 | tf_op jit(solution)/shard_map/ppermute | solution.py:366
  35.0 42.4 %copy-start.8 = (bf16[1,2,2048]{2,1,0:T(2,128)(2,1)S(1)}, bf16[1,2,2048]{2,1,0:T(2,128)(2,1)}, u32[]{:S(2)}) copy-start(bf16[1,2,2048]{2,1,0:T(2,128)(2,1)} %param.10) | copy-start | bytes 24580
  35.0 21.2 %all-to-all-start.1 = ((bf16[8,16,2048]{2,1,0:T(8,128)(2,1)}), bf16[8,16,2048]{2,1,0:T(8,128)(2,1)S(1)}, u32[]{:S(2)}, u32[]{:S(2)}) async-start(bf16[8,16,2048]{2,1,0:T(8,128)(2,1)} %bitcast.8), calls=%async_computation.1 | async-start | bytes 1048576 | tf_op jit(solution)/shard_map/all_to_all | solution.py:362
  38.6 17.5 %copy-start.11 = (bf16[128,2048]{1,0:T(8,128)(2,1)}, bf16[128,2048]{1,0:T(8,128)(2,1)S(1)}, u32[]{:S(2)}) copy-start(bf16[128,2048]{1,0:T(8,128)(2,1)S(1)} %collective-permute-done.4.an_ref) | copy-start | bytes 1572868
  39.6 16.6 %collective-permute-start.5 = (bf16[128,2048]{1,0:T(8,128)(2,1)}, bf16[128,2048]{1,0:T(8,128)(2,1)}, u32[]{:S(2)}, u32[]{:S(2)}) collective-permute-start(bf16[128,2048]{1,0:T(8,128)(2,1)} %broadcast_select_fusion.2), channel_id=1, source_target_pairs={{0,16},{8,24},{16,0},{24,8},{1,17},{9,25},{17,1},{25,9},{2,18},{10... | collective-permute-start | bytes 1572872 | tf_op jit(solution)/shard_map/ppermute | solution.py:366
  41.0 15.2 %collective-permute-start.9 = (bf16[128,1024]{1,0:T(8,128)(2,1)S(1)}, bf16[128,1024]{1,0:T(8,128)(2,1)S(1)}, u32[]{:S(2)}, u32[]{:S(2)}) collective-permute-start(bf16[128,1024]{1,0:T(8,128)(2,1)S(1)} %get-tuple-element.59.a_ref), channel_id=1, source_target_pairs={{0,8},{8,0},{16,24},{24,16},{1,9},{9,1},{17,25},{25,17},{2,10},{10... | collective-permute-start | bytes 786440 | tf_op jit(solution)/shard_map/ppermute | solution.py:366
  41.1 12.5 %collective-permute-start.8 = (bf16[32,2048]{1,0:T(8,128)(2,1)S(1)}, bf16[32,2048]{1,0:T(8,128)(2,1)}, u32[]{:S(2)}, u32[]{:S(2)}) collective-permute-start(bf16[32,2048]{1,0:T(8,128)(2,1)S(1)} %pad_maximum_fusion.3), channel_id=1, source_target_pairs={{0,3},{1,2},{2,1},{3,0},{4,7},{5,6},{6,5},{7,4},{8,11},{9,10},{10,... | collective-permute-start | bytes 393224 | tf_op jit(solution)/shard_map/ppermute | solution.py:366
  44.0 10.0 %collective-permute-start.7 = (bf16[32,2048]{1,0:T(8,128)(2,1)S(1)}, bf16[32,2048]{1,0:T(8,128)(2,1)}, u32[]{:S(2)}, u32[]{:S(2)}) collective-permute-start(bf16[32,2048]{1,0:T(8,128)(2,1)S(1)} %pad_maximum_fusion.3), channel_id=1, source_target_pairs={{0,1},{1,0},{2,3},{3,2},{4,5},{5,4},{6,7},{7,6},{8,9},{9,8},{10,11... | collective-permute-start | bytes 393224 | tf_op jit(solution)/shard_map/ppermute | solution.py:366
  44.6 11.6 %collective-permute-start.6 = (bf16[32,2048]{1,0:T(8,128)(2,1)S(1)}, bf16[32,2048]{1,0:T(8,128)(2,1)S(1)}, u32[]{:S(2)}, u32[]{:S(2)}) collective-permute-start(bf16[32,2048]{1,0:T(8,128)(2,1)S(1)} %pad_maximum_fusion.3), channel_id=1, source_target_pairs={{0,2},{1,3},{2,0},{3,1},{4,6},{5,7},{6,4},{7,5},{8,10},{9,11},{10,... | collective-permute-start | bytes 393224 | tf_op jit(solution)/shard_map/ppermute | solution.py:366
  56.2 26.5 %copy-start.13 = (bf16[128,1024]{1,0:T(8,128)(2,1)}, bf16[128,1024]{1,0:T(8,128)(2,1)S(1)}, u32[]{:S(2)}) copy-start(bf16[128,1024]{1,0:T(8,128)(2,1)S(1)} %collective-permute-done.9.an_ref) | copy-start | bytes 786436
  56.2 7.4 %collective-permute-start.11 = (bf16[64,2048]{1,0:T(8,128)(2,1)S(1)}, bf16[64,2048]{1,0:T(8,128)(2,1)}, u32[]{:S(2)}, u32[]{:S(2)}) collective-permute-start(bf16[64,2048]{1,0:T(8,128)(2,1)S(1)} %pad_maximum_fusion.1), channel_id=1, source_target_pairs={{0,8},{8,0},{16,24},{24,16},{1,9},{9,1},{17,25},{25,17},{2,10},{10... | collective-permute-start | bytes 786440 | tf_op jit(solution)/shard_map/ppermute | solution.py:366
  57.8 19.5 %all-to-all-start.2 = ((bf16[8,16,2048]{2,1,0:T(8,128)(2,1)}), bf16[8,16,2048]{2,1,0:T(8,128)(2,1)S(1)}, u32[]{:S(2)}, u32[]{:S(2)}) async-start(bf16[8,16,2048]{2,1,0:T(8,128)(2,1)} %get-tuple-element.58), calls=%async_computation.2 | async-start | bytes 1048576 | tf_op jit(solution)/shard_map/all_to_all | solution.py:355
  62.2 9.2 %collective-permute-start.10 = (bf16[128,1024]{1,0:T(8,128)(2,1)S(1)}, bf16[128,1024]{1,0:T(8,128)(2,1)S(1)}, u32[]{:S(2)}, u32[]{:S(2)}) collective-permute-start(bf16[128,1024]{1,0:T(8,128)(2,1)S(1)} %broadcast_select_fusion.6), channel_id=1, source_target_pairs={{0,16},{8,24},{16,0},{24,8},{1,17},{9,25},{17,1},{25,9},{2,18},{10... | collective-permute-start | bytes 786440 | tf_op jit(solution)/shard_map/ppermute | solution.py:366
  63.6 12.8 %collective-permute-start.12 = (bf16[64,2048]{1,0:T(8,128)(2,1)S(1)}, bf16[64,2048]{1,0:T(8,128)(2,1)}, u32[]{:S(2)}, u32[]{:S(2)}) collective-permute-start(bf16[64,2048]{1,0:T(8,128)(2,1)S(1)} %broadcast_select_fusion.4), channel_id=1, source_target_pairs={{0,16},{8,24},{16,0},{24,8},{1,17},{9,25},{17,1},{25,9},{2,18},{10... | collective-permute-start | bytes 786440 | tf_op jit(solution)/shard_map/ppermute | solution.py:366
  70.1 43.5 %copy-start.5 = (bf16[128,2048]{1,0:T(8,128)(2,1)}, bf16[128,2048]{1,0:T(8,128)(2,1)S(1)}, u32[]{:S(2)}) copy-start(bf16[128,2048]{1,0:T(8,128)(2,1)S(1)} %get-tuple-element.72.dy_ref.b_ref) | copy-start | bytes 1572868
  71.4 5.9 %copy-start.16 = (bf16[128,1024]{1,0:T(8,128)(2,1)}, bf16[128,1024]{1,0:T(8,128)(2,1)S(1)}, u32[]{:S(2)}) copy-start(bf16[128,1024]{1,0:T(8,128)(2,1)S(1)} %collective-permute-done.10.af_ref) | copy-start | bytes 786436
  82.7 38.7 %copy-start = (bf16[128,2048]{1,0:T(8,128)(2,1)}, bf16[128,2048]{1,0:T(8,128)(2,1)S(1)}, u32[]{:S(2)}) copy-start(bf16[128,2048]{1,0:T(8,128)(2,1)S(1)} %get-tuple-element.69.a_ref.b_ref) | copy-start | bytes 1572868
  82.7 43.7 %copy-start.4 = (bf16[128,2048]{1,0:T(8,128)(2,1)}, bf16[128,2048]{1,0:T(8,128)(2,1)S(1)}, u32[]{:S(2)}) copy-start(bf16[128,2048]{1,0:T(8,128)(2,1)S(1)} %get-tuple-element.75.a_ref) | copy-start | bytes 1572868
  82.7 5.1 %collective-permute-start.13 = (bf16[128,2048]{1,0:T(8,128)(2,1)S(1)}, bf16[128,2048]{1,0:T(8,128)(2,1)S(1)}, u32[]{:S(2)}, u32[]{:S(2)}) collective-permute-start(bf16[128,2048]{1,0:T(8,128)(2,1)S(1)} %get-tuple-element.69.a_ref.b_ref), channel_id=1, source_target_pairs={{0,8},{8,0},{16,24},{24,16},{1,9},{9,1},{17,25},{25,17},{2,10},{10... | collective-permute-start | bytes 1572872 | tf_op jit(solution)/shard_map/ppermute | solution.py:366
  82.8 20.0 %all-to-all-start.3 = ((bf16[8,16,2048]{2,1,0:T(8,128)(2,1)}), bf16[8,16,2048]{2,1,0:T(8,128)(2,1)S(1)}, u32[]{:S(2)}, u32[]{:S(2)}) async-start(bf16[8,16,2048]{2,1,0:T(8,128)(2,1)} %bitcast.10), calls=%async_computation.3 | async-start | bytes 1048576 | tf_op jit(solution)/shard_map/all_to_all | solution.py:362
  87.6 17.2 %collective-permute-start.16 = (bf16[128,2048]{1,0:T(8,128)(2,1)S(1)}, bf16[128,2048]{1,0:T(8,128)(2,1)}, u32[]{:S(2)}, u32[]{:S(2)}) collective-permute-start(bf16[128,2048]{1,0:T(8,128)(2,1)S(1)} %get-tuple-element.75.a_ref), channel_id=1, source_target_pairs={{0,8},{8,0},{16,24},{24,16},{1,9},{9,1},{17,25},{25,17},{2,10},{10... | collective-permute-start | bytes 1572872 | tf_op jit(solution)/shard_map/ppermute | solution.py:366
  87.8 33.6 %copy-start.10 = (bf16[128,2048]{1,0:T(8,128)(2,1)}, bf16[128,2048]{1,0:T(8,128)(2,1)S(1)}, u32[]{:S(2)}) copy-start(bf16[128,2048]{1,0:T(8,128)(2,1)S(1)} %collective-permute-done.13.an_ref.bn_ref) | copy-start | bytes 1572868
  88.7 14.5 %collective-permute-start.14 = (bf16[128,2048]{1,0:T(8,128)(2,1)}, bf16[128,2048]{1,0:T(8,128)(2,1)}, u32[]{:S(2)}, u32[]{:S(2)}) collective-permute-start(bf16[128,2048]{1,0:T(8,128)(2,1)} %broadcast_select_fusion.1), channel_id=1, source_target_pairs={{0,16},{8,24},{16,0},{24,8},{1,17},{9,25},{17,1},{25,9},{2,18},{10... | collective-permute-start | bytes 1572872 | tf_op jit(solution)/shard_map/ppermute | solution.py:366
  91.0 30.4 %copy-start.15 = (bf16[64,2048]{1,0:T(8,128)(2,1)}, bf16[64,2048]{1,0:T(8,128)(2,1)S(1)}, u32[]{:S(2)}) copy-start(bf16[64,2048]{1,0:T(8,128)(2,1)S(1)} %broadcast_select_fusion.3.bn_ref) | copy-start | bytes 786436
  91.0 11.6 %collective-permute-start.15 = (bf16[64,2048]{1,0:T(8,128)(2,1)S(1)}, bf16[64,2048]{1,0:T(8,128)(2,1)}, u32[]{:S(2)}, u32[]{:S(2)}) collective-permute-start(bf16[64,2048]{1,0:T(8,128)(2,1)S(1)} %broadcast_select_fusion.3.bn_ref), channel_id=1, source_target_pairs={{0,1},{1,0},{2,3},{3,2},{4,5},{5,4},{6,7},{7,6},{8,9},{9,8},{10,11... | collective-permute-start | bytes 786440 | tf_op jit(solution)/shard_map/ppermute | solution.py:366
  104.8 6.0 %collective-permute-start.18 = (bf16[16,2048]{1,0:T(8,128)(2,1)S(1)}, bf16[16,2048]{1,0:T(8,128)(2,1)S(1)}, u32[]{:S(2)}, u32[]{:S(2)}) collective-permute-start(bf16[16,2048]{1,0:T(8,128)(2,1)S(1)} %get-tuple-element.79), channel_id=1, source_target_pairs={{0,8},{8,0},{16,24},{24,16},{1,9},{9,1},{17,25},{25,17},{2,10},{10... | collective-permute-start | bytes 196616 | tf_op jit(solution)/shard_map/ppermute | solution.py:366
  104.8 24.7 %all-to-all-start.4 = ((bf16[8,16,2048]{2,1,0:T(8,128)(2,1)}), bf16[8,16,2048]{2,1,0:T(8,128)(2,1)S(1)}, u32[]{:S(2)}, u32[]{:S(2)}) async-start(bf16[8,16,2048]{2,1,0:T(8,128)(2,1)} %get-tuple-element.74), calls=%async_computation.4 | async-start | bytes 1048576 | tf_op jit(solution)/shard_map/all_to_all | solution.py:355
  111.4 4.6 %collective-permute-start.19 = (bf16[16,2048]{1,0:T(8,128)(2,1)}, bf16[16,2048]{1,0:T(8,128)(2,1)}, u32[]{:S(2)}, u32[]{:S(2)}) collective-permute-start(bf16[16,2048]{1,0:T(8,128)(2,1)} %broadcast_select_fusion.7), channel_id=1, source_target_pairs={{0,16},{8,24},{16,0},{24,8},{1,17},{9,25},{17,1},{25,9},{2,18},{10... | collective-permute-start | bytes 196616 | tf_op jit(solution)/shard_map/ppermute | solution.py:366
  113.6 14.1 %collective-permute-start.17 = (bf16[128,2048]{1,0:T(8,128)(2,1)}, bf16[128,2048]{1,0:T(8,128)(2,1)}, u32[]{:S(2)}, u32[]{:S(2)}) collective-permute-start(bf16[128,2048]{1,0:T(8,128)(2,1)} %broadcast_select_fusion), channel_id=1, source_target_pairs={{0,16},{8,24},{16,0},{24,8},{1,17},{9,25},{17,1},{25,9},{2,18},{10... | collective-permute-start | bytes 1572872 | tf_op jit(solution)/shard_map/ppermute | solution.py:366
  116.9 16.9 %collective-permute-start.22 = (bf16[16,2048]{1,0:T(8,128)(2,1)S(1)}, bf16[16,2048]{1,0:T(8,128)(2,1)S(1)}, u32[]{:S(2)}, u32[]{:S(2)}) collective-permute-start(bf16[16,2048]{1,0:T(8,128)(2,1)S(1)} %broadcast_select_fusion.8), channel_id=1, source_target_pairs={{0,6},{1,7},{2,4},{3,5},{4,2},{5,3},{6,0},{7,1},{8,14},{9,15},{10,... | collective-permute-start | bytes 196616 | tf_op jit(solution)/shard_map/ppermute | solution.py:366
  120.7 13.1 %collective-permute-start.21 = (bf16[16,2048]{1,0:T(8,128)(2,1)S(1)}, bf16[16,2048]{1,0:T(8,128)(2,1)S(1)}, u32[]{:S(2)}, u32[]{:S(2)}) collective-permute-start(bf16[16,2048]{1,0:T(8,128)(2,1)S(1)} %broadcast_select_fusion.8), channel_id=1, source_target_pairs={{0,2},{1,3},{2,0},{3,1},{4,6},{5,7},{6,4},{7,5},{8,10},{9,11},{10,... | collective-permute-start | bytes 196616 | tf_op jit(solution)/shard_map/ppermute | solution.py:366
  120.7 13.1 %collective-permute-start.20 = (bf16[16,2048]{1,0:T(8,128)(2,1)S(1)}, bf16[16,2048]{1,0:T(8,128)(2,1)S(1)}, u32[]{:S(2)}, u32[]{:S(2)}) collective-permute-start(bf16[16,2048]{1,0:T(8,128)(2,1)S(1)} %broadcast_select_fusion.8), channel_id=1, source_target_pairs={{0,4},{1,5},{2,6},{3,7},{4,0},{5,1},{6,2},{7,3},{8,12},{9,13},{10,... | collective-permute-start | bytes 196616 | tf_op jit(solution)/shard_map/ppermute | solution.py:366
  129.5 12.8 %copy-start.1 = (bf16[8,16,2048]{2,1,0:T(8,128)(2,1)}, bf16[8,16,2048]{2,1,0:T(8,128)(2,1)S(1)}, u32[]{:S(2)}) copy-start(bf16[8,16,2048]{2,1,0:T(8,128)(2,1)S(1)} %all-to-all-done.4) | copy-start | bytes 1572868
  133.8 14.6 %copy-start.2 = (bf16[128,1024]{1,0:T(8,128)(2,1)}, bf16[128,1024]{1,0:T(8,128)(2,1)S(1)}, u32[]{:S(2)}) copy-start(bf16[128,1024]{1,0:T(8,128)(2,1)S(1)} %low_grad.1.b_ref) | copy-start | bytes 786436
  133.8 1.6 %collective-permute-start.23 = (bf16[128,1024]{1,0:T(8,128)(2,1)S(1)}, bf16[128,1024]{1,0:T(8,128)(2,1)S(1)}, u32[]{:S(2)}, u32[]{:S(2)}) collective-permute-start(bf16[128,1024]{1,0:T(8,128)(2,1)S(1)} %low_grad.1.b_ref), channel_id=1, source_target_pairs={{0,8},{8,0},{16,24},{24,16},{1,9},{9,1},{17,25},{25,17},{2,10},{10... | collective-permute-start | bytes 786440 | tf_op jit(solution)/shard_map/ppermute | solution.py:366
  133.9 8.8 %copy-start.12 = (bf16[64,2048]{1,0:T(8,128)(2,1)}, bf16[64,2048]{1,0:T(8,128)(2,1)S(1)}, u32[]{:S(2)}) copy-start(bf16[64,2048]{1,0:T(8,128)(2,1)S(1)} %pad_maximum_fusion.2.bn_ref) | copy-start | bytes 786436
  133.9 8.8 %collective-permute-start.25 = (bf16[64,2048]{1,0:T(8,128)(2,1)S(1)}, bf16[64,2048]{1,0:T(8,128)(2,1)S(1)}, u32[]{:S(2)}, u32[]{:S(2)}) collective-permute-start(bf16[64,2048]{1,0:T(8,128)(2,1)S(1)} %pad_maximum_fusion.2.bn_ref), channel_id=1, source_target_pairs={{0,1},{1,0},{2,3},{3,2},{4,5},{5,4},{6,7},{7,6},{8,9},{9,8},{10,11... | collective-permute-start | bytes 786440 | tf_op jit(solution)/shard_map/ppermute | solution.py:366
  135.4 13.0 %copy-start.14 = (bf16[128,1024]{1,0:T(8,128)(2,1)}, bf16[128,1024]{1,0:T(8,128)(2,1)S(1)}, u32[]{:S(2)}) copy-start(bf16[128,1024]{1,0:T(8,128)(2,1)S(1)} %collective-permute-done.23.bn_ref) | copy-start | bytes 786436
  135.5 12.9 %collective-permute-start.24 = (bf16[128,1024]{1,0:T(8,128)(2,1)S(1)}, bf16[128,1024]{1,0:T(8,128)(2,1)S(1)}, u32[]{:S(2)}, u32[]{:S(2)}) collective-permute-start(bf16[128,1024]{1,0:T(8,128)(2,1)S(1)} %broadcast_select_fusion.5), channel_id=1, source_target_pairs={{0,16},{8,24},{16,0},{24,8},{1,17},{9,25},{17,1},{25,9},{2,18},{10... | collective-permute-start | bytes 786440 | tf_op jit(solution)/shard_map/ppermute | solution.py:366
  142.7 0.7 copy-start.18
  (2 other events, 1.4 us)

commit v4 on v3

v4 whole, which is shorter than its diff:
```python
import functools

import jax
import jax.numpy as jnp
from jax import lax
from jax.experimental import pallas as pl
from jax.experimental.pallas import tpu as pltpu
from jax.sharding import PartitionSpec as P

SLOTS = 16
BLOCK = 256
ROOT = 0.7978845608028654
CUBE = 0.044715
NT = (((1,), (1,)), ((), ()))
TN = (((0,), (0,)), ((), ()))
PARAMS = pltpu.CompilerParams(vmem_limit_bytes=16 * 1024 * 1024)
SMALL = pltpu.CompilerParams(vmem_limit_bytes=56 * 1024 * 1024)
STREAM = pltpu.CompilerParams(vmem_limit_bytes=50 * 1024 * 1024)
IN_VMEM = pl.BlockSpec(memory_space=pltpu.VMEM)
IN_HBM = pl.BlockSpec(memory_space=pltpu.HBM)
IN_SMEM = pl.BlockSpec(memory_space=pltpu.SMEM)
ANYWHERE = pl.BlockSpec(memory_space=pl.ANY)
FREE = pl.CostEstimate(flops=0, bytes_accessed=0, transcendentals=0)


def bf16(*shape):
    return jax.ShapeDtypeStruct(shape, jnp.bfloat16)


def f32(*shape):
    return jax.ShapeDtypeStruct(shape, jnp.float32)


def cuts(size, step=BLOCK):
    step = min(step, size)
    return [pl.ds(start, step) for start in range(0, size, step)]


def tie(*values):
    return lax.optimization_barrier(values)


def call(kernel, name, where, arrays, outs):
    operands = [] if where is None else [where]
    return pl.pallas_call(
        kernel,
        in_specs=[IN_SMEM] * len(operands) + [IN_VMEM] * len(arrays),
        out_specs=[IN_VMEM] * len(outs),
        out_shape=outs,
        compiler_params=PARAMS,
        cost_estimate=FREE,
        name=name,
    )(*operands, *arrays)


def stream(kernel, name, where, arrays, weights, outs, buffers, copies, away=0):
    operands = [] if where is None else [where]
    return pl.pallas_call(
        kernel,
        in_specs=[IN_SMEM] * len(operands) + [IN_VMEM] * len(arrays) + [ANYWHERE] * len(weights),
        out_specs=[IN_VMEM] * (len(outs) - away) + [IN_HBM] * away,
        out_shape=outs,
        scratch_shapes=[pltpu.VMEM(shape, jnp.bfloat16) for shape in buffers] + [pltpu.SemaphoreType.DMA((copies,))],
        compiler_params=STREAM,
        cost_estimate=FREE,
        name=name,
    )(*operands, *arrays, *weights)


def bring(w_ref, level, buffer, sems, first, along):
    pieces = []
    for i, cut in enumerate(cuts(buffer.shape[along])):
        source = w_ref.at[0, level, cut, :] if along == 0 else w_ref.at[0, level, :, cut]
        target = buffer.at[cut, :] if along == 0 else buffer.at[:, cut]
        copy = pltpu.make_async_copy(source, target, sems.at[first + i])
        copy.start()
        pieces.append((cut, copy))
    return pieces


def norm_value(v, gain):
    return v * lax.rsqrt(jnp.mean(v * v, axis=-1, keepdims=True) + 1e-05) * gain.astype(jnp.float32)


def gelu_both(a):
    t = jnp.tanh(ROOT * (a + CUBE * (a * a * a)))
    half = 0.5 * (1.0 + t)
    slope = half + 0.5 * a * (1.0 - t * t) * (ROOT * (1.0 + (3.0 * CUBE) * (a * a)))
    return a * half, slope


def slots_of_rows(routes_ref, cap, flip):
    count = routes_ref.shape[0]
    down = lax.broadcasted_iota(jnp.int32, (count, count), 0)
    along = lax.broadcasted_iota(jnp.int32, (count, count), 1)
    route_down = jnp.zeros((count, count), jnp.int32)
    route_along = jnp.zeros((count, count), jnp.int32)
    for r in range(count):
        route = routes_ref[r]
        route_down = jnp.where(down == r, route, route_down)
        route_along = jnp.where(along == r, route, route_along)
    earlier = jnp.where((route_down == route_along) & (down < along), 1, 0)
    rank = jnp.sum(earlier, axis=0, keepdims=True)
    return (route_along[0:1, :] ^ flip) * cap + rank


def pack_kernel(copies, flip_ref, routes_ref, rows_ref, *out_refs):
    count = routes_ref.shape[0]
    cap = out_refs[0].shape[-2]
    slots = slots_of_rows(routes_ref, cap, flip_ref[0])
    for group in range(SLOTS // cap):
        want = group * cap + lax.broadcasted_iota(jnp.int32, (cap, count), 0)
        pick = (want == slots).astype(jnp.float32).astype(jnp.bfloat16)
        value = jnp.dot(pick, rows_ref[...], preferred_element_type=jnp.float32).astype(jnp.bfloat16)
        if copies == 0:
            out_refs[group][...] = value
        for copy in range(copies):
            out_refs[0][group * copies + copy] = value


def pack(flip, routes, rows, paths, copies):
    cap, width = SLOTS // paths, rows.shape[1]
    outs = [bf16(paths * copies, cap, width)] if copies else [bf16(cap, width)] * paths
    got = pl.pallas_call(
        functools.partial(pack_kernel, copies),
        in_specs=[IN_SMEM, IN_SMEM, IN_VMEM],
        out_specs=[IN_VMEM] * len(outs),
        out_shape=outs,
        compiler_params=SMALL,
        cost_estimate=FREE,
        name="pack",
    )(flip.reshape(1), routes, rows)
    return got[0] if copies else got


def settle_kernel(where_ref, got_ref, x_ref, own_ref, spread_ref):
    count, rows, _ = got_ref.shape
    total = x_ref[pl.ds(pl.multiple_of(where_ref[2] * rows, rows), rows), :].astype(jnp.float32)
    for i in range(count):
        total += got_ref[i].astype(jnp.float32)
    total = total.astype(jnp.bfloat16)
    own_ref[...] = total
    for i in range(count):
        spread_ref[i] = total


def settle(where, got, x):
    count, rows, width = got.shape
    return call(settle_kernel, "settle", where, [got, x], [bf16(rows, width), bf16(count, rows, width)])


def pull_back(dy, h, gain, grad):
    grad = grad * gain.astype(jnp.float32)
    h = h.astype(jnp.float32)
    scale = lax.rsqrt(jnp.mean(h * h, axis=-1, keepdims=True) + 1e-05)
    unit = h * scale
    pull = scale * (grad - unit * jnp.mean(grad * unit, axis=-1, keepdims=True))
    return (dy.astype(jnp.float32) + pull).astype(jnp.bfloat16)


def settle_back_kernel(where_ref, got_ref, dy_ref, h_ref, gain_ref, own_ref, spread_ref):
    count, rows, _ = got_ref.shape
    grad = got_ref[0].astype(jnp.float32)
    for i in range(1, count):
        grad += got_ref[i].astype(jnp.float32)
    dy = dy_ref[pl.ds(pl.multiple_of(where_ref[2] * rows, rows), rows), :]
    total = pull_back(dy, h_ref[...], gain_ref[1:2, :], grad)
    own_ref[...] = total
    for i in range(count):
        spread_ref[i] = total


def settle_back(where, got, dy, h_own, gains):
    count, rows, width = got.shape
    outs = [bf16(rows, width), bf16(count, rows, width)]
    return call(settle_back_kernel, "settle_back", where, [got, dy, h_own, gains], outs)


def half_kernel(where_ref, keep_ref, got_ref, mine_ref, *rest):
    gives, total = rest[:-1], rest[-1]
    total[...] = keep_ref[...].astype(jnp.float32) + got_ref[...].astype(jnp.float32)
    z = where_ref[2] >> 1
    mine_ref[...] = total[z]
    for step, give_ref in enumerate(gives):
        give_ref[...] = total[z ^ (step + 1)].astype(jnp.bfloat16)


def half_sums(where, keep, got):
    groups, rows, width = keep.shape
    return pl.pallas_call(
        half_kernel,
        in_specs=[IN_SMEM] + [IN_VMEM] * 2,
        out_specs=[IN_VMEM] * groups,
        out_shape=[f32(rows, width)] + [bf16(rows, width)] * (groups - 1),
        scratch_shapes=[pltpu.VMEM(keep.shape, jnp.float32)],
        compiler_params=PARAMS,
        cost_estimate=FREE,
        name="half_sums",
    )(where, keep, got)


def last_kernel(x_ref, mine_ref, *rest):
    total = x_ref[...].astype(jnp.float32) + mine_ref[...]
    for got_ref in rest[:-1]:
        total += got_ref[...].astype(jnp.float32)
    rest[-1][...] = total.astype(jnp.bfloat16)


def last_sums(x_own, mine, got):
    return call(last_kernel, "last_sums", None, [x_own, mine, *got], [bf16(*x_own.shape)])[0]


def last_back_kernel(dy_ref, h_ref, gain_ref, mine_ref, *rest):
    grad = mine_ref[...]
    for got_ref in rest[:-1]:
        grad += got_ref[...].astype(jnp.float32)
    rest[-1][...] = pull_back(dy_ref[...], h_ref[...], gain_ref[1:2, :], grad)


def last_back(dy_own, h_own, gains, mine, got):
    return call(last_back_kernel, "last_back", None, [dy_own, h_own, gains, mine, *got], [bf16(*h_own.shape)])[0]


def low_kernel(steps, where_ref, x_ref, gain_ref, wi_ref, wo_ref, n_ref, u_ref, slope_ref, *rest):
    if steps:
        own_ref, keep_ref, give_ref, wi, wo, part_ref, sems = rest
        own_ref[...] = x_ref[pl.ds(pl.multiple_of(where_ref[2] * SLOTS, SLOTS), SLOTS), :]
    else:
        part_ref, wi, wo, sems = rest
    into = bring(wi_ref, 0, wi, sems, 0, 1)
    n_ref[...] = norm_value(x_ref[...].astype(jnp.float32), gain_ref[0:1, :]).astype(jnp.bfloat16)
    for i, (cut, copy) in enumerate(into):
        copy.wait()
        if i == 0:
            out_of = bring(wo_ref, 0, wo, sems, len(into), 1)
        a = jnp.dot(n_ref[...], wi[:, cut], preferred_element_type=jnp.float32)
        u, slope = gelu_both(a)
        u_ref[:, cut] = u.astype(jnp.bfloat16)
        slope_ref[:, cut] = slope
    for cut, copy in out_of:
        copy.wait()
        part = jnp.dot(u_ref[...], wo[:, cut], preferred_element_type=jnp.float32)
        part_ref[:, cut] = part.astype(jnp.bfloat16)
    if steps:
        split_rows(part_ref, where_ref[2], keep_ref, give_ref)


def split_rows(part_ref, shard, keep_ref, give_ref):
    groups = part_ref.shape[0] // (2 * SLOTS)
    for y in range(2):

        @pl.when((shard & 1) == y)
        def _():
            for z in range(groups):
                start = z * 2 * SLOTS
                keep_ref[z] = part_ref[start + y * SLOTS : start + (y + 1) * SLOTS, :]
                give_ref[z] = part_ref[start + (1 - y) * SLOTS : start + (2 - y) * SLOTS, :]


def place_rows(half_ref, other_ref, shard, out_ref):
    for step in range(half_ref.shape[0] // SLOTS):
        for flip, source in enumerate((half_ref, other_ref)):
            start = pl.multiple_of((shard ^ (2 * step) ^ flip) * SLOTS, SLOTS)
            out_ref[pl.ds(start, SLOTS), :] = source[step * SLOTS : (step + 1) * SLOTS, :]


def low_forward(where, x, gains, w_in, w_out, steps):
    rows, width = x.shape
    hidden = w_in.shape[3]
    outs = [bf16(rows, width), bf16(rows, hidden), f32(rows, hidden)]
    buffers = [(width, hidden), (hidden, width)]
    if steps:
        outs += [bf16(SLOTS, width)] + [bf16(rows // (2 * SLOTS), SLOTS, width)] * 2
        buffers.append((rows, width))
    else:
        outs.append(bf16(rows, width))
    copies = len(cuts(hidden)) + len(cuts(width))
    return stream(functools.partial(low_kernel, steps), "low_forward", where, [x, gains], [w_in, w_out], outs, buffers, copies)


def high_kernel(steps, where_ref, *refs):
    if steps:
        half_ref, other_ref, gain_ref, du_ref, wi_ref, n_ref, u_ref, da_ref, keep_ref, give_ref, wi, h_ref, part_ref, sems = refs
    else:
        h_ref, gain_ref, du_ref, wi_ref, n_ref, u_ref, da_ref, part_ref, wi, sems = refs
    into = bring(wi_ref, 1, wi, sems, 0, 1)
    if steps:
        place_rows(half_ref, other_ref, where_ref[2], h_ref)
    n_ref[...] = norm_value(h_ref[...].astype(jnp.float32), gain_ref[1:2, :]).astype(jnp.bfloat16)
    for cut, copy in into:
        copy.wait()
        a = jnp.dot(n_ref[...], wi[:, cut], preferred_element_type=jnp.float32)
        u, slope = gelu_both(a)
        u_ref[:, cut] = u.astype(jnp.bfloat16)
        da_ref[:, cut] = (slope * du_ref[:, cut]).astype(jnp.bfloat16)
    for cut in cuts(wi.shape[0]):
        part = lax.dot_general(da_ref[...], wi[cut, :], NT, preferred_element_type=jnp.float32)
        part_ref[:, cut] = part.astype(jnp.bfloat16)
    if steps:
        split_rows(part_ref, where_ref[2], keep_ref, give_ref)


def high_both(where, h, gains, w_in, du, steps):
    rows, width = du.shape[0], gains.shape[1]
    hidden = w_in.shape[3]
    outs = [bf16(rows, width), bf16(rows, hidden), bf16(rows, hidden)]
    buffers = [(width, hidden)]
    if steps:
        outs += [bf16(rows // (2 * SLOTS), SLOTS, width)] * 2
        buffers += [(rows, width)] * 2
    else:
        outs.append(bf16(rows, width))
    kernel = functools.partial(high_kernel, steps)
    return stream(kernel, "high_both", where, [*h, gains, du], [w_in], outs, buffers, len(cuts(hidden)))


def places(order, rows, path, shard):
    to = lax.broadcasted_iota(jnp.int32, (rows, rows), 0)
    source = lax.broadcasted_iota(jnp.int32, (rows, rows), 1)
    if order == "dispatch":
        far = ((to >> 2) & 7) ^ shard
        block = ((far & 1) << 2) | (far & 2) | (far >> 2)
        wanted = block * 16 + ((to >> 5) ^ path) * 4 + (to & 3)
    else:
        far = (to >> 4) ^ shard
        block = ((far & 1) << 2) | (far & 2) | (far >> 2)
        wanted = block * 16 + (to & 15)
    return (source == wanted).astype(jnp.float32).astype(jnp.bfloat16)


def high_grad_kernel(ordered, where_ref, raw_ref, wo_ref, own_ref, du_ref, out_ref, wo, dy_ref, sems):
    pieces = bring(wo_ref, 1, wo, sems, 0, 0)
    if ordered:
        dy_ref[...] = raw_ref[...]
    else:
        pick = places("dispatch", raw_ref.shape[0], where_ref[3], where_ref[2])
        dy_ref[...] = jnp.dot(pick, raw_ref[...], preferred_element_type=jnp.float32).astype(jnp.bfloat16)
    out = pltpu.make_async_copy(dy_ref, out_ref, sems.at[len(pieces)])
    out.start()
    own_ref[...] = dy_ref[pl.ds(pl.multiple_of(where_ref[2] * SLOTS, SLOTS), SLOTS), :]
    for cut, copy in pieces:
        copy.wait()
        du_ref[:, cut] = lax.dot_general(dy_ref[...], wo[cut, :], NT, preferred_element_type=jnp.float32)
    out.wait()


def high_grad(where, raw, w_out, ordered):
    rows, width = raw.shape
    hidden = w_out.shape[2]
    outs = [bf16(SLOTS, width), f32(rows, hidden), bf16(rows, width)]
    kernel = functools.partial(high_grad_kernel, ordered)
    buffers = [(hidden, width), (rows, width)]
    return stream(kernel, "high_grad", where, [raw], [w_out], outs, buffers, len(cuts(hidden)) + 1, 1)


def low_grad_kernel(steps, where_ref, *refs):
    if steps:
        half_ref, other_ref, slope_ref, wo_ref, da_ref, out_ref, wo, dh_ref, sems = refs
    else:
        dh_ref, slope_ref, wo_ref, da_ref, wo, sems = refs
    loads = bring(wo_ref, 0, wo, sems, 0, 0)
    if steps:
        place_rows(half_ref, other_ref, where_ref[2], dh_ref)
        out = pltpu.make_async_copy(dh_ref, out_ref, sems.at[len(loads)])
        out.start()
    for cut, copy in loads:
        copy.wait()
        du = lax.dot_general(dh_ref[...], wo[cut, :], NT, preferred_element_type=jnp.float32)
        da_ref[:, cut] = (du * slope_ref[:, cut]).astype(jnp.bfloat16)
    if steps:
        out.wait()


def low_grad(where, dh, w_out, slope, steps):
    rows, hidden = slope.shape
    width = w_out.shape[3]
    outs = [bf16(rows, hidden)] + ([bf16(rows, width)] if steps else [])
    kernel = functools.partial(low_grad_kernel, steps)
    buffers = [(hidden, width)] + ([(rows, width)] if steps else [])
    away = 1 if steps else 0
    return stream(kernel, "low_grad", where, [*dh, slope], [w_out], outs, buffers, len(cuts(hidden)) + 1, away)


def pair_kernel(level, jobs, where_ref, *refs):
    count = len(jobs)
    groups = [refs[6 * i : 6 * i + 6] for i in range(count)]
    outs = refs[-1 - 5 * count : -1 - 4 * count]
    scratch = [refs[-1 - 4 * count :][4 * i : 4 * i + 4] for i in range(count)]
    sems = refs[-1]
    own = []
    for i, (factor, order) in enumerate(jobs):
        a_ref, _, _, b_ref, bn_ref, bf_ref = groups[i]
        right, both, _, raw = scratch[i]
        rows, base = a_ref.shape[0], 8 * i
        own.append(pltpu.make_async_copy(a_ref, both.at[pl.ds(0, rows), :], sems.at[base + 2]))
        own.append(pltpu.make_async_copy(b_ref, right.at[pl.ds(0, rows), :], sems.at[base + 3]))
        if order:
            half = rows // 2
            own.append(pltpu.make_async_copy(bn_ref, raw.at[pl.ds(0, half), :], sems.at[base + 6]))
            own.append(pltpu.make_async_copy(bf_ref, raw.at[pl.ds(half, half), :], sems.at[base + 7]))
    for copy in own:
        copy.start()

    def take(which):
        copies = []
        for i, (factor, order) in enumerate(jobs):
            right, both, _, _ = scratch[i]
            rows, base = groups[i][0].shape[0], 8 * i
            theirs = pl.ds(rows, rows)
            copies.append(pltpu.make_async_copy(groups[i][1 + which], both.at[theirs, :], sems.at[base + 4]))
            if not order:
                copies.append(pltpu.make_async_copy(groups[i][4 + which], right.at[theirs, :], sems.at[base + 5]))
        for copy in copies:
            copy.start()
        for copy in copies:
            copy.wait()

    @pl.when(where_ref[level] == 1)
    def _():
        take(0)

    @pl.when(where_ref[level] != 1)
    def _():
        take(1)

    for copy in own:
        copy.wait()
    last = []
    for i, (factor, order) in enumerate(jobs):
        right, both, slots, raw = scratch[i]
        rows = groups[i][0].shape[0]
        if order:
            pick = places(order, rows, where_ref[3] ^ where_ref[level], where_ref[2])
            right[rows:, :] = jnp.dot(pick, raw[...], preferred_element_type=jnp.float32).astype(jnp.bfloat16)
        copies = []
        for step, cut in enumerate(cuts(both.shape[1], 2 * BLOCK)):
            slot = step % 2
            if step >= 2:
                copies[step - 2].wait()
            value = lax.dot_general(both[:, cut], right[...], TN, preferred_element_type=jnp.float32)
            slots[slot] = (value * factor).astype(jnp.bfloat16)
            copies.append(pltpu.make_async_copy(slots.at[slot], outs[i].at[0, level, cut, :], sems.at[8 * i + slot]))
            copies[-1].start()
        last += copies[-2:]
    for copy in last:
        copy.wait()


def pair_grads(where, level, *jobs):
    operands, befores, outs, scratch, settings = [where], [], [], [], []
    for a, a_mate, b, b_mate, before, order in jobs:
        (rows, left), right = a.shape, b.shape[1]
        operands += [a, *a_mate, b, *b_mate]
        befores += [] if before is None else [before]
        outs.append(bf16(1, 2, left, right))
        scratch += [
            pltpu.VMEM((2 * rows, right), jnp.bfloat16),
            pltpu.VMEM((2 * rows, left), jnp.bfloat16),
            pltpu.VMEM((2, min(2 * BLOCK, left), right), jnp.bfloat16),
            pltpu.VMEM((rows, right), jnp.bfloat16),
        ]
        settings.append((-0.5 / rows**0.5, order))
    return pl.pallas_call(
        functools.partial(pair_kernel, level, settings),
        in_specs=[IN_SMEM] + [ANYWHERE] * (len(operands) + len(befores) - 1),
        out_specs=[ANYWHERE] * len(outs),
        out_shape=outs,
        scratch_shapes=[*scratch, pltpu.SemaphoreType.DMA((8 * len(jobs),))],
        input_output_aliases={len(operands) + i: i for i in range(len(befores))},
        compiler_params=SMALL,
        cost_estimate=FREE,
        name="pair_grads",
    )(*operands, *befores)


def dispatch(spread):
    got = lax.all_to_all(spread, ("path", "shard"), split_axis=0, concat_axis=0, tiled=True)
    return got.reshape(got.shape[0] * got.shape[1], got.shape[2])


def gather_shard(spread):
    got = lax.all_to_all(spread, "shard", split_axis=0, concat_axis=0, tiled=True)
    return got.reshape(got.shape[0] * got.shape[1], got.shape[2])


def scatter_shard(part):
    shards = lax.axis_size("shard")
    blocks = part.reshape(shards, part.shape[0] // shards, part.shape[1])
    return lax.all_to_all(blocks, "shard", split_axis=0, concat_axis=0, tiled=True)


def swap(value, axis, bit):
    return lax.ppermute(value, axis, [(i, i ^ bit) for i in range(lax.axis_size(axis))])


def join(*values):
    return lax.optimization_barrier(jnp.concatenate(values, axis=0))


def gather_steps(own, *others):
    pieces = [swap(own, "shard", bit) for bit in (2, 4, 6)]
    own, *rest = tie(own, *pieces, *others)
    half = join(own, *rest[:3])
    return [half, swap(half, "shard", 1)], rest[3:]


def from_mate(values, *mates):
    paths = lax.axis_size("path")
    mates = mates if len(mates) == len(values) else mates * len(values)
    if paths == 4:
        nears = [swap(v, "path", 1) for v in values]
        sent = [jnp.where(mate == 3, near, v) for near, v, mate in zip(nears, values, mates)]
        return [[near, v] for near, v in zip(nears, sent)]
    me = lax.axis_index("path")
    pairs = []
    for value, mate in zip(values, mates):
        behind = (me - (me ^ mate)) % paths
        mine = value
        for shift in range(1, paths):
            got = lax.ppermute(value, "path", [(i, (i + shift) % paths) for i in range(paths)])
            value, mine = tie(value, jnp.where(behind == shift, got, mine))
        pairs.append([mine, mine])
    return pairs


def along_x(pair):
    if lax.axis_size("path") == 4:
        pair[1] = swap(pair[1], "path", 2)


def body(tokens, routes, cotangent, gains, w_in, w_out, partners):
    paths = lax.axis_size("path")
    shards = lax.axis_size("shard")
    cubes = paths == 4 and shards == 8
    me = lax.axis_index("path")
    shard = lax.axis_index("shard")
    mate_low = partners[0, me] ^ me
    mate_high = partners[1, me] ^ me
    where = jnp.stack([mate_low, mate_high, shard, me])
    none = jnp.int32(0)
    gain = gains[0]
    routes = routes.reshape(-1)

    width, hidden = w_in.shape[2:]

    spread = pack(none, routes, tokens, paths, shards)
    x = dispatch(spread)
    if cubes:
        by_path = pack(me, routes, cotangent, paths, 0)
        rows_1 = join(by_path[0], *[swap(by_path[k], "path", k) for k in (1, 2, 3)])
        hop_1 = swap(rows_1, "shard", 4)
        x, hop_1, where, mate_low, mate_high = tie(x, hop_1, where, mate_low, mate_high)
    n1, u1, slope1, *parts = low_forward(where, x, gain, w_in, w_out, cubes)

    (n1_mate,) = from_mate([n1], mate_low)
    if cubes:
        x_own, keep, give = parts
        rows_2 = join(rows_1, hop_1)
        got, hop_2, n1_mate[1] = tie(swap(give, "shard", 1), swap(rows_2, "shard", 2), n1_mate[1])
        along_x(n1_mate)
        mine, *gives = half_sums(where, keep, got)
        got = [swap(part, "shard", 2 * k + 2) for k, part in enumerate(gives)]
        rows_4 = join(tie(rows_2, mine)[0], hop_2)
        *got, hop_3 = tie(*got, swap(rows_4, "shard", 1))
        h_own = last_sums(x_own, mine, got)
    else:
        along_x(n1_mate)
        h_own, h_spread = settle(where, scatter_shard(parts[0]), x)

    (u1_mate,) = from_mate([u1], mate_low)
    if cubes:
        (half_mate,) = from_mate([rows_4], mate_high)
        dy_own, du2, dy = high_grad(where, join(rows_4, hop_3), w_out, False)
        h, (n1_mate[1], u1_mate[1], half_mate[1]) = gather_steps(h_own, n1_mate[1], u1_mate[1], half_mate[1])
        along_x(u1_mate)
        along_x(half_mate)
        *h, u1_mate[1], du2 = tie(*h, u1_mate[1], du2)
    else:
        h = [gather_shard(h_spread)]
        along_x(u1_mate)
        dy_own, du2, dy = high_grad(where, dispatch(pack(none, routes, cotangent, paths, shards)), w_out, True)
    n2, u2, da2, *parts = high_both(where, h, gain, w_in, du2, cubes)

    da2_mate, u2_mate = from_mate([da2, u2], mate_high)
    if cubes:
        keep, give = parts
        got, da2_mate[1], half_mate[1] = tie(swap(give, "shard", 1), da2_mate[1], half_mate[1])
        along_x(da2_mate)
        mine, *gives = half_sums(where, keep, got)
        got = [swap(part, "shard", 2 * k + 2) for k, part in enumerate(gives)]
        half = jnp.where(mate_high == 1, *half_mate)
        hop_4 = swap(tie(half, mine)[0], "shard", 1)
        *got, hop_4, da2_mate[1], u2_mate[1] = tie(*got, hop_4, da2_mate[1], u2_mate[1])
        along_x(u2_mate)
        dh_own = last_back(dy_own, h_own, gain, mine, got)
    else:
        along_x(da2_mate)
        along_x(u2_mate)
        dh_own, dh_spread = settle_back(where, scatter_shard(parts[0]), dy, h_own, gain)

    (n2_mate,) = from_mate([n2], mate_high)
    if cubes:
        (dh_pair,) = from_mate([dh_own], mate_low)
        along_x(dh_pair)
        dh_piece = jnp.where(mate_low == 1, *dh_pair)
        dh, (u2_mate[1], n2_mate[1], dh_piece) = gather_steps(dh_own, u2_mate[1], n2_mate[1], dh_piece)
        along_x(n2_mate)
        pieces = [swap(dh_piece, "shard", bit) for bit in (4, 2, 6)]
        dy_mate = [half, hop_4]
    else:
        along_x(n2_mate)
        dh = [gather_shard(dh_spread)]
    da1, *dh_ordered = low_grad(where, dh, w_out, slope1, cubes)
    dh = dh_ordered[0] if cubes else dh[0]

    if cubes:
        da1, n2_mate[1], *pieces = tie(da1, n2_mate[1], *pieces)
    (da1_mate,) = from_mate([da1], mate_low)
    along_x(da1_mate)
    if cubes:
        dh_half = join(dh_piece, *pieces)
        dh_mate = [dh_half, swap(dh_half, "shard", 1)]
    else:
        (dh_mate,) = from_mate([dh], mate_low)
        along_x(dh_mate)
        (dy_mate,) = from_mate([dy], mate_high)
        along_x(dy_mate)
    delta_in, delta_out = pair_grads(
        where,
        1,
        (n2, n2_mate, da2, da2_mate, None, ""),
        (u2, u2_mate, dy, dy_mate, None, "dispatch" if cubes else ""),
    )
    delta_in, delta_out = pair_grads(
        where,
        0,
        (n1, n1_mate, da1, da1_mate, delta_in, ""),
        (u1, u1_mate, dh, dh_mate, delta_out, "gather" if cubes else ""),
    )
    return (delta_in, delta_out)


def solution(mesh):
    in_specs = (
        P(("path", "shard"), None),
        P(("path", "shard"), None),
        P(("path", "shard"), None),
        P("path", None, None),
        P("path", None, None, "shard"),
        P("path", None, "shard", None),
        P(),
    )
    out_specs = (P("path", None, None, "shard"), P("path", None, "shard", None))
    return jax.shard_map(body, mesh=mesh, in_specs=in_specs, out_specs=out_specs, check_vma=False)
```

time: 156 us -> 148 us (0.949)
  Pallas kernels: 48 us -> 41.3 us
  other arithmetic: 7.16 us -> 3.89 us
  waiting for transfers between devices: 42.2 us -> 43.9 us
    ppermute x26 -> x43, starting transfers between devices: 25.2 us -> 44.2 us  [swap(): lax.ppermute(value, axis, [(i, i ^ bit) for i in range(lax.axis_size(axis...]
    all_to_all x4 -> x0, starting transfers between devices: 18.9 us -> none  [the longest x2 10.4 us: gather_shard(): lax.all_to_all(spread, 'shard', split_axis=0, concat_axis=0, tiled=True)]
    ppermute x26 -> x43, waiting for transfers between devices: 32.2 us -> 36.7 us  [swap(): lax.ppermute(value, axis, [(i, i ^ bit) for i in range(lax.axis_size(axis...]
    pallas_call x4, Pallas kernels: 20.8 us -> 16.8 us  [the longest x2 15.5 us: pair_grads(): pl.pallas_call(functools.partial(pair_kernel, level, settings), in_specs=...]
    all_to_all x4 -> x0, waiting for transfers between devices: 2.85 us -> none  [the longest x2 2.71 us: gather_shard(): lax.all_to_all(spread, 'shard', split_axis=0, concat_axis=0, tiled=True)]
    pallas_call x2, Pallas kernels: 3 us -> 0.27 us  [call(): pl.pallas_call(kernel, in_specs=[IN_SMEM] * len(operands) + [IN_VMEM] * l...]
    select_n x7 -> x8, other arithmetic: 3.43 us -> 1.93 us  [from_mate(): jnp.where(mate == 3, near, v)]
  transfers between devices with their start and end apart: 31 -> 44, of which waited for: 15 -> 16; matrix products, arithmetic and copies ran while one was open for 6% -> 4% of each run, Pallas kernels for 19% -> 14%
where the time goes in v4:
time: 148 us
  starting transfers between devices  51.5 us (35%)
  waiting for transfers between devices  43.9 us (30%)
  Pallas kernels  41.3 us (28%)
  local copies, waits for them, and re-layouts  4.63 us (3%)
  other arithmetic  3.89 us (3%)
  between operations  2.69 us (2%)
    ppermute x43, starting transfers between devices, swap(): lax.ppermute(value, axis, [(i, i ^ bit) for i in range(lax.axis_size(axis...  44.2 us
    ppermute x43, waiting for transfers between devices, swap(): lax.ppermute(value, axis, [(i, i ^ bit) for i in range(lax.axis_size(axis...  36.7 us
    pallas_call x4, Pallas kernels, stream(): pl.pallas_call(kernel, in_specs=[IN_SMEM] * len(operands) + [IN_VMEM] * l...  20.8 us
    pallas_call x2, Pallas kernels, pair_grads(): pl.pallas_call(functools.partial(pair_kernel, level, settings), in_specs=...  15.5 us
    all_to_all x1, starting transfers between devices, dispatch(): lax.all_to_all(spread, ('path', 'shard'), split_axis=0, concat_axis=0, ti...  7.3 us
    all_to_all x1, waiting for transfers between devices, dispatch(): lax.all_to_all(spread, ('path', 'shard'), split_axis=0, concat_axis=0, ti...  7.17 us
    pallas_call x2, Pallas kernels, pack(): pl.pallas_call(functools.partial(pack_kernel, copies), in_specs=[IN_SMEM,...  3.54 us
    unnamed x56, local copies, waits for them, and re-layouts  3.11 us
  transfers between devices with their start and end apart: 44, of which 16 were waited for; matrix products, arithmetic and copies ran while one was open for 4% of the time, Pallas kernels for 14%

profile of v4, /device:TPU:0, one launch (start us, length us, event | category | flops | bytes accessed | tf_op | source)
XLA Modules:
  0.0 147.9 jit_solution(13862674799933806769)
XLA Ops:
  0.6 1.9 %pack.2 = bf16[32,4,2048]{2,1,0:T(4,128)(2,1)} custom-call(s32[1]{0:T(128)} %constant.7.clone.1.flip_ref, s32[12]{0:T(128)} %bitcast.11, bf16[12,2048]{1,0:T(8,128)(2,1)} %rows_ref.2), custom_call_target="tpu_custom_call" | custom-call | tf_op jit(solution)/shard_map/pack/pallas_call | solution.py:124
  2.5 7.3 %all-to-all-start = ((bf16[32,4,2048]{2,1,0:T(4,128)(2,1)}), bf16[32,4,2048]{2,1,0:T(4,128)(2,1)S(1)}, u32[]{:S(2)}, u32[]{:S(2)}) async-start(bf16[32,4,2048]{2,1,0:T(4,128)(2,1)} %pack.2), calls=%async_computation | async-start | bytes 1048576 | tf_op jit(solution)/shard_map/all_to_all | solution.py:477
  9.8 1.7 %pack.3 = (bf16[4,2048]{1,0:T(4,128)(2,1)}, bf16[4,2048]{1,0:T(4,128)(2,1)}, bf16[4,2048]{1,0:T(4,128)(2,1)}, bf16[4,2048]{1,0:T(4,128)(2,1)}) custom-call(s32[1]{0:T(128)} %bitcast.1.flip_ref, s32[12]{0:T(128)} %bitcast.12, bf16[12,2048]{1,0:T(8,128)(2,1)} %rows_ref.3), custom_call_target="tpu_custom_call" | custom-call | tf_op jit(solution)/shard_map/pack/pallas_call | solution.py:124
  11.7 1.7 %collective-permute-start.1 = (bf16[4,2048]{1,0:T(4,128)(2,1)}, bf16[4,2048]{1,0:T(4,128)(2,1)S(1)}, u32[]{:S(2)}, u32[]{:S(2)}) collective-permute-start(bf16[4,2048]{1,0:T(4,128)(2,1)} %get-tuple-element.80), channel_id=1, source_target_pairs={{0,16},{8,24},{16,0},{24,8},{1,17},{9,25},{17,1},{25,9},{2,18},{10... | collective-permute-start | bytes 49160 | tf_op jit(solution)/shard_map/ppermute | solution.py:493
  13.4 1.4 constant_dynamic-slice_fusion.1
  17.6 2.7 %collective-permute-start.3 = (bf16[16,2048]{1,0:T(8,128)(2,1)S(1)}, bf16[16,2048]{1,0:T(8,128)(2,1)S(1)}, u32[]{:S(2)}, u32[]{:S(2)}) collective-permute-start(bf16[16,2048]{1,0:T(8,128)(2,1)S(1)} %pad_maximum_fusion.6), channel_id=1, source_target_pairs={{0,4},{1,5},{2,6},{3,7},{4,0},{5,1},{6,2},{7,3},{8,12},{9,13},{10,... | collective-permute-start | bytes 196616 | tf_op jit(solution)/shard_map/ppermute | solution.py:493
  20.4 7.2 %all-to-all-done = bf16[32,4,2048]{2,1,0:T(4,128)(2,1)S(1)} async-done(((bf16[32,4,2048]{2,1,0:T(4,128)(2,1)}), bf16[32,4,2048]{2,1,0:T(4,128)(2,1)S(1)}, u32[]{:S(2)}, u32[]{:S(2)}) %all-to-all-start) | async-done | bytes 524320 | tf_op jit(solution)/shard_map/all_to_all | solution.py:477
  28.4 6.1 %low_forward.1 = (bf16[128,2048]{1,0:T(8,128)(2,1)S(1)}, bf16[128,1024]{1,0:T(8,128)(2,1)S(1)}, f32[128,1024]{1,0:T(8,128)S(1)}, bf16[16,2048]{1,0:T(8,128)(2,1)...) custom-call(s32[4]{0:T(128)S(1)} %pad_add_fusion.where_ref, ...), custom_call_target="tpu_custom_call" | custom-call | tf_op jit(solution)/shard_map/low_forward/pallas_call | solution.py:58
  34.7 0.9 collective-permute-start.6
  36.5 0.9 broadcast_select_fusion.1
  37.5 3.2 %collective-permute-done.6 = bf16[32,2048]{1,0:T(8,128)(2,1)S(1)} collective-permute-done((bf16[32,2048]{1,0:T(8,128)(2,1)S(1)}, bf16[32,2048]{1,0:T(8,128)(2,1)S(1)}, u32[]{:S(2)}, u32[]{:S(2)}) %collective-permute-start.6) | collective-permute-done | bytes 131104 | tf_op jit(solution)/shard_map/ppermute | solution.py:493
  40.6 3.3 %collective-permute-done.5.got_ref = bf16[4,16,2048]{2,1,0:T(8,128)(2,1)S(1)} collective-permute-done((bf16[4,16,2048]{2,1,0:T(8,128)(2,1)S(1)}, bf16[4,16,2048]{2,1,0:T(8,128)(2,1)S(1)}, u32[]{:S(2)}, u32[]{:S(2)}) %collective-permute-start.5) | collective-permute-done | bytes 262176 | tf_op jit(solution)/shard_map/ppermute | solution.py:493
  44.6 1.3 collective-permute-start.7
  45.9 1.5 collective-permute-start.10
  47.7 2.4 %collective-permute-start.9 = (bf16[16,2048]{1,0:T(8,128)(2,1)S(1)}, bf16[16,2048]{1,0:T(8,128)(2,1)S(1)}, u32[]{:S(2)}, u32[]{:S(2)}) collective-permute-start(bf16[16,2048]{1,0:T(8,128)(2,1)S(1)} %get-tuple-element.94), channel_id=1, source_target_pairs={{0,6},{1,7},{2,4},{3,5},{4,2},{5,3},{6,0},{7,1},{8,14},{9,15},{10,... | collective-permute-start | bytes 196616 | tf_op jit(solution)/shard_map/ppermute | solution.py:493
  50.1 1.5 %collective-permute-start.14 = (bf16[128,2048]{1,0:T(8,128)(2,1)}, bf16[128,2048]{1,0:T(8,128)(2,1)S(1)}, u32[]{:S(2)}, u32[]{:S(2)}) collective-permute-start(bf16[128,2048]{1,0:T(8,128)(2,1)} %broadcast_select_fusion.1), channel_id=1, source_target_pairs={{0,16},{8,24},{16,0},{24,8},{1,17},{9,25},{17,1},{25,9},{2,18},{10... | collective-permute-start | bytes 1572872 | tf_op jit(solution)/shard_map/ppermute | solution.py:493
  51.6 3.8 %collective-permute-done.8.rest_1_ = bf16[16,2048]{1,0:T(8,128)(2,1)S(1)} collective-permute-done((bf16[16,2048]{1,0:T(8,128)(2,1)S(1)}, bf16[16,2048]{1,0:T(8,128)(2,1)S(1)}, u32[]{:S(2)}, u32[]{:S(2)}) %collective-permute-start.8) | collective-permute-done | bytes 65568 | tf_op jit(solution)/shard_map/ppermute | solution.py:493
  55.5 1.5 %collective-permute-start.13 = (bf16[16,2048]{1,0:T(8,128)(2,1)S(1)}, bf16[16,2048]{1,0:T(8,128)(2,1)S(1)}, u32[]{:S(2)}, u32[]{:S(2)}) collective-permute-start(bf16[16,2048]{1,0:T(8,128)(2,1)S(1)} %last_sums.1.h_ref), channel_id=1, source_target_pairs={{0,6},{1,7},{2,4},{3,5},{4,2},{5,3},{6,0},{7,1},{8,14},{9,15},{10,... | collective-permute-start | bytes 196616 | tf_op jit(solution)/shard_map/ppermute | solution.py:493
  57.0 1.9 %collective-permute-start.12 = (bf16[16,2048]{1,0:T(8,128)(2,1)S(1)}, bf16[16,2048]{1,0:T(8,128)(2,1)S(1)}, u32[]{:S(2)}, u32[]{:S(2)}) collective-permute-start(bf16[16,2048]{1,0:T(8,128)(2,1)S(1)} %last_sums.1.h_ref), channel_id=1, source_target_pairs={{0,4},{1,5},{2,6},{3,7},{4,0},{5,1},{6,2},{7,3},{8,12},{9,13},{10,... | collective-permute-start | bytes 196616 | tf_op jit(solution)/shard_map/ppermute | solution.py:493
  58.9 1.0 collective-permute-start.11
  59.9 0.8 broadcast_select_fusion.5
  60.8 1.6 %collective-permute-done.13 = bf16[16,2048]{1,0:T(8,128)(2,1)S(1)} collective-permute-done((bf16[16,2048]{1,0:T(8,128)(2,1)S(1)}, bf16[16,2048]{1,0:T(8,128)(2,1)S(1)}, u32[]{:S(2)}, u32[]{:S(2)}) %collective-permute-start.13) | collective-permute-done | bytes 65568 | tf_op jit(solution)/shard_map/ppermute | solution.py:493
  62.3 2.9 %collective-permute-done.12 = bf16[16,2048]{1,0:T(8,128)(2,1)S(1)} collective-permute-done((bf16[16,2048]{1,0:T(8,128)(2,1)S(1)}, bf16[16,2048]{1,0:T(8,128)(2,1)S(1)}, u32[]{:S(2)}, u32[]{:S(2)}) %collective-permute-start.12) | collective-permute-done | bytes 65568 | tf_op jit(solution)/shard_map/ppermute | solution.py:493
  65.8 1.5 collective-permute-start.18
  67.3 4.7 %high_grad.1 = (bf16[16,2048]{1,0:T(8,128)(2,1)S(1)}, f32[128,1024]{1,0:T(8,128)S(1)}, bf16[128,2048]{1,0:T(8,128)(2,1)S(1)}) custom-call(s32[4]{0:T(128)S(1)} %pad_add_fusion.where_ref, bf16[128,2048]{1,0:T(8,128)(2,1)S(1)} %pad_maximum_fusion.raw_ref, bf16[1,2,1024,2048]{3,2,1,0:T(8,128)(2,1)} %refs_3_.1), custom_call_target="tpu_custom_call" | custom-call | tf_op jit(solution)/shard_map/high_grad/pallas_call | solution.py:58
  73.3 5.3 %high_both.1 = (bf16[128,2048]{1,0:T(8,128)(2,1)S(1)}, bf16[128,1024]{1,0:T(8,128)(2,1)S(1)}, bf16[128,1024]{1,0:T(8,128)(2,1)S(1)}, bf16[4,16,2048]{2,1,0:T(8,128)(2,1)S(1)}, bf16[4,16,2048]{2,1,0:T(8,128)(2,1)S(1)}) custom-call(s32[4]{0:T(128)S(1)} %pad_add_fusion.where_ref, bf16[64,2048]{1,0:T(8,128)(2,1)S(1)} %pad_maximum_fusion.2.refs_0_, ...), custom_call_target="tpu_custom_call" | custom-call | tf_op jit(solution)/shard_map/high_both/pallas_call | solution.py:58
  78.8 1.6 %collective-permute-start.21 = (bf16[64,2048]{1,0:T(8,128)(2,1)}, bf16[64,2048]{1,0:T(8,128)(2,1)S(1)}, u32[]{:S(2)}, u32[]{:S(2)}) collective-permute-start(bf16[64,2048]{1,0:T(8,128)(2,1)} %broadcast_select_fusion.5), channel_id=1, source_target_pairs={{0,16},{8,24},{16,0},{24,8},{1,17},{9,25},{17,1},{25,9},{2,18},{10... | collective-permute-start | bytes 786440 | tf_op jit(solution)/shard_map/ppermute | solution.py:493
  80.4 1.5 %collective-permute-start.19 = (bf16[4,16,2048]{2,1,0:T(8,128)(2,1)S(1)}, bf16[4,16,2048]{2,1,0:T(8,128)(2,1)S(1)}, u32[]{:S(2)}, u32[]{:S(2)}) collective-permute-start(bf16[4,16,2048]{2,1,0:T(8,128)(2,1)S(1)} %get-tuple-element.116), channel_id=1, source_target_pairs={{0,1},{1,0},{2,3},{3,2},{4,5},{5,4},{6,7},{7,6},{8,9},{9,8},{10,11... | collective-permute-start | bytes 786440 | tf_op jit(solution)/shard_map/ppermute | solution.py:493
  81.9 5.8 %collective-permute-done.21 = bf16[64,2048]{1,0:T(8,128)(2,1)S(1)} collective-permute-done((bf16[64,2048]{1,0:T(8,128)(2,1)}, bf16[64,2048]{1,0:T(8,128)(2,1)S(1)}, u32[]{:S(2)}, u32[]{:S(2)}) %collective-permute-start.21) | collective-permute-done | bytes 262176 | tf_op jit(solution)/shard_map/ppermute | solution.py:493
  87.7 1.0 collective-permute-done.19.got_ref
  89.5 1.0 broadcast_select_fusion.2.refs_10_
  90.5 1.6 %collective-permute-start.25 = (bf16[64,2048]{1,0:T(8,128)(2,1)S(1)}, bf16[64,2048]{1,0:T(8,128)(2,1)S(1)}, u32[]{:S(2)}, u32[]{:S(2)}) collective-permute-start(bf16[64,2048]{1,0:T(8,128)(2,1)S(1)} %broadcast_select_fusion.2.refs_10_), channel_id=1, source_target_pairs={{0,1},{1,0},{2,3},{3,2},{4,5},{5,4},{6,7},{7,6},{8,9},{9,8},{10,11... | collective-permute-start | bytes 786440 | tf_op jit(solution)/shard_map/ppermute | solution.py:493
  92.6 2.0 %collective-permute-start.23 = (bf16[16,2048]{1,0:T(8,128)(2,1)S(1)}, bf16[16,2048]{1,0:T(8,128)(2,1)S(1)}, u32[]{:S(2)}, u32[]{:S(2)}) collective-permute-start(bf16[16,2048]{1,0:T(8,128)(2,1)S(1)} %get-tuple-element.122), channel_id=1, source_target_pairs={{0,4},{1,5},{2,6},{3,7},{4,0},{5,1},{6,2},{7,3},{8,12},{9,13},{10,... | collective-permute-start | bytes 196616 | tf_op jit(solution)/shard_map/ppermute | solution.py:493
  94.7 2.4 %collective-permute-start.24 = (bf16[16,2048]{1,0:T(8,128)(2,1)S(1)}, bf16[16,2048]{1,0:T(8,128)(2,1)S(1)}, u32[]{:S(2)}, u32[]{:S(2)}) collective-permute-start(bf16[16,2048]{1,0:T(8,128)(2,1)S(1)} %get-tuple-element.123), channel_id=1, source_target_pairs={{0,6},{1,7},{2,4},{3,5},{4,2},{5,3},{6,0},{7,1},{8,14},{9,15},{10,... | collective-permute-start | bytes 196616 | tf_op jit(solution)/shard_map/ppermute | solution.py:493
  97.1 4.2 %collective-permute-done.23.rest_1_ = bf16[16,2048]{1,0:T(8,128)(2,1)S(1)} collective-permute-done((bf16[16,2048]{1,0:T(8,128)(2,1)S(1)}, bf16[16,2048]{1,0:T(8,128)(2,1)S(1)}, u32[]{:S(2)}, u32[]{:S(2)}) %collective-permute-start.23) | collective-permute-done | bytes 65568 | tf_op jit(solution)/shard_map/ppermute | solution.py:493
  101.7 1.9 %collective-permute-start.30 = (bf16[16,2048]{1,0:T(8,128)(2,1)S(1)}, bf16[16,2048]{1,0:T(8,128)(2,1)S(1)}, u32[]{:S(2)}, u32[]{:S(2)}) collective-permute-start(bf16[16,2048]{1,0:T(8,128)(2,1)S(1)} %last_back.1), channel_id=1, source_target_pairs={{0,6},{1,7},{2,4},{3,5},{4,2},{5,3},{6,0},{7,1},{8,14},{9,15},{10,... | collective-permute-start | bytes 196616 | tf_op jit(solution)/shard_map/ppermute | solution.py:493
  103.6 1.1 collective-permute-start.29
  104.7 1.4 collective-permute-start.28
  106.1 1.5 %collective-permute-start.31 = (bf16[128,1024]{1,0:T(8,128)(2,1)S(1)}, bf16[128,1024]{1,0:T(8,128)(2,1)S(1)}, u32[]{:S(2)}, u32[]{:S(2)}) collective-permute-start(bf16[128,1024]{1,0:T(8,128)(2,1)S(1)} %broadcast_select_fusion.3), channel_id=1, source_target_pairs={{0,16},{8,24},{16,0},{24,8},{1,17},{9,25},{17,1},{25,9},{2,18},{10... | collective-permute-start | bytes 786440 | tf_op jit(solution)/shard_map/ppermute | solution.py:493
  108.3 7.0 %collective-permute-done.34 = bf16[16,2048]{1,0:T(8,128)(2,1)S(1)} collective-permute-done((bf16[16,2048]{1,0:T(8,128)(2,1)S(1)}, bf16[16,2048]{1,0:T(8,128)(2,1)S(1)}, u32[]{:S(2)}, u32[]{:S(2)}) %collective-permute-start.34) | collective-permute-done | bytes 65568 | tf_op jit(solution)/shard_map/ppermute | solution.py:493
  115.4 1.5 %collective-permute-start.36 = (bf16[128,2048]{1,0:T(8,128)(2,1)S(1)}, bf16[128,2048]{1,0:T(8,128)(2,1)S(1)}, u32[]{:S(2)}, u32[]{:S(2)}) collective-permute-start(bf16[128,2048]{1,0:T(8,128)(2,1)S(1)} %broadcast_select_fusion), channel_id=1, source_target_pairs={{0,16},{8,24},{16,0},{24,8},{1,17},{9,25},{17,1},{25,9},{2,18},{10... | collective-permute-start | bytes 1572872 | tf_op jit(solution)/shard_map/ppermute | solution.py:493
  117.5 1.9 %collective-permute-start.39 = (bf16[16,2048]{1,0:T(8,128)(2,1)S(1)}, bf16[16,2048]{1,0:T(8,128)(2,1)S(1)}, u32[]{:S(2)}, u32[]{:S(2)}) collective-permute-start(bf16[16,2048]{1,0:T(8,128)(2,1)S(1)} %broadcast_select_fusion.9), channel_id=1, source_target_pairs={{0,6},{1,7},{2,4},{3,5},{4,2},{5,3},{6,0},{7,1},{8,14},{9,15},{10,... | collective-permute-start | bytes 196616 | tf_op jit(solution)/shard_map/ppermute | solution.py:493
  119.4 2.5 %collective-permute-start.37 = (bf16[16,2048]{1,0:T(8,128)(2,1)S(1)}, bf16[16,2048]{1,0:T(8,128)(2,1)S(1)}, u32[]{:S(2)}, u32[]{:S(2)}) collective-permute-start(bf16[16,2048]{1,0:T(8,128)(2,1)S(1)} %broadcast_select_fusion.9), channel_id=1, source_target_pairs={{0,4},{1,5},{2,6},{3,7},{4,0},{5,1},{6,2},{7,3},{8,12},{9,13},{10,... | collective-permute-start | bytes 196616 | tf_op jit(solution)/shard_map/ppermute | solution.py:493
  121.9 1.7 %collective-permute-done.35.refs_1_ = bf16[64,2048]{1,0:T(8,128)(2,1)S(1)} collective-permute-done((bf16[64,2048]{1,0:T(8,128)(2,1)S(1)}, bf16[64,2048]{1,0:T(8,128)(2,1)S(1)}, u32[]{:S(2)}, u32[]{:S(2)}) %collective-permute-start.35) | collective-permute-done | bytes 262176 | tf_op jit(solution)/shard_map/ppermute | solution.py:493
  123.7 4.6 %low_grad.1 = (bf16[128,1024]{1,0:T(8,128)(2,1)S(1)}, bf16[128,2048]{1,0:T(8,128)(2,1)S(1)}) custom-call(s32[4]{0:T(128)S(1)} %pad_add_fusion.where_ref, bf16[64,2048]{1,0:T(8,128)(2,1)S(1)} %pad_maximum_fusion.3.refs_0_, bf16[64,2048]{1,0:T(8,128)(2,1)S(1)} %collective-permute-done.35.refs_1_, f32[128,1024]{1,0:T(8,128)S(1)} %get-tuple-element.137.refs_2_, ...), custom_call_target="tpu_custom_call" | custom-call | tf_op jit(solution)/shard_map/low_grad/pallas_call | solution.py:58
  129.8 0.9 collective-permute-done.40.refs_4_
  131.5 7.7 %pair_grads.2 = (bf16[1,2,2048,1024]{3,2,1,0:T(8,128)(2,1)}, bf16[1,2,1024,2048]{3,2,1,0:T(8,128)(2,1)}) custom-call(s32[4]{0:T(128)} %copy-done.10, bf16[128,2048]{1,0:T(8,128)(2,1)} %copy-done.1, bf16[128,2048]{1,0:T(8,128)(2,1)} %copy-done.12, bf16[128,2048]{1,0:T(8,128)(2,1)} %copy-done.21, bf16[128,1024]{1,0:T(8,128)(2,1)} %copy-done.5, ...), custom_call_target="tpu_custom_call" | custom-call | tf_op jit(solution)/shard_map/pair_grads/pallas_call | solution.py:463
  140.0 7.7 %pair_grads.3 = (bf16[1,2,2048,1024]{3,2,1,0:T(8,128)(2,1)}, bf16[1,2,1024,2048]{3,2,1,0:T(8,128)(2,1)}) custom-call(s32[4]{0:T(128)} %copy-done.10, bf16[128,2048]{1,0:T(8,128)(2,1)} %copy-done, bf16[128,2048]{1,0:T(8,128)(2,1)} %copy-done.11, bf16[128,2048]{1,0:T(8,128)(2,1)} %copy-done.20, ...), custom_call_target="tpu_custom_call", output_to_operand_aliasing={{0}: (13, {}), {1}: (14, {})} | custom-call | tf_op jit(solution)/shard_map/pair_grads/pallas_call | solution.py:463
  (128 shorter events, 12.5 us)
Async XLA Ops:
  2.5 25.1 %all-to-all-start = ((bf16[32,4,2048]{2,1,0:T(4,128)(2,1)}), bf16[32,4,2048]{2,1,0:T(4,128)(2,1)S(1)}, u32[]{:S(2)}, u32[]{:S(2)}) async-start(bf16[32,4,2048]{2,1,0:T(4,128)(2,1)} %pack.2), calls=%async_computation | async-start | bytes 1048576 | tf_op jit(solution)/shard_map/all_to_all | solution.py:477
  11.5 4.6 %collective-permute-start = (bf16[4,2048]{1,0:T(4,128)(2,1)}, bf16[4,2048]{1,0:T(4,128)(2,1)S(1)}, u32[]{:S(2)}, u32[]{:S(2)}) collective-permute-start(bf16[4,2048]{1,0:T(4,128)(2,1)} %get-tuple-element.79), channel_id=1, source_target_pairs={{0,8},{8,0},{16,24},{24,16},{1,9},{9,1},{17,25},{25,17},{2,10},{10... | collective-permute-start | bytes 49160 | tf_op jit(solution)/shard_map/ppermute | solution.py:493
  11.7 4.4 %collective-permute-start.1 = (bf16[4,2048]{1,0:T(4,128)(2,1)}, bf16[4,2048]{1,0:T(4,128)(2,1)S(1)}, u32[]{:S(2)}, u32[]{:S(2)}) collective-permute-start(bf16[4,2048]{1,0:T(4,128)(2,1)} %get-tuple-element.80), channel_id=1, source_target_pairs={{0,16},{8,24},{16,0},{24,8},{1,17},{9,25},{17,1},{25,9},{2,18},{10... | collective-permute-start | bytes 49160 | tf_op jit(solution)/shard_map/ppermute | solution.py:493
  13.4 3.4 %collective-permute-start.2 = (bf16[4,2048]{1,0:T(4,128)(2,1)}, bf16[4,2048]{1,0:T(4,128)(2,1)S(1)}, u32[]{:S(2)}, u32[]{:S(2)}) collective-permute-start(bf16[4,2048]{1,0:T(4,128)(2,1)} %get-tuple-element.81), channel_id=1, source_target_pairs={{0,24},{8,16},{16,8},{24,0},{1,25},{9,17},{17,9},{25,1},{2,26},{10... | collective-permute-start | bytes 49160 | tf_op jit(solution)/shard_map/ppermute | solution.py:493
  17.6 10.1 %collective-permute-start.3 = (bf16[16,2048]{1,0:T(8,128)(2,1)S(1)}, bf16[16,2048]{1,0:T(8,128)(2,1)S(1)}, u32[]{:S(2)}, u32[]{:S(2)}) collective-permute-start(bf16[16,2048]{1,0:T(8,128)(2,1)S(1)} %pad_maximum_fusion.6), channel_id=1, source_target_pairs={{0,4},{1,5},{2,6},{3,7},{4,0},{5,1},{6,2},{7,3},{8,12},{9,13},{10,... | collective-permute-start | bytes 196616 | tf_op jit(solution)/shard_map/ppermute | solution.py:493
  20.4 103.3 %copy-start.10 = (s32[4]{0:T(128)}, s32[4]{0:T(128)S(1)}, u32[]{:S(2)}) copy-start(s32[4]{0:T(128)S(1)} %pad_add_fusion.where_ref) | copy-start | bytes 52
  34.5 2.0 %collective-permute-start.4 = (bf16[128,2048]{1,0:T(8,128)(2,1)S(1)}, bf16[128,2048]{1,0:T(8,128)(2,1)S(1)}, u32[]{:S(2)}, u32[]{:S(2)}) collective-permute-start(bf16[128,2048]{1,0:T(8,128)(2,1)S(1)} %get-tuple-element.84.refs_0_), channel_id=1, source_target_pairs={{0,8},{8,0},{16,24},{24,16},{1,9},{9,1},{17,25},{25,17},{2,10},{10... | collective-permute-start | bytes 1572872 | tf_op jit(solution)/shard_map/ppermute | solution.py:493
  34.7 5.9 %collective-permute-start.6 = (bf16[32,2048]{1,0:T(8,128)(2,1)S(1)}, bf16[32,2048]{1,0:T(8,128)(2,1)S(1)}, u32[]{:S(2)}, u32[]{:S(2)}) collective-permute-start(bf16[32,2048]{1,0:T(8,128)(2,1)S(1)} %pad_maximum_fusion.5), channel_id=1, source_target_pairs={{0,2},{1,3},{2,0},{3,1},{4,6},{5,7},{6,4},{7,5},{8,10},{9,11},{10,... | collective-permute-start | bytes 393224 | tf_op jit(solution)/shard_map/ppermute | solution.py:493
  35.7 8.3 %collective-permute-start.5 = (bf16[4,16,2048]{2,1,0:T(8,128)(2,1)S(1)}, bf16[4,16,2048]{2,1,0:T(8,128)(2,1)S(1)}, u32[]{:S(2)}, u32[]{:S(2)}) collective-permute-start(bf16[4,16,2048]{2,1,0:T(8,128)(2,1)S(1)} %get-tuple-element.87), channel_id=1, source_target_pairs={{0,1},{1,0},{2,3},{3,2},{4,5},{5,4},{6,7},{7,6},{8,9},{9,8},{10,11... | collective-permute-start | bytes 786440 | tf_op jit(solution)/shard_map/ppermute | solution.py:493
  36.2 11.5 %collective-permute-start.15 = (bf16[128,1024]{1,0:T(8,128)(2,1)S(1)}, bf16[128,1024]{1,0:T(8,128)(2,1)S(1)}, u32[]{:S(2)}, u32[]{:S(2)}) collective-permute-start(bf16[128,1024]{1,0:T(8,128)(2,1)S(1)} %get-tuple-element.101.refs_6_), channel_id=1, source_target_pairs={{0,8},{8,0},{16,24},{24,16},{1,9},{9,1},{17,25},{25,17},{2,10},{10... | collective-permute-start | bytes 786440 | tf_op jit(solution)/shard_map/ppermute | solution.py:493
  44.6 5.5 %collective-permute-start.7 = (bf16[16,2048]{1,0:T(8,128)(2,1)S(1)}, bf16[16,2048]{1,0:T(8,128)(2,1)S(1)}, u32[]{:S(2)}, u32[]{:S(2)}) collective-permute-start(bf16[16,2048]{1,0:T(8,128)(2,1)S(1)} %get-tuple-element.92), channel_id=1, source_target_pairs={{0,2},{1,3},{2,0},{3,1},{4,6},{5,7},{6,4},{7,5},{8,10},{9,11},{10,... | collective-permute-start | bytes 196616 | tf_op jit(solution)/shard_map/ppermute | solution.py:493
  45.9 9.5 %collective-permute-start.10 = (bf16[64,2048]{1,0:T(8,128)(2,1)S(1)}, bf16[64,2048]{1,0:T(8,128)(2,1)S(1)}, u32[]{:S(2)}, u32[]{:S(2)}) collective-permute-start(bf16[64,2048]{1,0:T(8,128)(2,1)S(1)} %pad_maximum_fusion.1), channel_id=1, source_target_pairs={{0,1},{1,0},{2,3},{3,2},{4,5},{5,4},{6,7},{7,6},{8,9},{9,8},{10,11... | collective-permute-start | bytes 786440 | tf_op jit(solution)/shard_map/ppermute | solution.py:493
  47.4 12.6 %collective-permute-start.16 = (bf16[64,2048]{1,0:T(8,128)(2,1)S(1)}, bf16[64,2048]{1,0:T(8,128)(2,1)S(1)}, u32[]{:S(2)}, u32[]{:S(2)}) collective-permute-start(bf16[64,2048]{1,0:T(8,128)(2,1)S(1)} %pad_maximum_fusion.1), channel_id=1, source_target_pairs={{0,8},{8,0},{16,24},{24,16},{1,9},{9,1},{17,25},{25,17},{2,10},{10... | collective-permute-start | bytes 786440 | tf_op jit(solution)/shard_map/ppermute | solution.py:493
  47.4 8.0 %collective-permute-start.8 = (bf16[16,2048]{1,0:T(8,128)(2,1)S(1)}, bf16[16,2048]{1,0:T(8,128)(2,1)S(1)}, u32[]{:S(2)}, u32[]{:S(2)}) collective-permute-start(bf16[16,2048]{1,0:T(8,128)(2,1)S(1)} %get-tuple-element.93), channel_id=1, source_target_pairs={{0,4},{1,5},{2,6},{3,7},{4,0},{5,1},{6,2},{7,3},{8,12},{9,13},{10,... | collective-permute-start | bytes 196616 | tf_op jit(solution)/shard_map/ppermute | solution.py:493
  47.7 7.7 %collective-permute-start.9 = (bf16[16,2048]{1,0:T(8,128)(2,1)S(1)}, bf16[16,2048]{1,0:T(8,128)(2,1)S(1)}, u32[]{:S(2)}, u32[]{:S(2)}) collective-permute-start(bf16[16,2048]{1,0:T(8,128)(2,1)S(1)} %get-tuple-element.94), channel_id=1, source_target_pairs={{0,6},{1,7},{2,4},{3,5},{4,2},{5,3},{6,0},{7,1},{8,14},{9,15},{10,... | collective-permute-start | bytes 196616 | tf_op jit(solution)/shard_map/ppermute | solution.py:493
  50.1 15.1 %collective-permute-start.14 = (bf16[128,2048]{1,0:T(8,128)(2,1)}, bf16[128,2048]{1,0:T(8,128)(2,1)S(1)}, u32[]{:S(2)}, u32[]{:S(2)}) collective-permute-start(bf16[128,2048]{1,0:T(8,128)(2,1)} %broadcast_select_fusion.1), channel_id=1, source_target_pairs={{0,16},{8,24},{16,0},{24,8},{1,17},{9,25},{17,1},{25,9},{2,18},{10... | collective-permute-start | bytes 1572872 | tf_op jit(solution)/shard_map/ppermute | solution.py:493
  55.5 6.8 %collective-permute-start.13 = (bf16[16,2048]{1,0:T(8,128)(2,1)S(1)}, bf16[16,2048]{1,0:T(8,128)(2,1)S(1)}, u32[]{:S(2)}, u32[]{:S(2)}) collective-permute-start(bf16[16,2048]{1,0:T(8,128)(2,1)S(1)} %last_sums.1.h_ref), channel_id=1, source_target_pairs={{0,6},{1,7},{2,4},{3,5},{4,2},{5,3},{6,0},{7,1},{8,14},{9,15},{10,... | collective-permute-start | bytes 196616 | tf_op jit(solution)/shard_map/ppermute | solution.py:493
  57.0 8.2 %collective-permute-start.12 = (bf16[16,2048]{1,0:T(8,128)(2,1)S(1)}, bf16[16,2048]{1,0:T(8,128)(2,1)S(1)}, u32[]{:S(2)}, u32[]{:S(2)}) collective-permute-start(bf16[16,2048]{1,0:T(8,128)(2,1)S(1)} %last_sums.1.h_ref), channel_id=1, source_target_pairs={{0,4},{1,5},{2,6},{3,7},{4,0},{5,1},{6,2},{7,3},{8,12},{9,13},{10,... | collective-permute-start | bytes 196616 | tf_op jit(solution)/shard_map/ppermute | solution.py:493
  58.9 6.3 %collective-permute-start.11 = (bf16[16,2048]{1,0:T(8,128)(2,1)S(1)}, bf16[16,2048]{1,0:T(8,128)(2,1)S(1)}, u32[]{:S(2)}, u32[]{:S(2)}) collective-permute-start(bf16[16,2048]{1,0:T(8,128)(2,1)S(1)} %last_sums.1.h_ref), channel_id=1, source_target_pairs={{0,2},{1,3},{2,0},{3,1},{4,6},{5,7},{6,4},{7,5},{8,10},{9,11},{10,... | collective-permute-start | bytes 196616 | tf_op jit(solution)/shard_map/ppermute | solution.py:493
  65.2 7.9 %collective-permute-start.17 = (bf16[64,2048]{1,0:T(8,128)(2,1)S(1)}, bf16[64,2048]{1,0:T(8,128)(2,1)S(1)}, u32[]{:S(2)}, u32[]{:S(2)}) collective-permute-start(bf16[64,2048]{1,0:T(8,128)(2,1)S(1)} %pad_maximum_fusion.2.refs_0_), channel_id=1, source_target_pairs={{0,1},{1,0},{2,3},{3,2},{4,5},{5,4},{6,7},{7,6},{8,9},{9,8},{10,11... | collective-permute-start | bytes 786440 | tf_op jit(solution)/shard_map/ppermute | solution.py:493
  65.8 7.5 %collective-permute-start.18 = (bf16[128,1024]{1,0:T(8,128)(2,1)S(1)}, bf16[128,1024]{1,0:T(8,128)(2,1)S(1)}, u32[]{:S(2)}, u32[]{:S(2)}) collective-permute-start(bf16[128,1024]{1,0:T(8,128)(2,1)S(1)} %broadcast_select_fusion.7), channel_id=1, source_target_pairs={{0,16},{8,24},{16,0},{24,8},{1,17},{9,25},{17,1},{25,9},{2,18},{10... | collective-permute-start | bytes 786440 | tf_op jit(solution)/shard_map/ppermute | solution.py:493
  78.7 52.7 %copy-start.1 = (bf16[128,2048]{1,0:T(8,128)(2,1)}, bf16[128,2048]{1,0:T(8,128)(2,1)S(1)}, u32[]{:S(2)}) copy-start(bf16[128,2048]{1,0:T(8,128)(2,1)S(1)} %get-tuple-element.132.refs_0_) | copy-start | bytes 1572868
  78.7 52.7 %copy-start.4 = (bf16[128,1024]{1,0:T(8,128)(2,1)}, bf16[128,1024]{1,0:T(8,128)(2,1)S(1)}, u32[]{:S(2)}) copy-start(bf16[128,1024]{1,0:T(8,128)(2,1)S(1)} %get-tuple-element.127.refs_6_) | copy-start | bytes 786436
  78.7 52.7 %copy-start.5 = (bf16[128,1024]{1,0:T(8,128)(2,1)}, bf16[128,1024]{1,0:T(8,128)(2,1)S(1)}, u32[]{:S(2)}) copy-start(bf16[128,1024]{1,0:T(8,128)(2,1)S(1)} %get-tuple-element.117.refs_3_) | copy-start | bytes 786436
  78.7 3.2 %collective-permute-start.20 = (bf16[128,1024]{1,0:T(8,128)(2,1)S(1)}, bf16[128,1024]{1,0:T(8,128)(2,1)S(1)}, u32[]{:S(2)}, u32[]{:S(2)}) collective-permute-start(bf16[128,1024]{1,0:T(8,128)(2,1)S(1)} %get-tuple-element.117.refs_3_), channel_id=1, source_target_pairs={{0,8},{8,0},{16,24},{24,16},{1,9},{9,1},{17,25},{25,17},{2,10},{10... | collective-permute-start | bytes 786440 | tf_op jit(solution)/shard_map/ppermute | solution.py:493
  78.8 8.9 %collective-permute-start.21 = (bf16[64,2048]{1,0:T(8,128)(2,1)}, bf16[64,2048]{1,0:T(8,128)(2,1)S(1)}, u32[]{:S(2)}, u32[]{:S(2)}) collective-permute-start(bf16[64,2048]{1,0:T(8,128)(2,1)} %broadcast_select_fusion.5), channel_id=1, source_target_pairs={{0,16},{8,24},{16,0},{24,8},{1,17},{9,25},{17,1},{25,9},{2,18},{10... | collective-permute-start | bytes 786440 | tf_op jit(solution)/shard_map/ppermute | solution.py:493
  80.4 8.4 %collective-permute-start.19 = (bf16[4,16,2048]{2,1,0:T(8,128)(2,1)S(1)}, bf16[4,16,2048]{2,1,0:T(8,128)(2,1)S(1)}, u32[]{:S(2)}, u32[]{:S(2)}) collective-permute-start(bf16[4,16,2048]{2,1,0:T(8,128)(2,1)S(1)} %get-tuple-element.116), channel_id=1, source_target_pairs={{0,1},{1,0},{2,3},{3,2},{4,5},{5,4},{6,7},{7,6},{8,9},{9,8},{10,11... | collective-permute-start | bytes 786440 | tf_op jit(solution)/shard_map/ppermute | solution.py:493
  81.9 10.7 %collective-permute-start.27 = (bf16[128,1024]{1,0:T(8,128)(2,1)S(1)}, bf16[128,1024]{1,0:T(8,128)(2,1)S(1)}, u32[]{:S(2)}, u32[]{:S(2)}) collective-permute-start(bf16[128,1024]{1,0:T(8,128)(2,1)S(1)} %get-tuple-element.127.refs_6_), channel_id=1, source_target_pairs={{0,8},{8,0},{16,24},{24,16},{1,9},{9,1},{17,25},{25,17},{2,10},{10... | collective-permute-start | bytes 786440 | tf_op jit(solution)/shard_map/ppermute | solution.py:493
  89.4 5.3 %collective-permute-start.22 = (bf16[16,2048]{1,0:T(8,128)(2,1)S(1)}, bf16[16,2048]{1,0:T(8,128)(2,1)S(1)}, u32[]{:S(2)}, u32[]{:S(2)}) collective-permute-start(bf16[16,2048]{1,0:T(8,128)(2,1)S(1)} %get-tuple-element.121), channel_id=1, source_target_pairs={{0,2},{1,3},{2,0},{3,1},{4,6},{5,7},{6,4},{7,5},{8,10},{9,11},{10,... | collective-permute-start | bytes 196616 | tf_op jit(solution)/shard_map/ppermute | solution.py:493
  90.5 10.8 %collective-permute-start.25 = (bf16[64,2048]{1,0:T(8,128)(2,1)S(1)}, bf16[64,2048]{1,0:T(8,128)(2,1)S(1)}, u32[]{:S(2)}, u32[]{:S(2)}) collective-permute-start(bf16[64,2048]{1,0:T(8,128)(2,1)S(1)} %broadcast_select_fusion.2.refs_10_), channel_id=1, source_target_pairs={{0,1},{1,0},{2,3},{3,2},{4,5},{5,4},{6,7},{7,6},{8,9},{9,8},{10,11... | collective-permute-start | bytes 786440 | tf_op jit(solution)/shard_map/ppermute | solution.py:493
  92.1 9.2 %collective-permute-start.26 = (bf16[128,1024]{1,0:T(8,128)(2,1)S(1)}, bf16[128,1024]{1,0:T(8,128)(2,1)S(1)}, u32[]{:S(2)}, u32[]{:S(2)}) collective-permute-start(bf16[128,1024]{1,0:T(8,128)(2,1)S(1)} %broadcast_select_fusion.4), channel_id=1, source_target_pairs={{0,16},{8,24},{16,0},{24,8},{1,17},{9,25},{17,1},{25,9},{2,18},{10... | collective-permute-start | bytes 786440 | tf_op jit(solution)/shard_map/ppermute | solution.py:493
  92.6 15.0 %collective-permute-start.32 = (bf16[128,2048]{1,0:T(8,128)(2,1)S(1)}, bf16[128,2048]{1,0:T(8,128)(2,1)S(1)}, u32[]{:S(2)}, u32[]{:S(2)}) collective-permute-start(bf16[128,2048]{1,0:T(8,128)(2,1)S(1)} %get-tuple-element.132.refs_0_), channel_id=1, source_target_pairs={{0,8},{8,0},{16,24},{24,16},{1,9},{9,1},{17,25},{25,17},{2,10},{10... | collective-permute-start | bytes 1572872 | tf_op jit(solution)/shard_map/ppermute | solution.py:493
  92.6 8.7 %collective-permute-start.23 = (bf16[16,2048]{1,0:T(8,128)(2,1)S(1)}, bf16[16,2048]{1,0:T(8,128)(2,1)S(1)}, u32[]{:S(2)}, u32[]{:S(2)}) collective-permute-start(bf16[16,2048]{1,0:T(8,128)(2,1)S(1)} %get-tuple-element.122), channel_id=1, source_target_pairs={{0,4},{1,5},{2,6},{3,7},{4,0},{5,1},{6,2},{7,3},{8,12},{9,13},{10,... | collective-permute-start | bytes 196616 | tf_op jit(solution)/shard_map/ppermute | solution.py:493
  94.7 6.6 %collective-permute-start.24 = (bf16[16,2048]{1,0:T(8,128)(2,1)S(1)}, bf16[16,2048]{1,0:T(8,128)(2,1)S(1)}, u32[]{:S(2)}, u32[]{:S(2)}) collective-permute-start(bf16[16,2048]{1,0:T(8,128)(2,1)S(1)} %get-tuple-element.123), channel_id=1, source_target_pairs={{0,6},{1,7},{2,4},{3,5},{4,2},{5,3},{6,0},{7,1},{8,14},{9,15},{10,... | collective-permute-start | bytes 196616 | tf_op jit(solution)/shard_map/ppermute | solution.py:493
  101.6 4.5 %collective-permute-start.33 = (bf16[16,2048]{1,0:T(8,128)(2,1)S(1)}, bf16[16,2048]{1,0:T(8,128)(2,1)S(1)}, u32[]{:S(2)}, u32[]{:S(2)}) collective-permute-start(bf16[16,2048]{1,0:T(8,128)(2,1)S(1)} %last_back.1), channel_id=1, source_target_pairs={{0,8},{8,0},{16,24},{24,16},{1,9},{9,1},{17,25},{25,17},{2,10},{10... | collective-permute-start | bytes 196616 | tf_op jit(solution)/shard_map/ppermute | solution.py:493
  101.7 13.7 %collective-permute-start.30 = (bf16[16,2048]{1,0:T(8,128)(2,1)S(1)}, bf16[16,2048]{1,0:T(8,128)(2,1)S(1)}, u32[]{:S(2)}, u32[]{:S(2)}) collective-permute-start(bf16[16,2048]{1,0:T(8,128)(2,1)S(1)} %last_back.1), channel_id=1, source_target_pairs={{0,6},{1,7},{2,4},{3,5},{4,2},{5,3},{6,0},{7,1},{8,14},{9,15},{10,... | collective-permute-start | bytes 196616 | tf_op jit(solution)/shard_map/ppermute | solution.py:493
  103.6 11.8 %collective-permute-start.29 = (bf16[16,2048]{1,0:T(8,128)(2,1)S(1)}, bf16[16,2048]{1,0:T(8,128)(2,1)S(1)}, u32[]{:S(2)}, u32[]{:S(2)}) collective-permute-start(bf16[16,2048]{1,0:T(8,128)(2,1)S(1)} %last_back.1), channel_id=1, source_target_pairs={{0,4},{1,5},{2,6},{3,7},{4,0},{5,1},{6,2},{7,3},{8,12},{9,13},{10,... | collective-permute-start | bytes 196616 | tf_op jit(solution)/shard_map/ppermute | solution.py:493
  104.7 10.7 %collective-permute-start.28 = (bf16[16,2048]{1,0:T(8,128)(2,1)S(1)}, bf16[16,2048]{1,0:T(8,128)(2,1)S(1)}, u32[]{:S(2)}, u32[]{:S(2)}) collective-permute-start(bf16[16,2048]{1,0:T(8,128)(2,1)S(1)} %last_back.1), channel_id=1, source_target_pairs={{0,2},{1,3},{2,0},{3,1},{4,6},{5,7},{6,4},{7,5},{8,10},{9,11},{10,... | collective-permute-start | bytes 196616 | tf_op jit(solution)/shard_map/ppermute | solution.py:493
  106.1 9.3 %collective-permute-start.31 = (bf16[128,1024]{1,0:T(8,128)(2,1)S(1)}, bf16[128,1024]{1,0:T(8,128)(2,1)S(1)}, u32[]{:S(2)}, u32[]{:S(2)}) collective-permute-start(bf16[128,1024]{1,0:T(8,128)(2,1)S(1)} %broadcast_select_fusion.3), channel_id=1, source_target_pairs={{0,16},{8,24},{16,0},{24,8},{1,17},{9,25},{17,1},{25,9},{2,18},{10... | collective-permute-start | bytes 786440 | tf_op jit(solution)/shard_map/ppermute | solution.py:493
  107.6 7.7 %collective-permute-start.34 = (bf16[16,2048]{1,0:T(8,128)(2,1)S(1)}, bf16[16,2048]{1,0:T(8,128)(2,1)S(1)}, u32[]{:S(2)}, u32[]{:S(2)}) collective-permute-start(bf16[16,2048]{1,0:T(8,128)(2,1)S(1)} %broadcast_select_fusion.8), channel_id=1, source_target_pairs={{0,16},{8,24},{16,0},{24,8},{1,17},{9,25},{17,1},{25,9},{2,18},{10... | collective-permute-start | bytes 196616 | tf_op jit(solution)/shard_map/ppermute | solution.py:493
  115.4 13.7 %collective-permute-start.36 = (bf16[128,2048]{1,0:T(8,128)(2,1)S(1)}, bf16[128,2048]{1,0:T(8,128)(2,1)S(1)}, u32[]{:S(2)}, u32[]{:S(2)}) collective-permute-start(bf16[128,2048]{1,0:T(8,128)(2,1)S(1)} %broadcast_select_fusion), channel_id=1, source_target_pairs={{0,16},{8,24},{16,0},{24,8},{1,17},{9,25},{17,1},{25,9},{2,18},{10... | collective-permute-start | bytes 1572872 | tf_op jit(solution)/shard_map/ppermute | solution.py:493
  117.0 6.7 %collective-permute-start.35 = (bf16[64,2048]{1,0:T(8,128)(2,1)S(1)}, bf16[64,2048]{1,0:T(8,128)(2,1)S(1)}, u32[]{:S(2)}, u32[]{:S(2)}) collective-permute-start(bf16[64,2048]{1,0:T(8,128)(2,1)S(1)} %pad_maximum_fusion.3.refs_0_), channel_id=1, source_target_pairs={{0,1},{1,0},{2,3},{3,2},{4,5},{5,4},{6,7},{7,6},{8,9},{9,8},{10,11... | collective-permute-start | bytes 786440 | tf_op jit(solution)/shard_map/ppermute | solution.py:493
  117.5 11.6 %collective-permute-start.39 = (bf16[16,2048]{1,0:T(8,128)(2,1)S(1)}, bf16[16,2048]{1,0:T(8,128)(2,1)S(1)}, u32[]{:S(2)}, u32[]{:S(2)}) collective-permute-start(bf16[16,2048]{1,0:T(8,128)(2,1)S(1)} %broadcast_select_fusion.9), channel_id=1, source_target_pairs={{0,6},{1,7},{2,4},{3,5},{4,2},{5,3},{6,0},{7,1},{8,14},{9,15},{10,... | collective-permute-start | bytes 196616 | tf_op jit(solution)/shard_map/ppermute | solution.py:493
  119.4 9.7 %collective-permute-start.38 = (bf16[16,2048]{1,0:T(8,128)(2,1)S(1)}, bf16[16,2048]{1,0:T(8,128)(2,1)S(1)}, u32[]{:S(2)}, u32[]{:S(2)}) collective-permute-start(bf16[16,2048]{1,0:T(8,128)(2,1)S(1)} %broadcast_select_fusion.9), channel_id=1, source_target_pairs={{0,2},{1,3},{2,0},{3,1},{4,6},{5,7},{6,4},{7,5},{8,10},{9,11},{10,... | collective-permute-start | bytes 196616 | tf_op jit(solution)/shard_map/ppermute | solution.py:493
  119.4 9.7 %collective-permute-start.37 = (bf16[16,2048]{1,0:T(8,128)(2,1)S(1)}, bf16[16,2048]{1,0:T(8,128)(2,1)S(1)}, u32[]{:S(2)}, u32[]{:S(2)}) collective-permute-start(bf16[16,2048]{1,0:T(8,128)(2,1)S(1)} %broadcast_select_fusion.9), channel_id=1, source_target_pairs={{0,4},{1,5},{2,6},{3,7},{4,0},{5,1},{6,2},{7,3},{8,12},{9,13},{10,... | collective-permute-start | bytes 196616 | tf_op jit(solution)/shard_map/ppermute | solution.py:493
  129.2 1.6 %collective-permute-start.40 = (bf16[128,1024]{1,0:T(8,128)(2,1)S(1)}, bf16[128,1024]{1,0:T(8,128)(2,1)S(1)}, u32[]{:S(2)}, u32[]{:S(2)}) collective-permute-start(bf16[128,1024]{1,0:T(8,128)(2,1)S(1)} %get-tuple-element.141.refs_3_), channel_id=1, source_target_pairs={{0,8},{8,0},{16,24},{24,16},{1,9},{9,1},{17,25},{25,17},{2,10},{10... | collective-permute-start | bytes 786440 | tf_op jit(solution)/shard_map/ppermute | solution.py:493
  129.3 9.9 %collective-permute-start.42 = (bf16[64,2048]{1,0:T(8,128)(2,1)S(1)}, bf16[64,2048]{1,0:T(8,128)(2,1)S(1)}, u32[]{:S(2)}, u32[]{:S(2)}) collective-permute-start(bf16[64,2048]{1,0:T(8,128)(2,1)S(1)} %pad_maximum_fusion.4.refs_10_), channel_id=1, source_target_pairs={{0,1},{1,0},{2,3},{3,2},{4,5},{5,4},{6,7},{7,6},{8,9},{9,8},{10,11... | collective-permute-start | bytes 786440 | tf_op jit(solution)/shard_map/ppermute | solution.py:493
  130.8 8.4 %collective-permute-start.41 = (bf16[128,1024]{1,0:T(8,128)(2,1)S(1)}, bf16[128,1024]{1,0:T(8,128)(2,1)S(1)}, u32[]{:S(2)}, u32[]{:S(2)}) collective-permute-start(bf16[128,1024]{1,0:T(8,128)(2,1)S(1)} %broadcast_select_fusion.6), channel_id=1, source_target_pairs={{0,16},{8,24},{16,0},{24,8},{1,17},{9,25},{17,1},{25,9},{2,18},{10... | collective-permute-start | bytes 786440 | tf_op jit(solution)/shard_map/ppermute | solution.py:493
  (24 other events, 400.6 us)

commit v5 on v4

--- a/solution.py
+++ b/solution.py
@@ -17,7 +17,6 @@
 SMALL = pltpu.CompilerParams(vmem_limit_bytes=56 * 1024 * 1024)
 STREAM = pltpu.CompilerParams(vmem_limit_bytes=50 * 1024 * 1024)
 IN_VMEM = pl.BlockSpec(memory_space=pltpu.VMEM)
-IN_HBM = pl.BlockSpec(memory_space=pltpu.HBM)
 IN_SMEM = pl.BlockSpec(memory_space=pltpu.SMEM)
 ANYWHERE = pl.BlockSpec(memory_space=pl.ANY)
 FREE = pl.CostEstimate(flops=0, bytes_accessed=0, transcendentals=0)
@@ -53,12 +52,12 @@
     )(*operands, *arrays)
 
 
-def stream(kernel, name, where, arrays, weights, outs, buffers, copies, away=0):
+def stream(kernel, name, where, arrays, weights, outs, buffers, copies):
     operands = [] if where is None else [where]
     return pl.pallas_call(
         kernel,
         in_specs=[IN_SMEM] * len(operands) + [IN_VMEM] * len(arrays) + [ANYWHERE] * len(weights),
-        out_specs=[IN_VMEM] * (len(outs) - away) + [IN_HBM] * away,
+        out_specs=[IN_VMEM] * len(outs),
         out_shape=outs,
         scratch_shapes=[pltpu.VMEM(shape, jnp.bfloat16) for shape in buffers] + [pltpu.SemaphoreType.DMA((copies,))],
         compiler_params=STREAM,
@@ -323,25 +322,22 @@
         wanted = block * 16 + ((to >> 5) ^ path) * 4 + (to & 3)
     else:
         far = (to >> 4) ^ shard
-        block = ((far & 1) << 2) | (far & 2) | (far >> 2)
+        block = ((far & 1) << 2) | (far >> 1)
         wanted = block * 16 + (to & 15)
     return (source == wanted).astype(jnp.float32).astype(jnp.bfloat16)
 
 
-def high_grad_kernel(ordered, where_ref, raw_ref, wo_ref, own_ref, du_ref, out_ref, wo, dy_ref, sems):
+def high_grad_kernel(ordered, where_ref, raw_ref, wo_ref, own_ref, du_ref, dy_ref, wo, sems):
     pieces = bring(wo_ref, 1, wo, sems, 0, 0)
     if ordered:
         dy_ref[...] = raw_ref[...]
     else:
         pick = places("dispatch", raw_ref.shape[0], where_ref[3], where_ref[2])
         dy_ref[...] = jnp.dot(pick, raw_ref[...], preferred_element_type=jnp.float32).astype(jnp.bfloat16)
-    out = pltpu.make_async_copy(dy_ref, out_ref, sems.at[len(pieces)])
-    out.start()
     own_ref[...] = dy_ref[pl.ds(pl.multiple_of(where_ref[2] * SLOTS, SLOTS), SLOTS), :]
     for cut, copy in pieces:
         copy.wait()
         du_ref[:, cut] = lax.dot_general(dy_ref[...], wo[cut, :], NT, preferred_element_type=jnp.float32)
-    out.wait()
 
 
 def high_grad(where, raw, w_out, ordered):
@@ -349,117 +345,117 @@
     hidden = w_out.shape[2]
     outs = [bf16(SLOTS, width), f32(rows, hidden), bf16(rows, width)]
     kernel = functools.partial(high_grad_kernel, ordered)
-    buffers = [(hidden, width), (rows, width)]
-    return stream(kernel, "high_grad", where, [raw], [w_out], outs, buffers, len(cuts(hidden)) + 1, 1)
+    return stream(kernel, "high_grad", where, [raw], [w_out], outs, [(hidden, width)], len(cuts(hidden)))
 
 
 def low_grad_kernel(steps, where_ref, *refs):
     if steps:
-        half_ref, other_ref, slope_ref, wo_ref, da_ref, out_ref, wo, dh_ref, sems = refs
+        half_ref, other_ref, slope_ref, wo_ref, da_ref, wo, dh_ref, sems = refs
     else:
         dh_ref, slope_ref, wo_ref, da_ref, wo, sems = refs
     loads = bring(wo_ref, 0, wo, sems, 0, 0)
     if steps:
         place_rows(half_ref, other_ref, where_ref[2], dh_ref)
-        out = pltpu.make_async_copy(dh_ref, out_ref, sems.at[len(loads)])
-        out.start()
     for cut, copy in loads:
         copy.wait()
         du = lax.dot_general(dh_ref[...], wo[cut, :], NT, preferred_element_type=jnp.float32)
         da_ref[:, cut] = (du * slope_ref[:, cut]).astype(jnp.bfloat16)
-    if steps:
-        out.wait()
 
 
 def low_grad(where, dh, w_out, slope, steps):
     rows, hidden = slope.shape
     width = w_out.shape[3]
-    outs = [bf16(rows, hidden)] + ([bf16(rows, width)] if steps else [])
+    outs = [bf16(rows, hidden)]
     kernel = functools.partial(low_grad_kernel, steps)
     buffers = [(hidden, width)] + ([(rows, width)] if steps else [])
-    away = 1 if steps else 0
-    return stream(kernel, "low_grad", where, [*dh, slope], [w_out], outs, buffers, len(cuts(hidden)) + 1, away)
+    return stream(kernel, "low_grad", where, [*dh, slope], [w_out], outs, buffers, len(cuts(hidden)))[0]
 
 
 def pair_kernel(level, jobs, where_ref, *refs):
     count = len(jobs)
-    groups = [refs[6 * i : 6 * i + 6] for i in range(count)]
+    groups, used = [], 0
+    for _, _, halves in jobs:
+        size = 5 + halves
+        groups.append(refs[used : used + size])
+        used += size
     outs = refs[-1 - 5 * count : -1 - 4 * count]
     scratch = [refs[-1 - 4 * count :][4 * i : 4 * i + 4] for i in range(count)]
     sems = refs[-1]
-    own = []
-    for i, (factor, order) in enumerate(jobs):
-        a_ref, _, _, b_ref, bn_ref, bf_ref = groups[i]
-        right, both, _, raw = scratch[i]
-        rows, base = a_ref.shape[0], 8 * i
-        own.append(pltpu.make_async_copy(a_ref, both.at[pl.ds(0, rows), :], sems.at[base + 2]))
-        own.append(pltpu.make_async_copy(b_ref, right.at[pl.ds(0, rows), :], sems.at[base + 3]))
-        if order:
-            half = rows // 2
-            own.append(pltpu.make_async_copy(bn_ref, raw.at[pl.ds(0, half), :], sems.at[base + 6]))
-            own.append(pltpu.make_async_copy(bf_ref, raw.at[pl.ds(half, half), :], sems.at[base + 7]))
-    for copy in own:
-        copy.start()
-
-    def take(which):
-        copies = []
-        for i, (factor, order) in enumerate(jobs):
-            right, both, _, _ = scratch[i]
-            rows, base = groups[i][0].shape[0], 8 * i
-            theirs = pl.ds(rows, rows)
-            copies.append(pltpu.make_async_copy(groups[i][1 + which], both.at[theirs, :], sems.at[base + 4]))
-            if not order:
-                copies.append(pltpu.make_async_copy(groups[i][4 + which], right.at[theirs, :], sems.at[base + 5]))
-        for copy in copies:
-            copy.start()
-        for copy in copies:
+
+    def run(which):
+        waits = []
+        for i, (factor, order, halves) in enumerate(jobs):
+            a_ref, *b_refs = groups[i][0], *groups[i][3:]
+            right, both, _, raw = scratch[i]
+            rows, base = a_ref.shape[0], 8 * i
+            half, mine, theirs = rows // 2, pl.ds(0, rows), pl.ds(rows, rows)
+            copies = [
+                pltpu.make_async_copy(a_ref, both.at[mine, :], sems.at[base + 2]),
+                pltpu.make_async_copy(groups[i][1 + which], both.at[theirs, :], sems.at[base + 3]),
+            ]
+            targets = [raw.at[pl.ds(place * half, half), :] for place in range(4)] if order else []
+            if halves == 1:
+                copies.append(pltpu.make_async_copy(b_refs[0], right.at[mine, :], sems.at[base + 4]))
+            else:
+                copies.append(pltpu.make_async_copy(b_refs[0], targets[0], sems.at[base + 4]))
+                copies.append(pltpu.make_async_copy(b_refs[1], targets[1], sems.at[base + 5]))
+            if order:
+                copies.append(pltpu.make_async_copy(b_refs[-2], targets[2], sems.at[base + 6]))
+                copies.append(pltpu.make_async_copy(b_refs[-1], targets[3], sems.at[base + 7]))
+            else:
+                copies.append(pltpu.make_async_copy(b_refs[1 + which], right.at[theirs, :], sems.at[base + 6]))
+            for copy in copies:
+                copy.start()
+            waits.append(copies)
+        last = []
+        for i, (factor, order, halves) in enumerate(jobs):
+            right, both, slots, raw = scratch[i]
+            rows = groups[i][0].shape[0]
+            for copy in waits[i]:
+                copy.wait()
+            if order:
+                for part in (0, 1) if halves == 2 else (1,):
+                    path = where_ref[3] ^ where_ref[level] if part else where_ref[3]
+                    pick, span = places(order, rows, path, where_ref[2]), pl.ds(part * rows, rows)
+                    value = jnp.dot(pick, raw[span, :], preferred_element_type=jnp.float32)
+                    right[span, :] = value.astype(jnp.bfloat16)
+            copies = []
+            for step, cut in enumerate(cuts(both.shape[1], 2 * BLOCK)):
+                slot = step % 2
+                if step >= 2:
+                    copies[step - 2].wait()
+                value = lax.dot_general(both[:, cut], right[...], TN, preferred_element_type=jnp.float32)
+                slots[slot] = (value * factor).astype(jnp.bfloat16)
+                target = outs[i].at[0, level, cut, :]
+                copies.append(pltpu.make_async_copy(slots.at[slot], target, sems.at[8 * i + slot]))
+                copies[-1].start()
+            last += copies[-2:]
+        for copy in last:
             copy.wait()
 
     @pl.when(where_ref[level] == 1)
     def _():
-        take(0)
+        run(0)
 
     @pl.when(where_ref[level] != 1)
     def _():
-        take(1)
-
-    for copy in own:
-        copy.wait()
-    last = []
-    for i, (factor, order) in enumerate(jobs):
-        right, both, slots, raw = scratch[i]
-        rows = groups[i][0].shape[0]
-        if order:
-            pick = places(order, rows, where_ref[3] ^ where_ref[level], where_ref[2])
-            right[rows:, :] = jnp.dot(pick, raw[...], preferred_element_type=jnp.float32).astype(jnp.bfloat16)
-        copies = []
-        for step, cut in enumerate(cuts(both.shape[1], 2 * BLOCK)):
-            slot = step % 2
-            if step >= 2:
-                copies[step - 2].wait()
-            value = lax.dot_general(both[:, cut], right[...], TN, preferred_element_type=jnp.float32)
-            slots[slot] = (value * factor).astype(jnp.bfloat16)
-            copies.append(pltpu.make_async_copy(slots.at[slot], outs[i].at[0, level, cut, :], sems.at[8 * i + slot]))
-            copies[-1].start()
-        last += copies[-2:]
-    for copy in last:
-        copy.wait()
+        run(1)
 
 
 def pair_grads(where, level, *jobs):
     operands, befores, outs, scratch, settings = [where], [], [], [], []
     for a, a_mate, b, b_mate, before, order in jobs:
-        (rows, left), right = a.shape, b.shape[1]
-        operands += [a, *a_mate, b, *b_mate]
+        (rows, left), right = a.shape, b[0].shape[1]
+        operands += [a, *a_mate, *b, *b_mate]
         befores += [] if before is None else [before]
         outs.append(bf16(1, 2, left, right))
         scratch += [
             pltpu.VMEM((2 * rows, right), jnp.bfloat16),
             pltpu.VMEM((2 * rows, left), jnp.bfloat16),
             pltpu.VMEM((2, min(2 * BLOCK, left), right), jnp.bfloat16),
-            pltpu.VMEM((rows, right), jnp.bfloat16),
+            pltpu.VMEM((2 * rows if order else SLOTS, right), jnp.bfloat16),
         ]
-        settings.append((-0.5 / rows**0.5, order))
+        settings.append((-0.5 / rows**0.5, order, len(b)))
     return pl.pallas_call(
         functools.partial(pair_kernel, level, settings),
         in_specs=[IN_SMEM] + [ANYWHERE] * (len(operands) + len(befores) - 1),
@@ -578,7 +574,8 @@
     else:
         h = [gather_shard(h_spread)]
         along_x(u1_mate)
-        dy_own, du2, dy = high_grad(where, dispatch(pack(none, routes, cotangent, paths, shards)), w_out, True)
+        dy = dispatch(pack(none, routes, cotangent, paths, shards))
+        dy_own, du2, dy = high_grad(where, dy, w_out, True)
     n2, u2, da2, *parts = high_both(where, h, gain, w_in, du2, cubes)
 
     da2_mate, u2_mate = from_mate([da2, u2], mate_high)
@@ -601,17 +598,17 @@
     (n2_mate,) = from_mate([n2], mate_high)
     if cubes:
         (dh_pair,) = from_mate([dh_own], mate_low)
+        dh_own, dh_pair[1] = tie(dh_own, dh_pair[1])
         along_x(dh_pair)
         dh_piece = jnp.where(mate_low == 1, *dh_pair)
         dh, (u2_mate[1], n2_mate[1], dh_piece) = gather_steps(dh_own, u2_mate[1], n2_mate[1], dh_piece)
         along_x(n2_mate)
-        pieces = [swap(dh_piece, "shard", bit) for bit in (4, 2, 6)]
+        pieces = [swap(dh_piece, "shard", bit) for bit in (2, 4, 6)]
         dy_mate = [half, hop_4]
     else:
         along_x(n2_mate)
         dh = [gather_shard(dh_spread)]
-    da1, *dh_ordered = low_grad(where, dh, w_out, slope1, cubes)
-    dh = dh_ordered[0] if cubes else dh[0]
+    da1 = low_grad(where, dh, w_out, slope1, cubes)
 
     if cubes:
         da1, n2_mate[1], *pieces = tie(da1, n2_mate[1], *pieces)
@@ -621,20 +618,20 @@
         dh_half = join(dh_piece, *pieces)
         dh_mate = [dh_half, swap(dh_half, "shard", 1)]
     else:
-        (dh_mate,) = from_mate([dh], mate_low)
+        (dh_mate,) = from_mate(dh, mate_low)
         along_x(dh_mate)
         (dy_mate,) = from_mate([dy], mate_high)
         along_x(dy_mate)
     delta_in, delta_out = pair_grads(
         where,
         1,
-        (n2, n2_mate, da2, da2_mate, None, ""),
-        (u2, u2_mate, dy, dy_mate, None, "dispatch" if cubes else ""),
+        (n2, n2_mate, [da2], da2_mate, None, ""),
+        (u2, u2_mate, [dy], dy_mate, None, "dispatch" if cubes else ""),
     )
     delta_in, delta_out = pair_grads(
         where,
         0,
-        (n1, n1_mate, da1, da1_mate, delta_in, ""),
+        (n1, n1_mate, [da1], da1_mate, delta_in, ""),
         (u1, u1_mate, dh, dh_mate, delta_out, "gather" if cubes else ""),
     )
     return (delta_in, delta_out)

time: 148 us -> 146 us (0.986)
  waiting for transfers between devices: 43.9 us -> 42.4 us
    unnamed x56 -> x58, local copies, waits for them, and re-layouts: 3.11 us -> 2.32 us
  transfers between devices with their start and end apart: 44 -> 44, of which waited for: 16 -> 18; matrix products, arithmetic and copies ran while one was open for 4% -> 3% of each run, Pallas kernels for 14% -> 14%
where the time goes in v5:
time: 146 us; the launch traced here: 145 us
  starting transfers between devices  52.3 us (36%)
  waiting for transfers between devices  42.4 us (29%)
  Pallas kernels  41 us (28%)
  local copies, waits for them, and re-layouts  3.84 us (3%)
  other arithmetic  2.9 us (2%)
  between operations  2.68 us (2%)
    ppermute x43, starting transfers between devices, swap(): lax.ppermute(value, axis, [(i, i ^ bit) for i in range(lax.axis_size(axis...  45 us
    ppermute x43, waiting for transfers between devices, swap(): lax.ppermute(value, axis, [(i, i ^ bit) for i in range(lax.axis_size(axis...  35.2 us
    pallas_call x4, Pallas kernels, stream(): pl.pallas_call(kernel, in_specs=[IN_SMEM] * len(operands) + [IN_VMEM] * l...  20.6 us
    pallas_call x2, Pallas kernels, pair_grads(): pl.pallas_call(functools.partial(pair_kernel, level, settings), in_specs=...  15.2 us
    all_to_all x1, starting transfers between devices, dispatch(): lax.all_to_all(spread, ('path', 'shard'), split_axis=0, concat_axis=0, ti...  7.3 us
    all_to_all x1, waiting for transfers between devices, dispatch(): lax.all_to_all(spread, ('path', 'shard'), split_axis=0, concat_axis=0, ti...  7.17 us
    pallas_call x2, Pallas kernels, pack(): pl.pallas_call(functools.partial(pack_kernel, copies), in_specs=[IN_SMEM,...  3.54 us
  transfers between devices with their start and end apart: 44, of which 18 were waited for; matrix products, arithmetic and copies ran while one was open for 3% of the time, Pallas kernels for 14%

profile of v5, /device:TPU:0, one launch (start us, length us, event | category | flops | bytes accessed | tf_op | source)
XLA Modules:
  0.0 145.1 jit_solution(11704439853796040733)
XLA Ops:
  0.6 1.9 %pack.2 = bf16[32,4,2048]{2,1,0:T(4,128)(2,1)} custom-call(s32[1]{0:T(128)} %constant.7.clone.1.flip_ref, s32[12]{0:T(128)} %bitcast.11, bf16[12,2048]{1,0:T(8,128)(2,1)} %rows_ref.2), custom_call_target="tpu_custom_call" | custom-call | tf_op jit(solution)/shard_map/pack/pallas_call | solution.py:123
  2.5 7.3 %all-to-all-start = ((bf16[32,4,2048]{2,1,0:T(4,128)(2,1)}), bf16[32,4,2048]{2,1,0:T(4,128)(2,1)S(1)}, u32[]{:S(2)}, u32[]{:S(2)}) async-start(bf16[32,4,2048]{2,1,0:T(4,128)(2,1)} %pack.2), calls=%async_computation | async-start | bytes 1048576 | tf_op jit(solution)/shard_map/all_to_all | solution.py:473
  9.8 1.7 %pack.3 = (bf16[4,2048]{1,0:T(4,128)(2,1)}, bf16[4,2048]{1,0:T(4,128)(2,1)}, bf16[4,2048]{1,0:T(4,128)(2,1)}, bf16[4,2048]{1,0:T(4,128)(2,1)}) custom-call(s32[1]{0:T(128)} %bitcast.1.flip_ref, s32[12]{0:T(128)} %bitcast.12, bf16[12,2048]{1,0:T(8,128)(2,1)} %rows_ref.3), custom_call_target="tpu_custom_call" | custom-call | tf_op jit(solution)/shard_map/pack/pallas_call | solution.py:123
  11.7 1.7 %collective-permute-start.1 = (bf16[4,2048]{1,0:T(4,128)(2,1)}, bf16[4,2048]{1,0:T(4,128)(2,1)S(1)}, u32[]{:S(2)}, u32[]{:S(2)}) collective-permute-start(bf16[4,2048]{1,0:T(4,128)(2,1)} %get-tuple-element.80), channel_id=1, source_target_pairs={{0,16},{8,24},{16,0},{24,8},{1,17},{9,25},{17,1},{25,9},{2,18},{10... | collective-permute-start | bytes 49160 | tf_op jit(solution)/shard_map/ppermute | solution.py:489
  13.4 1.4 constant_dynamic-slice_fusion.1
  17.6 2.7 %collective-permute-start.3 = (bf16[16,2048]{1,0:T(8,128)(2,1)S(1)}, bf16[16,2048]{1,0:T(8,128)(2,1)S(1)}, u32[]{:S(2)}, u32[]{:S(2)}) collective-permute-start(bf16[16,2048]{1,0:T(8,128)(2,1)S(1)} %pad_maximum_fusion.6), channel_id=1, source_target_pairs={{0,4},{1,5},{2,6},{3,7},{4,0},{5,1},{6,2},{7,3},{8,12},{9,13},{10,... | collective-permute-start | bytes 196616 | tf_op jit(solution)/shard_map/ppermute | solution.py:489
  20.4 7.2 %all-to-all-done = bf16[32,4,2048]{2,1,0:T(4,128)(2,1)S(1)} async-done(((bf16[32,4,2048]{2,1,0:T(4,128)(2,1)}), bf16[32,4,2048]{2,1,0:T(4,128)(2,1)S(1)}, u32[]{:S(2)}, u32[]{:S(2)}) %all-to-all-start) | async-done | bytes 524320 | tf_op jit(solution)/shard_map/all_to_all | solution.py:473
  28.4 6.1 %low_forward.1 = (bf16[128,2048]{1,0:T(8,128)(2,1)S(1)}, bf16[128,1024]{1,0:T(8,128)(2,1)S(1)}, f32[128,1024]{1,0:T(8,128)S(1)}, bf16[16,2048]{1,0:T(8,128)(2,1)...) custom-call(s32[4]{0:T(128)S(1)} %pad_add_fusion.where_ref, ...), custom_call_target="tpu_custom_call" | custom-call | tf_op jit(solution)/shard_map/low_forward/pallas_call | solution.py:57
  34.7 0.9 collective-permute-start.6
  36.5 0.9 broadcast_select_fusion.1
  37.5 3.2 %collective-permute-done.6 = bf16[32,2048]{1,0:T(8,128)(2,1)S(1)} collective-permute-done((bf16[32,2048]{1,0:T(8,128)(2,1)S(1)}, bf16[32,2048]{1,0:T(8,128)(2,1)S(1)}, u32[]{:S(2)}, u32[]{:S(2)}) %collective-permute-start.6) | collective-permute-done | bytes 131104 | tf_op jit(solution)/shard_map/ppermute | solution.py:489
  40.6 3.3 %collective-permute-done.5.got_ref = bf16[4,16,2048]{2,1,0:T(8,128)(2,1)S(1)} collective-permute-done((bf16[4,16,2048]{2,1,0:T(8,128)(2,1)S(1)}, bf16[4,16,2048]{2,1,0:T(8,128)(2,1)S(1)}, u32[]{:S(2)}, u32[]{:S(2)}) %collective-permute-start.5) | collective-permute-done | bytes 262176 | tf_op jit(solution)/shard_map/ppermute | solution.py:489
  44.6 1.3 collective-permute-start.7
  45.9 1.5 %collective-permute-start.10 = (bf16[64,2048]{1,0:T(8,128)(2,1)S(1)}, bf16[64,2048]{1,0:T(8,128)(2,1)S(1)}, u32[]{:S(2)}, u32[]{:S(2)}) collective-permute-start(bf16[64,2048]{1,0:T(8,128)(2,1)S(1)} %pad_maximum_fusion.1), channel_id=1, source_target_pairs={{0,1},{1,0},{2,3},{3,2},{4,5},{5,4},{6,7},{7,6},{8,9},{9,8},{10,11... | collective-permute-start | bytes 786440 | tf_op jit(solution)/shard_map/ppermute | solution.py:489
  47.7 2.4 %collective-permute-start.9 = (bf16[16,2048]{1,0:T(8,128)(2,1)S(1)}, bf16[16,2048]{1,0:T(8,128)(2,1)S(1)}, u32[]{:S(2)}, u32[]{:S(2)}) collective-permute-start(bf16[16,2048]{1,0:T(8,128)(2,1)S(1)} %get-tuple-element.94), channel_id=1, source_target_pairs={{0,6},{1,7},{2,4},{3,5},{4,2},{5,3},{6,0},{7,1},{8,14},{9,15},{10,... | collective-permute-start | bytes 196616 | tf_op jit(solution)/shard_map/ppermute | solution.py:489
  50.1 1.5 %collective-permute-start.14 = (bf16[128,2048]{1,0:T(8,128)(2,1)}, bf16[128,2048]{1,0:T(8,128)(2,1)S(1)}, u32[]{:S(2)}, u32[]{:S(2)}) collective-permute-start(bf16[128,2048]{1,0:T(8,128)(2,1)} %broadcast_select_fusion.1), channel_id=1, source_target_pairs={{0,16},{8,24},{16,0},{24,8},{1,17},{9,25},{17,1},{25,9},{2,18},{10... | collective-permute-start | bytes 1572872 | tf_op jit(solution)/shard_map/ppermute | solution.py:489
  51.6 3.8 %collective-permute-done.8.rest_1_ = bf16[16,2048]{1,0:T(8,128)(2,1)S(1)} collective-permute-done((bf16[16,2048]{1,0:T(8,128)(2,1)S(1)}, bf16[16,2048]{1,0:T(8,128)(2,1)S(1)}, u32[]{:S(2)}, u32[]{:S(2)}) %collective-permute-start.8) | collective-permute-done | bytes 65568 | tf_op jit(solution)/shard_map/ppermute | solution.py:489
  55.5 1.5 %collective-permute-start.13 = (bf16[16,2048]{1,0:T(8,128)(2,1)S(1)}, bf16[16,2048]{1,0:T(8,128)(2,1)S(1)}, u32[]{:S(2)}, u32[]{:S(2)}) collective-permute-start(bf16[16,2048]{1,0:T(8,128)(2,1)S(1)} %last_sums.1.h_ref), channel_id=1, source_target_pairs={{0,6},{1,7},{2,4},{3,5},{4,2},{5,3},{6,0},{7,1},{8,14},{9,15},{10,... | collective-permute-start | bytes 196616 | tf_op jit(solution)/shard_map/ppermute | solution.py:489
  57.0 1.9 %collective-permute-start.12 = (bf16[16,2048]{1,0:T(8,128)(2,1)S(1)}, bf16[16,2048]{1,0:T(8,128)(2,1)S(1)}, u32[]{:S(2)}, u32[]{:S(2)}) collective-permute-start(bf16[16,2048]{1,0:T(8,128)(2,1)S(1)} %last_sums.1.h_ref), channel_id=1, source_target_pairs={{0,4},{1,5},{2,6},{3,7},{4,0},{5,1},{6,2},{7,3},{8,12},{9,13},{10,... | collective-permute-start | bytes 196616 | tf_op jit(solution)/shard_map/ppermute | solution.py:489
  58.9 1.0 collective-permute-start.11
  60.7 1.6 %collective-permute-done.13 = bf16[16,2048]{1,0:T(8,128)(2,1)S(1)} collective-permute-done((bf16[16,2048]{1,0:T(8,128)(2,1)S(1)}, bf16[16,2048]{1,0:T(8,128)(2,1)S(1)}, u32[]{:S(2)}, u32[]{:S(2)}) %collective-permute-start.13) | collective-permute-done | bytes 65568 | tf_op jit(solution)/shard_map/ppermute | solution.py:489
  62.3 2.9 %collective-permute-done.12 = bf16[16,2048]{1,0:T(8,128)(2,1)S(1)} collective-permute-done((bf16[16,2048]{1,0:T(8,128)(2,1)S(1)}, bf16[16,2048]{1,0:T(8,128)(2,1)S(1)}, u32[]{:S(2)}, u32[]{:S(2)}) %collective-permute-start.12) | collective-permute-done | bytes 65568 | tf_op jit(solution)/shard_map/ppermute | solution.py:489
  65.8 1.5 %collective-permute-start.18 = (bf16[128,1024]{1,0:T(8,128)(2,1)S(1)}, bf16[128,1024]{1,0:T(8,128)(2,1)S(1)}, u32[]{:S(2)}, u32[]{:S(2)}) collective-permute-start(bf16[128,1024]{1,0:T(8,128)(2,1)S(1)} %broadcast_select_fusion.7), channel_id=1, source_target_pairs={{0,16},{8,24},{16,0},{24,8},{1,17},{9,25},{17,1},{25,9},{2,18},{10... | collective-permute-start | bytes 786440 | tf_op jit(solution)/shard_map/ppermute | solution.py:489
  67.3 4.6 %high_grad.1 = (bf16[16,2048]{1,0:T(8,128)(2,1)S(1)}, f32[128,1024]{1,0:T(8,128)S(1)}, bf16[128,2048]{1,0:T(8,128)(2,1)S(1)}) custom-call(s32[4]{0:T(128)S(1)} %pad_add_fusion.where_ref, bf16[128,2048]{1,0:T(8,128)(2,1)S(1)} %pad_maximum_fusion.raw_ref, bf16[1,2,1024,2048]{3,2,1,0:T(8,128)(2,1)} %refs_3_.1), custom_call_target="tpu_custom_call" | custom-call | tf_op jit(solution)/shard_map/high_grad/pallas_call | solution.py:57
  73.3 5.3 %high_both.1 = (bf16[128,2048]{1,0:T(8,128)(2,1)S(1)}, bf16[128,1024]{1,0:T(8,128)(2,1)S(1)}, bf16[128,1024]{1,0:T(8,128)(2,1)S(1)}, bf16[4,16,2048]{2,1,0:T(8,128)(2,1)S(1)}, bf16[4,16,2048]{2,1,0:T(8,128)(2,1)S(1)}) custom-call(s32[4]{0:T(128)S(1)} %pad_add_fusion.where_ref, bf16[64,2048]{1,0:T(8,128)(2,1)S(1)} %pad_maximum_fusion.2.refs_0_, ...), custom_call_target="tpu_custom_call" | custom-call | tf_op jit(solution)/shard_map/high_both/pallas_call | solution.py:57
  78.8 1.6 %collective-permute-start.21 = (bf16[64,2048]{1,0:T(8,128)(2,1)}, bf16[64,2048]{1,0:T(8,128)(2,1)S(1)}, u32[]{:S(2)}, u32[]{:S(2)}) collective-permute-start(bf16[64,2048]{1,0:T(8,128)(2,1)} %broadcast_select_fusion.5), channel_id=1, source_target_pairs={{0,16},{8,24},{16,0},{24,8},{1,17},{9,25},{17,1},{25,9},{2,18},{10... | collective-permute-start | bytes 786440 | tf_op jit(solution)/shard_map/ppermute | solution.py:489
  80.4 1.5 %collective-permute-start.19 = (bf16[4,16,2048]{2,1,0:T(8,128)(2,1)S(1)}, bf16[4,16,2048]{2,1,0:T(8,128)(2,1)S(1)}, u32[]{:S(2)}, u32[]{:S(2)}) collective-permute-start(bf16[4,16,2048]{2,1,0:T(8,128)(2,1)S(1)} %get-tuple-element.116), channel_id=1, source_target_pairs={{0,1},{1,0},{2,3},{3,2},{4,5},{5,4},{6,7},{7,6},{8,9},{9,8},{10,11... | collective-permute-start | bytes 786440 | tf_op jit(solution)/shard_map/ppermute | solution.py:489
  81.9 5.8 %collective-permute-done.21 = bf16[64,2048]{1,0:T(8,128)(2,1)S(1)} collective-permute-done((bf16[64,2048]{1,0:T(8,128)(2,1)}, bf16[64,2048]{1,0:T(8,128)(2,1)S(1)}, u32[]{:S(2)}, u32[]{:S(2)}) %collective-permute-start.21) | collective-permute-done | bytes 262176 | tf_op jit(solution)/shard_map/ppermute | solution.py:489
  87.7 1.0 collective-permute-done.19.got_ref
  89.5 1.6 %collective-permute-start.25 = (bf16[64,2048]{1,0:T(8,128)(2,1)S(1)}, bf16[64,2048]{1,0:T(8,128)(2,1)S(1)}, u32[]{:S(2)}, u32[]{:S(2)}) collective-permute-start(bf16[64,2048]{1,0:T(8,128)(2,1)S(1)} %broadcast_select_fusion.2.refs_10_), channel_id=1, source_target_pairs={{0,1},{1,0},{2,3},{3,2},{4,5},{5,4},{6,7},{7,6},{8,9},{9,8},{10,11... | collective-permute-start | bytes 786440 | tf_op jit(solution)/shard_map/ppermute | solution.py:489
  91.7 2.0 %collective-permute-start.23 = (bf16[16,2048]{1,0:T(8,128)(2,1)S(1)}, bf16[16,2048]{1,0:T(8,128)(2,1)S(1)}, u32[]{:S(2)}, u32[]{:S(2)}) collective-permute-start(bf16[16,2048]{1,0:T(8,128)(2,1)S(1)} %get-tuple-element.122), channel_id=1, source_target_pairs={{0,4},{1,5},{2,6},{3,7},{4,0},{5,1},{6,2},{7,3},{8,12},{9,13},{10,... | collective-permute-start | bytes 196616 | tf_op jit(solution)/shard_map/ppermute | solution.py:489
  93.7 2.4 %collective-permute-start.24 = (bf16[16,2048]{1,0:T(8,128)(2,1)S(1)}, bf16[16,2048]{1,0:T(8,128)(2,1)S(1)}, u32[]{:S(2)}, u32[]{:S(2)}) collective-permute-start(bf16[16,2048]{1,0:T(8,128)(2,1)S(1)} %get-tuple-element.123), channel_id=1, source_target_pairs={{0,6},{1,7},{2,4},{3,5},{4,2},{5,3},{6,0},{7,1},{8,14},{9,15},{10,... | collective-permute-start | bytes 196616 | tf_op jit(solution)/shard_map/ppermute | solution.py:489
  96.2 4.2 %collective-permute-done.23.rest_1_ = bf16[16,2048]{1,0:T(8,128)(2,1)S(1)} collective-permute-done((bf16[16,2048]{1,0:T(8,128)(2,1)S(1)}, bf16[16,2048]{1,0:T(8,128)(2,1)S(1)}, u32[]{:S(2)}, u32[]{:S(2)}) %collective-permute-start.23) | collective-permute-done | bytes 65568 | tf_op jit(solution)/shard_map/ppermute | solution.py:489
  100.7 1.5 %collective-permute-start.32 = (bf16[128,1024]{1,0:T(8,128)(2,1)S(1)}, bf16[128,1024]{1,0:T(8,128)(2,1)S(1)}, u32[]{:S(2)}, u32[]{:S(2)}) collective-permute-start(bf16[128,1024]{1,0:T(8,128)(2,1)S(1)} %broadcast_select_fusion.3), channel_id=1, source_target_pairs={{0,16},{8,24},{16,0},{24,8},{1,17},{9,25},{17,1},{25,9},{2,18},{10... | collective-permute-start | bytes 786440 | tf_op jit(solution)/shard_map/ppermute | solution.py:489
  102.3 1.2 collective-permute-start.34
  103.6 1.9 %collective-permute-start.31 = (bf16[16,2048]{1,0:T(8,128)(2,1)S(1)}, bf16[16,2048]{1,0:T(8,128)(2,1)S(1)}, u32[]{:S(2)}, u32[]{:S(2)}) collective-permute-start(bf16[16,2048]{1,0:T(8,128)(2,1)S(1)} %last_back.1), channel_id=1, source_target_pairs={{0,6},{1,7},{2,4},{3,5},{4,2},{5,3},{6,0},{7,1},{8,14},{9,15},{10,... | collective-permute-start | bytes 196616 | tf_op jit(solution)/shard_map/ppermute | solution.py:489
  105.5 1.1 collective-permute-start.30
  106.6 1.4 collective-permute-start.29
  108.0 2.8 %collective-permute-done.34 = bf16[16,2048]{1,0:T(8,128)(2,1)S(1)} collective-permute-done((bf16[16,2048]{1,0:T(8,128)(2,1)S(1)}, bf16[16,2048]{1,0:T(8,128)(2,1)S(1)}, u32[]{:S(2)}, u32[]{:S(2)}) %collective-permute-start.34) | collective-permute-done | bytes 65568 | tf_op jit(solution)/shard_map/ppermute | solution.py:489
  110.9 2.0 %collective-permute-done.30 = bf16[16,2048]{1,0:T(8,128)(2,1)S(1)} collective-permute-done((bf16[16,2048]{1,0:T(8,128)(2,1)S(1)}, bf16[16,2048]{1,0:T(8,128)(2,1)S(1)}, u32[]{:S(2)}, u32[]{:S(2)}) %collective-permute-start.30) | collective-permute-done | bytes 65568 | tf_op jit(solution)/shard_map/ppermute | solution.py:489
  112.8 0.9 collective-permute-start.36
  114.6 1.6 %collective-permute-start.39 = (bf16[16,2048]{1,0:T(8,128)(2,1)S(1)}, bf16[16,2048]{1,0:T(8,128)(2,1)S(1)}, u32[]{:S(2)}, u32[]{:S(2)}) collective-permute-start(bf16[16,2048]{1,0:T(8,128)(2,1)S(1)} %broadcast_select_fusion.8), channel_id=1, source_target_pairs={{0,6},{1,7},{2,4},{3,5},{4,2},{5,3},{6,0},{7,1},{8,14},{9,15},{10,... | collective-permute-start | bytes 196616 | tf_op jit(solution)/shard_map/ppermute | solution.py:489
  116.2 2.7 %collective-permute-start.37 = (bf16[16,2048]{1,0:T(8,128)(2,1)S(1)}, bf16[16,2048]{1,0:T(8,128)(2,1)S(1)}, u32[]{:S(2)}, u32[]{:S(2)}) collective-permute-start(bf16[16,2048]{1,0:T(8,128)(2,1)S(1)} %broadcast_select_fusion.8), channel_id=1, source_target_pairs={{0,2},{1,3},{2,0},{3,1},{4,6},{5,7},{6,4},{7,5},{8,10},{9,11},{10,... | collective-permute-start | bytes 196616 | tf_op jit(solution)/shard_map/ppermute | solution.py:489
  119.0 2.3 %collective-permute-done.35.refs_1_.refs_10_ = bf16[64,2048]{1,0:T(8,128)(2,1)S(1)} collective-permute-done((bf16[64,2048]{1,0:T(8,128)(2,1)S(1)}, bf16[64,2048]{1,0:T(8,128)(2,1)S(1)}, u32[]{:S(2)}, u32[]{:S(2)}) %collective-permute-start.35) | collective-permute-done | bytes 262176 | tf_op jit(solution)/shard_map/ppermute | solution.py:489
  121.2 4.6 %low_grad.1.refs_3_ = bf16[128,1024]{1,0:T(8,128)(2,1)S(1)} custom-call(s32[4]{0:T(128)S(1)} %pad_add_fusion.where_ref, bf16[64,2048]{1,0:T(8,128)(2,1)S(1)} %pad_maximum_fusion.3.refs_0_.refs_9_, bf16[64,2048]{1,0:T(8,128)(2,1)S(1)} %collective-permute-done.35.refs_1_.refs_10_, f32[128,1024]{1,0:T(8,128)S(1)} %get-tuple-element.139.refs_2_, ...), custom_call_target="tpu_custom_call" | custom-call | tf_op jit(solution)/shard_map/low_grad/pallas_call | solution.py:57
  127.8 1.1 collective-permute-start.41
  128.9 7.4 %pair_grads.2 = (bf16[1,2,2048,1024]{3,2,1,0:T(8,128)(2,1)}, bf16[1,2,1024,2048]{3,2,1,0:T(8,128)(2,1)}) custom-call(s32[4]{0:T(128)} %copy-done.11, bf16[128,2048]{1,0:T(8,128)(2,1)} %copy-done.3, bf16[128,2048]{1,0:T(8,128)(2,1)} %copy-done.13, bf16[128,2048]{1,0:T(8,128)(2,1)} %copy-done.22, bf16[128,1024]{1,0:T(8,128)(2,1)} %copy-done.7, ...), custom_call_target="tpu_custom_call" | custom-call | tf_op jit(solution)/shard_map/pair_grads/pallas_call | solution.py:459
  137.2 7.8 %pair_grads.3 = (bf16[1,2,2048,1024]{3,2,1,0:T(8,128)(2,1)}, bf16[1,2,1024,2048]{3,2,1,0:T(8,128)(2,1)}) custom-call(s32[4]{0:T(128)} %copy-done.11, bf16[128,2048]{1,0:T(8,128)(2,1)} %copy-done.2, bf16[128,2048]{1,0:T(8,128)(2,1)} %copy-done.12, bf16[128,2048]{1,0:T(8,128)(2,1)} %copy-done.21, ...), custom_call_target="tpu_custom_call", output_to_operand_aliasing={{0}: (14, {}), {1}: (15, {})} | custom-call | tf_op jit(solution)/shard_map/pair_grads/pallas_call | solution.py:459
  (130 shorter events, 12.8 us)
Async XLA Ops:
  2.5 25.1 %all-to-all-start = ((bf16[32,4,2048]{2,1,0:T(4,128)(2,1)}), bf16[32,4,2048]{2,1,0:T(4,128)(2,1)S(1)}, u32[]{:S(2)}, u32[]{:S(2)}) async-start(bf16[32,4,2048]{2,1,0:T(4,128)(2,1)} %pack.2), calls=%async_computation | async-start | bytes 1048576 | tf_op jit(solution)/shard_map/all_to_all | solution.py:473
  11.5 4.6 %collective-permute-start = (bf16[4,2048]{1,0:T(4,128)(2,1)}, bf16[4,2048]{1,0:T(4,128)(2,1)S(1)}, u32[]{:S(2)}, u32[]{:S(2)}) collective-permute-start(bf16[4,2048]{1,0:T(4,128)(2,1)} %get-tuple-element.79), channel_id=1, source_target_pairs={{0,8},{8,0},{16,24},{24,16},{1,9},{9,1},{17,25},{25,17},{2,10},{10... | collective-permute-start | bytes 49160 | tf_op jit(solution)/shard_map/ppermute | solution.py:489
  11.7 4.4 %collective-permute-start.1 = (bf16[4,2048]{1,0:T(4,128)(2,1)}, bf16[4,2048]{1,0:T(4,128)(2,1)S(1)}, u32[]{:S(2)}, u32[]{:S(2)}) collective-permute-start(bf16[4,2048]{1,0:T(4,128)(2,1)} %get-tuple-element.80), channel_id=1, source_target_pairs={{0,16},{8,24},{16,0},{24,8},{1,17},{9,25},{17,1},{25,9},{2,18},{10... | collective-permute-start | bytes 49160 | tf_op jit(solution)/shard_map/ppermute | solution.py:489
  13.4 3.4 %collective-permute-start.2 = (bf16[4,2048]{1,0:T(4,128)(2,1)}, bf16[4,2048]{1,0:T(4,128)(2,1)S(1)}, u32[]{:S(2)}, u32[]{:S(2)}) collective-permute-start(bf16[4,2048]{1,0:T(4,128)(2,1)} %get-tuple-element.81), channel_id=1, source_target_pairs={{0,24},{8,16},{16,8},{24,0},{1,25},{9,17},{17,9},{25,1},{2,26},{10... | collective-permute-start | bytes 49160 | tf_op jit(solution)/shard_map/ppermute | solution.py:489
  17.6 10.1 %collective-permute-start.3 = (bf16[16,2048]{1,0:T(8,128)(2,1)S(1)}, bf16[16,2048]{1,0:T(8,128)(2,1)S(1)}, u32[]{:S(2)}, u32[]{:S(2)}) collective-permute-start(bf16[16,2048]{1,0:T(8,128)(2,1)S(1)} %pad_maximum_fusion.6), channel_id=1, source_target_pairs={{0,4},{1,5},{2,6},{3,7},{4,0},{5,1},{6,2},{7,3},{8,12},{9,13},{10,... | collective-permute-start | bytes 196616 | tf_op jit(solution)/shard_map/ppermute | solution.py:489
  20.4 100.9 %copy-start.11 = (s32[4]{0:T(128)}, s32[4]{0:T(128)S(1)}, u32[]{:S(2)}) copy-start(s32[4]{0:T(128)S(1)} %pad_add_fusion.where_ref) | copy-start | bytes 52
  34.5 2.0 %collective-permute-start.4 = (bf16[128,2048]{1,0:T(8,128)(2,1)S(1)}, bf16[128,2048]{1,0:T(8,128)(2,1)S(1)}, u32[]{:S(2)}, u32[]{:S(2)}) collective-permute-start(bf16[128,2048]{1,0:T(8,128)(2,1)S(1)} %get-tuple-element.84.refs_0_), channel_id=1, source_target_pairs={{0,8},{8,0},{16,24},{24,16},{1,9},{9,1},{17,25},{25,17},{2,10},{10... | collective-permute-start | bytes 1572872 | tf_op jit(solution)/shard_map/ppermute | solution.py:489
  34.7 5.9 %collective-permute-start.6 = (bf16[32,2048]{1,0:T(8,128)(2,1)S(1)}, bf16[32,2048]{1,0:T(8,128)(2,1)S(1)}, u32[]{:S(2)}, u32[]{:S(2)}) collective-permute-start(bf16[32,2048]{1,0:T(8,128)(2,1)S(1)} %pad_maximum_fusion.5), channel_id=1, source_target_pairs={{0,2},{1,3},{2,0},{3,1},{4,6},{5,7},{6,4},{7,5},{8,10},{9,11},{10,... | collective-permute-start | bytes 393224 | tf_op jit(solution)/shard_map/ppermute | solution.py:489
  35.7 8.3 %collective-permute-start.5 = (bf16[4,16,2048]{2,1,0:T(8,128)(2,1)S(1)}, bf16[4,16,2048]{2,1,0:T(8,128)(2,1)S(1)}, u32[]{:S(2)}, u32[]{:S(2)}) collective-permute-start(bf16[4,16,2048]{2,1,0:T(8,128)(2,1)S(1)} %get-tuple-element.87), channel_id=1, source_target_pairs={{0,1},{1,0},{2,3},{3,2},{4,5},{5,4},{6,7},{7,6},{8,9},{9,8},{10,11... | collective-permute-start | bytes 786440 | tf_op jit(solution)/shard_map/ppermute | solution.py:489
  36.2 11.5 %collective-permute-start.15 = (bf16[128,1024]{1,0:T(8,128)(2,1)S(1)}, bf16[128,1024]{1,0:T(8,128)(2,1)S(1)}, u32[]{:S(2)}, u32[]{:S(2)}) collective-permute-start(bf16[128,1024]{1,0:T(8,128)(2,1)S(1)} %get-tuple-element.101.refs_6_), channel_id=1, source_target_pairs={{0,8},{8,0},{16,24},{24,16},{1,9},{9,1},{17,25},{25,17},{2,10},{10... | collective-permute-start | bytes 786440 | tf_op jit(solution)/shard_map/ppermute | solution.py:489
  44.6 5.5 %collective-permute-start.7 = (bf16[16,2048]{1,0:T(8,128)(2,1)S(1)}, bf16[16,2048]{1,0:T(8,128)(2,1)S(1)}, u32[]{:S(2)}, u32[]{:S(2)}) collective-permute-start(bf16[16,2048]{1,0:T(8,128)(2,1)S(1)} %get-tuple-element.92), channel_id=1, source_target_pairs={{0,2},{1,3},{2,0},{3,1},{4,6},{5,7},{6,4},{7,5},{8,10},{9,11},{10,... | collective-permute-start | bytes 196616 | tf_op jit(solution)/shard_map/ppermute | solution.py:489
  45.9 9.5 %collective-permute-start.10 = (bf16[64,2048]{1,0:T(8,128)(2,1)S(1)}, bf16[64,2048]{1,0:T(8,128)(2,1)S(1)}, u32[]{:S(2)}, u32[]{:S(2)}) collective-permute-start(bf16[64,2048]{1,0:T(8,128)(2,1)S(1)} %pad_maximum_fusion.1), channel_id=1, source_target_pairs={{0,1},{1,0},{2,3},{3,2},{4,5},{5,4},{6,7},{7,6},{8,9},{9,8},{10,11... | collective-permute-start | bytes 786440 | tf_op jit(solution)/shard_map/ppermute | solution.py:489
  47.4 12.6 %collective-permute-start.16 = (bf16[64,2048]{1,0:T(8,128)(2,1)S(1)}, bf16[64,2048]{1,0:T(8,128)(2,1)S(1)}, u32[]{:S(2)}, u32[]{:S(2)}) collective-permute-start(bf16[64,2048]{1,0:T(8,128)(2,1)S(1)} %pad_maximum_fusion.1), channel_id=1, source_target_pairs={{0,8},{8,0},{16,24},{24,16},{1,9},{9,1},{17,25},{25,17},{2,10},{10... | collective-permute-start | bytes 786440 | tf_op jit(solution)/shard_map/ppermute | solution.py:489
  47.4 8.0 %collective-permute-start.8 = (bf16[16,2048]{1,0:T(8,128)(2,1)S(1)}, bf16[16,2048]{1,0:T(8,128)(2,1)S(1)}, u32[]{:S(2)}, u32[]{:S(2)}) collective-permute-start(bf16[16,2048]{1,0:T(8,128)(2,1)S(1)} %get-tuple-element.93), channel_id=1, source_target_pairs={{0,4},{1,5},{2,6},{3,7},{4,0},{5,1},{6,2},{7,3},{8,12},{9,13},{10,... | collective-permute-start | bytes 196616 | tf_op jit(solution)/shard_map/ppermute | solution.py:489
  47.7 7.7 %collective-permute-start.9 = (bf16[16,2048]{1,0:T(8,128)(2,1)S(1)}, bf16[16,2048]{1,0:T(8,128)(2,1)S(1)}, u32[]{:S(2)}, u32[]{:S(2)}) collective-permute-start(bf16[16,2048]{1,0:T(8,128)(2,1)S(1)} %get-tuple-element.94), channel_id=1, source_target_pairs={{0,6},{1,7},{2,4},{3,5},{4,2},{5,3},{6,0},{7,1},{8,14},{9,15},{10,... | collective-permute-start | bytes 196616 | tf_op jit(solution)/shard_map/ppermute | solution.py:489
  50.1 15.1 %collective-permute-start.14 = (bf16[128,2048]{1,0:T(8,128)(2,1)}, bf16[128,2048]{1,0:T(8,128)(2,1)S(1)}, u32[]{:S(2)}, u32[]{:S(2)}) collective-permute-start(bf16[128,2048]{1,0:T(8,128)(2,1)} %broadcast_select_fusion.1), channel_id=1, source_target_pairs={{0,16},{8,24},{16,0},{24,8},{1,17},{9,25},{17,1},{25,9},{2,18},{10... | collective-permute-start | bytes 1572872 | tf_op jit(solution)/shard_map/ppermute | solution.py:489
  55.5 6.8 %collective-permute-start.13 = (bf16[16,2048]{1,0:T(8,128)(2,1)S(1)}, bf16[16,2048]{1,0:T(8,128)(2,1)S(1)}, u32[]{:S(2)}, u32[]{:S(2)}) collective-permute-start(bf16[16,2048]{1,0:T(8,128)(2,1)S(1)} %last_sums.1.h_ref), channel_id=1, source_target_pairs={{0,6},{1,7},{2,4},{3,5},{4,2},{5,3},{6,0},{7,1},{8,14},{9,15},{10,... | collective-permute-start | bytes 196616 | tf_op jit(solution)/shard_map/ppermute | solution.py:489
  57.0 8.2 %collective-permute-start.12 = (bf16[16,2048]{1,0:T(8,128)(2,1)S(1)}, bf16[16,2048]{1,0:T(8,128)(2,1)S(1)}, u32[]{:S(2)}, u32[]{:S(2)}) collective-permute-start(bf16[16,2048]{1,0:T(8,128)(2,1)S(1)} %last_sums.1.h_ref), channel_id=1, source_target_pairs={{0,4},{1,5},{2,6},{3,7},{4,0},{5,1},{6,2},{7,3},{8,12},{9,13},{10,... | collective-permute-start | bytes 196616 | tf_op jit(solution)/shard_map/ppermute | solution.py:489
  58.9 6.3 %collective-permute-start.11 = (bf16[16,2048]{1,0:T(8,128)(2,1)S(1)}, bf16[16,2048]{1,0:T(8,128)(2,1)S(1)}, u32[]{:S(2)}, u32[]{:S(2)}) collective-permute-start(bf16[16,2048]{1,0:T(8,128)(2,1)S(1)} %last_sums.1.h_ref), channel_id=1, source_target_pairs={{0,2},{1,3},{2,0},{3,1},{4,6},{5,7},{6,4},{7,5},{8,10},{9,11},{10,... | collective-permute-start | bytes 196616 | tf_op jit(solution)/shard_map/ppermute | solution.py:489
  65.2 7.9 %collective-permute-start.17 = (bf16[64,2048]{1,0:T(8,128)(2,1)S(1)}, bf16[64,2048]{1,0:T(8,128)(2,1)S(1)}, u32[]{:S(2)}, u32[]{:S(2)}) collective-permute-start(bf16[64,2048]{1,0:T(8,128)(2,1)S(1)} %pad_maximum_fusion.2.refs_0_), channel_id=1, source_target_pairs={{0,1},{1,0},{2,3},{3,2},{4,5},{5,4},{6,7},{7,6},{8,9},{9,8},{10,11... | collective-permute-start | bytes 786440 | tf_op jit(solution)/shard_map/ppermute | solution.py:489
  65.8 7.5 %collective-permute-start.18 = (bf16[128,1024]{1,0:T(8,128)(2,1)S(1)}, bf16[128,1024]{1,0:T(8,128)(2,1)S(1)}, u32[]{:S(2)}, u32[]{:S(2)}) collective-permute-start(bf16[128,1024]{1,0:T(8,128)(2,1)S(1)} %broadcast_select_fusion.7), channel_id=1, source_target_pairs={{0,16},{8,24},{16,0},{24,8},{1,17},{9,25},{17,1},{25,9},{2,18},{10... | collective-permute-start | bytes 786440 | tf_op jit(solution)/shard_map/ppermute | solution.py:489
  78.7 49.1 %copy-start.3 = (bf16[128,2048]{1,0:T(8,128)(2,1)}, bf16[128,2048]{1,0:T(8,128)(2,1)S(1)}, u32[]{:S(2)}) copy-start(bf16[128,2048]{1,0:T(8,128)(2,1)S(1)} %get-tuple-element.133.refs_0_) | copy-start | bytes 1572868
  78.7 49.1 %copy-start.6 = (bf16[128,1024]{1,0:T(8,128)(2,1)}, bf16[128,1024]{1,0:T(8,128)(2,1)S(1)}, u32[]{:S(2)}) copy-start(bf16[128,1024]{1,0:T(8,128)(2,1)S(1)} %get-tuple-element.127.refs_6_) | copy-start | bytes 786436
  78.7 49.1 %copy-start.7 = (bf16[128,1024]{1,0:T(8,128)(2,1)}, bf16[128,1024]{1,0:T(8,128)(2,1)S(1)}, u32[]{:S(2)}) copy-start(bf16[128,1024]{1,0:T(8,128)(2,1)S(1)} %get-tuple-element.117.refs_3_) | copy-start | bytes 786436
  78.7 3.2 %collective-permute-start.20 = (bf16[128,1024]{1,0:T(8,128)(2,1)S(1)}, bf16[128,1024]{1,0:T(8,128)(2,1)S(1)}, u32[]{:S(2)}, u32[]{:S(2)}) collective-permute-start(bf16[128,1024]{1,0:T(8,128)(2,1)S(1)} %get-tuple-element.117.refs_3_), channel_id=1, source_target_pairs={{0,8},{8,0},{16,24},{24,16},{1,9},{9,1},{17,25},{25,17},{2,10},{10... | collective-permute-start | bytes 786440 | tf_op jit(solution)/shard_map/ppermute | solution.py:489
  78.8 8.9 %collective-permute-start.21 = (bf16[64,2048]{1,0:T(8,128)(2,1)}, bf16[64,2048]{1,0:T(8,128)(2,1)S(1)}, u32[]{:S(2)}, u32[]{:S(2)}) collective-permute-start(bf16[64,2048]{1,0:T(8,128)(2,1)} %broadcast_select_fusion.5), channel_id=1, source_target_pairs={{0,16},{8,24},{16,0},{24,8},{1,17},{9,25},{17,1},{25,9},{2,18},{10... | collective-permute-start | bytes 786440 | tf_op jit(solution)/shard_map/ppermute | solution.py:489
  80.4 8.4 %collective-permute-start.19 = (bf16[4,16,2048]{2,1,0:T(8,128)(2,1)S(1)}, bf16[4,16,2048]{2,1,0:T(8,128)(2,1)S(1)}, u32[]{:S(2)}, u32[]{:S(2)}) collective-permute-start(bf16[4,16,2048]{2,1,0:T(8,128)(2,1)S(1)} %get-tuple-element.116), channel_id=1, source_target_pairs={{0,1},{1,0},{2,3},{3,2},{4,5},{5,4},{6,7},{7,6},{8,9},{9,8},{10,11... | collective-permute-start | bytes 786440 | tf_op jit(solution)/shard_map/ppermute | solution.py:489
  81.9 9.8 %collective-permute-start.27 = (bf16[128,1024]{1,0:T(8,128)(2,1)S(1)}, bf16[128,1024]{1,0:T(8,128)(2,1)S(1)}, u32[]{:S(2)}, u32[]{:S(2)}) collective-permute-start(bf16[128,1024]{1,0:T(8,128)(2,1)S(1)} %get-tuple-element.127.refs_6_), channel_id=1, source_target_pairs={{0,8},{8,0},{16,24},{24,16},{1,9},{9,1},{17,25},{25,17},{2,10},{10... | collective-permute-start | bytes 786440 | tf_op jit(solution)/shard_map/ppermute | solution.py:489
  89.4 4.3 %collective-permute-start.22 = (bf16[16,2048]{1,0:T(8,128)(2,1)S(1)}, bf16[16,2048]{1,0:T(8,128)(2,1)S(1)}, u32[]{:S(2)}, u32[]{:S(2)}) collective-permute-start(bf16[16,2048]{1,0:T(8,128)(2,1)S(1)} %get-tuple-element.121), channel_id=1, source_target_pairs={{0,2},{1,3},{2,0},{3,1},{4,6},{5,7},{6,4},{7,5},{8,10},{9,11},{10,... | collective-permute-start | bytes 196616 | tf_op jit(solution)/shard_map/ppermute | solution.py:489
  89.5 10.8 %collective-permute-start.25 = (bf16[64,2048]{1,0:T(8,128)(2,1)S(1)}, bf16[64,2048]{1,0:T(8,128)(2,1)S(1)}, u32[]{:S(2)}, u32[]{:S(2)}) collective-permute-start(bf16[64,2048]{1,0:T(8,128)(2,1)S(1)} %broadcast_select_fusion.2.refs_10_), channel_id=1, source_target_pairs={{0,1},{1,0},{2,3},{3,2},{4,5},{5,4},{6,7},{7,6},{8,9},{9,8},{10,11... | collective-permute-start | bytes 786440 | tf_op jit(solution)/shard_map/ppermute | solution.py:489
  91.1 9.2 %collective-permute-start.26 = (bf16[128,1024]{1,0:T(8,128)(2,1)S(1)}, bf16[128,1024]{1,0:T(8,128)(2,1)S(1)}, u32[]{:S(2)}, u32[]{:S(2)}) collective-permute-start(bf16[128,1024]{1,0:T(8,128)(2,1)S(1)} %broadcast_select_fusion.4), channel_id=1, source_target_pairs={{0,16},{8,24},{16,0},{24,8},{1,17},{9,25},{17,1},{25,9},{2,18},{10... | collective-permute-start | bytes 786440 | tf_op jit(solution)/shard_map/ppermute | solution.py:489
  91.7 11.8 %collective-permute-start.33 = (bf16[128,2048]{1,0:T(8,128)(2,1)S(1)}, bf16[128,2048]{1,0:T(8,128)(2,1)S(1)}, u32[]{:S(2)}, u32[]{:S(2)}) collective-permute-start(bf16[128,2048]{1,0:T(8,128)(2,1)S(1)} %get-tuple-element.133.refs_0_), channel_id=1, source_target_pairs={{0,8},{8,0},{16,24},{24,16},{1,9},{9,1},{17,25},{25,17},{2,10},{10... | collective-permute-start | bytes 1572872 | tf_op jit(solution)/shard_map/ppermute | solution.py:489
  91.7 8.7 %collective-permute-start.23 = (bf16[16,2048]{1,0:T(8,128)(2,1)S(1)}, bf16[16,2048]{1,0:T(8,128)(2,1)S(1)}, u32[]{:S(2)}, u32[]{:S(2)}) collective-permute-start(bf16[16,2048]{1,0:T(8,128)(2,1)S(1)} %get-tuple-element.122), channel_id=1, source_target_pairs={{0,4},{1,5},{2,6},{3,7},{4,0},{5,1},{6,2},{7,3},{8,12},{9,13},{10,... | collective-permute-start | bytes 196616 | tf_op jit(solution)/shard_map/ppermute | solution.py:489
  93.7 6.6 %collective-permute-start.24 = (bf16[16,2048]{1,0:T(8,128)(2,1)S(1)}, bf16[16,2048]{1,0:T(8,128)(2,1)S(1)}, u32[]{:S(2)}, u32[]{:S(2)}) collective-permute-start(bf16[16,2048]{1,0:T(8,128)(2,1)S(1)} %get-tuple-element.123), channel_id=1, source_target_pairs={{0,6},{1,7},{2,4},{3,5},{4,2},{5,3},{6,0},{7,1},{8,14},{9,15},{10,... | collective-permute-start | bytes 196616 | tf_op jit(solution)/shard_map/ppermute | solution.py:489
  100.6 1.6 %collective-permute-start.28 = (bf16[16,2048]{1,0:T(8,128)(2,1)S(1)}, bf16[16,2048]{1,0:T(8,128)(2,1)S(1)}, u32[]{:S(2)}, u32[]{:S(2)}) collective-permute-start(bf16[16,2048]{1,0:T(8,128)(2,1)S(1)} %last_back.1), channel_id=1, source_target_pairs={{0,8},{8,0},{16,24},{24,16},{1,9},{9,1},{17,25},{25,17},{2,10},{10... | collective-permute-start | bytes 196616 | tf_op jit(solution)/shard_map/ppermute | solution.py:489
  100.7 12.1 %collective-permute-start.32 = (bf16[128,1024]{1,0:T(8,128)(2,1)S(1)}, bf16[128,1024]{1,0:T(8,128)(2,1)S(1)}, u32[]{:S(2)}, u32[]{:S(2)}) collective-permute-start(bf16[128,1024]{1,0:T(8,128)(2,1)S(1)} %broadcast_select_fusion.3), channel_id=1, source_target_pairs={{0,16},{8,24},{16,0},{24,8},{1,17},{9,25},{17,1},{25,9},{2,18},{10... | collective-permute-start | bytes 786440 | tf_op jit(solution)/shard_map/ppermute | solution.py:489
  102.3 8.6 %collective-permute-start.34 = (bf16[16,2048]{1,0:T(8,128)(2,1)S(1)}, bf16[16,2048]{1,0:T(8,128)(2,1)S(1)}, u32[]{:S(2)}, u32[]{:S(2)}) collective-permute-start(bf16[16,2048]{1,0:T(8,128)(2,1)S(1)} %broadcast_select_fusion.9), channel_id=1, source_target_pairs={{0,16},{8,24},{16,0},{24,8},{1,17},{9,25},{17,1},{25,9},{2,18},{10... | collective-permute-start | bytes 196616 | tf_op jit(solution)/shard_map/ppermute | solution.py:489
  103.6 7.3 %collective-permute-start.31 = (bf16[16,2048]{1,0:T(8,128)(2,1)S(1)}, bf16[16,2048]{1,0:T(8,128)(2,1)S(1)}, u32[]{:S(2)}, u32[]{:S(2)}) collective-permute-start(bf16[16,2048]{1,0:T(8,128)(2,1)S(1)} %last_back.1), channel_id=1, source_target_pairs={{0,6},{1,7},{2,4},{3,5},{4,2},{5,3},{6,0},{7,1},{8,14},{9,15},{10,... | collective-permute-start | bytes 196616 | tf_op jit(solution)/shard_map/ppermute | solution.py:489
  105.5 7.3 %collective-permute-start.30 = (bf16[16,2048]{1,0:T(8,128)(2,1)S(1)}, bf16[16,2048]{1,0:T(8,128)(2,1)S(1)}, u32[]{:S(2)}, u32[]{:S(2)}) collective-permute-start(bf16[16,2048]{1,0:T(8,128)(2,1)S(1)} %last_back.1), channel_id=1, source_target_pairs={{0,4},{1,5},{2,6},{3,7},{4,0},{5,1},{6,2},{7,3},{8,12},{9,13},{10,... | collective-permute-start | bytes 196616 | tf_op jit(solution)/shard_map/ppermute | solution.py:489
  106.6 6.2 %collective-permute-start.29 = (bf16[16,2048]{1,0:T(8,128)(2,1)S(1)}, bf16[16,2048]{1,0:T(8,128)(2,1)S(1)}, u32[]{:S(2)}, u32[]{:S(2)}) collective-permute-start(bf16[16,2048]{1,0:T(8,128)(2,1)S(1)} %last_back.1), channel_id=1, source_target_pairs={{0,2},{1,3},{2,0},{3,1},{4,6},{5,7},{6,4},{7,5},{8,10},{9,11},{10,... | collective-permute-start | bytes 196616 | tf_op jit(solution)/shard_map/ppermute | solution.py:489
  112.8 13.3 %collective-permute-start.36 = (bf16[128,2048]{1,0:T(8,128)(2,1)S(1)}, bf16[128,2048]{1,0:T(8,128)(2,1)S(1)}, u32[]{:S(2)}, u32[]{:S(2)}) collective-permute-start(bf16[128,2048]{1,0:T(8,128)(2,1)S(1)} %broadcast_select_fusion), channel_id=1, source_target_pairs={{0,16},{8,24},{16,0},{24,8},{1,17},{9,25},{17,1},{25,9},{2,18},{10... | collective-permute-start | bytes 1572872 | tf_op jit(solution)/shard_map/ppermute | solution.py:489
  113.8 7.4 %collective-permute-start.35 = (bf16[64,2048]{1,0:T(8,128)(2,1)S(1)}, bf16[64,2048]{1,0:T(8,128)(2,1)S(1)}, u32[]{:S(2)}, u32[]{:S(2)}) collective-permute-start(bf16[64,2048]{1,0:T(8,128)(2,1)S(1)} %pad_maximum_fusion.3.refs_0_.refs_9_), channel_id=1, source_target_pairs={{0,1},{1,0},{2,3},{3,2},{4,5},{5,4},{6,7},{7,6},{8,9},{9,8},{10,11... | collective-permute-start | bytes 786440 | tf_op jit(solution)/shard_map/ppermute | solution.py:489
  114.6 11.3 %collective-permute-start.39 = (bf16[16,2048]{1,0:T(8,128)(2,1)S(1)}, bf16[16,2048]{1,0:T(8,128)(2,1)S(1)}, u32[]{:S(2)}, u32[]{:S(2)}) collective-permute-start(bf16[16,2048]{1,0:T(8,128)(2,1)S(1)} %broadcast_select_fusion.8), channel_id=1, source_target_pairs={{0,6},{1,7},{2,4},{3,5},{4,2},{5,3},{6,0},{7,1},{8,14},{9,15},{10,... | collective-permute-start | bytes 196616 | tf_op jit(solution)/shard_map/ppermute | solution.py:489
  116.2 9.7 %collective-permute-start.38 = (bf16[16,2048]{1,0:T(8,128)(2,1)S(1)}, bf16[16,2048]{1,0:T(8,128)(2,1)S(1)}, u32[]{:S(2)}, u32[]{:S(2)}) collective-permute-start(bf16[16,2048]{1,0:T(8,128)(2,1)S(1)} %broadcast_select_fusion.8), channel_id=1, source_target_pairs={{0,4},{1,5},{2,6},{3,7},{4,0},{5,1},{6,2},{7,3},{8,12},{9,13},{10,... | collective-permute-start | bytes 196616 | tf_op jit(solution)/shard_map/ppermute | solution.py:489
  116.2 9.7 %collective-permute-start.37 = (bf16[16,2048]{1,0:T(8,128)(2,1)S(1)}, bf16[16,2048]{1,0:T(8,128)(2,1)S(1)}, u32[]{:S(2)}, u32[]{:S(2)}) collective-permute-start(bf16[16,2048]{1,0:T(8,128)(2,1)S(1)} %broadcast_select_fusion.8), channel_id=1, source_target_pairs={{0,2},{1,3},{2,0},{3,1},{4,6},{5,7},{6,4},{7,5},{8,10},{9,11},{10,... | collective-permute-start | bytes 196616 | tf_op jit(solution)/shard_map/ppermute | solution.py:489
  126.2 1.5 %collective-permute-start.40 = (bf16[128,1024]{1,0:T(8,128)(2,1)S(1)}, bf16[128,1024]{1,0:T(8,128)(2,1)S(1)}, u32[]{:S(2)}, u32[]{:S(2)}) collective-permute-start(bf16[128,1024]{1,0:T(8,128)(2,1)S(1)} %low_grad.1.refs_3_), channel_id=1, source_target_pairs={{0,8},{8,0},{16,24},{24,16},{1,9},{9,1},{17,25},{25,17},{2,10},{10... | collective-permute-start | bytes 786440 | tf_op jit(solution)/shard_map/ppermute | solution.py:489
  126.2 10.1 %collective-permute-start.42 = (bf16[64,2048]{1,0:T(8,128)(2,1)S(1)}, bf16[64,2048]{1,0:T(8,128)(2,1)S(1)}, u32[]{:S(2)}, u32[]{:S(2)}) collective-permute-start(bf16[64,2048]{1,0:T(8,128)(2,1)S(1)} %pad_maximum_fusion.4.refs_11_), channel_id=1, source_target_pairs={{0,1},{1,0},{2,3},{3,2},{4,5},{5,4},{6,7},{7,6},{8,9},{9,8},{10,11... | collective-permute-start | bytes 786440 | tf_op jit(solution)/shard_map/ppermute | solution.py:489
  127.8 8.6 %collective-permute-start.41 = (bf16[128,1024]{1,0:T(8,128)(2,1)S(1)}, bf16[128,1024]{1,0:T(8,128)(2,1)S(1)}, u32[]{:S(2)}, u32[]{:S(2)}) collective-permute-start(bf16[128,1024]{1,0:T(8,128)(2,1)S(1)} %broadcast_select_fusion.6), channel_id=1, source_target_pairs={{0,16},{8,24},{16,0},{24,8},{1,17},{9,25},{17,1},{25,9},{2,18},{10... | collective-permute-start | bytes 786440 | tf_op jit(solution)/shard_map/ppermute | solution.py:489
  (25 other events, 434.4 us)

commit v6 on v5

--- a/solution.py
+++ b/solution.py
@@ -555,7 +555,7 @@
         got, hop_2, n1_mate[1] = tie(swap(give, "shard", 1), swap(rows_2, "shard", 2), n1_mate[1])
         along_x(n1_mate)
         mine, *gives = half_sums(where, keep, got)
-        got = [swap(part, "shard", 2 * k + 2) for k, part in enumerate(gives)]
+        got = [swap(gives[k], "shard", 2 * k + 2) for k in (1, 0, 2)]
         rows_4 = join(tie(rows_2, mine)[0], hop_2)
         *got, hop_3 = tie(*got, swap(rows_4, "shard", 1))
         h_own = last_sums(x_own, mine, got)
@@ -584,7 +584,7 @@
         got, da2_mate[1], half_mate[1] = tie(swap(give, "shard", 1), da2_mate[1], half_mate[1])
         along_x(da2_mate)
         mine, *gives = half_sums(where, keep, got)
-        got = [swap(part, "shard", 2 * k + 2) for k, part in enumerate(gives)]
+        got = [swap(gives[k], "shard", 2 * k + 2) for k in (1, 0, 2)]
         half = jnp.where(mate_high == 1, *half_mate)
         hop_4 = swap(tie(half, mine)[0], "shard", 1)
         *got, hop_4, da2_mate[1], u2_mate[1] = tie(*got, hop_4, da2_mate[1], u2_mate[1])

time: 146 us -> 145 us (level)
  transfers between devices with their start and end apart: 44 -> 44, of which waited for: 18 -> 20; matrix products, arithmetic and copies ran while one was open for 3% -> 3% of each run, Pallas kernels for 14% -> 14%
where the time goes in v6:
time: 145 us; the launch traced here: 144 us
  starting transfers between devices  52.6 us (36%)
  waiting for transfers between devices  41.1 us (28%)
  Pallas kernels  41 us (28%)
  local copies, waits for them, and re-layouts  3.84 us (3%)
  other arithmetic  2.89 us (2%)
  between operations  2.68 us (2%)
    ppermute x43, starting transfers between devices, swap(): lax.ppermute(value, axis, [(i, i ^ bit) for i in range(lax.axis_size(axis...  45.3 us
    ppermute x43, waiting for transfers between devices, swap(): lax.ppermute(value, axis, [(i, i ^ bit) for i in range(lax.axis_size(axis...  34 us
    pallas_call x4, Pallas kernels, stream(): pl.pallas_call(kernel, in_specs=[IN_SMEM] * len(operands) + [IN_VMEM] * l...  20.6 us
    pallas_call x2, Pallas kernels, pair_grads(): pl.pallas_call(functools.partial(pair_kernel, level, settings), in_specs=...  15.2 us
    all_to_all x1, starting transfers between devices, dispatch(): lax.all_to_all(spread, ('path', 'shard'), split_axis=0, concat_axis=0, ti...  7.3 us
    all_to_all x1, waiting for transfers between devices, dispatch(): lax.all_to_all(spread, ('path', 'shard'), split_axis=0, concat_axis=0, ti...  7.17 us
    pallas_call x2, Pallas kernels, pack(): pl.pallas_call(functools.partial(pack_kernel, copies), in_specs=[IN_SMEM,...  3.54 us
  transfers between devices with their start and end apart: 44, of which 20 were waited for; matrix products, arithmetic and copies ran while one was open for 3% of the time, Pallas kernels for 14%

profile of v6, /device:TPU:0, one launch (start us, length us, event | category | flops | bytes accessed | tf_op | source)
XLA Modules:
  0.0 144.1 jit_solution(1413155528030549705)
XLA Ops:
  0.6 1.9 %pack.2 = bf16[32,4,2048]{2,1,0:T(4,128)(2,1)} custom-call(s32[1]{0:T(128)} %constant.7.clone.1.flip_ref, s32[12]{0:T(128)} %bitcast.11, bf16[12,2048]{1,0:T(8,128)(2,1)} %rows_ref.2), custom_call_target="tpu_custom_call" | custom-call | tf_op jit(solution)/shard_map/pack/pallas_call | solution.py:123
  2.5 7.3 %all-to-all-start = ((bf16[32,4,2048]{2,1,0:T(4,128)(2,1)}), bf16[32,4,2048]{2,1,0:T(4,128)(2,1)S(1)}, u32[]{:S(2)}, u32[]{:S(2)}) async-start(bf16[32,4,2048]{2,1,0:T(4,128)(2,1)} %pack.2), calls=%async_computation | async-start | bytes 1048576 | tf_op jit(solution)/shard_map/all_to_all | solution.py:473
  9.8 1.7 %pack.3 = (bf16[4,2048]{1,0:T(4,128)(2,1)}, bf16[4,2048]{1,0:T(4,128)(2,1)}, bf16[4,2048]{1,0:T(4,128)(2,1)}, bf16[4,2048]{1,0:T(4,128)(2,1)}) custom-call(s32[1]{0:T(128)} %bitcast.1.flip_ref, s32[12]{0:T(128)} %bitcast.12, bf16[12,2048]{1,0:T(8,128)(2,1)} %rows_ref.3), custom_call_target="tpu_custom_call" | custom-call | tf_op jit(solution)/shard_map/pack/pallas_call | solution.py:123
  11.7 1.7 %collective-permute-start.1 = (bf16[4,2048]{1,0:T(4,128)(2,1)}, bf16[4,2048]{1,0:T(4,128)(2,1)S(1)}, u32[]{:S(2)}, u32[]{:S(2)}) collective-permute-start(bf16[4,2048]{1,0:T(4,128)(2,1)} %get-tuple-element.80), channel_id=1, source_target_pairs={{0,16},{8,24},{16,0},{24,8},{1,17},{9,25},{17,1},{25,9},{2,18},{10... | collective-permute-start | bytes 49160 | tf_op jit(solution)/shard_map/ppermute | solution.py:489
  13.4 1.4 constant_dynamic-slice_fusion.1
  17.6 2.7 %collective-permute-start.3 = (bf16[16,2048]{1,0:T(8,128)(2,1)S(1)}, bf16[16,2048]{1,0:T(8,128)(2,1)S(1)}, u32[]{:S(2)}, u32[]{:S(2)}) collective-permute-start(bf16[16,2048]{1,0:T(8,128)(2,1)S(1)} %pad_maximum_fusion.6), channel_id=1, source_target_pairs={{0,4},{1,5},{2,6},{3,7},{4,0},{5,1},{6,2},{7,3},{8,12},{9,13},{10,... | collective-permute-start | bytes 196616 | tf_op jit(solution)/shard_map/ppermute | solution.py:489
  20.4 7.2 %all-to-all-done = bf16[32,4,2048]{2,1,0:T(4,128)(2,1)S(1)} async-done(((bf16[32,4,2048]{2,1,0:T(4,128)(2,1)}), bf16[32,4,2048]{2,1,0:T(4,128)(2,1)S(1)}, u32[]{:S(2)}, u32[]{:S(2)}) %all-to-all-start) | async-done | bytes 524320 | tf_op jit(solution)/shard_map/all_to_all | solution.py:473
  28.4 6.1 %low_forward.1 = (bf16[128,2048]{1,0:T(8,128)(2,1)S(1)}, bf16[128,1024]{1,0:T(8,128)(2,1)S(1)}, f32[128,1024]{1,0:T(8,128)S(1)}, bf16[16,2048]{1,0:T(8,128)(2,1)...) custom-call(s32[4]{0:T(128)S(1)} %pad_add_fusion.where_ref, ...), custom_call_target="tpu_custom_call" | custom-call | tf_op jit(solution)/shard_map/low_forward/pallas_call | solution.py:57
  34.7 0.9 collective-permute-start.6
  36.5 0.9 broadcast_select_fusion.1
  37.5 3.2 %collective-permute-done.6 = bf16[32,2048]{1,0:T(8,128)(2,1)S(1)} collective-permute-done((bf16[32,2048]{1,0:T(8,128)(2,1)S(1)}, bf16[32,2048]{1,0:T(8,128)(2,1)S(1)}, u32[]{:S(2)}, u32[]{:S(2)}) %collective-permute-start.6) | collective-permute-done | bytes 131104 | tf_op jit(solution)/shard_map/ppermute | solution.py:489
  40.6 3.3 %collective-permute-done.5.got_ref = bf16[4,16,2048]{2,1,0:T(8,128)(2,1)S(1)} collective-permute-done((bf16[4,16,2048]{2,1,0:T(8,128)(2,1)S(1)}, bf16[4,16,2048]{2,1,0:T(8,128)(2,1)S(1)}, u32[]{:S(2)}, u32[]{:S(2)}) %collective-permute-start.5) | collective-permute-done | bytes 262176 | tf_op jit(solution)/shard_map/ppermute | solution.py:489
  44.6 1.0 collective-permute-start.7
  45.6 1.7 %collective-permute-start.10 = (bf16[64,2048]{1,0:T(8,128)(2,1)S(1)}, bf16[64,2048]{1,0:T(8,128)(2,1)S(1)}, u32[]{:S(2)}, u32[]{:S(2)}) collective-permute-start(bf16[64,2048]{1,0:T(8,128)(2,1)S(1)} %pad_maximum_fusion.1), channel_id=1, source_target_pairs={{0,1},{1,0},{2,3},{3,2},{4,5},{5,4},{6,7},{7,6},{8,9},{9,8},{10,11... | collective-permute-start | bytes 786440 | tf_op jit(solution)/shard_map/ppermute | solution.py:489
  47.7 2.4 %collective-permute-start.9 = (bf16[16,2048]{1,0:T(8,128)(2,1)S(1)}, bf16[16,2048]{1,0:T(8,128)(2,1)S(1)}, u32[]{:S(2)}, u32[]{:S(2)}) collective-permute-start(bf16[16,2048]{1,0:T(8,128)(2,1)S(1)} %get-tuple-element.94), channel_id=1, source_target_pairs={{0,6},{1,7},{2,4},{3,5},{4,2},{5,3},{6,0},{7,1},{8,14},{9,15},{10,... | collective-permute-start | bytes 196616 | tf_op jit(solution)/shard_map/ppermute | solution.py:489
  50.1 1.5 %collective-permute-start.14 = (bf16[128,2048]{1,0:T(8,128)(2,1)}, bf16[128,2048]{1,0:T(8,128)(2,1)S(1)}, u32[]{:S(2)}, u32[]{:S(2)}) collective-permute-start(bf16[128,2048]{1,0:T(8,128)(2,1)} %broadcast_select_fusion.1), channel_id=1, source_target_pairs={{0,16},{8,24},{16,0},{24,8},{1,17},{9,25},{17,1},{25,9},{2,18},{10... | collective-permute-start | bytes 1572872 | tf_op jit(solution)/shard_map/ppermute | solution.py:489
  51.9 2.2 %collective-permute-done.9.rest_2_ = bf16[16,2048]{1,0:T(8,128)(2,1)S(1)} collective-permute-done((bf16[16,2048]{1,0:T(8,128)(2,1)S(1)}, bf16[16,2048]{1,0:T(8,128)(2,1)S(1)}, u32[]{:S(2)}, u32[]{:S(2)}) %collective-permute-start.9) | collective-permute-done | bytes 65568 | tf_op jit(solution)/shard_map/ppermute | solution.py:489
  54.1 2.2 %collective-permute-start.13 = (bf16[16,2048]{1,0:T(8,128)(2,1)S(1)}, bf16[16,2048]{1,0:T(8,128)(2,1)S(1)}, u32[]{:S(2)}, u32[]{:S(2)}) collective-permute-start(bf16[16,2048]{1,0:T(8,128)(2,1)S(1)} %last_sums.1.h_ref), channel_id=1, source_target_pairs={{0,6},{1,7},{2,4},{3,5},{4,2},{5,3},{6,0},{7,1},{8,14},{9,15},{10,... | collective-permute-start | bytes 196616 | tf_op jit(solution)/shard_map/ppermute | solution.py:489
  56.6 2.0 %collective-permute-start.11 = (bf16[16,2048]{1,0:T(8,128)(2,1)S(1)}, bf16[16,2048]{1,0:T(8,128)(2,1)S(1)}, u32[]{:S(2)}, u32[]{:S(2)}) collective-permute-start(bf16[16,2048]{1,0:T(8,128)(2,1)S(1)} %last_sums.1.h_ref), channel_id=1, source_target_pairs={{0,2},{1,3},{2,0},{3,1},{4,6},{5,7},{6,4},{7,5},{8,10},{9,11},{10,... | collective-permute-start | bytes 196616 | tf_op jit(solution)/shard_map/ppermute | solution.py:489
  59.4 1.3 collective-permute-done.13
  60.7 2.3 %collective-permute-done.12 = bf16[16,2048]{1,0:T(8,128)(2,1)S(1)} collective-permute-done((bf16[16,2048]{1,0:T(8,128)(2,1)S(1)}, bf16[16,2048]{1,0:T(8,128)(2,1)S(1)}, u32[]{:S(2)}, u32[]{:S(2)}) %collective-permute-start.12) | collective-permute-done | bytes 65568 | tf_op jit(solution)/shard_map/ppermute | solution.py:489
  63.1 1.0 collective-permute-done.14.refs_2_
  64.1 1.1 collective-permute-start.17
  65.3 0.9 collective-permute-start.18
  66.2 4.6 %high_grad.1 = (bf16[16,2048]{1,0:T(8,128)(2,1)S(1)}, f32[128,1024]{1,0:T(8,128)S(1)}, bf16[128,2048]{1,0:T(8,128)(2,1)S(1)}) custom-call(s32[4]{0:T(128)S(1)} %pad_add_fusion.where_ref, bf16[128,2048]{1,0:T(8,128)(2,1)S(1)} %pad_maximum_fusion.raw_ref, bf16[1,2,1024,2048]{3,2,1,0:T(8,128)(2,1)} %refs_3_.1), custom_call_target="tpu_custom_call" | custom-call | tf_op jit(solution)/shard_map/high_grad/pallas_call | solution.py:57
  72.3 5.3 %high_both.1 = (bf16[128,2048]{1,0:T(8,128)(2,1)S(1)}, bf16[128,1024]{1,0:T(8,128)(2,1)S(1)}, bf16[128,1024]{1,0:T(8,128)(2,1)S(1)}, bf16[4,16,2048]{2,1,0:T(8,128)(2,1)S(1)}, bf16[4,16,2048]{2,1,0:T(8,128)(2,1)S(1)}) custom-call(s32[4]{0:T(128)S(1)} %pad_add_fusion.where_ref, bf16[64,2048]{1,0:T(8,128)(2,1)S(1)} %pad_maximum_fusion.2.refs_0_, ...), custom_call_target="tpu_custom_call" | custom-call | tf_op jit(solution)/shard_map/high_both/pallas_call | solution.py:57
  78.5 1.7 %collective-permute-start.19 = (bf16[4,16,2048]{2,1,0:T(8,128)(2,1)S(1)}, bf16[4,16,2048]{2,1,0:T(8,128)(2,1)S(1)}, u32[]{:S(2)}, u32[]{:S(2)}) collective-permute-start(bf16[4,16,2048]{2,1,0:T(8,128)(2,1)S(1)} %get-tuple-element.116), channel_id=1, source_target_pairs={{0,1},{1,0},{2,3},{3,2},{4,5},{5,4},{6,7},{7,6},{8,9},{9,8},{10,11... | collective-permute-start | bytes 786440 | tf_op jit(solution)/shard_map/ppermute | solution.py:489
  80.3 6.4 %collective-permute-done.21 = bf16[64,2048]{1,0:T(8,128)(2,1)S(1)} collective-permute-done((bf16[64,2048]{1,0:T(8,128)(2,1)}, bf16[64,2048]{1,0:T(8,128)(2,1)S(1)}, u32[]{:S(2)}, u32[]{:S(2)}) %collective-permute-start.21) | collective-permute-done | bytes 262176 | tf_op jit(solution)/shard_map/ppermute | solution.py:489
  88.3 1.8 %collective-permute-start.25 = (bf16[64,2048]{1,0:T(8,128)(2,1)S(1)}, bf16[64,2048]{1,0:T(8,128)(2,1)S(1)}, u32[]{:S(2)}, u32[]{:S(2)}) collective-permute-start(bf16[64,2048]{1,0:T(8,128)(2,1)S(1)} %broadcast_select_fusion.2.refs_10_), channel_id=1, source_target_pairs={{0,1},{1,0},{2,3},{3,2},{4,5},{5,4},{6,7},{7,6},{8,9},{9,8},{10,11... | collective-permute-start | bytes 786440 | tf_op jit(solution)/shard_map/ppermute | solution.py:489
  90.8 1.3 collective-permute-start.23
  92.1 1.4 collective-permute-done.22.rest_0_
  93.5 1.4 collective-permute-start.24
  95.3 4.3 %collective-permute-done.24.rest_2_ = bf16[16,2048]{1,0:T(8,128)(2,1)S(1)} collective-permute-done((bf16[16,2048]{1,0:T(8,128)(2,1)S(1)}, bf16[16,2048]{1,0:T(8,128)(2,1)S(1)}, u32[]{:S(2)}, u32[]{:S(2)}) %collective-permute-start.24) | collective-permute-done | bytes 65568 | tf_op jit(solution)/shard_map/ppermute | solution.py:489
  99.9 0.9 collective-permute-start.32
  101.2 0.9 collective-permute-start.34
  102.2 1.6 %collective-permute-start.31 = (bf16[16,2048]{1,0:T(8,128)(2,1)S(1)}, bf16[16,2048]{1,0:T(8,128)(2,1)S(1)}, u32[]{:S(2)}, u32[]{:S(2)}) collective-permute-start(bf16[16,2048]{1,0:T(8,128)(2,1)S(1)} %last_back.1), channel_id=1, source_target_pairs={{0,6},{1,7},{2,4},{3,5},{4,2},{5,3},{6,0},{7,1},{8,14},{9,15},{10,... | collective-permute-start | bytes 196616 | tf_op jit(solution)/shard_map/ppermute | solution.py:489
  103.8 2.8 %collective-permute-start.29 = (bf16[16,2048]{1,0:T(8,128)(2,1)S(1)}, bf16[16,2048]{1,0:T(8,128)(2,1)S(1)}, u32[]{:S(2)}, u32[]{:S(2)}) collective-permute-start(bf16[16,2048]{1,0:T(8,128)(2,1)S(1)} %last_back.1), channel_id=1, source_target_pairs={{0,2},{1,3},{2,0},{3,1},{4,6},{5,7},{6,4},{7,5},{8,10},{9,11},{10,... | collective-permute-start | bytes 196616 | tf_op jit(solution)/shard_map/ppermute | solution.py:489
  106.6 3.4 %collective-permute-done.34 = bf16[16,2048]{1,0:T(8,128)(2,1)S(1)} collective-permute-done((bf16[16,2048]{1,0:T(8,128)(2,1)S(1)}, bf16[16,2048]{1,0:T(8,128)(2,1)S(1)}, u32[]{:S(2)}, u32[]{:S(2)}) %collective-permute-start.34) | collective-permute-done | bytes 65568 | tf_op jit(solution)/shard_map/ppermute | solution.py:489
  110.7 1.2 collective-permute-start.36
  112.0 1.9 %collective-permute-start.35 = (bf16[64,2048]{1,0:T(8,128)(2,1)S(1)}, bf16[64,2048]{1,0:T(8,128)(2,1)S(1)}, u32[]{:S(2)}, u32[]{:S(2)}) collective-permute-start(bf16[64,2048]{1,0:T(8,128)(2,1)S(1)} %pad_maximum_fusion.3.refs_0_.refs_9_), channel_id=1, source_target_pairs={{0,1},{1,0},{2,3},{3,2},{4,5},{5,4},{6,7},{7,6},{8,9},{9,8},{10,11... | collective-permute-start | bytes 786440 | tf_op jit(solution)/shard_map/ppermute | solution.py:489
  113.8 1.3 collective-permute-start.39
  115.4 2.8 %collective-permute-start.37 = (bf16[16,2048]{1,0:T(8,128)(2,1)S(1)}, bf16[16,2048]{1,0:T(8,128)(2,1)S(1)}, u32[]{:S(2)}, u32[]{:S(2)}) collective-permute-start(bf16[16,2048]{1,0:T(8,128)(2,1)S(1)} %broadcast_select_fusion.8), channel_id=1, source_target_pairs={{0,2},{1,3},{2,0},{3,1},{4,6},{5,7},{6,4},{7,5},{8,10},{9,11},{10,... | collective-permute-start | bytes 196616 | tf_op jit(solution)/shard_map/ppermute | solution.py:489
  118.2 1.8 %collective-permute-done.35.refs_1_.refs_10_ = bf16[64,2048]{1,0:T(8,128)(2,1)S(1)} collective-permute-done((bf16[64,2048]{1,0:T(8,128)(2,1)S(1)}, bf16[64,2048]{1,0:T(8,128)(2,1)S(1)}, u32[]{:S(2)}, u32[]{:S(2)}) %collective-permute-start.35) | collective-permute-done | bytes 262176 | tf_op jit(solution)/shard_map/ppermute | solution.py:489
  120.0 4.6 %low_grad.1.refs_3_ = bf16[128,1024]{1,0:T(8,128)(2,1)S(1)} custom-call(s32[4]{0:T(128)S(1)} %pad_add_fusion.where_ref, bf16[64,2048]{1,0:T(8,128)(2,1)S(1)} %pad_maximum_fusion.3.refs_0_.refs_9_, bf16[64,2048]{1,0:T(8,128)(2,1)S(1)} %collective-permute-done.35.refs_1_.refs_10_, f32[128,1024]{1,0:T(8,128)S(1)} %get-tuple-element.139.refs_2_, ...), custom_call_target="tpu_custom_call" | custom-call | tf_op jit(solution)/shard_map/low_grad/pallas_call | solution.py:57
  124.9 1.8 %collective-permute-start.42 = (bf16[64,2048]{1,0:T(8,128)(2,1)S(1)}, bf16[64,2048]{1,0:T(8,128)(2,1)S(1)}, u32[]{:S(2)}, u32[]{:S(2)}) collective-permute-start(bf16[64,2048]{1,0:T(8,128)(2,1)S(1)} %pad_maximum_fusion.4.refs_11_), channel_id=1, source_target_pairs={{0,1},{1,0},{2,3},{3,2},{4,5},{5,4},{6,7},{7,6},{8,9},{9,8},{10,11... | collective-permute-start | bytes 786440 | tf_op jit(solution)/shard_map/ppermute | solution.py:489
  126.7 1.1 collective-permute-start.41
  127.9 7.4 %pair_grads.2 = (bf16[1,2,2048,1024]{3,2,1,0:T(8,128)(2,1)}, bf16[1,2,1024,2048]{3,2,1,0:T(8,128)(2,1)}) custom-call(s32[4]{0:T(128)} %copy-done.11, bf16[128,2048]{1,0:T(8,128)(2,1)} %copy-done.3, bf16[128,2048]{1,0:T(8,128)(2,1)} %copy-done.13, bf16[128,2048]{1,0:T(8,128)(2,1)} %copy-done.22, bf16[128,1024]{1,0:T(8,128)(2,1)} %copy-done.7, ...), custom_call_target="tpu_custom_call" | custom-call | tf_op jit(solution)/shard_map/pair_grads/pallas_call | solution.py:459
  136.1 7.8 %pair_grads.3 = (bf16[1,2,2048,1024]{3,2,1,0:T(8,128)(2,1)}, bf16[1,2,1024,2048]{3,2,1,0:T(8,128)(2,1)}) custom-call(s32[4]{0:T(128)} %copy-done.11, bf16[128,2048]{1,0:T(8,128)(2,1)} %copy-done.2, bf16[128,2048]{1,0:T(8,128)(2,1)} %copy-done.12, bf16[128,2048]{1,0:T(8,128)(2,1)} %copy-done.21, ...), custom_call_target="tpu_custom_call", output_to_operand_aliasing={{0}: (14, {}), {1}: (15, {})} | custom-call | tf_op jit(solution)/shard_map/pair_grads/pallas_call | solution.py:459
  (130 shorter events, 13.6 us)
Async XLA Ops:
  2.5 25.1 %all-to-all-start = ((bf16[32,4,2048]{2,1,0:T(4,128)(2,1)}), bf16[32,4,2048]{2,1,0:T(4,128)(2,1)S(1)}, u32[]{:S(2)}, u32[]{:S(2)}) async-start(bf16[32,4,2048]{2,1,0:T(4,128)(2,1)} %pack.2), calls=%async_computation | async-start | bytes 1048576 | tf_op jit(solution)/shard_map/all_to_all | solution.py:473
  11.5 4.6 %collective-permute-start = (bf16[4,2048]{1,0:T(4,128)(2,1)}, bf16[4,2048]{1,0:T(4,128)(2,1)S(1)}, u32[]{:S(2)}, u32[]{:S(2)}) collective-permute-start(bf16[4,2048]{1,0:T(4,128)(2,1)} %get-tuple-element.79), channel_id=1, source_target_pairs={{0,8},{8,0},{16,24},{24,16},{1,9},{9,1},{17,25},{25,17},{2,10},{10... | collective-permute-start | bytes 49160 | tf_op jit(solution)/shard_map/ppermute | solution.py:489
  11.7 4.4 %collective-permute-start.1 = (bf16[4,2048]{1,0:T(4,128)(2,1)}, bf16[4,2048]{1,0:T(4,128)(2,1)S(1)}, u32[]{:S(2)}, u32[]{:S(2)}) collective-permute-start(bf16[4,2048]{1,0:T(4,128)(2,1)} %get-tuple-element.80), channel_id=1, source_target_pairs={{0,16},{8,24},{16,0},{24,8},{1,17},{9,25},{17,1},{25,9},{2,18},{10... | collective-permute-start | bytes 49160 | tf_op jit(solution)/shard_map/ppermute | solution.py:489
  13.4 3.4 %collective-permute-start.2 = (bf16[4,2048]{1,0:T(4,128)(2,1)}, bf16[4,2048]{1,0:T(4,128)(2,1)S(1)}, u32[]{:S(2)}, u32[]{:S(2)}) collective-permute-start(bf16[4,2048]{1,0:T(4,128)(2,1)} %get-tuple-element.81), channel_id=1, source_target_pairs={{0,24},{8,16},{16,8},{24,0},{1,25},{9,17},{17,9},{25,1},{2,26},{10... | collective-permute-start | bytes 49160 | tf_op jit(solution)/shard_map/ppermute | solution.py:489
  17.6 10.1 %collective-permute-start.3 = (bf16[16,2048]{1,0:T(8,128)(2,1)S(1)}, bf16[16,2048]{1,0:T(8,128)(2,1)S(1)}, u32[]{:S(2)}, u32[]{:S(2)}) collective-permute-start(bf16[16,2048]{1,0:T(8,128)(2,1)S(1)} %pad_maximum_fusion.6), channel_id=1, source_target_pairs={{0,4},{1,5},{2,6},{3,7},{4,0},{5,1},{6,2},{7,3},{8,12},{9,13},{10,... | collective-permute-start | bytes 196616 | tf_op jit(solution)/shard_map/ppermute | solution.py:489
  20.4 99.7 %copy-start.11 = (s32[4]{0:T(128)}, s32[4]{0:T(128)S(1)}, u32[]{:S(2)}) copy-start(s32[4]{0:T(128)S(1)} %pad_add_fusion.where_ref) | copy-start | bytes 52
  34.5 2.0 %collective-permute-start.4 = (bf16[128,2048]{1,0:T(8,128)(2,1)S(1)}, bf16[128,2048]{1,0:T(8,128)(2,1)S(1)}, u32[]{:S(2)}, u32[]{:S(2)}) collective-permute-start(bf16[128,2048]{1,0:T(8,128)(2,1)S(1)} %get-tuple-element.84.refs_0_), channel_id=1, source_target_pairs={{0,8},{8,0},{16,24},{24,16},{1,9},{9,1},{17,25},{25,17},{2,10},{10... | collective-permute-start | bytes 1572872 | tf_op jit(solution)/shard_map/ppermute | solution.py:489
  34.7 5.9 %collective-permute-start.6 = (bf16[32,2048]{1,0:T(8,128)(2,1)S(1)}, bf16[32,2048]{1,0:T(8,128)(2,1)S(1)}, u32[]{:S(2)}, u32[]{:S(2)}) collective-permute-start(bf16[32,2048]{1,0:T(8,128)(2,1)S(1)} %pad_maximum_fusion.5), channel_id=1, source_target_pairs={{0,2},{1,3},{2,0},{3,1},{4,6},{5,7},{6,4},{7,5},{8,10},{9,11},{10,... | collective-permute-start | bytes 393224 | tf_op jit(solution)/shard_map/ppermute | solution.py:489
  35.7 8.3 %collective-permute-start.5 = (bf16[4,16,2048]{2,1,0:T(8,128)(2,1)S(1)}, bf16[4,16,2048]{2,1,0:T(8,128)(2,1)S(1)}, u32[]{:S(2)}, u32[]{:S(2)}) collective-permute-start(bf16[4,16,2048]{2,1,0:T(8,128)(2,1)S(1)} %get-tuple-element.87), channel_id=1, source_target_pairs={{0,1},{1,0},{2,3},{3,2},{4,5},{5,4},{6,7},{7,6},{8,9},{9,8},{10,11... | collective-permute-start | bytes 786440 | tf_op jit(solution)/shard_map/ppermute | solution.py:489
  36.2 11.5 %collective-permute-start.15 = (bf16[128,1024]{1,0:T(8,128)(2,1)S(1)}, bf16[128,1024]{1,0:T(8,128)(2,1)S(1)}, u32[]{:S(2)}, u32[]{:S(2)}) collective-permute-start(bf16[128,1024]{1,0:T(8,128)(2,1)S(1)} %get-tuple-element.101.refs_6_), channel_id=1, source_target_pairs={{0,8},{8,0},{16,24},{24,16},{1,9},{9,1},{17,25},{25,17},{2,10},{10... | collective-permute-start | bytes 786440 | tf_op jit(solution)/shard_map/ppermute | solution.py:489
  44.6 5.5 %collective-permute-start.7 = (bf16[16,2048]{1,0:T(8,128)(2,1)S(1)}, bf16[16,2048]{1,0:T(8,128)(2,1)S(1)}, u32[]{:S(2)}, u32[]{:S(2)}) collective-permute-start(bf16[16,2048]{1,0:T(8,128)(2,1)S(1)} %get-tuple-element.92), channel_id=1, source_target_pairs={{0,4},{1,5},{2,6},{3,7},{4,0},{5,1},{6,2},{7,3},{8,12},{9,13},{10,... | collective-permute-start | bytes 196616 | tf_op jit(solution)/shard_map/ppermute | solution.py:489
  45.6 8.5 %collective-permute-start.10 = (bf16[64,2048]{1,0:T(8,128)(2,1)S(1)}, bf16[64,2048]{1,0:T(8,128)(2,1)S(1)}, u32[]{:S(2)}, u32[]{:S(2)}) collective-permute-start(bf16[64,2048]{1,0:T(8,128)(2,1)S(1)} %pad_maximum_fusion.1), channel_id=1, source_target_pairs={{0,1},{1,0},{2,3},{3,2},{4,5},{5,4},{6,7},{7,6},{8,9},{9,8},{10,11... | collective-permute-start | bytes 786440 | tf_op jit(solution)/shard_map/ppermute | solution.py:489
  47.4 11.2 %collective-permute-start.16 = (bf16[64,2048]{1,0:T(8,128)(2,1)S(1)}, bf16[64,2048]{1,0:T(8,128)(2,1)S(1)}, u32[]{:S(2)}, u32[]{:S(2)}) collective-permute-start(bf16[64,2048]{1,0:T(8,128)(2,1)S(1)} %pad_maximum_fusion.1), channel_id=1, source_target_pairs={{0,8},{8,0},{16,24},{24,16},{1,9},{9,1},{17,25},{25,17},{2,10},{10... | collective-permute-start | bytes 786440 | tf_op jit(solution)/shard_map/ppermute | solution.py:489
  47.4 4.5 %collective-permute-start.8 = (bf16[16,2048]{1,0:T(8,128)(2,1)S(1)}, bf16[16,2048]{1,0:T(8,128)(2,1)S(1)}, u32[]{:S(2)}, u32[]{:S(2)}) collective-permute-start(bf16[16,2048]{1,0:T(8,128)(2,1)S(1)} %get-tuple-element.93), channel_id=1, source_target_pairs={{0,2},{1,3},{2,0},{3,1},{4,6},{5,7},{6,4},{7,5},{8,10},{9,11},{10,... | collective-permute-start | bytes 196616 | tf_op jit(solution)/shard_map/ppermute | solution.py:489
  47.7 6.4 %collective-permute-start.9 = (bf16[16,2048]{1,0:T(8,128)(2,1)S(1)}, bf16[16,2048]{1,0:T(8,128)(2,1)S(1)}, u32[]{:S(2)}, u32[]{:S(2)}) collective-permute-start(bf16[16,2048]{1,0:T(8,128)(2,1)S(1)} %get-tuple-element.94), channel_id=1, source_target_pairs={{0,6},{1,7},{2,4},{3,5},{4,2},{5,3},{6,0},{7,1},{8,14},{9,15},{10,... | collective-permute-start | bytes 196616 | tf_op jit(solution)/shard_map/ppermute | solution.py:489
  50.1 14.0 %collective-permute-start.14 = (bf16[128,2048]{1,0:T(8,128)(2,1)}, bf16[128,2048]{1,0:T(8,128)(2,1)S(1)}, u32[]{:S(2)}, u32[]{:S(2)}) collective-permute-start(bf16[128,2048]{1,0:T(8,128)(2,1)} %broadcast_select_fusion.1), channel_id=1, source_target_pairs={{0,16},{8,24},{16,0},{24,8},{1,17},{9,25},{17,1},{25,9},{2,18},{10... | collective-permute-start | bytes 1572872 | tf_op jit(solution)/shard_map/ppermute | solution.py:489
  54.1 6.6 %collective-permute-start.13 = (bf16[16,2048]{1,0:T(8,128)(2,1)S(1)}, bf16[16,2048]{1,0:T(8,128)(2,1)S(1)}, u32[]{:S(2)}, u32[]{:S(2)}) collective-permute-start(bf16[16,2048]{1,0:T(8,128)(2,1)S(1)} %last_sums.1.h_ref), channel_id=1, source_target_pairs={{0,6},{1,7},{2,4},{3,5},{4,2},{5,3},{6,0},{7,1},{8,14},{9,15},{10,... | collective-permute-start | bytes 196616 | tf_op jit(solution)/shard_map/ppermute | solution.py:489
  56.4 6.7 %collective-permute-start.12 = (bf16[16,2048]{1,0:T(8,128)(2,1)S(1)}, bf16[16,2048]{1,0:T(8,128)(2,1)S(1)}, u32[]{:S(2)}, u32[]{:S(2)}) collective-permute-start(bf16[16,2048]{1,0:T(8,128)(2,1)S(1)} %last_sums.1.h_ref), channel_id=1, source_target_pairs={{0,4},{1,5},{2,6},{3,7},{4,0},{5,1},{6,2},{7,3},{8,12},{9,13},{10,... | collective-permute-start | bytes 196616 | tf_op jit(solution)/shard_map/ppermute | solution.py:489
  56.6 6.5 %collective-permute-start.11 = (bf16[16,2048]{1,0:T(8,128)(2,1)S(1)}, bf16[16,2048]{1,0:T(8,128)(2,1)S(1)}, u32[]{:S(2)}, u32[]{:S(2)}) collective-permute-start(bf16[16,2048]{1,0:T(8,128)(2,1)S(1)} %last_sums.1.h_ref), channel_id=1, source_target_pairs={{0,2},{1,3},{2,0},{3,1},{4,6},{5,7},{6,4},{7,5},{8,10},{9,11},{10,... | collective-permute-start | bytes 196616 | tf_op jit(solution)/shard_map/ppermute | solution.py:489
  64.1 7.6 %collective-permute-start.17 = (bf16[64,2048]{1,0:T(8,128)(2,1)S(1)}, bf16[64,2048]{1,0:T(8,128)(2,1)S(1)}, u32[]{:S(2)}, u32[]{:S(2)}) collective-permute-start(bf16[64,2048]{1,0:T(8,128)(2,1)S(1)} %pad_maximum_fusion.2.refs_0_), channel_id=1, source_target_pairs={{0,1},{1,0},{2,3},{3,2},{4,5},{5,4},{6,7},{7,6},{8,9},{9,8},{10,11... | collective-permute-start | bytes 786440 | tf_op jit(solution)/shard_map/ppermute | solution.py:489
  65.3 7.0 %collective-permute-start.18 = (bf16[128,1024]{1,0:T(8,128)(2,1)S(1)}, bf16[128,1024]{1,0:T(8,128)(2,1)S(1)}, u32[]{:S(2)}, u32[]{:S(2)}) collective-permute-start(bf16[128,1024]{1,0:T(8,128)(2,1)S(1)} %broadcast_select_fusion.7), channel_id=1, source_target_pairs={{0,16},{8,24},{16,0},{24,8},{1,17},{9,25},{17,1},{25,9},{2,18},{10... | collective-permute-start | bytes 786440 | tf_op jit(solution)/shard_map/ppermute | solution.py:489
  77.6 49.1 %copy-start.3 = (bf16[128,2048]{1,0:T(8,128)(2,1)}, bf16[128,2048]{1,0:T(8,128)(2,1)S(1)}, u32[]{:S(2)}) copy-start(bf16[128,2048]{1,0:T(8,128)(2,1)S(1)} %get-tuple-element.133.refs_0_) | copy-start | bytes 1572868
  77.6 49.1 %copy-start.6 = (bf16[128,1024]{1,0:T(8,128)(2,1)}, bf16[128,1024]{1,0:T(8,128)(2,1)S(1)}, u32[]{:S(2)}) copy-start(bf16[128,1024]{1,0:T(8,128)(2,1)S(1)} %get-tuple-element.127.refs_6_) | copy-start | bytes 786436
  77.6 49.1 %copy-start.7 = (bf16[128,1024]{1,0:T(8,128)(2,1)}, bf16[128,1024]{1,0:T(8,128)(2,1)S(1)}, u32[]{:S(2)}) copy-start(bf16[128,1024]{1,0:T(8,128)(2,1)S(1)} %get-tuple-element.117.refs_3_) | copy-start | bytes 786436
  77.6 2.6 %collective-permute-start.20 = (bf16[128,1024]{1,0:T(8,128)(2,1)S(1)}, bf16[128,1024]{1,0:T(8,128)(2,1)S(1)}, u32[]{:S(2)}, u32[]{:S(2)}) collective-permute-start(bf16[128,1024]{1,0:T(8,128)(2,1)S(1)} %get-tuple-element.117.refs_3_), channel_id=1, source_target_pairs={{0,8},{8,0},{16,24},{24,16},{1,9},{9,1},{17,25},{25,17},{2,10},{10... | collective-permute-start | bytes 786440 | tf_op jit(solution)/shard_map/ppermute | solution.py:489
  77.7 8.9 %collective-permute-start.21 = (bf16[64,2048]{1,0:T(8,128)(2,1)}, bf16[64,2048]{1,0:T(8,128)(2,1)S(1)}, u32[]{:S(2)}, u32[]{:S(2)}) collective-permute-start(bf16[64,2048]{1,0:T(8,128)(2,1)} %broadcast_select_fusion.5), channel_id=1, source_target_pairs={{0,16},{8,24},{16,0},{24,8},{1,17},{9,25},{17,1},{25,9},{2,18},{10... | collective-permute-start | bytes 786440 | tf_op jit(solution)/shard_map/ppermute | solution.py:489
  78.5 8.4 %collective-permute-start.19 = (bf16[4,16,2048]{2,1,0:T(8,128)(2,1)S(1)}, bf16[4,16,2048]{2,1,0:T(8,128)(2,1)S(1)}, u32[]{:S(2)}, u32[]{:S(2)}) collective-permute-start(bf16[4,16,2048]{2,1,0:T(8,128)(2,1)S(1)} %get-tuple-element.116), channel_id=1, source_target_pairs={{0,1},{1,0},{2,3},{3,2},{4,5},{5,4},{6,7},{7,6},{8,9},{9,8},{10,11... | collective-permute-start | bytes 786440 | tf_op jit(solution)/shard_map/ppermute | solution.py:489
  80.2 10.5 %collective-permute-start.27 = (bf16[128,1024]{1,0:T(8,128)(2,1)S(1)}, bf16[128,1024]{1,0:T(8,128)(2,1)S(1)}, u32[]{:S(2)}, u32[]{:S(2)}) collective-permute-start(bf16[128,1024]{1,0:T(8,128)(2,1)S(1)} %get-tuple-element.127.refs_6_), channel_id=1, source_target_pairs={{0,8},{8,0},{16,24},{24,16},{1,9},{9,1},{17,25},{25,17},{2,10},{10... | collective-permute-start | bytes 786440 | tf_op jit(solution)/shard_map/ppermute | solution.py:489
  87.6 5.9 %collective-permute-start.22 = (bf16[16,2048]{1,0:T(8,128)(2,1)S(1)}, bf16[16,2048]{1,0:T(8,128)(2,1)S(1)}, u32[]{:S(2)}, u32[]{:S(2)}) collective-permute-start(bf16[16,2048]{1,0:T(8,128)(2,1)S(1)} %get-tuple-element.121), channel_id=1, source_target_pairs={{0,4},{1,5},{2,6},{3,7},{4,0},{5,1},{6,2},{7,3},{8,12},{9,13},{10,... | collective-permute-start | bytes 196616 | tf_op jit(solution)/shard_map/ppermute | solution.py:489
  88.3 11.3 %collective-permute-start.25 = (bf16[64,2048]{1,0:T(8,128)(2,1)S(1)}, bf16[64,2048]{1,0:T(8,128)(2,1)S(1)}, u32[]{:S(2)}, u32[]{:S(2)}) collective-permute-start(bf16[64,2048]{1,0:T(8,128)(2,1)S(1)} %broadcast_select_fusion.2.refs_10_), channel_id=1, source_target_pairs={{0,1},{1,0},{2,3},{3,2},{4,5},{5,4},{6,7},{7,6},{8,9},{9,8},{10,11... | collective-permute-start | bytes 786440 | tf_op jit(solution)/shard_map/ppermute | solution.py:489
  90.1 9.5 %collective-permute-start.26 = (bf16[128,1024]{1,0:T(8,128)(2,1)S(1)}, bf16[128,1024]{1,0:T(8,128)(2,1)S(1)}, u32[]{:S(2)}, u32[]{:S(2)}) collective-permute-start(bf16[128,1024]{1,0:T(8,128)(2,1)S(1)} %broadcast_select_fusion.4), channel_id=1, source_target_pairs={{0,16},{8,24},{16,0},{24,8},{1,17},{9,25},{17,1},{25,9},{2,18},{10... | collective-permute-start | bytes 786440 | tf_op jit(solution)/shard_map/ppermute | solution.py:489
  90.7 11.4 %collective-permute-start.33 = (bf16[128,2048]{1,0:T(8,128)(2,1)S(1)}, bf16[128,2048]{1,0:T(8,128)(2,1)S(1)}, u32[]{:S(2)}, u32[]{:S(2)}) collective-permute-start(bf16[128,2048]{1,0:T(8,128)(2,1)S(1)} %get-tuple-element.133.refs_0_), channel_id=1, source_target_pairs={{0,8},{8,0},{16,24},{24,16},{1,9},{9,1},{17,25},{25,17},{2,10},{10... | collective-permute-start | bytes 1572872 | tf_op jit(solution)/shard_map/ppermute | solution.py:489
  90.8 4.5 %collective-permute-start.23 = (bf16[16,2048]{1,0:T(8,128)(2,1)S(1)}, bf16[16,2048]{1,0:T(8,128)(2,1)S(1)}, u32[]{:S(2)}, u32[]{:S(2)}) collective-permute-start(bf16[16,2048]{1,0:T(8,128)(2,1)S(1)} %get-tuple-element.122), channel_id=1, source_target_pairs={{0,2},{1,3},{2,0},{3,1},{4,6},{5,7},{6,4},{7,5},{8,10},{9,11},{10,... | collective-permute-start | bytes 196616 | tf_op jit(solution)/shard_map/ppermute | solution.py:489
  93.5 6.1 %collective-permute-start.24 = (bf16[16,2048]{1,0:T(8,128)(2,1)S(1)}, bf16[16,2048]{1,0:T(8,128)(2,1)S(1)}, u32[]{:S(2)}, u32[]{:S(2)}) collective-permute-start(bf16[16,2048]{1,0:T(8,128)(2,1)S(1)} %get-tuple-element.123), channel_id=1, source_target_pairs={{0,6},{1,7},{2,4},{3,5},{4,2},{5,3},{6,0},{7,1},{8,14},{9,15},{10,... | collective-permute-start | bytes 196616 | tf_op jit(solution)/shard_map/ppermute | solution.py:489
  99.8 1.3 collective-permute-start.28
  99.9 10.8 %collective-permute-start.32 = (bf16[128,1024]{1,0:T(8,128)(2,1)S(1)}, bf16[128,1024]{1,0:T(8,128)(2,1)S(1)}, u32[]{:S(2)}, u32[]{:S(2)}) collective-permute-start(bf16[128,1024]{1,0:T(8,128)(2,1)S(1)} %broadcast_select_fusion.3), channel_id=1, source_target_pairs={{0,16},{8,24},{16,0},{24,8},{1,17},{9,25},{17,1},{25,9},{2,18},{10... | collective-permute-start | bytes 786440 | tf_op jit(solution)/shard_map/ppermute | solution.py:489
  101.2 8.9 %collective-permute-start.34 = (bf16[16,2048]{1,0:T(8,128)(2,1)S(1)}, bf16[16,2048]{1,0:T(8,128)(2,1)S(1)}, u32[]{:S(2)}, u32[]{:S(2)}) collective-permute-start(bf16[16,2048]{1,0:T(8,128)(2,1)S(1)} %broadcast_select_fusion.9), channel_id=1, source_target_pairs={{0,16},{8,24},{16,0},{24,8},{1,17},{9,25},{17,1},{25,9},{2,18},{10... | collective-permute-start | bytes 196616 | tf_op jit(solution)/shard_map/ppermute | solution.py:489
  102.2 7.9 %collective-permute-start.31 = (bf16[16,2048]{1,0:T(8,128)(2,1)S(1)}, bf16[16,2048]{1,0:T(8,128)(2,1)S(1)}, u32[]{:S(2)}, u32[]{:S(2)}) collective-permute-start(bf16[16,2048]{1,0:T(8,128)(2,1)S(1)} %last_back.1), channel_id=1, source_target_pairs={{0,6},{1,7},{2,4},{3,5},{4,2},{5,3},{6,0},{7,1},{8,14},{9,15},{10,... | collective-permute-start | bytes 196616 | tf_op jit(solution)/shard_map/ppermute | solution.py:489
  103.8 6.9 %collective-permute-start.30 = (bf16[16,2048]{1,0:T(8,128)(2,1)S(1)}, bf16[16,2048]{1,0:T(8,128)(2,1)S(1)}, u32[]{:S(2)}, u32[]{:S(2)}) collective-permute-start(bf16[16,2048]{1,0:T(8,128)(2,1)S(1)} %last_back.1), channel_id=1, source_target_pairs={{0,4},{1,5},{2,6},{3,7},{4,0},{5,1},{6,2},{7,3},{8,12},{9,13},{10,... | collective-permute-start | bytes 196616 | tf_op jit(solution)/shard_map/ppermute | solution.py:489
  103.8 6.9 %collective-permute-start.29 = (bf16[16,2048]{1,0:T(8,128)(2,1)S(1)}, bf16[16,2048]{1,0:T(8,128)(2,1)S(1)}, u32[]{:S(2)}, u32[]{:S(2)}) collective-permute-start(bf16[16,2048]{1,0:T(8,128)(2,1)S(1)} %last_back.1), channel_id=1, source_target_pairs={{0,2},{1,3},{2,0},{3,1},{4,6},{5,7},{6,4},{7,5},{8,10},{9,11},{10,... | collective-permute-start | bytes 196616 | tf_op jit(solution)/shard_map/ppermute | solution.py:489
  110.7 14.0 %collective-permute-start.36 = (bf16[128,2048]{1,0:T(8,128)(2,1)S(1)}, bf16[128,2048]{1,0:T(8,128)(2,1)S(1)}, u32[]{:S(2)}, u32[]{:S(2)}) collective-permute-start(bf16[128,2048]{1,0:T(8,128)(2,1)S(1)} %broadcast_select_fusion), channel_id=1, source_target_pairs={{0,16},{8,24},{16,0},{24,8},{1,17},{9,25},{17,1},{25,9},{2,18},{10... | collective-permute-start | bytes 1572872 | tf_op jit(solution)/shard_map/ppermute | solution.py:489
  112.0 8.1 %collective-permute-start.35 = (bf16[64,2048]{1,0:T(8,128)(2,1)S(1)}, bf16[64,2048]{1,0:T(8,128)(2,1)S(1)}, u32[]{:S(2)}, u32[]{:S(2)}) collective-permute-start(bf16[64,2048]{1,0:T(8,128)(2,1)S(1)} %pad_maximum_fusion.3.refs_0_.refs_9_), channel_id=1, source_target_pairs={{0,1},{1,0},{2,3},{3,2},{4,5},{5,4},{6,7},{7,6},{8,9},{9,8},{10,11... | collective-permute-start | bytes 786440 | tf_op jit(solution)/shard_map/ppermute | solution.py:489
  113.8 10.9 %collective-permute-start.39 = (bf16[16,2048]{1,0:T(8,128)(2,1)S(1)}, bf16[16,2048]{1,0:T(8,128)(2,1)S(1)}, u32[]{:S(2)}, u32[]{:S(2)}) collective-permute-start(bf16[16,2048]{1,0:T(8,128)(2,1)S(1)} %broadcast_select_fusion.8), channel_id=1, source_target_pairs={{0,6},{1,7},{2,4},{3,5},{4,2},{5,3},{6,0},{7,1},{8,14},{9,15},{10,... | collective-permute-start | bytes 196616 | tf_op jit(solution)/shard_map/ppermute | solution.py:489
  115.2 9.5 %collective-permute-start.38 = (bf16[16,2048]{1,0:T(8,128)(2,1)S(1)}, bf16[16,2048]{1,0:T(8,128)(2,1)S(1)}, u32[]{:S(2)}, u32[]{:S(2)}) collective-permute-start(bf16[16,2048]{1,0:T(8,128)(2,1)S(1)} %broadcast_select_fusion.8), channel_id=1, source_target_pairs={{0,4},{1,5},{2,6},{3,7},{4,0},{5,1},{6,2},{7,3},{8,12},{9,13},{10,... | collective-permute-start | bytes 196616 | tf_op jit(solution)/shard_map/ppermute | solution.py:489
  115.4 9.3 %collective-permute-start.37 = (bf16[16,2048]{1,0:T(8,128)(2,1)S(1)}, bf16[16,2048]{1,0:T(8,128)(2,1)S(1)}, u32[]{:S(2)}, u32[]{:S(2)}) collective-permute-start(bf16[16,2048]{1,0:T(8,128)(2,1)S(1)} %broadcast_select_fusion.8), channel_id=1, source_target_pairs={{0,2},{1,3},{2,0},{3,1},{4,6},{5,7},{6,4},{7,5},{8,10},{9,11},{10,... | collective-permute-start | bytes 196616 | tf_op jit(solution)/shard_map/ppermute | solution.py:489
  124.7 1.9 %collective-permute-start.40 = (bf16[128,1024]{1,0:T(8,128)(2,1)S(1)}, bf16[128,1024]{1,0:T(8,128)(2,1)S(1)}, u32[]{:S(2)}, u32[]{:S(2)}) collective-permute-start(bf16[128,1024]{1,0:T(8,128)(2,1)S(1)} %low_grad.1.refs_3_), channel_id=1, source_target_pairs={{0,8},{8,0},{16,24},{24,16},{1,9},{9,1},{17,25},{25,17},{2,10},{10... | collective-permute-start | bytes 786440 | tf_op jit(solution)/shard_map/ppermute | solution.py:489
  124.9 10.5 %collective-permute-start.42 = (bf16[64,2048]{1,0:T(8,128)(2,1)S(1)}, bf16[64,2048]{1,0:T(8,128)(2,1)S(1)}, u32[]{:S(2)}, u32[]{:S(2)}) collective-permute-start(bf16[64,2048]{1,0:T(8,128)(2,1)S(1)} %pad_maximum_fusion.4.refs_11_), channel_id=1, source_target_pairs={{0,1},{1,0},{2,3},{3,2},{4,5},{5,4},{6,7},{7,6},{8,9},{9,8},{10,11... | collective-permute-start | bytes 786440 | tf_op jit(solution)/shard_map/ppermute | solution.py:489
  126.7 8.6 %collective-permute-start.41 = (bf16[128,1024]{1,0:T(8,128)(2,1)S(1)}, bf16[128,1024]{1,0:T(8,128)(2,1)S(1)}, u32[]{:S(2)}, u32[]{:S(2)}) collective-permute-start(bf16[128,1024]{1,0:T(8,128)(2,1)S(1)} %broadcast_select_fusion.6), channel_id=1, source_target_pairs={{0,16},{8,24},{16,0},{24,8},{1,17},{9,25},{17,1},{25,9},{2,18},{10... | collective-permute-start | bytes 786440 | tf_op jit(solution)/shard_map/ppermute | solution.py:489
  (25 other events, 432.5 us)
